TPU v7x, 256 devices: a whole 4x4x8 slice. The times are simulated.
256 devices in a mesh: trainer: 8 (over y_hi, x), table: 32 (over y_lo, z, core).
Axes of the slice: x: 4, y: 4 (y_hi: 2, y_lo: 2; y = y_hi * 2 + y_lo), z: 8, core: 2. Of those that a mesh axis runs over, the one named last changes fastest.
Arguments:
- slot_ids: int32 [65536, 32], P(('trainer', 'table')), may hold values from 0 to 1023, as said below
- labels: int32 [65536], P(('trainer', 'table')), may hold values 0 or 1
- cache_rows: float32 [262144, 256], P(('trainer', 'table')), may hold values from -3 to 3
- cache_accum: float32 [262144], P(('trainer', 'table')), may hold values from 0.01 to 1
- table_rows: float32 [262144, 256], P(('trainer', 'table')), may hold values from -3 to 3
- table_accum: float32 [262144], P(('trainer', 'table')), may hold values from 0.01 to 1
- miss_dest: int32 [16384, 2], P(('trainer', 'table')), may hold values from 0 to 1023, as said below
- evict_slot: int32 [16384], P(('trainer', 'table')), may hold values from 0 to 1023, as said below
- evict_dest: int32 [16384, 2], P(('trainer', 'table')), may hold values from 0 to 1023, as said below
- proj_u: bfloat16 [2048, 256], replicated, may hold values from -0.375 to 0.375
- proj_v: bfloat16 [2048, 256], replicated, may hold values from -0.125 to 0.125
- cross_bias: float32 [2048], replicated, may hold values from -3 to 3
- head: float32 [2048], replicated, may hold values from 0.002 to 0.05
Outputs:
- new_cache_rows: float32 [262144, 256], P(('trainer', 'table'))
- new_cache_accum: float32 [262144], P(('trainer', 'table'))
- new_table_rows: float32 [262144, 256], P(('trainer', 'table'))
- new_table_accum: float32 [262144], P(('trainer', 'table'))
- clipped_proj: float32 [2, 2048, 256], replicated
- clipped_vecs: float32 [2, 2048], replicated
- loss: float32 [], replicated
Inputs may be any that keep to these rules, and one draw needn't show every extreme that they name: `slot_ids`: no sample names a slot that its device evicts. `evict_slot`: the 64 slots of one device are distinct. `evict_dest`: column 0 is an owner's index along table, column 1 a row of that owner. No owned row is named twice among the devices of one trainer index. One device names one owner at most 6 times; in every draw some owner is named 6 times by every device of its trainer index. `miss_dest`: column 0 is an owner's index along table, column 1 a row of that owner. One device names one owner at most 6 times; in every draw some owner is named 6 times by every device of its trainer index.
All inputs are finite; a program needn't handle non-finite values. No bound on the sum of `labels` on one device may be relied on, other than what follows from the above.
Results may differ from a plain program's by a relative error of at most 0.0024.
Values sent between devices are 32-bit elements; how exact they have to be, the bound alone decides.
No kernel may reach another device: no remote copies, remote signals or barrier semaphores. Data moves between devices by JAX's collectives and lax.ppermute only.
A program may use at most 64 MiB of HBM per device.

v0:
```python
import jax
import jax.numpy as jnp
from jax import lax
from jax.sharding import PartitionSpec as P

EPS = 1e-06
ETA = 0.05


def bucket_place(owner, owners, slots_per):
    marks = (owner[:, None] == jnp.arange(owners, dtype=jnp.int32)[None, :]).astype(jnp.int32)
    before = jnp.cumsum(marks, axis=0) - marks
    rank = jnp.sum(before * marks, axis=1)
    return owner * slots_per + rank


def store_rows(table_rows, table_accum, rows_in, accum_in, ids_in):
    width = table_rows.shape[1]
    flat_ids = ids_in.reshape(-1)
    table_new = table_rows.at[flat_ids].set(rows_in.reshape(-1, width), mode="drop")
    accum_new = table_accum.at[flat_ids].set(accum_in.reshape(-1), mode="drop")
    return (table_new, accum_new)


def shards(
    slot_ids,
    labels,
    cache_rows,
    cache_accum,
    table_rows,
    table_accum,
    miss_dest,
    evict_slot,
    evict_dest,
    proj_u,
    proj_v,
    cross_bias,
    head,
):
    owners = lax.axis_size("table")
    listed = evict_slot.shape[0]
    slots_per = 3 * listed // owners
    width = cache_rows.shape[1]
    owned = table_rows.shape[0]
    cells = cache_rows.shape[0]
    total_slots = owners * slots_per
    out_place = bucket_place(evict_dest[:, 0], owners, slots_per)
    leaving_rows = jnp.take(cache_rows, evict_slot, axis=0)
    leaving_accum = jnp.take(cache_accum, evict_slot)
    send_rows = (
        jnp.zeros((total_slots, width), jnp.float32)
        .at[out_place]
        .set(leaving_rows)
        .reshape(owners, slots_per, width)
    )
    send_accum = (
        jnp.zeros((total_slots,), jnp.float32)
        .at[out_place]
        .set(leaving_accum)
        .reshape(owners, slots_per)
    )
    send_ids = (
        jnp.full((total_slots,), owned, jnp.int32)
        .at[out_place]
        .set(evict_dest[:, 1])
        .reshape(owners, slots_per)
    )
    in_place = bucket_place(miss_dest[:, 0], owners, slots_per)
    ask_ids = (
        jnp.zeros((total_slots,), jnp.int32)
        .at[in_place]
        .set(miss_dest[:, 1])
        .reshape(owners, slots_per)
    )
    arrived = (
        lax.all_to_all(send_rows, "table", split_axis=0, concat_axis=0, tiled=True),
        lax.all_to_all(send_accum, "table", split_axis=0, concat_axis=0, tiled=True),
        lax.all_to_all(send_ids, "table", split_axis=0, concat_axis=0, tiled=True),
    )
    table_new, accum_table = store_rows(table_rows, table_accum, arrived[0], arrived[1], arrived[2])
    asked = lax.all_to_all(ask_ids, "table", split_axis=0, concat_axis=0, tiled=True)
    back_rows = lax.all_to_all(
        jnp.take(table_new, asked, axis=0), "table", split_axis=0, concat_axis=0, tiled=True
    )
    back_accum = lax.all_to_all(
        jnp.take(accum_table, asked), "table", split_axis=0, concat_axis=0, tiled=True
    )
    fetched_rows = jnp.take(back_rows.reshape(total_slots, width), in_place, axis=0)
    fetched_accum = jnp.take(back_accum.reshape(total_slots), in_place)
    count = slot_ids.shape[0]
    feats = proj_u.shape[0] // width
    looks = slot_ids.shape[1] // feats
    pieces = []
    for feature in range(feats):
        picked = slot_ids[:, feature * looks : (feature + 1) * looks]
        pieces.append(jnp.sum(jnp.take(cache_rows, picked, axis=0), axis=1))
    pooled = jnp.concatenate(pieces, axis=1).astype(jnp.bfloat16)
    latent = jnp.dot(pooled, proj_v, preferred_element_type=jnp.float32).astype(jnp.bfloat16)
    shifted = jnp.dot(latent, proj_u.T, preferred_element_type=jnp.float32) + cross_bias
    pooled_f = pooled.astype(jnp.float32)
    crossed = pooled_f * shifted + pooled_f
    logit = jnp.dot(crossed, head, precision=lax.Precision.HIGHEST)
    target = labels.astype(jnp.float32)
    objective = jnp.sum(jax.nn.softplus(logit) - target * logit)
    dlogit = jax.nn.sigmoid(logit) - target
    dcross = dlogit[:, None] * head[None, :]
    dhead = jnp.dot(dlogit, crossed, precision=lax.Precision.HIGHEST)
    dlift_full = dcross * pooled_f
    dbias = jnp.sum(dlift_full, axis=0)
    dlift = dlift_full.astype(jnp.bfloat16)
    grad_u = lax.dot_general(
        dlift, latent, (((0,), (0,)), ((), ())), preferred_element_type=jnp.float32
    )
    dlatent = jnp.dot(dlift, proj_u, preferred_element_type=jnp.float32).astype(jnp.bfloat16)
    grad_v = lax.dot_general(
        pooled, dlatent, (((0,), (0,)), ((), ())), preferred_element_type=jnp.float32
    )
    dpooled = (
        dcross * (shifted + 1.0) + jnp.dot(dlatent, proj_v.T, preferred_element_type=jnp.float32)
    ).astype(jnp.bfloat16)
    slot_range = jnp.arange(cells, dtype=jnp.int32)
    row_grad = jnp.zeros((cells, width), jnp.float32)
    for feature in range(feats):
        counts = jnp.zeros((count, cells), jnp.bfloat16)
        for lookup in range(looks):
            column = slot_ids[:, feature * looks + lookup]
            counts = counts + (column[:, None] == slot_range[None, :]).astype(jnp.bfloat16)
        block = dpooled[:, feature * width : (feature + 1) * width]
        row_grad = row_grad + lax.dot_general(
            counts, block, (((0,), (0,)), ((), ())), preferred_element_type=jnp.float32
        )
    accum_new = cache_accum + jnp.mean(row_grad * row_grad, axis=1)
    rows_new = cache_rows - ETA * row_grad * lax.rsqrt(accum_new)[:, None]
    rows_new = rows_new.at[evict_slot].set(fetched_rows)
    accum_new = accum_new.at[evict_slot].set(fetched_accum)
    grad_uv = jnp.stack([grad_u, grad_v])
    grad_vecs = jnp.stack([dbias, dhead])
    samples_all = count * lax.axis_size("trainer") * lax.axis_size("table")
    proj_sums, vec_sums, total = lax.psum((grad_uv, grad_vecs, objective), ("trainer", "table"))
    clipped_proj = proj_sums * lax.rsqrt(
        jnp.mean(proj_sums * proj_sums, axis=(1, 2), keepdims=True) + EPS
    )
    clipped_vecs = vec_sums * lax.rsqrt(jnp.mean(vec_sums * vec_sums, axis=1, keepdims=True) + EPS)
    loss = total / samples_all
    return (rows_new, accum_new, table_new, accum_table, clipped_proj, clipped_vecs, loss)


def solution(mesh):
    placed = (
        P(("trainer", "table"), None),
        P(("trainer", "table")),
        P(("trainer", "table"), None),
        P(("trainer", "table")),
        P(("trainer", "table"), None),
        P(("trainer", "table")),
        P(("trainer", "table"), None),
        P(("trainer", "table")),
        P(("trainer", "table"), None),
        P(),
        P(),
        P(),
        P(),
    )
    return jax.shard_map(
        shards,
        mesh=mesh,
        in_specs=placed,
        out_specs=(
            P(("trainer", "table"), None),
            P(("trainer", "table")),
            P(("trainer", "table"), None),
            P(("trainer", "table")),
            P(),
            P(),
            P(),
        ),
        check_vma=False,
    )
```

profile of v0, /device:TPU:3, one launch (start us, length us, event | category | flops | bytes accessed | tf_op | source)
XLA Modules:
  0.0 384.4 jit_solution(4396983963180084820)
XLA Ops:
  9.8 10.3 %all-to-all-start.1 = ((s32[32,1,6]{2,1,0:T(1,128)}), s32[32,1,6]{2,1,0:T(1,128)S(1)}, u32[]{:S(2)}, u32[]{:S(2)}) async-start(s32[32,1,6]{2,1,0:T(1,128)} %bitcast.45), calls=%async_computation.1 | async-start | bytes 32768 | tf_op jit(solution)/shard_map/all_to_all | solution.py:78
  23.9 3.7 gather_fusion.9
  28.9 4.7 %gather_fusion.7 = f32[1024,256]{1,0:T(8,128)} fusion(f32[1024,256]{1,0:T(8,128)S(1)} %copy-done.3, s32[1024]{0:T(1024)S(1)} %get-tuple-element.84), kind=kCustom, calls=%fused_computation.3.clone | custom fusion | bytes 2101248 | tf_op jit(solution)/shard_map/jit(_take)/gather | solution.py:96
  33.6 2.5 reshape.369
  36.1 4.7 %gather_fusion.5 = f32[1024,256]{1,0:T(8,128)} fusion(f32[1024,256]{1,0:T(8,128)S(1)} %copy-done.3, s32[1024]{0:T(1024)S(1)} %get-tuple-element.86), kind=kCustom, calls=%fused_computation.1.clone | custom fusion | bytes 2101248 | tf_op jit(solution)/shard_map/jit(_take)/gather | solution.py:96
  40.8 2.5 reshape.361
  43.3 4.7 %gather_fusion.4 = f32[1024,256]{1,0:T(8,128)} fusion(f32[1024,256]{1,0:T(8,128)S(1)} %copy-done.3, s32[1024]{0:T(1024)S(1)} %broadcast_clamp_fusion.7), kind=kCustom, calls=%fused_computation.clone | custom fusion | bytes 2101248 | tf_op jit(solution)/shard_map/jit(_take)/gather | solution.py:96
  48.0 1.5 reshape.357
  49.5 1.5 select_reduce_fusion.7
  51.0 4.7 %gather_fusion.6 = f32[1024,256]{1,0:T(8,128)} fusion(f32[1024,256]{1,0:T(8,128)S(1)} %copy-done.3, s32[1024]{0:T(1024)S(1)} %get-tuple-element.85), kind=kCustom, calls=%fused_computation.2.clone | custom fusion | bytes 2101248 | tf_op jit(solution)/shard_map/jit(_take)/gather | solution.py:96
  55.7 2.5 reshape.365
  58.2 4.7 %gather_fusion.8 = f32[1024,256]{1,0:T(8,128)} fusion(f32[1024,256]{1,0:T(8,128)S(1)} %copy-done.3, s32[1024]{0:T(1024)S(1)} %get-tuple-element.83), kind=kCustom, calls=%fused_computation.4.clone | custom fusion | bytes 2101248 | tf_op jit(solution)/shard_map/jit(_take)/gather | solution.py:96
  62.9 2.6 reshape.373
  65.4 4.7 %gather_fusion.10 = f32[1024,256]{1,0:T(8,128)} fusion(f32[1024,256]{1,0:T(8,128)S(1)} %copy-done.3, s32[1024]{0:T(1024)S(1)} %get-tuple-element.81), kind=kCustom, calls=%fused_computation.6.clone | custom fusion | bytes 2101248 | tf_op jit(solution)/shard_map/jit(_take)/gather | solution.py:96
  70.1 2.5 reshape.381
  72.6 4.7 %gather_fusion.11 = f32[1024,256]{1,0:T(8,128)} fusion(f32[1024,256]{1,0:T(8,128)S(1)} %copy-done.3, s32[1024]{0:T(1024)S(1)} %get-tuple-element.80), kind=kCustom, calls=%fused_computation.7.clone | custom fusion | bytes 2101248 | tf_op jit(solution)/shard_map/jit(_take)/gather | solution.py:96
  77.3 2.5 reshape.385
  79.8 2.7 select_reduce_fusion.2
  82.5 2.6 select_reduce_fusion.4
  85.2 1.5 select_reduce_fusion.6
  86.7 1.5 select_reduce_fusion.5
  88.3 1.5 select_reduce_fusion.3
  89.8 1.5 select_reduce_fusion.1
  91.4 2.0 select_reduce_fusion
  94.6 1.8 fusion.4
  98.7 2.3 pad_maximum_fusion
  101.4 3.4 fusion
  105.2 2.9 fusion.3
  108.1 76.9 %all-reduce = (f32[2,2048]{1,0:T(2,128)S(1)}, f32[]{:T(128)}) all-reduce(f32[2,2048]{1,0:T(2,128)S(1)} %pad_maximum_fusion.1, f32[]{:T(128)} %get-tuple-element.71), channel_id=1, replica_groups=mesh['trainer'=8,'table'=32] {'trainer','table'}, use_global_device_ids=true, to_apply=%region_24.26 | all-reduce | flops 4097 | bytes 32776 | tf_op jit(solution)/shard_map/psum | solution.py:139
  185.8 1.7 fusion.87
  192.4 1.8 multiply_reduce_fusion.1
  196.4 6.0 %all-to-all-start = ((s32[32,1,6]{2,1,0:T(1,128)}), s32[32,1,6]{2,1,0:T(1,128)S(1)}, u32[]{:S(2)}, u32[]{:S(2)}) async-start(s32[32,1,6]{2,1,0:T(1,128)} %bitcast.39), calls=%async_computation | async-start | bytes 32768 | tf_op jit(solution)/shard_map/all_to_all | solution.py:81
  206.0 4.2 %all-to-all-done = s32[32,1,6]{2,1,0:T(1,128)S(1)} async-done(((s32[32,1,6]{2,1,0:T(1,128)}), s32[32,1,6]{2,1,0:T(1,128)S(1)}, u32[]{:S(2)}, u32[]{:S(2)}) %all-to-all-start) | async-done | bytes 800 | tf_op jit(solution)/shard_map/all_to_all | solution.py:81
  210.3 4.2 %all-to-all-start.4 = ((f32[32,1,6]{2,1,0:T(1,128)}), f32[32,1,6]{2,1,0:T(1,128)S(1)}, u32[]{:S(2)}, u32[]{:S(2)}) async-start(f32[32,1,6]{2,1,0:T(1,128)} %bitcast.51), calls=%async_computation.4 | async-start | bytes 32768 | tf_op jit(solution)/shard_map/all_to_all | solution.py:77
  215.9 6.5 %all-to-all-done.4 = f32[32,1,6]{2,1,0:T(1,128)S(1)} async-done(((f32[32,1,6]{2,1,0:T(1,128)}), f32[32,1,6]{2,1,0:T(1,128)S(1)}, u32[]{:S(2)}, u32[]{:S(2)}) %all-to-all-start.4) | async-done | bytes 800 | tf_op jit(solution)/shard_map/all_to_all | solution.py:77
  222.5 4.3 %all-to-all-start.2 = ((f32[32,6,256]{2,1,0:T(8,128)}), f32[32,6,256]{2,1,0:T(8,128)S(1)}, u32[]{:S(2)}, u32[]{:S(2)}) async-start(f32[32,6,256]{2,1,0:T(8,128)} %reshape.150), calls=%async_computation.2 | async-start | bytes 524288 | tf_op jit(solution)/shard_map/all_to_all | solution.py:76
  231.3 7.4 %all-to-all-done.2 = f32[32,6,256]{2,1,0:T(8,128)S(1)} async-done(((f32[32,6,256]{2,1,0:T(8,128)}), f32[32,6,256]{2,1,0:T(8,128)S(1)}, u32[]{:S(2)}, u32[]{:S(2)}) %all-to-all-start.2) | async-done | bytes 196640 | tf_op jit(solution)/shard_map/all_to_all | solution.py:76
  238.7 5.2 %all-to-all-start.5 = ((f32[32,1,6]{2,1,0:T(1,128)}), f32[32,1,6]{2,1,0:T(1,128)S(1)}, u32[]{:S(2)}, u32[]{:S(2)}) async-start(f32[32,1,6]{2,1,0:T(1,128)} %bitcast.52), calls=%async_computation.5 | async-start | bytes 32768 | tf_op jit(solution)/shard_map/all_to_all | solution.py:85
  244.5 2.2 scatter_fusion
  248.3 1.7 broadcast_select_fusion
  250.1 1.7 all-to-all-done.5
  251.8 6.7 %all-to-all-start.3 = ((f32[32,6,256]{2,1,0:T(8,128)}), f32[32,6,256]{2,1,0:T(8,128)S(1)}, u32[]{:S(2)}, u32[]{:S(2)}) async-start(f32[32,6,256]{2,1,0:T(8,128)} %broadcast_select_fusion), calls=%async_computation.3 | async-start | bytes 524288 | tf_op jit(solution)/shard_map/all_to_all | solution.py:82
  258.5 2.4 multiply_subtract_fusion
  260.9 1.6 copy.69
  265.5 5.0 %all-to-all-done.3 = f32[32,6,256]{2,1,0:T(8,128)S(1)} async-done(((f32[32,6,256]{2,1,0:T(8,128)}), f32[32,6,256]{2,1,0:T(8,128)S(1)}, u32[]{:S(2)}, u32[]{:S(2)}) %all-to-all-start.3) | async-done | bytes 196640 | tf_op jit(solution)/shard_map/all_to_all | solution.py:82
  272.0 98.5 %all-reduce.3.cloned.1.call-done = f32[2,2048,256]{2,1,0:T(8,128)} async-done(((f32[2,2048,256]{2,1,0:T(8,128)}), f32[2,2048,256]{2,1,0:T(8,128)}) %all-reduce.3.cloned.1.call-update) | async-done | bytes 4194320 | tf_op jit(solution)/shard_map/psum | solution.py:139
  370.4 3.0 multiply_reduce_fusion
  373.9 2.4 broadcast_multiply_fusion
  (162 shorter events, 35.5 us)
Async XLA Ops:
  7.2 86.7 %copy-start = (bf16[2048,256]{1,0:T(8,128)(2,1)S(1)}, bf16[2048,256]{1,0:T(8,128)(2,1)}, u32[]{:S(2)}) copy-start(bf16[2048,256]{1,0:T(8,128)(2,1)} %param.24) | copy-start | bytes 3145732
  7.2 13.0 %copy-start.18 = (s32[256,32]{0,1:T(8,128)S(1)}, s32[256,32]{0,1:T(8,128)}, u32[]{:S(2)}) copy-start(s32[256,32]{0,1:T(8,128)} %param.15) | copy-start | bytes 98308
  7.2 13.1 %copy-start.24 = (s32[64]{0:T(128)S(1)}, s32[64]{0:T(128)}, u32[]{:S(2)}) copy-start(s32[64]{0:T(128)} %param.22) | copy-start | bytes 772
  7.2 0.8 copy-start.23
  7.2 16.7 %copy-start.3 = (f32[1024,256]{1,0:T(8,128)S(1)}, f32[1024,256]{1,0:T(8,128)}, u32[]{:S(2)}) copy-start(f32[1024,256]{1,0:T(8,128)} %param.17) | copy-start | bytes 3145732
  9.8 186.6 %all-to-all-start.1 = ((s32[32,1,6]{2,1,0:T(1,128)}), s32[32,1,6]{2,1,0:T(1,128)S(1)}, u32[]{:S(2)}, u32[]{:S(2)}) async-start(s32[32,1,6]{2,1,0:T(1,128)} %bitcast.45), calls=%async_computation.1 | async-start | bytes 32768 | tf_op jit(solution)/shard_map/all_to_all | solution.py:78
  20.1 350.3 %all-reduce.3.cloned.1.call-start = ((), (), s32[]{:S(2)}) async-start(), calls=%async_computation.6 | async-start | bytes 8388608 | tf_op jit(solution)/shard_map/psum | solution.py:139
  79.8 5.4 %copy-start.11 = (f32[256,4,256]{2,1,0:T(4,128)S(1)}, f32[256,4,256]{2,1,0:T(4,128)}, u32[]{:S(2)}) copy-start(f32[256,4,256]{2,1,0:T(4,128)} %reshape.361) | copy-start | bytes 3145732
  79.8 6.9 %copy-start.15 = (f32[256,4,256]{2,1,0:T(4,128)S(1)}, f32[256,4,256]{2,1,0:T(4,128)}, u32[]{:S(2)}) copy-start(f32[256,4,256]{2,1,0:T(4,128)} %reshape.365) | copy-start | bytes 3145732
  82.5 5.8 %copy-start.14 = (f32[256,4,256]{2,1,0:T(4,128)S(1)}, f32[256,4,256]{2,1,0:T(4,128)}, u32[]{:S(2)}) copy-start(f32[256,4,256]{2,1,0:T(4,128)} %reshape.373) | copy-start | bytes 3145732
  86.7 3.2 copy-start.12
  88.2 3.2 copy-start.13
  88.3 5.1 %copy-start.10 = (bf16[2048,256]{1,0:T(8,128)(2,1)S(1)}, bf16[2048,256]{1,0:T(8,128)(2,1)}, u32[]{:S(2)}) copy-start(bf16[2048,256]{1,0:T(8,128)(2,1)} %param.25) | copy-start | bytes 3145732
  91.4 2.5 copy-start.20
  93.9 0.7 copy-start.19
  94.4 3.2 copy-start.6
  94.4 2.0 copy-start.22
  101.4 3.4 copy-start.21
  108.1 79.5 %copy-start.16 = (bf16[256,2048]{1,0:T(8,128)(2,1)S(1)}, bf16[256,2048]{1,0:T(8,128)(2,1)}, u32[]{:S(2)}) copy-start(bf16[256,2048]{1,0:T(8,128)(2,1)} %fusion) | copy-start | bytes 3145732
  192.4 1.8 copy-start.5
  196.4 13.9 %all-to-all-start = ((s32[32,1,6]{2,1,0:T(1,128)}), s32[32,1,6]{2,1,0:T(1,128)S(1)}, u32[]{:S(2)}, u32[]{:S(2)}) async-start(s32[32,1,6]{2,1,0:T(1,128)} %bitcast.39), calls=%async_computation | async-start | bytes 32768 | tf_op jit(solution)/shard_map/all_to_all | solution.py:81
  202.4 25.7 %copy-start.2 = (f32[1024]{0:T(1024)S(1)}, f32[1024]{0:T(1024)}, u32[]{:S(2)}) copy-start(f32[1024]{0:T(1024)} %param.20) | copy-start | bytes 12292
  210.3 12.2 %all-to-all-start.4 = ((f32[32,1,6]{2,1,0:T(1,128)}), f32[32,1,6]{2,1,0:T(1,128)S(1)}, u32[]{:S(2)}, u32[]{:S(2)}) async-start(f32[32,1,6]{2,1,0:T(1,128)} %bitcast.51), calls=%async_computation.4 | async-start | bytes 32768 | tf_op jit(solution)/shard_map/all_to_all | solution.py:77
  222.5 16.2 %all-to-all-start.2 = ((f32[32,6,256]{2,1,0:T(8,128)}), f32[32,6,256]{2,1,0:T(8,128)S(1)}, u32[]{:S(2)}, u32[]{:S(2)}) async-start(f32[32,6,256]{2,1,0:T(8,128)} %reshape.150), calls=%async_computation.2 | async-start | bytes 524288 | tf_op jit(solution)/shard_map/all_to_all | solution.py:76
  229.3 1.2 copy-start.1
  229.4 15.2 %copy-start.8 = (f32[1024,256]{1,0:T(8,128)S(1)}, f32[1024,256]{1,0:T(8,128)}, u32[]{:S(2)}) copy-start(f32[1024,256]{1,0:T(8,128)} %param.19) | copy-start | bytes 3145732
  238.7 13.1 %all-to-all-start.5 = ((f32[32,1,6]{2,1,0:T(1,128)}), f32[32,1,6]{2,1,0:T(1,128)S(1)}, u32[]{:S(2)}, u32[]{:S(2)}) async-start(f32[32,1,6]{2,1,0:T(1,128)} %bitcast.52), calls=%async_computation.5 | async-start | bytes 32768 | tf_op jit(solution)/shard_map/all_to_all | solution.py:85
  246.7 14.2 %copy-start.7 = (f32[1024,256]{1,0:T(8,128)}, f32[1024,256]{1,0:T(8,128)S(1)}, u32[]{:S(2)}) copy-start(f32[1024,256]{1,0:T(8,128)S(1)} %scatter_fusion) | copy-start | bytes 3145732
  251.8 18.8 %all-to-all-start.3 = ((f32[32,6,256]{2,1,0:T(8,128)}), f32[32,6,256]{2,1,0:T(8,128)S(1)}, u32[]{:S(2)}, u32[]{:S(2)}) async-start(f32[32,6,256]{2,1,0:T(8,128)} %broadcast_select_fusion), calls=%async_computation.3 | async-start | bytes 524288 | tf_op jit(solution)/shard_map/all_to_all | solution.py:82
  265.5 107.9 %copy-start.4 = (f32[1024]{0:T(1024)}, f32[1024]{0:T(1024)S(1)}, u32[]{:S(2)}) copy-start(f32[1024]{0:T(1024)S(1)} %scatter_fusion.2) | copy-start | bytes 12292
  271.9 101.5 %copy-start.17 = (f32[1024,256]{1,0:T(8,128)}, f32[1024,256]{1,0:T(8,128)S(1)}, u32[]{:S(2)}) copy-start(f32[1024,256]{1,0:T(8,128)S(1)} %scatter_custom_fusion.4) | copy-start | bytes 3145732
  370.4 3.4 copy-start.9
Sparse Core Ops, SparseCore 0:
  101.1 269.2 all-reduce.2
where the time goes:
time: 390 us; the launch traced here: 384 us
  waiting for transfers between devices  123 us (32%)
  local copies, waits for them, and re-layouts  77.2 us (20%)
  blocking collectives  76.9 us (20%)
  starting transfers between devices  36.8 us (9%)
  other arithmetic  34.2 us (9%)
  matrix products  18.9 us (5%)
  between operations  17 us (4%)
    psum x1, waiting for transfers between devices, shards(): lax.psum((grad_uv, grad_vecs, objective), ('trainer', 'table'))  98.5 us
    psum x1, blocking collectives, shards(): lax.psum((grad_uv, grad_vecs, objective), ('trainer', 'table'))  76.9 us
    gather x16, local copies, waits for them, and re-layouts, shards(): pieces.append(jnp.sum(jnp.take(cache_rows, picked, axis=0), axis=1))  54.4 us
    reduce_sum x8, other arithmetic, shards(): pieces.append(jnp.sum(jnp.take(cache_rows, picked, axis=0), axis=1))  14.8 us
    all_to_all x1, starting transfers between devices, shards(): lax.all_to_all(send_ids, 'table', split_axis=0, concat_axis=0, tiled=True)  10.3 us
    dot_general x8, matrix products, shards(): lax.dot_general(counts, block, (((0,), (0,)), ((), ())), preferred_elemen...  8.23 us
  transfers between devices with their start and end apart: 7, of which 6 were waited for; matrix products, arithmetic and copies ran while one was open for 31% of the time, Pallas kernels for 0%

commit v1 on v0

v1 whole, which is shorter than its diff:
```python
import jax
import jax.numpy as jnp
from jax import lax
from jax.sharding import PartitionSpec as P

EPS = 1e-06
ETA = 0.05
AXES = ("trainer", "table")


def device_at(y, x, z, core):
    return (((y // 2 * 4 + x) * 2 + y % 2) * 8 + z % 8) * 2 + core


def first_groups():
    groups = []
    for y in range(4):
        for pair in range(4):
            groups.append([device_at(y, x, 2 * pair + b, 0) for x in range(4) for b in range(2)])
    for x in range(4):
        for pair in range(4):
            groups.append([device_at(y, x, 2 * pair + 1 + b, 1) for y in range(4) for b in range(2)])
    return groups


def second_groups():
    groups = []
    for x in range(4):
        for b in range(2):
            groups.append([device_at(y, x, 2 * k + b, 0) for y in range(4) for k in range(4)])
    for y in range(4):
        for b in range(2):
            groups.append([device_at(y, x, 2 * k + b, 1) for x in range(4) for k in range(4)])
    return groups


def swap_cores(value):
    return lax.ppermute(value, AXES, [(i, i ^ 1) for i in range(256)])


def exchange(value, groups):
    return lax.all_to_all(
        value, AXES, split_axis=0, concat_axis=0, tiled=True, axis_index_groups=groups
    )


def ranks(owner):
    listed = owner.shape[0]
    order = jnp.arange(listed, dtype=jnp.int32)
    earlier = (owner[:, None] == owner[None, :]) & (order[None, :] < order[:, None])
    return jnp.sum(earlier.astype(jnp.int32), axis=1)


def placed_at(place, values, cells):
    hit = place[None, :] == jnp.arange(cells, dtype=jnp.int32)[:, None]
    return jnp.sum(jnp.where(hit, values[None, :], 0), axis=1)


def split3(value):
    high = lax.reduce_precision(value, 8, 7)
    rest = value - high
    mid = lax.reduce_precision(rest, 8, 7)
    return [part.astype(jnp.bfloat16) for part in (high, mid, rest - mid)]


def meta_row(columns, width):
    block = jnp.concatenate(columns, axis=1)
    return jnp.pad(block, ((0, 0), (0, width - block.shape[1])))[:, None, :]


def shards(
    slot_ids,
    labels,
    cache_rows,
    cache_accum,
    table_rows,
    table_accum,
    miss_dest,
    evict_slot,
    evict_dest,
    proj_u,
    proj_v,
    cross_bias,
    head,
):
    owners = 32
    per = 8
    cap = 6
    width = cache_rows.shape[1]
    owned = table_rows.shape[0]
    cells = cache_rows.shape[0]
    spots = owners * per
    core = lax.axis_index("table") % 2

    out_place = evict_dest[:, 0] * per + ranks(evict_dest[:, 0])
    in_place = miss_dest[:, 0] * per + ranks(miss_dest[:, 0])
    source = placed_at(out_place, evict_slot, spots)
    leave_id = placed_at(out_place, evict_dest[:, 1] + 1, spots) - 1
    ask_id = placed_at(in_place, miss_dest[:, 1], spots)
    rows_out = jnp.take(cache_rows, source, axis=0, mode="clip").reshape(owners, per, width)
    accum_out = jnp.take(cache_accum, source, mode="clip").reshape(owners, per)
    meta = meta_row(
        [
            accum_out,
            leave_id.reshape(owners, per).astype(jnp.float32),
            ask_id.reshape(owners, per).astype(jnp.float32),
        ],
        width,
    )
    is_meta = (jnp.arange(per) == per - 1)[None, :, None]
    sent = jnp.where(is_meta, meta, rows_out)
    got = lax.all_to_all(sent, "table", split_axis=0, concat_axis=0, tiled=True)
    got_meta = got[:, per - 1, :]
    got_id = got_meta[:, per : per + cap].astype(jnp.int32)
    got_ask = got_meta[:, 2 * per : 2 * per + cap].astype(jnp.int32)
    flat = jnp.where(got_id < 0, owned, got_id).reshape(-1)
    table_new = table_rows.at[flat].set(got[:, :cap, :].reshape(-1, width), mode="drop")
    accum_table = table_accum.at[flat].set(got_meta[:, :cap].reshape(-1), mode="drop")

    asked = jnp.pad(got_ask, ((0, 0), (0, per - cap)))
    reply_rows = jnp.take(table_new, asked, axis=0, mode="clip")
    reply_accum = jnp.take(accum_table, asked, mode="clip")
    reply = jnp.where(is_meta, meta_row([reply_accum], width), reply_rows)
    back = lax.all_to_all(reply, "table", split_axis=0, concat_axis=0, tiled=True)
    fetched_rows = jnp.take(back.reshape(spots, width), in_place, axis=0, mode="clip")
    fetched_accum = jnp.take(back[:, per - 1, :per].reshape(-1), in_place, mode="clip")

    count = slot_ids.shape[0]
    feats = proj_u.shape[0] // width
    looks = slot_ids.shape[1] // feats
    slot_range = jnp.arange(cells, dtype=jnp.int32)
    parts = jnp.concatenate(split3(cache_rows), axis=1)
    pieces = []
    counted = []
    for feature in range(feats):
        counts = jnp.zeros((count, cells), jnp.bfloat16)
        for lookup in range(looks):
            column = slot_ids[:, feature * looks + lookup]
            counts = counts + (column[:, None] == slot_range[None, :]).astype(jnp.bfloat16)
        counted.append(counts)
        summed = jnp.dot(counts, parts, preferred_element_type=jnp.float32)
        pieces.append(
            (summed[:, 2 * width :] + summed[:, width : 2 * width] + summed[:, :width]).astype(
                jnp.bfloat16
            )
        )
    pooled = jnp.concatenate(pieces, axis=1)
    latent = jnp.dot(pooled, proj_v, preferred_element_type=jnp.float32).astype(jnp.bfloat16)
    shifted = jnp.dot(latent, proj_u.T, preferred_element_type=jnp.float32) + cross_bias
    pooled_f = pooled.astype(jnp.float32)
    crossed = pooled_f * shifted + pooled_f
    logit = jnp.sum(crossed * head, axis=1)
    target = labels.astype(jnp.float32)
    objective = jnp.sum(jax.nn.softplus(logit) - target * logit)
    dlogit = jax.nn.sigmoid(logit) - target
    dcross = dlogit[:, None] * head[None, :]
    dhead = jnp.sum(dlogit[:, None] * crossed, axis=0)
    dlift_full = dcross * pooled_f
    dbias = jnp.sum(dlift_full, axis=0)
    dlift = dlift_full.astype(jnp.bfloat16)
    grad_u = lax.dot_general(
        dlift, latent, (((0,), (0,)), ((), ())), preferred_element_type=jnp.float32
    )
    dlatent = jnp.dot(dlift, proj_u, preferred_element_type=jnp.float32).astype(jnp.bfloat16)
    grad_v = lax.dot_general(
        pooled, dlatent, (((0,), (0,)), ((), ())), preferred_element_type=jnp.float32
    )
    dpooled = (
        dcross * (shifted + 1.0) + jnp.dot(dlatent, proj_v.T, preferred_element_type=jnp.float32)
    ).astype(jnp.bfloat16)

    blocks = 8
    depth = grad_u.shape[0] // blocks
    loss_row = jnp.pad(objective[None, None, None], ((0, 0), (0, 0), (0, width - 1)))
    loss_row = jnp.broadcast_to(loss_row, (blocks, 1, width))
    blank = jnp.zeros((blocks, 6, width), jnp.float32)

    def bundle(grad, vector):
        extra = jnp.concatenate([vector.reshape(blocks, 1, width), loss_row, blank], axis=1)
        return jnp.concatenate([grad.reshape(blocks, depth, width), extra], axis=1)

    with_u = bundle(grad_u, dbias)
    with_v = bundle(grad_v, dhead)
    mine = core == 0
    held = jnp.where(mine, with_u, with_v) + swap_cores(jnp.where(mine, with_v, with_u))
    held = jnp.sum(exchange(held, first_groups()), axis=0)
    fine = depth // 16
    pieces16 = jnp.concatenate(
        [
            held[:depth].reshape(16, fine, width),
            jnp.broadcast_to(held[None, depth:], (16, 8, width)),
        ],
        axis=1,
    )
    summed16 = jnp.sum(exchange(pieces16, second_groups()), axis=0)
    extras = summed16[fine:]
    spread = jnp.broadcast_to(summed16[None, :fine], (16, fine, width))
    whole = exchange(spread, second_groups()).reshape(depth, width)
    whole = jnp.concatenate([whole, extras], axis=0)
    whole = exchange(jnp.broadcast_to(whole[None], (blocks, depth + 8, width)), first_groups())
    other = swap_cores(whole)
    sum_u = jnp.where(mine, whole, other)
    sum_v = jnp.where(mine, other, whole)

    def main_part(value):
        return value[:, :depth].reshape(1, blocks * depth, width)

    def vector_part(value):
        return value[:, depth].reshape(1, blocks * width)

    proj_sums = jnp.concatenate([main_part(sum_u), main_part(sum_v)], axis=0)
    vec_sums = jnp.concatenate([vector_part(sum_u), vector_part(sum_v)], axis=0)
    clipped_proj = proj_sums * lax.rsqrt(
        jnp.mean(proj_sums * proj_sums, axis=(1, 2), keepdims=True) + EPS
    )
    clipped_vecs = vec_sums * lax.rsqrt(jnp.mean(vec_sums * vec_sums, axis=1, keepdims=True) + EPS)
    loss = sum_v[0, depth + 1, 0] / (count * 256)

    row_grad = jnp.zeros((cells, width), jnp.float32)
    for feature in range(feats):
        block = dpooled[:, feature * width : (feature + 1) * width]
        row_grad = row_grad + lax.dot_general(
            counted[feature], block, (((0,), (0,)), ((), ())), preferred_element_type=jnp.float32
        )
    accum_new = cache_accum + jnp.mean(row_grad * row_grad, axis=1)
    rows_new = cache_rows - ETA * row_grad * lax.rsqrt(accum_new)[:, None]
    rows_new = rows_new.at[evict_slot].set(fetched_rows)
    accum_new = accum_new.at[evict_slot].set(fetched_accum)
    return (rows_new, accum_new, table_new, accum_table, clipped_proj, clipped_vecs, loss)


def solution(mesh):
    split = P(AXES)
    rows = P(AXES, None)
    return jax.shard_map(
        shards,
        mesh=mesh,
        in_specs=(
            rows,
            split,
            rows,
            split,
            rows,
            split,
            rows,
            split,
            rows,
            P(),
            P(),
            P(),
            P(),
        ),
        out_specs=(rows, split, rows, split, P(), P(), P()),
        check_vma=False,
    )
```

time: 390 us -> 176 us (0.45)
  waiting for transfers between devices: 123 us -> 26.9 us
  local copies, waits for them, and re-layouts: 77.2 us -> 26.5 us
  blocking collectives: 76.9 us -> 45.2 us
  other arithmetic: 34.2 us -> 20.1 us
  starting transfers between devices: 36.8 us -> 23 us
  between operations: 17 us -> 4.2 us
  matrix products: 18.9 us -> 26.8 us
    psum x1 -> x0, waiting for transfers between devices: 98.5 us -> none  [shards(): lax.psum((grad_uv, grad_vecs, objective), ('trainer', 'table'))]
    psum x1 -> x0, blocking collectives: 76.9 us -> none  [shards(): lax.psum((grad_uv, grad_vecs, objective), ('trainer', 'table'))]
    gather x22 -> x6, local copies, waits for them, and re-layouts: 58.7 us -> 7.6 us  [the longest x1 2.32 us: shards(): jnp.take(cache_rows, source, axis=0, mode='clip')]
    all_to_all x0 -> x2, blocking collectives: none -> 45.2 us  [exchange(): lax.all_to_all(value, AXES, split_axis=0, concat_axis=0, tiled=True, axis...]
    all_to_all x6 -> x4, starting transfers between devices: 36.8 us -> 21.8 us  [the longest x2 11.4 us: exchange(): lax.all_to_all(value, AXES, split_axis=0, concat_axis=0, tiled=True, axis...]
    reduce_sum x10 -> x6, other arithmetic: 15.1 us -> 1.29 us  [the longest x2 0.77 us: placed_at(): return jnp.sum(jnp.where(hit, values[None, :], 0), axis=1)]
    dot_general x10 -> x16, matrix products: 13 us -> 19.7 us  [the longest x8 11.9 us: shards(): lax.dot_general(counted[feature], block, (((0,), (0,)), ((), ())), prefer...]
    all_to_all x6 -> x4, waiting for transfers between devices: 24.8 us -> 23 us  [the longest x2 10.1 us: exchange(): lax.all_to_all(value, AXES, split_axis=0, concat_axis=0, tiled=True, axis...]
  transfers between devices with their start and end apart: 7 -> 6, of which waited for: 6 -> 4; matrix products, arithmetic and copies ran while one was open for 31% -> 25% of each run, Pallas kernels for 0% -> 0%
where the time goes in v1:
time: 176 us; the launch traced here: 173 us
  blocking collectives  45.2 us (26%)
  waiting for transfers between devices  26.9 us (15%)
  matrix products  26.8 us (15%)
  local copies, waits for them, and re-layouts  26.5 us (15%)
  starting transfers between devices  23 us (13%)
  other arithmetic  20.1 us (11%)
  between operations  4.2 us (2%)
    all_to_all x2, blocking collectives, exchange(): lax.all_to_all(value, AXES, split_axis=0, concat_axis=0, tiled=True, axis...  45.2 us
    dot_general x8, matrix products, shards(): lax.dot_general(counted[feature], block, (((0,), (0,)), ((), ())), prefer...  11.9 us
    all_to_all x2, starting transfers between devices, exchange(): lax.all_to_all(value, AXES, split_axis=0, concat_axis=0, tiled=True, axis...  11.4 us
    all_to_all x2, waiting for transfers between devices, exchange(): lax.all_to_all(value, AXES, split_axis=0, concat_axis=0, tiled=True, axis...  10.1 us
    all_to_all x1, waiting for transfers between devices, shards(): lax.all_to_all(reply, 'table', split_axis=0, concat_axis=0, tiled=True)  7.98 us
    dot_general x8, matrix products, shards(): summed = jnp.dot(counts, parts, preferred_element_type=jnp.float32)  7.85 us
    all_to_all x1, starting transfers between devices, shards(): got = lax.all_to_all(sent, 'table', split_axis=0, concat_axis=0, tiled=True)  5.38 us
    all_to_all x1, starting transfers between devices, shards(): lax.all_to_all(reply, 'table', split_axis=0, concat_axis=0, tiled=True)  5.02 us
  transfers between devices with their start and end apart: 6, of which 4 were waited for; matrix products, arithmetic and copies ran while one was open for 25% of the time, Pallas kernels for 0%

profile of v1, /device:TPU:3, one launch (start us, length us, event | category | flops | bytes accessed | tf_op | source)
XLA Modules:
  0.0 172.7 jit_solution(7806241866755959287)
XLA Ops:
  0.7 1.0 fusion.125
  2.5 1.0 fusion.66
  3.6 1.0 fusion.69
  4.7 1.0 fusion.72
  5.8 1.0 fusion.75
  6.9 1.0 fusion.78
  7.9 1.0 fusion.81
  9.0 1.0 fusion.84
  10.1 1.0 fusion.87
  11.8 2.0 %multiply_reduce_fusion.2 = (f32[256]{0:T(256)S(1)}, f32[256,2048]{1,0:T(8,128)}) fusion(bf16[256,2048]{1,0:T(8,128)(2,1)S(1)} %fusion.107, f32[2048]{0:T(1024)S(1)} %copy-done.16, f32[2048]{0:T(1024)S(1)} %copy-done.20, bf16[256,256]{1,0:T(8,128)(2,1)S(1)} %convolution_convert_fusion.1, bf16[2048,256]{1,0:T(8,128)(2,1)S(1)} %copy-done), kind=kOutput, calls=%fused_computation.27 | convolution fusion | flops 271580928 | bytes 4342784 | tf_op jit(solution)/shard_map/dot_general | solution.py:149
  14.9 1.9 %fusion.89 = f32[2048,256]{1,0:T(8,128)} fusion(bf16[256,256]{1,0:T(8,128)(2,1)S(1)} %convolution_convert_fusion.1, bf16[256,2048]{1,0:T(8,128)(2,1)S(1)} %fusion.107, f32[256]{0:T(256)S(1)} %get-tuple-element.60, f32[2048]{0:T(1024)S(1)} %copy-done.16), kind=kOutput, calls=%fused_computation.146 | convolution fusion | flops 270532608 | bytes 3286016 | tf_op jit(solution)/shard_map/dot_general | solution.py:161
  16.9 2.2 %fusion.2 = (f32[2048]{0:T(1024)S(1)}, f32[2048]{0:T(1024)S(1)}) fusion(bf16[256,2048]{1,0:T(8,128)(2,1)S(1)} %fusion.107, f32[256]{0:T(256)S(1)} %get-tuple-element.60, f32[2048]{0:T(1024)S(1)} %copy-done.16, f32[256,2048]{1,0:T(8,128)} %get-tuple-element.66), kind=kLoop, calls=%fused_computation.21 | loop fusion | flops 4190208 | bytes 3171328 | tf_op jit(solution)/shard_map/reduce_sum | solution.py:159
  21.0 0.9 collective-permute-start
  22.0 3.9 %collective-permute-done = f32[8,264,256]{2,1,0:T(8,128)S(1)} collective-permute-done((f32[8,264,256]{2,1,0:T(8,128)S(1)}, f32[8,264,256]{2,1,0:T(8,128)S(1)}, u32[]{:S(2)}, u32[]{:S(2)}) %collective-permute-start) | collective-permute-done | bytes 2162720 | tf_op jit(solution)/shard_map/ppermute | solution.py:38
  26.3 25.0 %all_to_all.30 = f32[8,264,256]{2,1,0:T(8,128)S(1)} all-to-all(f32[8,264,256]{2,1,0:T(8,128)S(1)} %select_add_fusion), channel_id=1, replica_groups={{0,2,32,34,64,66,96,98},{4,6,36,38,68,70,100,102},{8,10,40,42,72,74,104..., dimensions={0} | all-to-all | bytes 4325376 | tf_op jit(solution)/shard_map/all_to_all | solution.py:42
  51.6 20.2 %all_to_all.31 = f32[16,24,256]{2,1,0:T(8,128)S(1)} all-to-all(f32[16,24,256]{2,1,0:T(8,128)S(1)} %pad_maximum_fusion.4), channel_id=1, replica_groups={{0,4,8,12,16,20,24,28,128,132,136,140,144,148,152,156},{2,6,10,14,18,22..., dimensions={0} | all-to-all | bytes 786432 | tf_op jit(solution)/shard_map/all_to_all | solution.py:42
  72.6 6.9 %all-to-all-start.4 = ((f32[16,16,256]{2,1,0:T(8,128)}), f32[16,16,256]{2,1,0:T(8,128)S(1)}, u32[]{:S(2)}, u32[]{:S(2)}) async-start(f32[16,16,256]{2,1,0:T(8,128)} %broadcast_in_dim.105), calls=%async_computation.4 | async-start | bytes 524288 | tf_op jit(solution)/shard_map/all_to_all | solution.py:42
  80.2 10.1 %all-to-all-done.4 = f32[16,16,256]{2,1,0:T(8,128)S(1)} async-done(((f32[16,16,256]{2,1,0:T(8,128)}), f32[16,16,256]{2,1,0:T(8,128)S(1)}, u32[]{:S(2)}, u32[]{:S(2)}) %all-to-all-start.4) | async-done | bytes 262176 | tf_op jit(solution)/shard_map/all_to_all | solution.py:42
  90.3 1.5 broadcast_in_dim.106
  91.7 4.5 %all-to-all-start.5 = ((f32[8,264,256]{2,1,0:T(8,128)}), f32[8,264,256]{2,1,0:T(8,128)}, u32[]{:S(2)}, u32[]{:S(2)}) async-start(f32[8,264,256]{2,1,0:T(8,128)} %broadcast_in_dim.106), calls=%async_computation.5 | async-start | bytes 4325376 | tf_op jit(solution)/shard_map/all_to_all | solution.py:42
  98.4 2.3 %gather_fusion.1 = f32[256,256]{1,0:T(8,128)S(1)} fusion(f32[1024,256]{1,0:T(8,128)} %param.15, s32[1024]{0:T(1024)} %pad_clamp_fusion.2), kind=kCustom, calls=%fused_computation.1 | custom fusion | bytes 525312 | tf_op jit(solution)/shard_map/jit(_take)/gather | solution.py:100
  100.8 2.1 %gather_fusion = f32[256]{0:T(256)} fusion(f32[1024]{0:T(1024)S(1)} %copy-done.3, s32[1024]{0:T(1024)} %pad_clamp_fusion.2), kind=kCustom, calls=%fused_computation | custom fusion | bytes 3072 | tf_op jit(solution)/shard_map/jit(_take)/gather | solution.py:101
  102.8 1.4 reshape.152
  104.2 1.2 add_convert_fusion
  105.4 1.4 convert_element_type.228
  106.8 1.4 convert_element_type.231
  108.2 0.8 select_maximum_fusion
  109.0 0.8 bitcast_select_fusion.1
  109.9 1.8 %fusion.1 = bf16[256,2048]{1,0:T(8,128)(2,1)S(1)} fusion(bf16[256,256]{1,0:T(8,128)(2,1)S(1)} %copy-done.15, bf16[2048,256]{1,0:T(8,128)(2,1)} %param.23, f32[256,2048]{1,0:T(8,128)S(1)} %copy-done.7, f32[256]{0:T(256)S(1)} %copy-done.19, f32[2048]{0:T(1024)S(1)} %copy-done.16), kind=kOutput, calls=%fused_computation.20 | convolution fusion | flops 271056896 | bytes 4334592 | tf_op jit(solution)/shard_map/dot_general | solution.py:169
  112.7 0.8 convolution_add_fusion.8
  115.3 0.8 convolution_add_fusion.5
  116.2 1.8 %convolution_add_fusion.4 = f32[1024,256]{0,1:T(8,128)} fusion(f32[1024,256]{0,1:T(8,128)S(1)} %convolution_add_fusion.5, s32[256]{0:T(256)S(1)} %bitcast.125, s32[256]{0:T(256)S(1)} %bitcast.127, s32[256]{0:T(256)S(1)} %bitcast.129, s32[256]{0:T(256)S(1)} %bitcast.131, bf16[256,2048]{1,0:T(8,128)(2,1)S(1)} %fusion.1), kind=kOutput, calls=%fused_computation.36 | convolution fusion | flops 138674176 | bytes 2232320 | tf_op jit(solution)/shard_map/dot_general | solution.py:222
  117.9 5.4 %all-to-all-start = ((f32[32,8,256]{2,1,0:T(8,128)}), f32[32,8,256]{2,1,0:T(8,128)S(1)}, u32[]{:S(2)}, u32[]{:S(2)}) async-start(f32[32,8,256]{2,1,0:T(8,128)} %bitcast_select_fusion.1), calls=%async_computation | async-start | bytes 524288 | tf_op jit(solution)/shard_map/all_to_all | solution.py:112
  123.4 3.1 %convolution_add_fusion.3 = f32[1024,256]{0,1:T(8,128)} fusion(f32[1024,256]{0,1:T(8,128)} %convolution_add_fusion.4, s32[256]{0:T(256)S(1)} %bitcast.117, s32[256]{0:T(256)S(1)} %bitcast.119, s32[256]{0:T(256)S(1)} %bitcast.121, s32[256]{0:T(256)S(1)} %bitcast.123, bf16[256,2048]{1,0:T(8,128)(2,1)} %copy-done.12), kind=kOutput, calls=%fused_computation.35 | convolution fusion | flops 138674176 | bytes 2232320 | tf_op jit(solution)/shard_map/dot_general | solution.py:222
  127.2 3.1 %multiply_reduce_fusion.3 = (f32[1024]{0:T(1024)S(1)}, f32[1024,256]{0,1:T(8,128)}) fusion(f32[1024,256]{0,1:T(8,128)} %convolution_add_fusion.3, bf16[256,2048]{1,0:T(8,128)(2,1)} %copy-done.12, s32[256]{0:T(256)S(1)} %bitcast.153, s32[256]{0:T(256)S(1)} %bitcast.151, s32[256]{0:T(256)S(1)} %bitcast.115, s32[256]{0:T(256)S(1)} %bitcast.113), kind=kOutput, calls=%fused_computation.47 | convolution fusion | flops 139197440 | bytes 2236416 | tf_op jit(solution)/shard_map/dot_general | solution.py:222
  130.3 5.0 %all-to-all-done = f32[32,8,256]{2,1,0:T(8,128)S(1)} async-done(((f32[32,8,256]{2,1,0:T(8,128)}), f32[32,8,256]{2,1,0:T(8,128)S(1)}, u32[]{:S(2)}, u32[]{:S(2)}) %all-to-all-start) | async-done | bytes 262176 | tf_op jit(solution)/shard_map/all_to_all | solution.py:112
  135.8 1.4 scatter_fusion
  137.3 1.4 gather_fusion.2
  139.4 2.0 %scatter_fusion.1 = f32[1024,256]{1,0:T(8,128)S(1)} fusion(f32[1024,256]{1,0:T(8,128)S(1)} %copy-done.6, s32[192]{0:T(256)S(1)} %bitcast.110, f32[192,256]{1,0:T(8,128)} %reshape.226), kind=kCustom, calls=%fused_computation.7 | custom fusion | bytes 590592 | tf_op jit(solution)/shard_map/scatter | solution.py:117
  141.5 1.0 gather_fusion.3
  143.2 5.0 %all-to-all-start.1 = ((f32[32,8,256]{2,1,0:T(8,128)}), f32[32,8,256]{2,1,0:T(8,128)S(1)}, u32[]{:S(2)}, u32[]{:S(2)}) async-start(f32[32,8,256]{2,1,0:T(8,128)} %bitcast_select_fusion), calls=%async_computation.1 | async-start | bytes 524288 | tf_op jit(solution)/shard_map/all_to_all | solution.py:124
  148.3 2.4 %multiply_subtract_fusion = f32[1024,256]{0,1:T(8,128)} fusion(f32[1024,256]{0,1:T(8,128)S(1)} %copy.31, f32[1024,256]{0,1:T(8,128)} %get-tuple-element.68, f32[1024]{0:T(1024)S(1)} %get-tuple-element.18), kind=kLoop, calls=%fused_computation.46 | loop fusion | flops 524288 | bytes 3149824 | tf_op jit(solution)/shard_map/sub | solution.py:226
  150.7 1.6 copy.32
  152.3 8.0 %all-to-all-done.1 = f32[32,8,256]{2,1,0:T(8,128)S(1)} async-done(((f32[32,8,256]{2,1,0:T(8,128)}), f32[32,8,256]{2,1,0:T(8,128)S(1)}, u32[]{:S(2)}, u32[]{:S(2)}) %all-to-all-start.1) | async-done | bytes 262176 | tf_op jit(solution)/shard_map/all_to_all | solution.py:124
  160.5 0.8 gather_fusion.4
  161.2 1.4 scatter_custom_fusion.2
  163.5 2.6 %broadcast_select_fusion.1 = (f32[8,264,256]{2,1,0:T(8,128)S(1)}, f32[8,264,256]{2,1,0:T(8,128)S(1)}) fusion(f32[8,264,256]{2,1,0:T(8,128)} %all-to-all-done.5, f32[8,264,256]{2,1,0:T(8,128)} %collective-permute-done.1, pred[]{:T(512)S(6)} %eq.694), kind=kLoop, calls=%fused_computation.44 | loop fusion | flops 1081344 | bytes 8650753 | tf_op jit(solution)/shard_map/jit(_where)/select_n | solution.py:202
  168.6 2.4 %fusion = f32[2,2048,256]{2,1,0:T(8,128)} fusion(f32[1,2048,256]{2,1,0:T(8,128)S(1)} %bitcast.94, f32[1,2048,256]{2,1,0:T(8,128)S(1)} %bitcast.92, f32[2]{0:T(128)S(1)} %add_rsqrt_fusion.1), kind=kLoop, calls=%fused_computation.12 | loop fusion | flops 2097152 | bytes 8388616 | tf_op jit(solution)/shard_map/mul | solution.py:213
  (265 shorter events, 17.7 us)
Async XLA Ops:
  0.6 11.1 %copy-start = (bf16[2048,256]{1,0:T(8,128)(2,1)S(1)}, bf16[2048,256]{1,0:T(8,128)(2,1)}, u32[]{:S(2)}) copy-start(bf16[2048,256]{1,0:T(8,128)(2,1)} %param.22) | copy-start | bytes 3145732
  1.8 8.2 %copy-start.65 = (s32[256,1]{0,1:T(1,128)}, s32[256,1]{0,1:T(1,128)S(1)}, u32[]{:S(2)}) copy-start(s32[256,1]{0,1:T(1,128)S(1)} %get-tuple-element.46) | copy-start | bytes 3076
  1.9 8.2 %copy-start.67 = (s32[256,1]{0,1:T(1,128)}, s32[256,1]{0,1:T(1,128)S(1)}, u32[]{:S(2)}) copy-start(s32[256,1]{0,1:T(1,128)S(1)} %get-tuple-element.58) | copy-start | bytes 3076
  2.1 3.7 %copy-start.55 = (s32[256,1]{0,1:T(1,128)}, s32[256,1]{0,1:T(1,128)S(1)}, u32[]{:S(2)}) copy-start(s32[256,1]{0,1:T(1,128)S(1)} %get-tuple-element.42) | copy-start | bytes 3076
  2.1 3.7 %copy-start.57 = (s32[256,1]{0,1:T(1,128)}, s32[256,1]{0,1:T(1,128)S(1)}, u32[]{:S(2)}) copy-start(s32[256,1]{0,1:T(1,128)S(1)} %get-tuple-element.43) | copy-start | bytes 3076
  2.1 3.7 %copy-start.59 = (s32[256,1]{0,1:T(1,128)}, s32[256,1]{0,1:T(1,128)S(1)}, u32[]{:S(2)}) copy-start(s32[256,1]{0,1:T(1,128)S(1)} %get-tuple-element.44) | copy-start | bytes 3076
  2.1 4.7 %copy-start.45 = (s32[256,1]{0,1:T(1,128)}, s32[256,1]{0,1:T(1,128)S(1)}, u32[]{:S(2)}) copy-start(s32[256,1]{0,1:T(1,128)S(1)} %get-tuple-element.37) | copy-start | bytes 3076
  2.1 4.7 %copy-start.47 = (s32[256,1]{0,1:T(1,128)}, s32[256,1]{0,1:T(1,128)S(1)}, u32[]{:S(2)}) copy-start(s32[256,1]{0,1:T(1,128)S(1)} %get-tuple-element.38) | copy-start | bytes 3076
  2.1 4.7 %copy-start.49 = (s32[256,1]{0,1:T(1,128)}, s32[256,1]{0,1:T(1,128)S(1)}, u32[]{:S(2)}) copy-start(s32[256,1]{0,1:T(1,128)S(1)} %get-tuple-element.39) | copy-start | bytes 3076
  2.1 4.7 %copy-start.51 = (s32[256,1]{0,1:T(1,128)}, s32[256,1]{0,1:T(1,128)S(1)}, u32[]{:S(2)}) copy-start(s32[256,1]{0,1:T(1,128)S(1)} %get-tuple-element.40) | copy-start | bytes 3076
  2.2 5.7 %copy-start.37 = (s32[256,1]{0,1:T(1,128)}, s32[256,1]{0,1:T(1,128)S(1)}, u32[]{:S(2)}) copy-start(s32[256,1]{0,1:T(1,128)S(1)} %get-tuple-element.33) | copy-start | bytes 3076
  2.2 5.7 %copy-start.39 = (s32[256,1]{0,1:T(1,128)}, s32[256,1]{0,1:T(1,128)S(1)}, u32[]{:S(2)}) copy-start(s32[256,1]{0,1:T(1,128)S(1)} %get-tuple-element.34) | copy-start | bytes 3076
  2.2 5.7 %copy-start.41 = (s32[256,1]{0,1:T(1,128)}, s32[256,1]{0,1:T(1,128)S(1)}, u32[]{:S(2)}) copy-start(s32[256,1]{0,1:T(1,128)S(1)} %get-tuple-element.35) | copy-start | bytes 3076
  2.2 5.7 %copy-start.43 = (s32[256,1]{0,1:T(1,128)}, s32[256,1]{0,1:T(1,128)S(1)}, u32[]{:S(2)}) copy-start(s32[256,1]{0,1:T(1,128)S(1)} %get-tuple-element.36) | copy-start | bytes 3076
  2.2 6.8 %copy-start.29 = (s32[256,1]{0,1:T(1,128)}, s32[256,1]{0,1:T(1,128)S(1)}, u32[]{:S(2)}) copy-start(s32[256,1]{0,1:T(1,128)S(1)} %get-tuple-element.29) | copy-start | bytes 3076
  2.2 6.8 %copy-start.31 = (s32[256,1]{0,1:T(1,128)}, s32[256,1]{0,1:T(1,128)S(1)}, u32[]{:S(2)}) copy-start(s32[256,1]{0,1:T(1,128)S(1)} %get-tuple-element.30) | copy-start | bytes 3076
  2.2 6.8 %copy-start.33 = (s32[256,1]{0,1:T(1,128)}, s32[256,1]{0,1:T(1,128)S(1)}, u32[]{:S(2)}) copy-start(s32[256,1]{0,1:T(1,128)S(1)} %get-tuple-element.31) | copy-start | bytes 3076
  2.2 6.8 %copy-start.35 = (s32[256,1]{0,1:T(1,128)}, s32[256,1]{0,1:T(1,128)S(1)}, u32[]{:S(2)}) copy-start(s32[256,1]{0,1:T(1,128)S(1)} %get-tuple-element.32) | copy-start | bytes 3076
  2.2 7.8 %copy-start.25 = (s32[256,1]{0,1:T(1,128)}, s32[256,1]{0,1:T(1,128)S(1)}, u32[]{:S(2)}) copy-start(s32[256,1]{0,1:T(1,128)S(1)} %get-tuple-element.27) | copy-start | bytes 3076
  2.2 7.8 %copy-start.27 = (s32[256,1]{0,1:T(1,128)}, s32[256,1]{0,1:T(1,128)S(1)}, u32[]{:S(2)}) copy-start(s32[256,1]{0,1:T(1,128)S(1)} %get-tuple-element.28) | copy-start | bytes 3076
  14.9 4.1 %copy-start.14 = (bf16[256,256]{1,0:T(8,128)(2,1)}, bf16[256,256]{1,0:T(8,128)(2,1)S(1)}, u32[]{:S(2)}) copy-start(bf16[256,256]{1,0:T(8,128)(2,1)S(1)} %convolution_convert_fusion) | copy-start | bytes 393220
  21.0 4.8 %collective-permute-start = (f32[8,264,256]{2,1,0:T(8,128)S(1)}, f32[8,264,256]{2,1,0:T(8,128)S(1)}, u32[]{:S(2)}, u32[]{:S(2)}) collective-permute-start(f32[8,264,256]{2,1,0:T(8,128)S(1)} %fusion.6), channel_id=1, source_target_pairs={{0,1},{1,0},{2,3},{3,2},{4,5},{5,4},{6,7},{7,6},{8,9},{9,8},{10,11... | collective-permute-start | bytes 6488072 | tf_op jit(solution)/shard_map/ppermute | solution.py:38
  51.5 28.0 %copy-start.63 = (s32[64,2]{0,1:T(2,128)S(1)}, s32[64,2]{0,1:T(2,128)}, u32[]{:S(2)}) copy-start(s32[64,2]{0,1:T(2,128)} %param.19) | copy-start | bytes 1540
  72.6 17.7 %all-to-all-start.4 = ((f32[16,16,256]{2,1,0:T(8,128)}), f32[16,16,256]{2,1,0:T(8,128)S(1)}, u32[]{:S(2)}, u32[]{:S(2)}) async-start(f32[16,16,256]{2,1,0:T(8,128)} %broadcast_in_dim.105), calls=%async_computation.4 | async-start | bytes 524288 | tf_op jit(solution)/shard_map/all_to_all | solution.py:42
  91.7 5.2 %copy-start.64 = (s32[64,2]{0,1:T(2,128)S(1)}, s32[64,2]{0,1:T(2,128)}, u32[]{:S(2)}) copy-start(s32[64,2]{0,1:T(2,128)} %param.21) | copy-start | bytes 1540
  91.7 5.4 %copy-start.91 = (s32[64]{0:T(128)S(1)}, s32[64]{0:T(128)}, u32[]{:S(2)}) copy-start(s32[64]{0:T(128)} %param.20) | copy-start | bytes 772
  91.7 26.2 %all-to-all-start.5 = ((f32[8,264,256]{2,1,0:T(8,128)}), f32[8,264,256]{2,1,0:T(8,128)}, u32[]{:S(2)}, u32[]{:S(2)}) async-start(f32[8,264,256]{2,1,0:T(8,128)} %broadcast_in_dim.106), calls=%async_computation.5 | async-start | bytes 4325376 | tf_op jit(solution)/shard_map/all_to_all | solution.py:42
  96.2 4.6 %copy-start.3 = (f32[1024]{0:T(1024)S(1)}, f32[1024]{0:T(1024)}, u32[]{:S(2)}) copy-start(f32[1024]{0:T(1024)} %param.16) | copy-start | bytes 12292
  96.2 13.6 %copy-start.7 = (f32[256,2048]{1,0:T(8,128)S(1)}, f32[256,2048]{1,0:T(8,128)}, u32[]{:S(2)}) copy-start(f32[256,2048]{1,0:T(8,128)} %get-tuple-element.66) | copy-start | bytes 6291460
  96.2 13.6 %copy-start.15 = (bf16[256,256]{1,0:T(8,128)(2,1)S(1)}, bf16[256,256]{1,0:T(8,128)(2,1)}, u32[]{:S(2)}) copy-start(bf16[256,256]{1,0:T(8,128)(2,1)} %copy-done.14) | copy-start | bytes 393220
  96.2 13.6 %copy-start.19 = (f32[256]{0:T(256)S(1)}, f32[256]{0:T(256)}, u32[]{:S(2)}) copy-start(f32[256]{0:T(256)} %copy-done.18) | copy-start | bytes 3076
  111.7 4.4 %copy-start.12 = (bf16[256,2048]{1,0:T(8,128)(2,1)}, bf16[256,2048]{1,0:T(8,128)(2,1)S(1)}, u32[]{:S(2)}) copy-start(bf16[256,2048]{1,0:T(8,128)(2,1)S(1)} %fusion.1) | copy-start | bytes 3145732
  116.1 7.2 %copy-start.30 = (s32[256,1]{0,1:T(1,128)S(1)}, s32[256,1]{0,1:T(1,128)}, u32[]{:S(2)}) copy-start(s32[256,1]{0,1:T(1,128)} %copy-done.29) | copy-start | bytes 3076
  116.1 7.2 %copy-start.32 = (s32[256,1]{0,1:T(1,128)S(1)}, s32[256,1]{0,1:T(1,128)}, u32[]{:S(2)}) copy-start(s32[256,1]{0,1:T(1,128)} %copy-done.31) | copy-start | bytes 3076
  116.1 7.2 %copy-start.34 = (s32[256,1]{0,1:T(1,128)S(1)}, s32[256,1]{0,1:T(1,128)}, u32[]{:S(2)}) copy-start(s32[256,1]{0,1:T(1,128)} %copy-done.33) | copy-start | bytes 3076
  116.2 7.2 %copy-start.36 = (s32[256,1]{0,1:T(1,128)S(1)}, s32[256,1]{0,1:T(1,128)}, u32[]{:S(2)}) copy-start(s32[256,1]{0,1:T(1,128)} %copy-done.35) | copy-start | bytes 3076
  117.9 8.6 %copy-start.10 = (f32[1024,256]{1,0:T(8,128)S(1)}, f32[1024,256]{1,0:T(8,128)}, u32[]{:S(2)}) copy-start(f32[1024,256]{1,0:T(8,128)} %param.15) | copy-start | bytes 3145732
  117.9 17.3 %all-to-all-start = ((f32[32,8,256]{2,1,0:T(8,128)}), f32[32,8,256]{2,1,0:T(8,128)S(1)}, u32[]{:S(2)}, u32[]{:S(2)}) async-start(f32[32,8,256]{2,1,0:T(8,128)} %bitcast_select_fusion.1), calls=%async_computation | async-start | bytes 524288 | tf_op jit(solution)/shard_map/all_to_all | solution.py:112
  123.4 3.8 %copy-start.26 = (s32[256,1]{0,1:T(1,128)S(1)}, s32[256,1]{0,1:T(1,128)}, u32[]{:S(2)}) copy-start(s32[256,1]{0,1:T(1,128)} %copy-done.25) | copy-start | bytes 3076
  123.4 3.8 %copy-start.28 = (s32[256,1]{0,1:T(1,128)S(1)}, s32[256,1]{0,1:T(1,128)}, u32[]{:S(2)}) copy-start(s32[256,1]{0,1:T(1,128)} %copy-done.27) | copy-start | bytes 3076
  123.4 3.8 %copy-start.66 = (s32[256,1]{0,1:T(1,128)S(1)}, s32[256,1]{0,1:T(1,128)}, u32[]{:S(2)}) copy-start(s32[256,1]{0,1:T(1,128)} %copy-done.65) | copy-start | bytes 3076
  123.4 3.8 %copy-start.68 = (s32[256,1]{0,1:T(1,128)S(1)}, s32[256,1]{0,1:T(1,128)}, u32[]{:S(2)}) copy-start(s32[256,1]{0,1:T(1,128)} %copy-done.67) | copy-start | bytes 3076
  126.8 8.9 %copy-start.2 = (f32[1024]{0:T(1024)S(1)}, f32[1024]{0:T(1024)}, u32[]{:S(2)}) copy-start(f32[1024]{0:T(1024)} %param.18) | copy-start | bytes 12292
  126.8 36.6 %collective-permute-start.1 = (f32[8,264,256]{2,1,0:T(8,128)}, f32[8,264,256]{2,1,0:T(8,128)}, u32[]{:S(2)}, u32[]{:S(2)}) collective-permute-start(f32[8,264,256]{2,1,0:T(8,128)} %all-to-all-done.5), channel_id=1, source_target_pairs={{0,1},{1,0},{2,3},{3,2},{4,5},{5,4},{6,7},{7,6},{8,9},{9,8},{10,11... | collective-permute-start | bytes 6488072 | tf_op jit(solution)/shard_map/ppermute | solution.py:38
  141.5 9.3 %copy-start.5 = (f32[1024,256]{1,0:T(8,128)}, f32[1024,256]{1,0:T(8,128)S(1)}, u32[]{:S(2)}) copy-start(f32[1024,256]{1,0:T(8,128)S(1)} %scatter_fusion.1) | copy-start | bytes 3145732
  143.2 17.1 %all-to-all-start.1 = ((f32[32,8,256]{2,1,0:T(8,128)}), f32[32,8,256]{2,1,0:T(8,128)S(1)}, u32[]{:S(2)}, u32[]{:S(2)}) async-start(f32[32,8,256]{2,1,0:T(8,128)} %bitcast_select_fusion), calls=%async_computation.1 | async-start | bytes 524288 | tf_op jit(solution)/shard_map/all_to_all | solution.py:124
  148.3 4.0 %copy-start.23 = (s32[64]{0:T(128)S(1)}, s32[64]{0:T(128)}, u32[]{:S(2)}) copy-start(s32[64]{0:T(128)} %get-tuple-element.61) | copy-start | bytes 772
  148.3 4.0 %copy-start.92 = (s32[64]{0:T(128)S(1)}, s32[64]{0:T(128)}, u32[]{:S(2)}) copy-start(s32[64]{0:T(128)} %param.20) | copy-start | bytes 772
  (51 other events, 92.2 us)

commit v2 on v1

--- a/solution.py
+++ b/solution.py
@@ -66,6 +66,18 @@
 def meta_row(columns, width):
     block = jnp.concatenate(columns, axis=1)
     return jnp.pad(block, ((0, 0), (0, width - block.shape[1])))[:, None, :]
+
+
+def picked(values, index):
+    hit = index[:, None] == jnp.arange(values.shape[0], dtype=jnp.int32)[None, :]
+    return jnp.sum(jnp.where(hit, values[None, :], 0.0), axis=1)
+
+
+def cross(value, bit):
+    split = value.reshape(value.shape[0] // (2 * bit), 2, bit, *value.shape[1:])
+    there = [(i, i ^ bit) for i in range(256)]
+    came = lax.ppermute(split[:, 1], AXES, there)
+    return jnp.stack([split[:, 0], came], axis=1).reshape(value.shape)
 
 
 def shards(
@@ -92,13 +104,14 @@
     spots = owners * per
     core = lax.axis_index("table") % 2
 
-    out_place = evict_dest[:, 0] * per + ranks(evict_dest[:, 0])
-    in_place = miss_dest[:, 0] * per + ranks(miss_dest[:, 0])
+    me = lax.axis_index("table")
+    out_place = (evict_dest[:, 0] ^ me) * per + ranks(evict_dest[:, 0])
+    in_place = (miss_dest[:, 0] ^ me) * per + ranks(miss_dest[:, 0])
     source = placed_at(out_place, evict_slot, spots)
     leave_id = placed_at(out_place, evict_dest[:, 1] + 1, spots) - 1
     ask_id = placed_at(in_place, miss_dest[:, 1], spots)
     rows_out = jnp.take(cache_rows, source, axis=0, mode="clip").reshape(owners, per, width)
-    accum_out = jnp.take(cache_accum, source, mode="clip").reshape(owners, per)
+    accum_out = picked(cache_accum, source).reshape(owners, per)
     meta = meta_row(
         [
             accum_out,
@@ -109,21 +122,6 @@
     )
     is_meta = (jnp.arange(per) == per - 1)[None, :, None]
     sent = jnp.where(is_meta, meta, rows_out)
-    got = lax.all_to_all(sent, "table", split_axis=0, concat_axis=0, tiled=True)
-    got_meta = got[:, per - 1, :]
-    got_id = got_meta[:, per : per + cap].astype(jnp.int32)
-    got_ask = got_meta[:, 2 * per : 2 * per + cap].astype(jnp.int32)
-    flat = jnp.where(got_id < 0, owned, got_id).reshape(-1)
-    table_new = table_rows.at[flat].set(got[:, :cap, :].reshape(-1, width), mode="drop")
-    accum_table = table_accum.at[flat].set(got_meta[:, :cap].reshape(-1), mode="drop")
-
-    asked = jnp.pad(got_ask, ((0, 0), (0, per - cap)))
-    reply_rows = jnp.take(table_new, asked, axis=0, mode="clip")
-    reply_accum = jnp.take(accum_table, asked, mode="clip")
-    reply = jnp.where(is_meta, meta_row([reply_accum], width), reply_rows)
-    back = lax.all_to_all(reply, "table", split_axis=0, concat_axis=0, tiled=True)
-    fetched_rows = jnp.take(back.reshape(spots, width), in_place, axis=0, mode="clip")
-    fetched_accum = jnp.take(back[:, per - 1, :per].reshape(-1), in_place, mode="clip")
 
     count = slot_ids.shape[0]
     feats = proj_u.shape[0] // width
@@ -183,7 +181,11 @@
     with_v = bundle(grad_v, dhead)
     mine = core == 0
     held = jnp.where(mine, with_u, with_v) + swap_cores(jnp.where(mine, with_v, with_u))
-    held = jnp.sum(exchange(held, first_groups()), axis=0)
+    held, sent = lax.optimization_barrier((held, sent))
+    held = exchange(held, first_groups())
+    got = cross(cross(cross(sent, 1), 16), 2)
+    held, got = lax.optimization_barrier((held, got))
+    held = jnp.sum(held, axis=0)
     fine = depth // 16
     pieces16 = jnp.concatenate(
         [
@@ -192,12 +194,35 @@
         ],
         axis=1,
     )
-    summed16 = jnp.sum(exchange(pieces16, second_groups()), axis=0)
+    held = exchange(pieces16, second_groups())
+    got = cross(cross(got, 4), 8)
+    got_meta = got[:, per - 1, :]
+    got_id = got_meta[:, per : per + cap].astype(jnp.int32)
+    asked = got_meta[:, 2 * per : 3 * per].astype(jnp.int32).reshape(-1)
+    flat = got_id.reshape(-1)
+    table_new = table_rows.at[jnp.where(flat < 0, owned, flat)].set(
+        got[:, :cap, :].reshape(-1, width), mode="drop"
+    )
+    stored = flat[:, None] == jnp.arange(owned, dtype=jnp.int32)[None, :]
+    stored_sum = jnp.sum(jnp.where(stored, got_meta[:, :cap].reshape(-1)[:, None], 0.0), axis=0)
+    accum_table = jnp.where(jnp.any(stored, axis=0), stored_sum, table_accum)
+    reply_rows = jnp.take(table_new, asked, axis=0, mode="clip").reshape(owners, per, width)
+    reply_accum = picked(accum_table, asked).reshape(owners, per)
+    reply = jnp.where(is_meta, meta_row([reply_accum], width), reply_rows)
+    held, reply = lax.optimization_barrier((held, reply))
+    summed16 = jnp.sum(held, axis=0)
     extras = summed16[fine:]
     spread = jnp.broadcast_to(summed16[None, :fine], (16, fine, width))
-    whole = exchange(spread, second_groups()).reshape(depth, width)
-    whole = jnp.concatenate([whole, extras], axis=0)
+
+    held = exchange(spread, second_groups())
+    back = cross(cross(reply, 1), 16)
+    held, back = lax.optimization_barrier((held, back))
+    whole = jnp.concatenate([held.reshape(depth, width), extras], axis=0)
     whole = exchange(jnp.broadcast_to(whole[None], (blocks, depth + 8, width)), first_groups())
+    back = cross(cross(cross(back, 2), 4), 8)
+    whole, back = lax.optimization_barrier((whole, back))
+    fetched_rows = jnp.take(back.reshape(spots, width), in_place, axis=0, mode="clip")
+    fetched_accum = picked(back[:, per - 1, :per].reshape(-1), in_place)
     other = swap_cores(whole)
     sum_u = jnp.where(mine, whole, other)
     sum_v = jnp.where(mine, other, whole)

time: 176 us -> 183 us (1.040)
  blocking collectives: 45.2 us -> 0 us
  waiting for transfers between devices: 26.9 us -> 61.6 us
  starting transfers between devices: 23 us -> 50.7 us
  local copies, waits for them, and re-layouts: 26.5 us -> 16.9 us
  other arithmetic: 20.1 us -> 23.7 us
  matrix products: 26.8 us -> 23.5 us
    ppermute x0 -> x10, waiting for transfers between devices: none -> 47.8 us  [cross(): came = lax.ppermute(split[:, 1], AXES, there)]
    all_to_all x2 -> x0, blocking collectives: 45.2 us -> none  [exchange(): lax.all_to_all(value, AXES, split_axis=0, concat_axis=0, tiled=True, axis...]
    ppermute x0 -> x10, starting transfers between devices: none -> 14.3 us  [cross(): came = lax.ppermute(split[:, 1], AXES, there)]
    all_to_all x2 -> x4, starting transfers between devices: 11.4 us -> 24.5 us  [exchange(): lax.all_to_all(value, AXES, split_axis=0, concat_axis=0, tiled=True, axis...]
    all_to_all x2 -> x0, waiting for transfers between devices: 13 us -> none  [the longest x1 7.98 us: shards(): lax.all_to_all(reply, 'table', split_axis=0, concat_axis=0, tiled=True)]
    ppermute x2, starting transfers between devices: 1.26 us -> 11.9 us  [swap_cores(): return lax.ppermute(value, AXES, [(i, i ^ 1) for i in range(256)])]
    all_to_all x2 -> x0, starting transfers between devices: 10.4 us -> none  [the longest x1 5.38 us: shards(): got = lax.all_to_all(sent, 'table', split_axis=0, concat_axis=0, tiled=True)]
    gather x5 -> x1, local copies, waits for them, and re-layouts: 5.27 us -> 0.97 us  [shards(): jnp.take(table_new, asked, axis=0, mode='clip').reshape(owners, per, width)]
  transfers between devices with their start and end apart: 6 -> 16, of which waited for: 4 -> 10; matrix products, arithmetic and copies ran while one was open for 25% -> 16% of each run, Pallas kernels for 0% -> 0%
where the time goes in v2:
time: 183 us; the launch traced here: 181 us
  waiting for transfers between devices  61.6 us (34%)
  starting transfers between devices  50.7 us (28%)
  other arithmetic  23.7 us (13%)
  matrix products  23.5 us (13%)
  local copies, waits for them, and re-layouts  16.9 us (9%)
  between operations  4.36 us (2%)
    ppermute x10, waiting for transfers between devices, cross(): came = lax.ppermute(split[:, 1], AXES, there)  47.8 us
    all_to_all x4, starting transfers between devices, exchange(): lax.all_to_all(value, AXES, split_axis=0, concat_axis=0, tiled=True, axis...  24.5 us
    ppermute x10, starting transfers between devices, cross(): came = lax.ppermute(split[:, 1], AXES, there)  14.3 us
    all_to_all x4, waiting for transfers between devices, exchange(): lax.all_to_all(value, AXES, split_axis=0, concat_axis=0, tiled=True, axis...  13.7 us
    ppermute x2, starting transfers between devices, swap_cores(): return lax.ppermute(value, AXES, [(i, i ^ 1) for i in range(256)])  11.9 us
    dot_general x8, matrix products, shards(): lax.dot_general(counted[feature], block, (((0,), (0,)), ((), ())), prefer...  8.57 us
    dot_general x8, matrix products, shards(): summed = jnp.dot(counts, parts, preferred_element_type=jnp.float32)  7.84 us
    add x1, other arithmetic, shards(): jnp.where(mine, with_u, with_v)  4.14 us
  transfers between devices with their start and end apart: 16, of which 10 were waited for; matrix products, arithmetic and copies ran while one was open for 16% of the time, Pallas kernels for 0%

profile of v2, /device:TPU:3, one launch (start us, length us, event | category | flops | bytes accessed | tf_op | source)
XLA Modules:
  0.0 180.7 jit_solution(14620556738180141161)
XLA Ops:
  0.7 1.0 fusion.130
  1.8 1.0 fusion.129
  3.3 1.0 fusion.67
  4.4 1.0 fusion.70
  5.5 1.0 fusion.73
  6.6 1.0 fusion.76
  7.6 1.0 fusion.79
  8.7 1.0 fusion.82
  9.8 1.0 fusion.85
  10.9 1.0 fusion.88
  12.6 2.0 %multiply_reduce_fusion.2 = (f32[256]{0:T(256)S(1)}, f32[256,2048]{1,0:T(8,128)}) fusion(bf16[256,2048]{1,0:T(8,128)(2,1)S(1)} %fusion.108, f32[2048]{0:T(1024)S(1)} %copy-done.15, f32[2048]{0:T(1024)S(1)} %copy-done.22, bf16[256,256]{1,0:T(8,128)(2,1)S(1)} %convolution_convert_fusion.1, bf16[2048,256]{1,0:T(8,128)(2,1)S(1)} %copy-done), kind=kOutput, calls=%fused_computation.23 | convolution fusion | flops 271580928 | bytes 4342784 | tf_op jit(solution)/shard_map/dot_general | solution.py:147
  15.7 2.0 %fusion.90 = f32[2048,256]{1,0:T(8,128)} fusion(bf16[256,256]{1,0:T(8,128)(2,1)S(1)} %convolution_convert_fusion.1, bf16[256,2048]{1,0:T(8,128)(2,1)S(1)} %fusion.108, f32[256]{0:T(256)S(1)} %get-tuple-element.100, f32[2048]{0:T(1024)S(1)} %copy-done.15), kind=kOutput, calls=%fused_computation.149 | convolution fusion | flops 270532608 | bytes 3286016 | tf_op jit(solution)/shard_map/dot_general | solution.py:159
  17.7 2.2 %fusion.2 = (f32[2048]{0:T(1024)S(1)}, f32[2048]{0:T(1024)S(1)}) fusion(bf16[256,2048]{1,0:T(8,128)(2,1)S(1)} %fusion.108, f32[256]{0:T(256)S(1)} %get-tuple-element.100, f32[2048]{0:T(1024)S(1)} %copy-done.15, f32[256,2048]{1,0:T(8,128)} %get-tuple-element.106), kind=kLoop, calls=%fused_computation.17 | loop fusion | flops 4190208 | bytes 3171328 | tf_op jit(solution)/shard_map/reduce_sum | solution.py:157
  20.4 1.1 pad.12
  21.8 1.7 fusion.6
  23.5 0.9 collective-permute-start
  28.5 1.1 gather_fusion
  31.3 4.1 %select_add_fusion = f32[8,264,256]{2,1,0:T(8,128)} fusion(f32[8,264,256]{2,1,0:T(8,128)} %collective-permute-done, f32[8,1,256]{2,1,0:T(1,128)} %copy-done.18, f32[8,1,256]{2,1,0:T(1,128)} %bitcast.189, f32[8,256,256]{2,1,0:T(8,128)} %bitcast.149, f32[8,1,256]{2,1,0:T(1,128)} %bitcast.187, f32[8,256,256]{2,1,0:T(8,128)S(1)} %bitcast.147, ...), kind=kLoop, calls=%fused_computation.21 | loop fusion | flops 4325376 | bytes 8545313 | tf_op jit(solution)/shard_map/add | solution.py:183
  35.4 10.0 %all-to-all-start = ((f32[8,264,256]{2,1,0:T(8,128)}), f32[8,264,256]{2,1,0:T(8,128)}, u32[]{:S(2)}, u32[]{:S(2)}) async-start(f32[8,264,256]{2,1,0:T(8,128)} %select_add_fusion), calls=%async_computation | async-start | bytes 4325376 | tf_op jit(solution)/shard_map/all_to_all | solution.py:42
  45.5 1.3 collective-permute-done.1
  46.9 1.3 collective-permute-start.2
  48.2 14.2 %collective-permute-done.2 = f32[1,16,8,256]{3,2,1,0:T(8,128)S(1)} collective-permute-done((f32[1,16,8,256]{3,2,1,0:T(8,128)S(1)}, f32[1,16,8,256]{3,2,1,0:T(8,128)S(1)}, u32[]{:S(2)}, u32[]{:S(2)}) %collective-permute-start.2) | collective-permute-done | bytes 131104 | tf_op jit(solution)/shard_map/ppermute | solution.py:79
  62.6 3.8 %collective-permute-done.3 = f32[8,2,8,256]{3,2,1,0:T(8,128)S(1)} collective-permute-done((f32[8,2,8,256]{3,2,1,0:T(8,128)S(1)}, f32[8,2,8,256]{3,2,1,0:T(8,128)S(1)}, u32[]{:S(2)}, u32[]{:S(2)}) %collective-permute-start.3) | collective-permute-done | bytes 131104 | tf_op jit(solution)/shard_map/ppermute | solution.py:79
  66.4 1.0 collective-permute-start.4
  67.4 5.2 %collective-permute-done.4 = f32[4,4,8,256]{3,2,1,0:T(8,128)S(1)} collective-permute-done((f32[4,4,8,256]{3,2,1,0:T(8,128)S(1)}, f32[4,4,8,256]{3,2,1,0:T(8,128)S(1)}, u32[]{:S(2)}, u32[]{:S(2)}) %collective-permute-start.4) | collective-permute-done | bytes 131104 | tf_op jit(solution)/shard_map/ppermute | solution.py:79
  72.7 3.6 %collective-permute-start.5 = (f32[2,8,8,256]{3,2,1,0:T(8,128)S(1)}, f32[2,8,8,256]{3,2,1,0:T(8,128)S(1)}, u32[]{:S(2)}, u32[]{:S(2)}) collective-permute-start(f32[2,8,8,256]{3,2,1,0:T(8,128)S(1)} %get-tuple-element.56), channel_id=1, source_target_pairs={{0,8},{1,9},{2,10},{3,11},{4,12},{5,13},{6,14},{7,15},{8,0},{9,1},... | collective-permute-start | bytes 393224 | tf_op jit(solution)/shard_map/ppermute | solution.py:79
  76.3 1.8 reduce_sum.175
  78.9 5.8 %all-to-all-start.1 = ((f32[16,24,256]{2,1,0:T(8,128)}), f32[16,24,256]{2,1,0:T(8,128)S(1)}, u32[]{:S(2)}, u32[]{:S(2)}) async-start(f32[16,24,256]{2,1,0:T(8,128)} %pad_maximum_fusion.4), calls=%async_computation.1 | async-start | bytes 786432 | tf_op jit(solution)/shard_map/all_to_all | solution.py:42
  86.3 1.6 scatter_fusion
  87.9 1.0 gather_fusion.1
  89.0 7.8 %all-to-all-done.1 = f32[16,24,256]{2,1,0:T(8,128)S(1)} async-done(((f32[16,24,256]{2,1,0:T(8,128)}), f32[16,24,256]{2,1,0:T(8,128)S(1)}, u32[]{:S(2)}, u32[]{:S(2)}) %all-to-all-start.1) | async-done | bytes 393248 | tf_op jit(solution)/shard_map/all_to_all | solution.py:42
  96.9 5.5 %collective-permute-start.6 = (f32[16,1,8,256]{3,2,0,1:T(8,128)S(1)}, f32[16,1,8,256]{3,2,0,1:T(8,128)S(1)}, u32[]{:S(2)}, u32[]{:S(2)}) collective-permute-start(f32[16,1,8,256]{3,2,0,1:T(8,128)S(1)} %get-tuple-element.54), channel_id=1, source_target_pairs={{0,1},{1,0},{2,3},{3,2},{4,5},{5,4},{6,7},{7,6},{8,9},{9,8},{10,11... | collective-permute-start | bytes 393224 | tf_op jit(solution)/shard_map/ppermute | solution.py:79
  103.1 4.3 %all-to-all-start.2 = ((f32[16,16,256]{2,1,0:T(8,128)}), f32[16,16,256]{2,1,0:T(8,128)S(1)}, u32[]{:S(2)}, u32[]{:S(2)}) async-start(f32[16,16,256]{2,1,0:T(8,128)} %broadcast_in_dim.233), calls=%async_computation.2 | async-start | bytes 524288 | tf_op jit(solution)/shard_map/all_to_all | solution.py:42
  107.6 5.4 %collective-permute-done.7 = f32[1,16,8,256]{3,2,1,0:T(8,128)S(1)} collective-permute-done((f32[1,16,8,256]{3,2,1,0:T(8,128)S(1)}, f32[1,16,8,256]{3,2,1,0:T(8,128)S(1)}, u32[]{:S(2)}, u32[]{:S(2)}) %collective-permute-start.7) | collective-permute-done | bytes 131104 | tf_op jit(solution)/shard_map/ppermute | solution.py:79
  113.0 5.9 %all-to-all-done.2 = f32[16,16,256]{2,1,0:T(8,128)S(1)} async-done(((f32[16,16,256]{2,1,0:T(8,128)}), f32[16,16,256]{2,1,0:T(8,128)S(1)}, u32[]{:S(2)}, u32[]{:S(2)}) %all-to-all-start.2) | async-done | bytes 262176 | tf_op jit(solution)/shard_map/all_to_all | solution.py:42
  118.9 1.5 broadcast_in_dim.234
  120.4 4.4 %all-to-all-start.3 = ((f32[8,264,256]{2,1,0:T(8,128)}), f32[8,264,256]{2,1,0:T(8,128)}, u32[]{:S(2)}, u32[]{:S(2)}) async-start(f32[8,264,256]{2,1,0:T(8,128)} %broadcast_in_dim.234), calls=%async_computation.3 | async-start | bytes 4325376 | tf_op jit(solution)/shard_map/all_to_all | solution.py:42
  124.9 1.8 fusion.1
  129.0 4.4 %collective-permute-done.8 = f32[8,2,8,256]{3,2,1,0:T(8,128)S(1)} collective-permute-done((f32[8,2,8,256]{3,2,1,0:T(8,128)S(1)}, f32[8,2,8,256]{3,2,1,0:T(8,128)S(1)}, u32[]{:S(2)}, u32[]{:S(2)}) %collective-permute-start.8) | collective-permute-done | bytes 131104 | tf_op jit(solution)/shard_map/ppermute | solution.py:79
  133.5 1.8 %collective-permute-start.9 = (f32[4,4,8,256]{3,2,1,0:T(8,128)S(1)}, f32[4,4,8,256]{3,2,1,0:T(8,128)S(1)}, u32[]{:S(2)}, u32[]{:S(2)}) collective-permute-start(f32[4,4,8,256]{3,2,1,0:T(8,128)S(1)} %get-tuple-element.48), channel_id=1, source_target_pairs={{0,4},{1,5},{2,6},{3,7},{4,0},{5,1},{6,2},{7,3},{8,12},{9,13},{10,... | collective-permute-start | bytes 393224 | tf_op jit(solution)/shard_map/ppermute | solution.py:79
  136.1 6.9 %collective-permute-done.9 = f32[4,4,8,256]{3,2,1,0:T(8,128)S(1)} collective-permute-done((f32[4,4,8,256]{3,2,1,0:T(8,128)S(1)}, f32[4,4,8,256]{3,2,1,0:T(8,128)S(1)}, u32[]{:S(2)}, u32[]{:S(2)}) %collective-permute-start.9) | collective-permute-done | bytes 131104 | tf_op jit(solution)/shard_map/ppermute | solution.py:79
  143.3 1.8 convolution_add_fusion.6
  145.5 6.6 %collective-permute-done.10 = f32[2,8,8,256]{3,2,1,0:T(8,128)S(1)} collective-permute-done((f32[2,8,8,256]{3,2,1,0:T(8,128)S(1)}, f32[2,8,8,256]{3,2,1,0:T(8,128)S(1)}, u32[]{:S(2)}, u32[]{:S(2)}) %collective-permute-start.10) | collective-permute-done | bytes 131104 | tf_op jit(solution)/shard_map/ppermute | solution.py:79
  152.2 10.9 %collective-permute-start.11 = (f32[8,264,256]{2,1,0:T(8,128)}, f32[8,264,256]{2,1,0:T(8,128)}, u32[]{:S(2)}, u32[]{:S(2)}) collective-permute-start(f32[8,264,256]{2,1,0:T(8,128)} %all-to-all-done.3), channel_id=1, source_target_pairs={{0,1},{1,0},{2,3},{3,2},{4,5},{5,4},{6,7},{7,6},{8,9},{9,8},{10,11... | collective-permute-start | bytes 6488072 | tf_op jit(solution)/shard_map/ppermute | solution.py:38
  163.2 2.0 %convolution_add_fusion.5 = f32[1024,256]{0,1:T(8,128)S(1)} fusion(f32[1024,256]{0,1:T(8,128)} %convolution_add_fusion.6, s32[256]{0:T(256)S(1)} %bitcast.213, s32[256]{0:T(256)S(1)} %bitcast.215, s32[256]{0:T(256)S(1)} %bitcast.217, s32[256]{0:T(256)} %bitcast.219, bf16[256,2048]{1,0:T(8,128)(2,1)S(1)} %copy-done.12), kind=kOutput, calls=%fused_computation.33 | convolution fusion | flops 138674176 | bytes 2232320 | tf_op jit(solution)/shard_map/dot_general | solution.py:247
  169.6 1.4 scatter_custom_fusion.1
  171.1 3.0 %broadcast_select_fusion.1 = (f32[8,264,256]{2,1,0:T(8,128)S(1)}, f32[8,264,256]{2,1,0:T(8,128)S(1)}) fusion(f32[8,264,256]{2,1,0:T(8,128)} %all-to-all-done.3, f32[8,264,256]{2,1,0:T(8,128)} %collective-permute-done.11, pred[]{:T(512)S(6)} %eq.739), kind=kLoop, calls=%fused_computation.40 | loop fusion | flops 1081344 | bytes 8650753 | tf_op jit(solution)/shard_map/jit(_where)/select_n | solution.py:227
  176.5 2.4 %fusion = f32[2,2048,256]{2,1,0:T(8,128)} fusion(f32[1,2048,256]{2,1,0:T(8,128)S(1)} %bitcast.153, f32[1,2048,256]{2,1,0:T(8,128)S(1)} %bitcast.151, f32[2]{0:T(128)S(1)} %add_rsqrt_fusion.1), kind=kLoop, calls=%fused_computation.8 | loop fusion | flops 2097152 | bytes 8388616 | tf_op jit(solution)/shard_map/mul | solution.py:238
  (314 shorter events, 22.9 us)
Async XLA Ops:
  0.6 11.9 %copy-start = (bf16[2048,256]{1,0:T(8,128)(2,1)S(1)}, bf16[2048,256]{1,0:T(8,128)(2,1)}, u32[]{:S(2)}) copy-start(bf16[2048,256]{1,0:T(8,128)(2,1)} %param.22) | copy-start | bytes 3145732
  1.8 9.0 %copy-start.67 = (s32[256,1]{0,1:T(1,128)}, s32[256,1]{0,1:T(1,128)S(1)}, u32[]{:S(2)}) copy-start(s32[256,1]{0,1:T(1,128)S(1)} %get-tuple-element.86) | copy-start | bytes 3076
  1.8 9.0 %copy-start.69 = (s32[256,1]{0,1:T(1,128)}, s32[256,1]{0,1:T(1,128)S(1)}, u32[]{:S(2)}) copy-start(s32[256,1]{0,1:T(1,128)S(1)} %get-tuple-element.98) | copy-start | bytes 3076
  3.0 6.8 %copy-start.34 = (s32[256,1]{0,1:T(1,128)}, s32[256,1]{0,1:T(1,128)S(1)}, u32[]{:S(2)}) copy-start(s32[256,1]{0,1:T(1,128)S(1)} %get-tuple-element.69) | copy-start | bytes 3076
  3.0 7.8 %copy-start.30 = (s32[256,1]{0,1:T(1,128)}, s32[256,1]{0,1:T(1,128)S(1)}, u32[]{:S(2)}) copy-start(s32[256,1]{0,1:T(1,128)S(1)} %get-tuple-element.67) | copy-start | bytes 3076
  3.0 7.8 %copy-start.32 = (s32[256,1]{0,1:T(1,128)}, s32[256,1]{0,1:T(1,128)S(1)}, u32[]{:S(2)}) copy-start(s32[256,1]{0,1:T(1,128)S(1)} %get-tuple-element.68) | copy-start | bytes 3076
  23.5 7.8 %copy-start.7 = (f32[2048,256]{1,0:T(8,128)S(1)}, f32[2048,256]{1,0:T(8,128)}, u32[]{:S(2)}) copy-start(f32[2048,256]{1,0:T(8,128)} %fusion.90) | copy-start | bytes 6291460
  23.5 7.8 %collective-permute-start = (f32[8,264,256]{2,1,0:T(8,128)}, f32[8,264,256]{2,1,0:T(8,128)}, u32[]{:S(2)}, u32[]{:S(2)}) collective-permute-start(f32[8,264,256]{2,1,0:T(8,128)} %fusion.6), channel_id=1, source_target_pairs={{0,1},{1,0},{2,3},{3,2},{4,5},{5,4},{6,7},{7,6},{8,9},{9,8},{10,11... | collective-permute-start | bytes 6488072 | tf_op jit(solution)/shard_map/ppermute | solution.py:38
  35.4 10.0 %copy-start.13 = (f32[32,8,256]{2,1,0:T(8,128)S(1)}, f32[32,8,256]{2,1,0:T(8,128)}, u32[]{:S(2)}) copy-start(f32[32,8,256]{2,1,0:T(8,128)} %bitcast_select_fusion.1) | copy-start | bytes 786436
  35.4 31.0 %all-to-all-start = ((f32[8,264,256]{2,1,0:T(8,128)}), f32[8,264,256]{2,1,0:T(8,128)}, u32[]{:S(2)}, u32[]{:S(2)}) async-start(f32[8,264,256]{2,1,0:T(8,128)} %select_add_fusion), calls=%async_computation | async-start | bytes 4325376 | tf_op jit(solution)/shard_map/all_to_all | solution.py:42
  45.4 1.4 collective-permute-start.1
  46.9 15.5 %collective-permute-start.2 = (f32[1,16,8,256]{3,2,1,0:T(8,128)S(1)}, f32[1,16,8,256]{3,2,1,0:T(8,128)S(1)}, u32[]{:S(2)}, u32[]{:S(2)}) collective-permute-start(f32[1,16,8,256]{3,2,1,0:T(8,128)S(1)} %get-tuple-element.62), channel_id=1, source_target_pairs={{0,16},{1,17},{2,18},{3,19},{4,20},{5,21},{6,22},{7,23},{8,24},{9,... | collective-permute-start | bytes 393224 | tf_op jit(solution)/shard_map/ppermute | solution.py:79
  62.5 3.9 %collective-permute-start.3 = (f32[8,2,8,256]{3,2,1,0:T(8,128)S(1)}, f32[8,2,8,256]{3,2,1,0:T(8,128)S(1)}, u32[]{:S(2)}, u32[]{:S(2)}) collective-permute-start(f32[8,2,8,256]{3,2,1,0:T(8,128)S(1)} %get-tuple-element.60), channel_id=1, source_target_pairs={{0,2},{1,3},{2,0},{3,1},{4,6},{5,7},{6,4},{7,5},{8,10},{9,11},{10,... | collective-permute-start | bytes 393224 | tf_op jit(solution)/shard_map/ppermute | solution.py:79
  66.4 6.2 %collective-permute-start.4 = (f32[4,4,8,256]{3,2,1,0:T(8,128)S(1)}, f32[4,4,8,256]{3,2,1,0:T(8,128)S(1)}, u32[]{:S(2)}, u32[]{:S(2)}) collective-permute-start(f32[4,4,8,256]{3,2,1,0:T(8,128)S(1)} %get-tuple-element.58), channel_id=1, source_target_pairs={{0,4},{1,5},{2,6},{3,7},{4,0},{5,1},{6,2},{7,3},{8,12},{9,13},{10,... | collective-permute-start | bytes 393224 | tf_op jit(solution)/shard_map/ppermute | solution.py:79
  72.7 12.1 %collective-permute-start.5 = (f32[2,8,8,256]{3,2,1,0:T(8,128)S(1)}, f32[2,8,8,256]{3,2,1,0:T(8,128)S(1)}, u32[]{:S(2)}, u32[]{:S(2)}) collective-permute-start(f32[2,8,8,256]{3,2,1,0:T(8,128)S(1)} %get-tuple-element.56), channel_id=1, source_target_pairs={{0,8},{1,9},{2,10},{3,11},{4,12},{5,13},{6,14},{7,15},{8,0},{9,1},... | collective-permute-start | bytes 393224 | tf_op jit(solution)/shard_map/ppermute | solution.py:79
  78.1 7.7 %copy-start.24 = (f32[1024]{0:T(1024)S(1)}, f32[1024]{0:T(1024)}, u32[]{:S(2)}) copy-start(f32[1024]{0:T(1024)} %param.18) | copy-start | bytes 12292
  78.1 8.1 %copy-start.4 = (f32[1024,256]{1,0:T(8,128)S(1)}, f32[1024,256]{1,0:T(8,128)}, u32[]{:S(2)}) copy-start(f32[1024,256]{1,0:T(8,128)} %param.17) | copy-start | bytes 3145732
  78.9 17.9 %all-to-all-start.1 = ((f32[16,24,256]{2,1,0:T(8,128)}), f32[16,24,256]{2,1,0:T(8,128)S(1)}, u32[]{:S(2)}, u32[]{:S(2)}) async-start(f32[16,24,256]{2,1,0:T(8,128)} %pad_maximum_fusion.4), calls=%async_computation.1 | async-start | bytes 786432 | tf_op jit(solution)/shard_map/all_to_all | solution.py:42
  87.9 15.2 %copy-start.3 = (f32[1024,256]{1,0:T(8,128)}, f32[1024,256]{1,0:T(8,128)S(1)}, u32[]{:S(2)}) copy-start(f32[1024,256]{1,0:T(8,128)S(1)} %scatter_fusion) | copy-start | bytes 3145732
  96.9 10.5 %collective-permute-start.6 = (f32[16,1,8,256]{3,2,0,1:T(8,128)S(1)}, f32[16,1,8,256]{3,2,0,1:T(8,128)S(1)}, u32[]{:S(2)}, u32[]{:S(2)}) collective-permute-start(f32[16,1,8,256]{3,2,0,1:T(8,128)S(1)} %get-tuple-element.54), channel_id=1, source_target_pairs={{0,1},{1,0},{2,3},{3,2},{4,5},{5,4},{6,7},{7,6},{8,9},{9,8},{10,11... | collective-permute-start | bytes 393224 | tf_op jit(solution)/shard_map/ppermute | solution.py:79
  103.1 15.8 %all-to-all-start.2 = ((f32[16,16,256]{2,1,0:T(8,128)}), f32[16,16,256]{2,1,0:T(8,128)S(1)}, u32[]{:S(2)}, u32[]{:S(2)}) async-start(f32[16,16,256]{2,1,0:T(8,128)} %broadcast_in_dim.233), calls=%async_computation.2 | async-start | bytes 524288 | tf_op jit(solution)/shard_map/all_to_all | solution.py:42
  107.5 5.5 %collective-permute-start.7 = (f32[1,16,8,256]{3,2,1,0:T(8,128)S(1)}, f32[1,16,8,256]{3,2,1,0:T(8,128)S(1)}, u32[]{:S(2)}, u32[]{:S(2)}) collective-permute-start(f32[1,16,8,256]{3,2,1,0:T(8,128)S(1)} %get-tuple-element.52), channel_id=1, source_target_pairs={{0,16},{1,17},{2,18},{3,19},{4,20},{5,21},{6,22},{7,23},{8,24},{9,... | collective-permute-start | bytes 393224 | tf_op jit(solution)/shard_map/ppermute | solution.py:79
  120.4 31.8 %all-to-all-start.3 = ((f32[8,264,256]{2,1,0:T(8,128)}), f32[8,264,256]{2,1,0:T(8,128)}, u32[]{:S(2)}, u32[]{:S(2)}) async-start(f32[8,264,256]{2,1,0:T(8,128)} %broadcast_in_dim.234), calls=%async_computation.3 | async-start | bytes 4325376 | tf_op jit(solution)/shard_map/all_to_all | solution.py:42
  126.7 16.6 %copy-start.11 = (bf16[256,2048]{1,0:T(8,128)(2,1)}, bf16[256,2048]{1,0:T(8,128)(2,1)S(1)}, u32[]{:S(2)}) copy-start(bf16[256,2048]{1,0:T(8,128)(2,1)S(1)} %fusion.1) | copy-start | bytes 3145732
  127.6 7.8 %copy-start.66 = (s32[256,1]{0,1:T(1,128)S(1)}, s32[256,1]{0,1:T(1,128)}, u32[]{:S(2)}) copy-start(s32[256,1]{0,1:T(1,128)} %copy-done.65) | copy-start | bytes 3076
  127.6 7.8 %copy-start.72 = (s32[256,1]{0,1:T(1,128)S(1)}, s32[256,1]{0,1:T(1,128)}, u32[]{:S(2)}) copy-start(s32[256,1]{0,1:T(1,128)} %copy-done.71) | copy-start | bytes 3076
  127.6 7.7 %copy-start.74 = (s32[256,1]{0,1:T(1,128)S(1)}, s32[256,1]{0,1:T(1,128)}, u32[]{:S(2)}) copy-start(s32[256,1]{0,1:T(1,128)} %copy-done.73) | copy-start | bytes 3076
  127.6 7.7 %copy-start.76 = (s32[256,1]{0,1:T(1,128)S(1)}, s32[256,1]{0,1:T(1,128)}, u32[]{:S(2)}) copy-start(s32[256,1]{0,1:T(1,128)} %copy-done.75) | copy-start | bytes 3076
  127.6 5.8 %collective-permute-start.8 = (f32[8,2,8,256]{3,2,1,0:T(8,128)S(1)}, f32[8,2,8,256]{3,2,1,0:T(8,128)S(1)}, u32[]{:S(2)}, u32[]{:S(2)}) collective-permute-start(f32[8,2,8,256]{3,2,1,0:T(8,128)S(1)} %get-tuple-element.50), channel_id=1, source_target_pairs={{0,2},{1,3},{2,0},{3,1},{4,6},{5,7},{6,4},{7,5},{8,10},{9,11},{10,... | collective-permute-start | bytes 393224 | tf_op jit(solution)/shard_map/ppermute | solution.py:79
  133.5 9.9 %copy-start.58 = (s32[256,1]{0,1:T(1,128)S(1)}, s32[256,1]{0,1:T(1,128)}, u32[]{:S(2)}) copy-start(s32[256,1]{0,1:T(1,128)} %copy-done.57) | copy-start | bytes 3076
  133.5 9.9 %copy-start.60 = (s32[256,1]{0,1:T(1,128)S(1)}, s32[256,1]{0,1:T(1,128)}, u32[]{:S(2)}) copy-start(s32[256,1]{0,1:T(1,128)} %copy-done.59) | copy-start | bytes 3076
  133.5 9.8 %copy-start.62 = (s32[256,1]{0,1:T(1,128)S(1)}, s32[256,1]{0,1:T(1,128)}, u32[]{:S(2)}) copy-start(s32[256,1]{0,1:T(1,128)} %copy-done.61) | copy-start | bytes 3076
  133.5 9.8 %copy-start.64 = (s32[256,1]{0,1:T(1,128)S(1)}, s32[256,1]{0,1:T(1,128)}, u32[]{:S(2)}) copy-start(s32[256,1]{0,1:T(1,128)} %copy-done.63) | copy-start | bytes 3076
  133.5 9.6 %collective-permute-start.9 = (f32[4,4,8,256]{3,2,1,0:T(8,128)S(1)}, f32[4,4,8,256]{3,2,1,0:T(8,128)S(1)}, u32[]{:S(2)}, u32[]{:S(2)}) collective-permute-start(f32[4,4,8,256]{3,2,1,0:T(8,128)S(1)} %get-tuple-element.48), channel_id=1, source_target_pairs={{0,4},{1,5},{2,6},{3,7},{4,0},{5,1},{6,2},{7,3},{8,12},{9,13},{10,... | collective-permute-start | bytes 393224 | tf_op jit(solution)/shard_map/ppermute | solution.py:79
  143.1 9.0 %collective-permute-start.10 = (f32[2,8,8,256]{3,2,1,0:T(8,128)S(1)}, f32[2,8,8,256]{3,2,1,0:T(8,128)S(1)}, u32[]{:S(2)}, u32[]{:S(2)}) collective-permute-start(f32[2,8,8,256]{3,2,1,0:T(8,128)S(1)} %get-tuple-element.46), channel_id=1, source_target_pairs={{0,8},{1,9},{2,10},{3,11},{4,12},{5,13},{6,14},{7,15},{8,0},{9,1},... | collective-permute-start | bytes 393224 | tf_op jit(solution)/shard_map/ppermute | solution.py:79
  145.1 18.0 %copy-start.12 = (bf16[256,2048]{1,0:T(8,128)(2,1)S(1)}, bf16[256,2048]{1,0:T(8,128)(2,1)}, u32[]{:S(2)}) copy-start(bf16[256,2048]{1,0:T(8,128)(2,1)} %copy-done.11) | copy-start | bytes 3145732
  145.1 18.0 %copy-start.51 = (s32[256,1]{0,1:T(1,128)S(1)}, s32[256,1]{0,1:T(1,128)}, u32[]{:S(2)}) copy-start(s32[256,1]{0,1:T(1,128)} %copy-done.50) | copy-start | bytes 3076
  145.1 18.0 %copy-start.53 = (s32[256,1]{0,1:T(1,128)S(1)}, s32[256,1]{0,1:T(1,128)}, u32[]{:S(2)}) copy-start(s32[256,1]{0,1:T(1,128)} %copy-done.52) | copy-start | bytes 3076
  145.1 18.0 %copy-start.55 = (s32[256,1]{0,1:T(1,128)S(1)}, s32[256,1]{0,1:T(1,128)}, u32[]{:S(2)}) copy-start(s32[256,1]{0,1:T(1,128)} %copy-done.54) | copy-start | bytes 3076
  145.5 19.7 %copy-start.43 = (s32[256,1]{0,1:T(1,128)S(1)}, s32[256,1]{0,1:T(1,128)}, u32[]{:S(2)}) copy-start(s32[256,1]{0,1:T(1,128)} %copy-done.42) | copy-start | bytes 3076
  145.5 19.7 %copy-start.45 = (s32[256,1]{0,1:T(1,128)S(1)}, s32[256,1]{0,1:T(1,128)}, u32[]{:S(2)}) copy-start(s32[256,1]{0,1:T(1,128)} %copy-done.44) | copy-start | bytes 3076
  145.5 19.7 %copy-start.47 = (s32[256,1]{0,1:T(1,128)S(1)}, s32[256,1]{0,1:T(1,128)}, u32[]{:S(2)}) copy-start(s32[256,1]{0,1:T(1,128)} %copy-done.46) | copy-start | bytes 3076
  145.5 19.7 %copy-start.49 = (s32[256,1]{0,1:T(1,128)S(1)}, s32[256,1]{0,1:T(1,128)}, u32[]{:S(2)}) copy-start(s32[256,1]{0,1:T(1,128)} %copy-done.48) | copy-start | bytes 3076
  152.2 13.9 %copy-start.35 = (s32[256,1]{0,1:T(1,128)S(1)}, s32[256,1]{0,1:T(1,128)}, u32[]{:S(2)}) copy-start(s32[256,1]{0,1:T(1,128)} %copy-done.34) | copy-start | bytes 3076
  152.2 13.9 %copy-start.37 = (s32[256,1]{0,1:T(1,128)S(1)}, s32[256,1]{0,1:T(1,128)}, u32[]{:S(2)}) copy-start(s32[256,1]{0,1:T(1,128)} %copy-done.36) | copy-start | bytes 3076
  152.2 13.9 %copy-start.39 = (s32[256,1]{0,1:T(1,128)S(1)}, s32[256,1]{0,1:T(1,128)}, u32[]{:S(2)}) copy-start(s32[256,1]{0,1:T(1,128)} %copy-done.38) | copy-start | bytes 3076
  152.2 13.9 %copy-start.41 = (s32[256,1]{0,1:T(1,128)S(1)}, s32[256,1]{0,1:T(1,128)}, u32[]{:S(2)}) copy-start(s32[256,1]{0,1:T(1,128)} %copy-done.40) | copy-start | bytes 3076
  152.2 18.9 %collective-permute-start.11 = (f32[8,264,256]{2,1,0:T(8,128)}, f32[8,264,256]{2,1,0:T(8,128)}, u32[]{:S(2)}, u32[]{:S(2)}) collective-permute-start(f32[8,264,256]{2,1,0:T(8,128)} %all-to-all-done.3), channel_id=1, source_target_pairs={{0,1},{1,0},{2,3},{3,2},{4,5},{5,4},{6,7},{7,6},{8,9},{9,8},{10,11... | collective-permute-start | bytes 6488072 | tf_op jit(solution)/shard_map/ppermute | solution.py:38
  (63 other events, 189.8 us)

commit v3 on v2

v3 whole, which is shorter than its diff:
```python
import jax
import jax.numpy as jnp
from jax import lax
from jax.experimental import pallas as pl
from jax.experimental.pallas import tpu as pltpu
from jax.sharding import PartitionSpec as P

EPS = 1e-06
ETA = 0.05
AXES = ("trainer", "table")


def device_at(y, x, z, core):
    return (((y // 2 * 4 + x) * 2 + y % 2) * 8 + z % 8) * 2 + core


def first_groups():
    groups = []
    for y in range(4):
        for pair in range(4):
            groups.append([device_at(y, x, 2 * pair + b, 0) for x in range(4) for b in range(2)])
    for x in range(4):
        for pair in range(4):
            groups.append([device_at(y, x, 2 * pair + 1 + b, 1) for y in range(4) for b in range(2)])
    return groups


def second_groups():
    groups = []
    for x in range(4):
        for b in range(2):
            groups.append([device_at(y, x, 2 * k + b, 0) for y in range(4) for k in range(4)])
    for y in range(4):
        for b in range(2):
            groups.append([device_at(y, x, 2 * k + b, 1) for x in range(4) for k in range(4)])
    return groups


def swap_cores(value):
    return lax.ppermute(value, AXES, [(i, i ^ 1) for i in range(256)])


def exchange(value, groups):
    return lax.all_to_all(
        value, AXES, split_axis=0, concat_axis=0, tiled=True, axis_index_groups=groups
    )


def ranks(owner):
    listed = owner.shape[0]
    order = jnp.arange(listed, dtype=jnp.int32)
    earlier = (owner[:, None] == owner[None, :]) & (order[None, :] < order[:, None])
    return jnp.sum(earlier.astype(jnp.int32), axis=1)


def meta_row(columns, width):
    block = jnp.concatenate(columns, axis=1)
    return jnp.pad(block, ((0, 0), (0, width - block.shape[1])))[:, None, :]


def picked(values, index):
    hit = index[:, None] == jnp.arange(values.shape[0], dtype=jnp.int32)[None, :]
    return jnp.sum(jnp.where(hit, values[None, :], 0.0), axis=1)


def cross(value, bit):
    split = value.reshape(value.shape[0] // (2 * bit), 2, bit, *value.shape[1:])
    there = [(i, i ^ bit) for i in range(256)]
    came = lax.ppermute(split[:, 1], AXES, there)
    return jnp.stack([split[:, 0], came], axis=1).reshape(value.shape)


def dense_kernel(
    core_ref,
    slots_ref,
    labels_ref,
    cache_ref,
    u_ref,
    v_ref,
    bias_ref,
    head_ref,
    keep_ref,
    send_ref,
    dpooled_ref,
    high,
    mid,
    low,
    pooled,
    shifted,
    dlift,
):
    f32, bf16 = jnp.float32, jnp.bfloat16
    count, cells, width = slots_ref.shape[1], cache_ref.shape[0], cache_ref.shape[1]
    feats = u_ref.shape[0] // width
    looks = slots_ref.shape[0] // feats
    slots = jnp.transpose(slots_ref[...])
    rows = cache_ref[...]
    first = rows.astype(bf16)
    rest = rows - first.astype(f32)
    second = rest.astype(bf16)
    high[...] = first
    mid[...] = second
    low[...] = (rest - second.astype(f32)).astype(bf16)

    lane = lax.broadcasted_iota(jnp.int32, (count, cells), 1)
    for f in range(feats):
        counts = jnp.zeros((count, cells), f32)
        for look in range(looks):
            at = f * looks + look
            counts = counts + jnp.where(lane == slots[:, at : at + 1], 1.0, 0.0)
        counts = counts.astype(bf16)
        total = jnp.dot(counts, low[...], preferred_element_type=f32)
        total = total + jnp.dot(counts, mid[...], preferred_element_type=f32)
        total = total + jnp.dot(counts, high[...], preferred_element_type=f32)
        pooled[:, f * width : (f + 1) * width] = total.astype(bf16)

    latent = jnp.dot(pooled[...], v_ref[...], preferred_element_type=f32).astype(bf16)
    across = (((1,), (1,)), ((), ()))
    logit_wide = jnp.zeros((count, width), f32)
    for c in range(feats):
        cut = slice(c * width, (c + 1) * width)
        moved = lax.dot_general(latent, u_ref[cut, :], across, preferred_element_type=f32)
        moved = moved + bias_ref[:, cut]
        shifted[:, cut] = moved
        part = pooled[:, cut].astype(f32)
        logit_wide = logit_wide + (part * moved + part) * head_ref[:, cut]
    logit = jnp.sum(logit_wide, axis=1, keepdims=True)
    target = jnp.transpose(labels_ref[...]).astype(f32)
    small = jnp.exp(-jnp.abs(logit))
    losses = jnp.maximum(logit, 0.0) + jnp.log1p(small) - target * logit
    loss = jnp.sum(losses, axis=0, keepdims=True)
    dlogit = jnp.where(logit >= 0, 1.0, small) / (1.0 + small) - target

    mine = core_ref[0] == 0
    lane1 = lax.broadcasted_iota(jnp.int32, (1, width), 1)
    loss_row = jnp.where(lane1 == 0, loss, 0.0)
    back = jnp.zeros((count, width), f32)
    for c in range(feats):
        cut = slice(c * width, (c + 1) * width)
        part = pooled[:, cut].astype(f32)
        lift = dlogit * head_ref[:, cut] * part
        crossed = part * shifted[:, cut] + part
        dbias = jnp.sum(lift, axis=0, keepdims=True)
        dhead = jnp.sum(dlogit * crossed, axis=0, keepdims=True)
        lift = lift.astype(bf16)
        dlift[:, cut] = lift
        back = back + jnp.dot(lift, u_ref[cut, :], preferred_element_type=f32)
        keep_ref[c, width : width + 1, :] = jnp.where(mine, dbias, dhead)
        send_ref[c, width : width + 1, :] = jnp.where(mine, dhead, dbias)
        for ref in (keep_ref, send_ref):
            ref[c, width + 1 : width + 2, :] = loss_row
            ref[c, width + 2 : width + 8, :] = jnp.zeros((6, width), f32)
    dlatent = back.astype(bf16)

    down = (((0,), (0,)), ((), ()))
    right_keep = jnp.where(mine, latent, dlatent)
    right_send = jnp.where(mine, dlatent, latent)
    for c in range(feats):
        cut = slice(c * width, (c + 1) * width)
        lift, part = dlift[:, cut], pooled[:, cut]
        send_ref[c, :width, :] = lax.dot_general(
            jnp.where(mine, part, lift), right_send, down, preferred_element_type=f32
        )
        keep_ref[c, :width, :] = lax.dot_general(
            jnp.where(mine, lift, part), right_keep, down, preferred_element_type=f32
        )
    for c in range(feats):
        cut = slice(c * width, (c + 1) * width)
        through = lax.dot_general(dlatent, v_ref[cut, :], across, preferred_element_type=f32)
        through = through + dlogit * head_ref[:, cut] * (shifted[:, cut] + 1.0)
        dpooled_ref[:, cut] = through.astype(bf16)


def dense(core, slot_ids, labels, cache_rows, proj_u, proj_v, cross_bias, head):
    count, (cells, width) = slot_ids.shape[0], cache_rows.shape
    wide = proj_u.shape[0]
    blocks = wide // width
    vmem = pl.BlockSpec(memory_space=pltpu.VMEM)
    bundle = jax.ShapeDtypeStruct((blocks, width + 8, width), jnp.float32)
    return pl.pallas_call(
        dense_kernel,
        out_shape=(bundle, bundle, jax.ShapeDtypeStruct((count, wide), jnp.bfloat16)),
        in_specs=[pl.BlockSpec(memory_space=pltpu.SMEM)] + [vmem] * 7,
        out_specs=(vmem, vmem, vmem),
        scratch_shapes=[pltpu.VMEM((cells, width), jnp.bfloat16)] * 3
        + [
            pltpu.VMEM((count, wide), jnp.bfloat16),
            pltpu.VMEM((count, wide), jnp.float32),
            pltpu.VMEM((count, wide), jnp.bfloat16),
        ],
        compiler_params=pltpu.CompilerParams(vmem_limit_bytes=32 * 1024 * 1024),
        cost_estimate=pl.CostEstimate(flops=5_000_000_000, bytes_accessed=9_000_000, transcendentals=1000),
        name="dense",
    )(
        core[None],
        slot_ids.T,
        labels[None, :],
        cache_rows,
        proj_u,
        proj_v,
        cross_bias[None, :],
        head[None, :],
    )


def payload_kernel(
    slot_ref, evict_ref, miss_ref, accum_ref, cache_ref, out_ref, taken
):
    owners, per = taken.shape[0], out_ref.shape[0] // taken.shape[0]
    width = out_ref.shape[1]
    lane = lax.broadcasted_iota(jnp.int32, (1, width), 1)
    base = jnp.where((lane >= per) & (lane < 2 * per), -1.0, 0.0)

    def clear(o, _):
        taken[o] = 0
        out_ref[pl.ds(o * per, per - 1), :] = jnp.zeros((per - 1, width), jnp.float32)
        out_ref[pl.ds(o * per + per - 1, 1), :] = base
        return 0

    lax.fori_loop(0, owners, clear, 0, unroll=True)

    def leave(i, _):
        owner = evict_ref[0, i]
        rank = taken[owner]
        taken[owner] = rank + 1
        slot = slot_ref[i]
        out_ref[pl.ds(owner * per + rank, 1), :] = cache_ref[pl.ds(slot, 1), :]
        spot = pl.ds(owner * per + per - 1, 1)
        meta = jnp.where(lane == rank, accum_ref[slot], out_ref[spot, :])
        row = evict_ref[1, i].astype(jnp.float32)
        out_ref[spot, :] = jnp.where(lane == per + rank, row, meta)
        return 0

    lax.fori_loop(0, slot_ref.shape[0], leave, 0, unroll=8)

    def reset(o, _):
        taken[o] = 0
        return 0

    lax.fori_loop(0, owners, reset, 0, unroll=True)

    def ask(i, _):
        owner = miss_ref[0, i]
        rank = taken[owner]
        taken[owner] = rank + 1
        spot = pl.ds(owner * per + per - 1, 1)
        row = miss_ref[1, i].astype(jnp.float32)
        out_ref[spot, :] = jnp.where(lane == 2 * per + rank, row, out_ref[spot, :])
        return 0

    lax.fori_loop(0, slot_ref.shape[0], ask, 0, unroll=8)


def payload(evict_slot, evict_dest, miss_dest, cache_accum, cache_rows, owners, per):
    smem = pl.BlockSpec(memory_space=pltpu.SMEM)
    vmem = pl.BlockSpec(memory_space=pltpu.VMEM)
    return pl.pallas_call(
        payload_kernel,
        out_shape=jax.ShapeDtypeStruct((owners * per, cache_rows.shape[1]), jnp.float32),
        in_specs=[smem] * 4 + [vmem],
        out_specs=vmem,
        scratch_shapes=[pltpu.SMEM((owners,), jnp.int32)],
        cost_estimate=pl.CostEstimate(flops=100_000, bytes_accessed=1_500_000, transcendentals=0),
        name="payload",
    )(evict_slot, evict_dest.T, miss_dest.T, cache_accum, cache_rows)


def scaled(index, half_ref, proj_ref, stage, sems):
    blocks, width = half_ref.shape[0], half_ref.shape[2]
    squares = jnp.zeros((width, width), jnp.float32)
    for c in range(blocks):
        block = half_ref[c, :width, :]
        squares = squares + block * block
    total = jnp.sum(jnp.sum(squares, axis=0, keepdims=True), axis=1, keepdims=True)
    scale = lax.rsqrt(total / (blocks * width * width) + EPS)
    copies = []
    for c in range(blocks):
        stage[c] = half_ref[c, :width, :] * scale
        copies.append(
            pltpu.make_async_copy(
                stage.at[c], proj_ref.at[index, pl.ds(c * width, width), :], sems.at[c]
            )
        )
        copies[-1].start()
    return copies


def own_kernel(core_ref, half_ref, proj_ref, stage, sems):
    for copy in scaled(core_ref[0], half_ref, proj_ref, stage, sems):
        copy.wait()


def other_kernel(
    core_ref, proj_in, own_ref, half_ref, proj_ref, vec_ref, loss_ref, stage, sems
):
    core = core_ref[0]
    copies = scaled(1 - core, half_ref, proj_ref, stage, sems)
    blocks, width = half_ref.shape[0], half_ref.shape[2]
    mine = core == 0
    own = [own_ref[c, 0:1, :] for c in range(blocks)]
    far = [half_ref[c, width : width + 1, :] for c in range(blocks)]
    for index in (0, 1):
        rows = [jnp.where(mine, *((a, b) if index == 0 else (b, a))) for a, b in zip(own, far)]
        squares = sum(row * row for row in rows)
        total = jnp.sum(squares, axis=1, keepdims=True)
        scale = lax.rsqrt(total / (blocks * width) + EPS)
        for c in range(blocks):
            vec_ref[index : index + 1, c * width : (c + 1) * width] = rows[c] * scale
    loss_ref[...] = jnp.where(
        mine, half_ref[0, width + 1 : width + 2, :128], own_ref[0, 1:2, :128]
    )
    for copy in copies:
        copy.wait()


def normalized(core, own, other):
    blocks, depth, width = own.shape
    wide = blocks * width
    smem = pl.BlockSpec(memory_space=pltpu.SMEM)
    vmem = pl.BlockSpec(memory_space=pltpu.VMEM)
    anywhere = pl.BlockSpec(memory_space=pl.ANY)
    scratch = [
        pltpu.VMEM((blocks, width, width), jnp.float32),
        pltpu.SemaphoreType.DMA((blocks,)),
    ]
    proj = jax.ShapeDtypeStruct((2, wide, width), jnp.float32)
    limit = pltpu.CompilerParams(vmem_limit_bytes=16 * 1024 * 1024)
    half = pl.pallas_call(
        own_kernel,
        out_shape=proj,
        in_specs=[smem, vmem],
        out_specs=anywhere,
        scratch_shapes=scratch,
        compiler_params=limit,
        name="scale_own",
    )(core[None], own)
    return pl.pallas_call(
        other_kernel,
        out_shape=(
            proj,
            jax.ShapeDtypeStruct((2, wide), jnp.float32),
            jax.ShapeDtypeStruct((1, 128), jnp.float32),
        ),
        in_specs=[smem, anywhere, vmem, vmem],
        out_specs=(anywhere, vmem, vmem),
        scratch_shapes=scratch,
        input_output_aliases={1: 0},
        compiler_params=limit,
        name="scale_other",
    )(core[None], half, own[:, width:, :], other)


def shards(
    slot_ids,
    labels,
    cache_rows,
    cache_accum,
    table_rows,
    table_accum,
    miss_dest,
    evict_slot,
    evict_dest,
    proj_u,
    proj_v,
    cross_bias,
    head,
):
    owners = 32
    per = 8
    cap = 6
    width = cache_rows.shape[1]
    owned = table_rows.shape[0]
    cells = cache_rows.shape[0]
    spots = owners * per
    core = lax.axis_index("table") % 2

    me = lax.axis_index("table")
    sent = payload(
        evict_slot, evict_dest, miss_dest, cache_accum, cache_rows, owners, per
    ).reshape(owners, per, width)
    sent, slots_late = lax.optimization_barrier((sent, slot_ids))
    got = lax.all_to_all(sent, "table", split_axis=0, concat_axis=0, tiled=True)

    count = slot_ids.shape[0]
    feats = proj_u.shape[0] // width
    looks = slot_ids.shape[1] // feats
    keep, send, dpooled = dense(
        core, slots_late, labels, cache_rows, proj_u, proj_v, cross_bias, head
    )

    blocks = feats
    depth = width
    send, got = lax.optimization_barrier((send, got))
    held = keep + swap_cores(send)
    held, got = lax.optimization_barrier((held, got))

    got_meta = got[:, per - 1, :]
    got_id = got_meta[:, per : per + cap].astype(jnp.int32)
    flat = got_id.reshape(-1)
    table_new = table_rows.at[jnp.where(flat < 0, owned, flat)].set(
        got[:, :cap, :].reshape(-1, width), mode="drop"
    )
    stored = flat[:, None] == jnp.arange(owned, dtype=jnp.int32)[None, :]
    stored_sum = jnp.sum(jnp.where(stored, got_meta[:, :cap].reshape(-1)[:, None], 0.0), axis=0)
    accum_table = jnp.where(jnp.any(stored, axis=0), stored_sum, table_accum)
    order = jnp.arange(owners, dtype=jnp.int32)
    turned = (order ^ me)[:, None] == order[None, :]
    asked = jnp.sum(
        jnp.where(turned[:, :, None], got_meta[None, :, 2 * per : 3 * per], 0.0), axis=1
    )
    asked = asked.astype(jnp.int32).reshape(-1)
    is_meta = (jnp.arange(per) == per - 1)[None, :, None]
    reply_rows = jnp.take(table_new, asked, axis=0, mode="clip").reshape(owners, per, width)
    reply_accum = picked(accum_table, asked).reshape(owners, per)
    back = jnp.where(is_meta, meta_row([reply_accum], width), reply_rows)

    held = exchange(held, first_groups())
    back = cross(cross(back, 1), 16)
    held, back = lax.optimization_barrier((held, back))
    held = jnp.sum(held, axis=0)
    fine = depth // 16
    pieces16 = jnp.concatenate(
        [
            held[:depth].reshape(16, fine, width),
            jnp.broadcast_to(held[None, depth:], (16, 8, width)),
        ],
        axis=1,
    )
    held = exchange(pieces16, second_groups())
    back = cross(back, 2)
    held, back = lax.optimization_barrier((held, back))
    summed16 = jnp.sum(held, axis=0)
    extras = summed16[fine:]
    spread = jnp.broadcast_to(summed16[None, :fine], (16, fine, width))
    held = exchange(spread, second_groups())
    back = cross(back, 4)
    held, back = lax.optimization_barrier((held, back))
    whole = jnp.concatenate([held.reshape(depth, width), extras], axis=0)
    whole = exchange(jnp.broadcast_to(whole[None], (blocks, depth + 8, width)), first_groups())
    back = cross(back, 8)
    whole, back = lax.optimization_barrier((whole, back))
    in_place = (miss_dest[:, 0] ^ me) * per + ranks(miss_dest[:, 0])
    fetched_rows = jnp.take(back.reshape(spots, width), in_place, axis=0, mode="clip")
    fetched_accum = picked(back[:, per - 1, :per].reshape(-1), in_place)
    clipped_proj, clipped_vecs, loss_row = normalized(core, whole, swap_cores(whole))
    loss = loss_row[0, 0] / (count * 256)

    slot_range = jnp.arange(cells, dtype=jnp.int32)
    row_grad = jnp.zeros((cells, width), jnp.float32)
    for feature in range(feats):
        counts = jnp.zeros((count, cells), jnp.bfloat16)
        for lookup in range(looks):
            column = slot_ids[:, feature * looks + lookup]
            counts = counts + (column[:, None] == slot_range[None, :]).astype(jnp.bfloat16)
        block = dpooled[:, feature * width : (feature + 1) * width]
        row_grad = row_grad + lax.dot_general(
            counts, block, (((0,), (0,)), ((), ())), preferred_element_type=jnp.float32
        )
    accum_new = cache_accum + jnp.mean(row_grad * row_grad, axis=1)
    rows_new = cache_rows - ETA * row_grad * lax.rsqrt(accum_new)[:, None]
    rows_new = rows_new.at[evict_slot].set(fetched_rows)
    accum_new = accum_new.at[evict_slot].set(fetched_accum)
    return (rows_new, accum_new, table_new, accum_table, clipped_proj, clipped_vecs, loss)


def solution(mesh):
    split = P(AXES)
    rows = P(AXES, None)
    return jax.shard_map(
        shards,
        mesh=mesh,
        in_specs=(
            rows,
            split,
            rows,
            split,
            rows,
            split,
            rows,
            split,
            rows,
            P(),
            P(),
            P(),
            P(),
        ),
        out_specs=(rows, split, rows, split, P(), P(), P()),
        check_vma=False,
    )
```

time: 183 us -> 155 us (0.85)
  Pallas kernels: 0 us -> 17.8 us
  other arithmetic: 23.7 us -> 6.81 us
  waiting for transfers between devices: 61.6 us -> 46 us
  matrix products: 23.5 us -> 10.7 us
  local copies, waits for them, and re-layouts: 16.9 us -> 19.4 us
  between operations: 4.36 us -> 2.45 us
    pallas_call x0 -> x4, Pallas kernels: none -> 17.8 us  [the longest x1 9.05 us: dense(): pl.pallas_call(dense_kernel, out_shape=(bundle, bundle, jax.ShapeDtypeStr...]
    dot_general x22 -> x8, matrix products: 23.5 us -> 10.7 us  [shards(): lax.dot_general(counts, block, (((0,), (0,)), ((), ())), preferred_elemen...]
    all_to_all x4, waiting for transfers between devices: 13.7 us -> 2.32 us  [exchange(): lax.all_to_all(value, AXES, split_axis=0, concat_axis=0, tiled=True, axis...]
    all_to_all x0 -> x1, starting transfers between devices: none -> 10.3 us  [shards(): got = lax.all_to_all(sent, 'table', split_axis=0, concat_axis=0, tiled=True)]
    ppermute x10 -> x5, starting transfers between devices: 14.3 us -> 5.59 us  [cross(): came = lax.ppermute(split[:, 1], AXES, there)]
    ppermute x10 -> x5, waiting for transfers between devices: 47.8 us -> 39.4 us  [cross(): came = lax.ppermute(split[:, 1], AXES, there)]
    ppermute x2, starting transfers between devices: 11.9 us -> 5.64 us  [swap_cores(): return lax.ppermute(value, AXES, [(i, i ^ 1) for i in range(256)])]
    unnamed x198 -> x44, local copies, waits for them, and re-layouts: 1.28 us -> 6.86 us
  transfers between devices with their start and end apart: 16 -> 12, of which waited for: 10 -> 8; matrix products, arithmetic and copies ran while one was open for 16% -> 17% of each run, Pallas kernels for 0% -> 7%
where the time goes in v3:
time: 155 us; the launch traced here: 154 us
  starting transfers between devices  50.5 us (33%)
  waiting for transfers between devices  46 us (30%)
  local copies, waits for them, and re-layouts  19.4 us (13%)
  Pallas kernels  17.8 us (11%)
  matrix products  10.7 us (7%)
  other arithmetic  6.81 us (4%)
  between operations  2.45 us (2%)
    ppermute x5, waiting for transfers between devices, cross(): came = lax.ppermute(split[:, 1], AXES, there)  39.4 us
    all_to_all x4, starting transfers between devices, exchange(): lax.all_to_all(value, AXES, split_axis=0, concat_axis=0, tiled=True, axis...  28.9 us
    dot_general x8, matrix products, shards(): lax.dot_general(counts, block, (((0,), (0,)), ((), ())), preferred_elemen...  10.7 us
    all_to_all x1, starting transfers between devices, shards(): got = lax.all_to_all(sent, 'table', split_axis=0, concat_axis=0, tiled=True)  10.3 us
    pallas_call x1, Pallas kernels, dense(): pl.pallas_call(dense_kernel, out_shape=(bundle, bundle, jax.ShapeDtypeStr...  9.05 us
    unnamed x44, local copies, waits for them, and re-layouts  6.86 us
    ppermute x2, starting transfers between devices, swap_cores(): return lax.ppermute(value, AXES, [(i, i ^ 1) for i in range(256)])  5.64 us
    ppermute x5, starting transfers between devices, cross(): came = lax.ppermute(split[:, 1], AXES, there)  5.59 us
  transfers between devices with their start and end apart: 12, of which 8 were waited for; matrix products, arithmetic and copies ran while one was open for 17% of the time, Pallas kernels for 7%

profile of v3, /device:TPU:3, one launch (start us, length us, event | category | flops | bytes accessed | tf_op | source)
XLA Modules:
  0.0 153.5 jit_solution(4307989352862361741)
XLA Ops:
  0.7 3.2 %payload.1 = f32[256,256]{1,0:T(8,128)} custom-call(s32[64]{0:T(128)} %slot_ref.1, s32[2,64]{1,0:T(2,128)} %bitcast.118, s32[2,64]{1,0:T(2,128)} %bitcast.117, f32[1024]{0:T(1024)} %accum_ref.1, f32[1024,256]{1,0:T(8,128)} %cache_ref.3), custom_call_target="tpu_custom_call" | custom-call | flops 100000 | bytes 1500000 | tf_op jit(solution)/shard_map/payload/pallas_call | solution.py:257
  3.9 10.3 %all-to-all-start = ((f32[32,8,256]{2,1,0:T(8,128)}), f32[32,8,256]{2,1,0:T(8,128)S(1)}, u32[]{:S(2)}, u32[]{:S(2)}) async-start(f32[32,8,256]{2,1,0:T(8,128)} %bitcast.100), calls=%async_computation | async-start | bytes 524288 | tf_op jit(solution)/shard_map/all_to_all | solution.py:382
  14.3 1.2 copy-done.3
  15.5 1.2 copy-done.4
  16.7 9.0 %dense.1 = (f32[8,264,256]{2,1,0:T(8,128)S(1)}, f32[8,264,256]{2,1,0:T(8,128)S(1)}, bf16[256,2048]{1,0:T(8,128)(2,1)S(1)}) custom-call(s32[1]{0:T(128)} %bitcast.4.core_ref, s32[32,256]{1,0:T(8,128)S(1)} %bitcast.93, s32[1,256]{1,0:T(1,128)S(1)} %bitcast.96, f32[1024,256]{1,0:T(8,128)S(1)} %copy-done, bf16[2048,256]{1,0:T(8,128)(2,1)S(1)} %copy-done.3, ...), custom_call_target="tpu_custom_call" | custom-call | flops 5000000000 | bytes 9000000 | tf_op jit(solution)/shard_map/dense/pallas_call | solution.py:180
  25.8 1.3 copy-done.2
  27.1 1.0 copy-done.8
  28.1 0.2 collective-permute-start
  28.3 4.2 %collective-permute-done = f32[8,264,256]{2,1,0:T(8,128)S(1)} collective-permute-done((f32[8,264,256]{2,1,0:T(8,128)}, f32[8,264,256]{2,1,0:T(8,128)S(1)}, u32[]{:S(2)}, u32[]{:S(2)}) %collective-permute-start) | collective-permute-done | bytes 2162720 | tf_op jit(solution)/shard_map/ppermute | solution.py:40
  32.5 1.6 %add.158 = f32[8,264,256]{2,1,0:T(8,128)} add(f32[8,264,256]{2,1,0:T(8,128)S(1)} %get-tuple-element.29, f32[8,264,256]{2,1,0:T(8,128)S(1)} %collective-permute-done) | non-fusion elementwise | flops 540672 | bytes 6488064 | tf_op jit(solution)/shard_map/add | solution.py:394
  34.1 7.0 %all-to-all-start.1 = ((f32[8,264,256]{2,1,0:T(8,128)}), f32[8,264,256]{2,1,0:T(8,128)}, u32[]{:S(2)}, u32[]{:S(2)}) async-start(f32[8,264,256]{2,1,0:T(8,128)} %add.158), calls=%async_computation.1 | async-start | bytes 4325376 | tf_op jit(solution)/shard_map/all_to_all | solution.py:44
  42.4 0.2 select_reduce_fusion
  42.8 1.8 %scatter_fusion = f32[1024,256]{1,0:T(8,128)S(1)} fusion(f32[1024,256]{1,0:T(8,128)S(1)} %copy-done.12, s32[192]{0:T(256)S(1)} %bitcast.116, f32[192,256]{1,0:T(8,128)S(1)} %reshape.193), kind=kCustom, calls=%fused_computation.2 | custom fusion | bytes 590592 | tf_op jit(solution)/shard_map/scatter | solution.py:400
  44.7 1.0 gather_fusion
  45.9 1.3 collective-permute-done.1
  47.3 1.3 collective-permute-start.2
  48.6 9.3 %collective-permute-done.2 = f32[1,16,8,256]{3,2,1,0:T(8,128)S(1)} collective-permute-done((f32[1,16,8,256]{3,2,1,0:T(8,128)S(1)}, f32[1,16,8,256]{3,2,1,0:T(8,128)S(1)}, u32[]{:S(2)}, u32[]{:S(2)}) %collective-permute-start.2) | collective-permute-done | bytes 131104 | tf_op jit(solution)/shard_map/ppermute | solution.py:69
  57.9 0.2 all-to-all-done.1
  58.1 1.8 %reduce_sum.78 = f32[264,256]{1,0:T(8,128)S(1)} reduce(f32[8,264,256]{2,1,0:T(8,128)} %all-to-all-done.1, f32[]{:T(128)} %constant.16.clone.1), dimensions={0}, to_apply=%region_6.7 | reduce | flops 473088 | bytes 2433028 | tf_op jit(solution)/shard_map/reduce_sum | solution.py:420
  59.9 0.8 pad_maximum_fusion
  60.7 8.8 %all-to-all-start.2 = ((f32[16,24,256]{2,1,0:T(8,128)}), f32[16,24,256]{2,1,0:T(8,128)S(1)}, u32[]{:S(2)}, u32[]{:S(2)}) async-start(f32[16,24,256]{2,1,0:T(8,128)} %pad_maximum_fusion), calls=%async_computation.2 | async-start | bytes 786432 | tf_op jit(solution)/shard_map/all_to_all | solution.py:44
  69.6 11.1 %collective-permute-done.3 = f32[8,2,8,256]{3,2,1,0:T(8,128)S(1)} collective-permute-done((f32[8,2,8,256]{3,2,1,0:T(8,128)S(1)}, f32[8,2,8,256]{3,2,1,0:T(8,128)S(1)}, u32[]{:S(2)}, u32[]{:S(2)}) %collective-permute-start.3) | collective-permute-done | bytes 131104 | tf_op jit(solution)/shard_map/ppermute | solution.py:69
  80.7 2.1 %all-to-all-done.2 = f32[16,24,256]{2,1,0:T(8,128)S(1)} async-done(((f32[16,24,256]{2,1,0:T(8,128)}), f32[16,24,256]{2,1,0:T(8,128)S(1)}, u32[]{:S(2)}, u32[]{:S(2)}) %all-to-all-start.2) | async-done | bytes 393248 | tf_op jit(solution)/shard_map/all_to_all | solution.py:44
  82.9 0.7 broadcast_in_dim.120
  83.6 6.9 %all-to-all-start.3 = ((f32[16,16,256]{2,1,0:T(8,128)}), f32[16,16,256]{2,1,0:T(8,128)S(1)}, u32[]{:S(2)}, u32[]{:S(2)}) async-start(f32[16,16,256]{2,1,0:T(8,128)} %broadcast_in_dim.120), calls=%async_computation.3 | async-start | bytes 524288 | tf_op jit(solution)/shard_map/all_to_all | solution.py:44
  90.5 2.2 %collective-permute-start.4 = (f32[4,4,8,256]{3,2,1,0:T(8,128)S(1)}, f32[4,4,8,256]{3,2,1,0:T(8,128)S(1)}, u32[]{:S(2)}, u32[]{:S(2)}) collective-permute-start(f32[4,4,8,256]{3,2,1,0:T(8,128)S(1)} %get-tuple-element.59), channel_id=1, source_target_pairs={{0,4},{1,5},{2,6},{3,7},{4,0},{5,1},{6,2},{7,3},{8,12},{9,13},{10,... | collective-permute-start | bytes 393224 | tf_op jit(solution)/shard_map/ppermute | solution.py:69
  92.7 12.3 %collective-permute-done.4 = f32[4,4,8,256]{3,2,1,0:T(8,128)S(1)} collective-permute-done((f32[4,4,8,256]{3,2,1,0:T(8,128)S(1)}, f32[4,4,8,256]{3,2,1,0:T(8,128)S(1)}, u32[]{:S(2)}, u32[]{:S(2)}) %collective-permute-start.4) | collective-permute-done | bytes 131104 | tf_op jit(solution)/shard_map/ppermute | solution.py:69
  105.0 1.5 broadcast_in_dim.121
  106.5 6.3 %all-to-all-start.4 = ((f32[8,264,256]{2,1,0:T(8,128)}), f32[8,264,256]{2,1,0:T(8,128)S(1)}, u32[]{:S(2)}, u32[]{:S(2)}) async-start(f32[8,264,256]{2,1,0:T(8,128)} %broadcast_in_dim.121), calls=%async_computation.4 | async-start | bytes 4325376 | tf_op jit(solution)/shard_map/all_to_all | solution.py:44
  112.9 1.8 %fusion.83 = f32[1024,256]{0,1:T(8,128)S(1)} fusion(s32[256]{0:T(256)S(1)} %bitcast.147, s32[256]{0:T(256)S(1)} %bitcast.148, s32[256]{0:T(256)S(1)} %bitcast.149, s32[256]{0:T(256)S(1)} %bitcast.150, bf16[256,2048]{1,0:T(8,128)(2,1)} %copy-done.8), kind=kOutput, calls=%fused_computation.105 | convolution fusion | flops 138412032 | bytes 1183744 | tf_op jit(solution)/shard_map/dot_general | solution.py:456
  114.7 0.8 convolution_add_fusion.6
  115.5 0.8 convolution_add_fusion.5
  116.3 0.8 convolution_add_fusion.4
  117.1 0.8 convolution_add_fusion.3
  117.9 0.7 slice_bitcast_fusion.1
  118.6 1.9 %collective-permute-start.5 = (f32[2,8,8,256]{3,2,1,0:T(8,128)}, f32[2,8,8,256]{3,2,1,0:T(8,128)S(1)}, u32[]{:S(2)}, u32[]{:S(2)}) collective-permute-start(f32[2,8,8,256]{3,2,1,0:T(8,128)} %get-tuple-element.57), channel_id=1, source_target_pairs={{0,8},{1,9},{2,10},{3,11},{4,12},{5,13},{6,14},{7,15},{8,0},{9,1},... | collective-permute-start | bytes 393224 | tf_op jit(solution)/shard_map/ppermute | solution.py:69
  120.6 1.8 %convolution_add_fusion.2 = f32[1024,256]{0,1:T(8,128)} fusion(f32[1024,256]{0,1:T(8,128)S(1)} %convolution_add_fusion.3, s32[256]{0:T(256)S(1)} %bitcast.125, s32[256]{0:T(256)S(1)} %bitcast.126, s32[256]{0:T(256)S(1)} %bitcast.127, s32[256]{0:T(256)S(1)} %bitcast.128, bf16[256,2048]{1,0:T(8,128)(2,1)S(1)} %copy-done.9), kind=kOutput, calls=%fused_computation.7 | convolution fusion | flops 138674176 | bytes 2232320 | tf_op jit(solution)/shard_map/dot_general | solution.py:456
  122.4 1.3 copy.47
  123.7 5.4 %collective-permute-done.5 = f32[2,8,8,256]{3,2,1,0:T(8,128)S(1)} collective-permute-done((f32[2,8,8,256]{3,2,1,0:T(8,128)}, f32[2,8,8,256]{3,2,1,0:T(8,128)S(1)}, u32[]{:S(2)}, u32[]{:S(2)}) %collective-permute-start.5) | collective-permute-done | bytes 131104 | tf_op jit(solution)/shard_map/ppermute | solution.py:69
  129.1 5.4 %collective-permute-start.6 = (f32[8,264,256]{2,1,0:T(8,128)S(1)}, f32[8,264,256]{2,1,0:T(8,128)}, u32[]{:S(2)}, u32[]{:S(2)}) collective-permute-start(f32[8,264,256]{2,1,0:T(8,128)S(1)} %all-to-all-done.4.half_ref), channel_id=1, source_target_pairs={{0,1},{1,0},{2,3},{3,2},{4,5},{5,4},{6,7},{7,6},{8,9},{9,8},{10,11... | collective-permute-start | bytes 6488072 | tf_op jit(solution)/shard_map/ppermute | solution.py:40
  134.5 2.1 %convolution_add_fusion.1 = f32[1024,256]{0,1:T(8,128)S(1)} fusion(f32[1024,256]{0,1:T(8,128)} %convolution_add_fusion.2, s32[256]{0:T(256)S(1)} %bitcast.121, s32[256]{0:T(256)S(1)} %bitcast.122, s32[256]{0:T(256)S(1)} %bitcast.123, s32[256]{0:T(256)S(1)} %bitcast.124, bf16[256,2048]{1,0:T(8,128)(2,1)} %copy-done.8), kind=kOutput, calls=%fused_computation.6 | convolution fusion | flops 138674176 | bytes 2232320 | tf_op jit(solution)/shard_map/dot_general | solution.py:456
  136.6 1.8 %multiply_reduce_fusion = (f32[1024]{0:T(1024)S(1)}, f32[1024,256]{0,1:T(8,128)S(1)}) fusion(f32[1024,256]{0,1:T(8,128)S(1)} %convolution_add_fusion.1, bf16[256,2048]{1,0:T(8,128)(2,1)} %copy-done.8, s32[256]{0:T(256)S(1)} %bitcast.139, s32[256]{0:T(256)S(1)} %bitcast.138, s32[256]{0:T(256)S(1)} %bitcast.120, s32[256]{0:T(256)S(1)} %bitcast.119), kind=kOutput, calls=%fused_computation.15 | convolution fusion | flops 139197440 | bytes 2236416 | tf_op jit(solution)/shard_map/dot_general | solution.py:456
  138.5 1.2 multiply_subtract_fusion
  139.7 2.5 %copy.57 = f32[1024,256]{1,0:T(8,128)} copy(f32[1024,256]{0,1:T(8,128)} %multiply_subtract_fusion) | data formatting | bytes 2097152 | tf_op jit(solution)/shard_map/sub | solution.py:460
  142.4 1.7 %scale_own.1.proj_in = f32[2,2048,256]{2,1,0:T(8,128)} custom-call(s32[1]{0:T(128)} %bitcast.4.core_ref, f32[8,264,256]{2,1,0:T(8,128)S(1)} %all-to-all-done.4.half_ref), custom_call_target="tpu_custom_call" | custom-call | tf_op jit(solution)/shard_map/scale_own/pallas_call | solution.py:328
  144.5 0.8 scatter_fusion.1
  145.3 3.2 %scatter_custom_fusion.1 = f32[1024,256]{1,0:T(8,128)} fusion(f32[1024,256]{1,0:T(8,128)} %copy.57, s32[64]{0:T(128)S(1)} %compare_select_fusion.2, f32[256,256]{1,0:T(8,128)S(1)} %bitcast.108, s32[1024]{0:T(1024)S(1)} %pad_clamp_fusion), kind=kCustom, calls=%fused_computation.165 | custom fusion | bytes 1048576 | tf_op jit(solution)/shard_map/scatter | solution.py:461
  148.4 3.9 %scale_other.1 = (f32[2,2048,256]{2,1,0:T(8,128)}, f32[2,2048]{1,0:T(2,128)}, f32[1,128]{1,0:T(1,128)S(1)}) custom-call(s32[1]{0:T(128)} %bitcast.4.core_ref, f32[2,2048,256]{2,1,0:T(8,128)} %scale_own.1.proj_in, f32[8,8,256]{2,1,0:T(8,128)S(1)} %slice.251.own_ref, f32[8,264,256]{2,1,0:T(8,128)} %collective-permute-done.6.half_ref), custom_call_target="tpu_custom_call", output_to_operand_aliasing={{0}: (1, {})} | custom-call | tf_op jit(solution)/shard_map/scale_other/pallas_call | solution.py:337
  (97 shorter events, 2.6 us)
Async XLA Ops:
  0.6 13.6 %copy-start.1 = (s32[256,32]{0,1:T(8,128)S(1)}, s32[256,32]{0,1:T(8,128)}, u32[]{:S(2)}) copy-start(s32[256,32]{0,1:T(8,128)} %param.13) | copy-start | bytes 98308
  0.6 13.6 %copy-start.7 = (s32[256]{0:T(256)S(1)}, s32[256]{0:T(256)}, u32[]{:S(2)}) copy-start(s32[256]{0:T(256)} %param.14) | copy-start | bytes 3076
  0.7 13.6 %copy-start = (f32[1024,256]{1,0:T(8,128)S(1)}, f32[1024,256]{1,0:T(8,128)}, u32[]{:S(2)}) copy-start(f32[1024,256]{1,0:T(8,128)} %cache_ref.3) | copy-start | bytes 3145732
  0.7 13.6 %copy-start.5 = (f32[2048]{0:T(1024)S(1)}, f32[2048]{0:T(1024)}, u32[]{:S(2)}) copy-start(f32[2048]{0:T(1024)} %param.24) | copy-start | bytes 24580
  0.7 13.6 %copy-start.6 = (f32[2048]{0:T(1024)S(1)}, f32[2048]{0:T(1024)}, u32[]{:S(2)}) copy-start(f32[2048]{0:T(1024)} %param.25) | copy-start | bytes 24580
  3.9 24.2 %all-to-all-start = ((f32[32,8,256]{2,1,0:T(8,128)}), f32[32,8,256]{2,1,0:T(8,128)S(1)}, u32[]{:S(2)}, u32[]{:S(2)}) async-start(f32[32,8,256]{2,1,0:T(8,128)} %bitcast.100), calls=%async_computation | async-start | bytes 524288 | tf_op jit(solution)/shard_map/all_to_all | solution.py:382
  14.2 1.2 copy-start.3
  15.5 1.2 copy-start.4
  25.7 1.3 copy-start.2
  27.1 1.0 copy-start.8
  28.1 4.5 %collective-permute-start = (f32[8,264,256]{2,1,0:T(8,128)}, f32[8,264,256]{2,1,0:T(8,128)S(1)}, u32[]{:S(2)}, u32[]{:S(2)}) collective-permute-start(f32[8,264,256]{2,1,0:T(8,128)} %copy-done.2), channel_id=1, source_target_pairs={{0,1},{1,0},{2,3},{3,2},{4,5},{5,4},{6,7},{7,6},{8,9},{9,8},{10,11... | collective-permute-start | bytes 6488072 | tf_op jit(solution)/shard_map/ppermute | solution.py:40
  34.1 8.2 %copy-start.17 = (f32[1024]{0:T(1024)S(1)}, f32[1024]{0:T(1024)}, u32[]{:S(2)}) copy-start(f32[1024]{0:T(1024)} %param.18) | copy-start | bytes 12292
  34.1 8.7 %copy-start.12 = (f32[1024,256]{1,0:T(8,128)S(1)}, f32[1024,256]{1,0:T(8,128)}, u32[]{:S(2)}) copy-start(f32[1024,256]{1,0:T(8,128)} %param.17) | copy-start | bytes 3145732
  34.1 23.9 %all-to-all-start.1 = ((f32[8,264,256]{2,1,0:T(8,128)}), f32[8,264,256]{2,1,0:T(8,128)}, u32[]{:S(2)}, u32[]{:S(2)}) async-start(f32[8,264,256]{2,1,0:T(8,128)} %add.158), calls=%async_computation.1 | async-start | bytes 4325376 | tf_op jit(solution)/shard_map/all_to_all | solution.py:44
  42.4 3.3 %copy-start.16 = (f32[1024]{0:T(1024)}, f32[1024]{0:T(1024)S(1)}, u32[]{:S(2)}) copy-start(f32[1024]{0:T(1024)S(1)} %select_n.67) | copy-start | bytes 12292
  44.7 2.6 %copy-start.11 = (f32[1024,256]{1,0:T(8,128)}, f32[1024,256]{1,0:T(8,128)S(1)}, u32[]{:S(2)}) copy-start(f32[1024,256]{1,0:T(8,128)S(1)} %scatter_fusion) | copy-start | bytes 3145732
  45.8 1.4 collective-permute-start.1
  47.3 10.6 %collective-permute-start.2 = (f32[1,16,8,256]{3,2,1,0:T(8,128)S(1)}, f32[1,16,8,256]{3,2,1,0:T(8,128)S(1)}, u32[]{:S(2)}, u32[]{:S(2)}) collective-permute-start(f32[1,16,8,256]{3,2,1,0:T(8,128)S(1)} %get-tuple-element.63), channel_id=1, source_target_pairs={{0,16},{1,17},{2,18},{3,19},{4,20},{5,21},{6,22},{7,23},{8,24},{9,... | collective-permute-start | bytes 393224 | tf_op jit(solution)/shard_map/ppermute | solution.py:69
  60.7 22.1 %all-to-all-start.2 = ((f32[16,24,256]{2,1,0:T(8,128)}), f32[16,24,256]{2,1,0:T(8,128)S(1)}, u32[]{:S(2)}, u32[]{:S(2)}) async-start(f32[16,24,256]{2,1,0:T(8,128)} %pad_maximum_fusion), calls=%async_computation.2 | async-start | bytes 786432 | tf_op jit(solution)/shard_map/all_to_all | solution.py:44
  69.5 11.2 %collective-permute-start.3 = (f32[8,2,8,256]{3,2,1,0:T(8,128)S(1)}, f32[8,2,8,256]{3,2,1,0:T(8,128)S(1)}, u32[]{:S(2)}, u32[]{:S(2)}) collective-permute-start(f32[8,2,8,256]{3,2,1,0:T(8,128)S(1)} %get-tuple-element.61), channel_id=1, source_target_pairs={{0,2},{1,3},{2,0},{3,1},{4,6},{5,7},{6,4},{7,5},{8,10},{9,11},{10,... | collective-permute-start | bytes 393224 | tf_op jit(solution)/shard_map/ppermute | solution.py:69
  83.6 21.4 %all-to-all-start.3 = ((f32[16,16,256]{2,1,0:T(8,128)}), f32[16,16,256]{2,1,0:T(8,128)S(1)}, u32[]{:S(2)}, u32[]{:S(2)}) async-start(f32[16,16,256]{2,1,0:T(8,128)} %broadcast_in_dim.120), calls=%async_computation.3 | async-start | bytes 524288 | tf_op jit(solution)/shard_map/all_to_all | solution.py:44
  90.5 14.5 %collective-permute-start.4 = (f32[4,4,8,256]{3,2,1,0:T(8,128)S(1)}, f32[4,4,8,256]{3,2,1,0:T(8,128)S(1)}, u32[]{:S(2)}, u32[]{:S(2)}) collective-permute-start(f32[4,4,8,256]{3,2,1,0:T(8,128)S(1)} %get-tuple-element.59), channel_id=1, source_target_pairs={{0,4},{1,5},{2,6},{3,7},{4,0},{5,1},{6,2},{7,3},{8,12},{9,13},{10,... | collective-permute-start | bytes 393224 | tf_op jit(solution)/shard_map/ppermute | solution.py:69
  106.5 22.6 %all-to-all-start.4 = ((f32[8,264,256]{2,1,0:T(8,128)}), f32[8,264,256]{2,1,0:T(8,128)S(1)}, u32[]{:S(2)}, u32[]{:S(2)}) async-start(f32[8,264,256]{2,1,0:T(8,128)} %broadcast_in_dim.121), calls=%async_computation.4 | async-start | bytes 4325376 | tf_op jit(solution)/shard_map/all_to_all | solution.py:44
  112.9 1.8 %copy-start.9 = (bf16[256,2048]{1,0:T(8,128)(2,1)S(1)}, bf16[256,2048]{1,0:T(8,128)(2,1)}, u32[]{:S(2)}) copy-start(bf16[256,2048]{1,0:T(8,128)(2,1)} %copy-done.8) | copy-start | bytes 3145732
  118.6 10.4 %collective-permute-start.5 = (f32[2,8,8,256]{3,2,1,0:T(8,128)}, f32[2,8,8,256]{3,2,1,0:T(8,128)S(1)}, u32[]{:S(2)}, u32[]{:S(2)}) collective-permute-start(f32[2,8,8,256]{3,2,1,0:T(8,128)} %get-tuple-element.57), channel_id=1, source_target_pairs={{0,8},{1,9},{2,10},{3,11},{4,12},{5,13},{6,14},{7,15},{8,0},{9,1},... | collective-permute-start | bytes 393224 | tf_op jit(solution)/shard_map/ppermute | solution.py:69
  120.6 8.5 %copy-start.14 = (f32[2,1,8,8,256]{4,3,2,0,1:T(8,128)S(1)}, f32[2,1,8,8,256]{4,3,2,0,1:T(8,128)}, u32[]{:S(2)}) copy-start(f32[2,1,8,8,256]{4,3,2,0,1:T(8,128)} %get-tuple-element.56) | copy-start | bytes 393220
  129.1 19.3 %collective-permute-start.6 = (f32[8,264,256]{2,1,0:T(8,128)S(1)}, f32[8,264,256]{2,1,0:T(8,128)}, u32[]{:S(2)}, u32[]{:S(2)}) collective-permute-start(f32[8,264,256]{2,1,0:T(8,128)S(1)} %all-to-all-done.4.half_ref), channel_id=1, source_target_pairs={{0,1},{1,0},{2,3},{3,2},{4,5},{5,4},{6,7},{7,6},{8,9},{9,8},{10,11... | collective-permute-start | bytes 6488072 | tf_op jit(solution)/shard_map/ppermute | solution.py:40
  136.6 1.8 %copy-start.15 = (f32[1024]{0:T(1024)S(1)}, f32[1024]{0:T(1024)}, u32[]{:S(2)}) copy-start(f32[1024]{0:T(1024)} %accum_ref.1) | copy-start | bytes 12292
  136.6 1.9 %copy-start.13 = (f32[1024,256]{0,1:T(8,128)S(1)}, f32[1024,256]{0,1:T(8,128)}, u32[]{:S(2)}) copy-start(f32[1024,256]{0,1:T(8,128)} %copy.47) | copy-start | bytes 3145732
  138.5 3.7 %copy-start.18 = (s32[64,2]{0,1:T(2,128)S(1)}, s32[64,2]{0,1:T(2,128)}, u32[]{:S(2)}) copy-start(s32[64,2]{0,1:T(2,128)} %param.19) | copy-start | bytes 1540
  138.5 3.9 %copy-start.19 = (s32[64]{0:T(128)S(1)}, s32[64]{0:T(128)}, u32[]{:S(2)}) copy-start(s32[64]{0:T(128)} %slot_ref.1) | copy-start | bytes 772
  145.3 7.1 %copy-start.10 = (f32[1024]{0:T(1024)}, f32[1024]{0:T(1024)S(1)}, u32[]{:S(2)}) copy-start(f32[1024]{0:T(1024)S(1)} %scatter_fusion.1) | copy-start | bytes 12292

commit v4 on v3

--- a/solution.py
+++ b/solution.py
@@ -75,10 +75,15 @@
     slots_ref,
     labels_ref,
     cache_ref,
+    u_any,
+    v_any,
+    bias_ref,
+    head_ref,
+    keep_out,
+    send_out,
+    dpooled_out,
     u_ref,
     v_ref,
-    bias_ref,
-    head_ref,
     keep_ref,
     send_ref,
     dpooled_ref,
@@ -88,8 +93,14 @@
     pooled,
     shifted,
     dlift,
+    in_sems,
+    out_sems,
 ):
     f32, bf16 = jnp.float32, jnp.bfloat16
+    load_v = pltpu.make_async_copy(v_any, v_ref, in_sems.at[0])
+    load_u = pltpu.make_async_copy(u_any, u_ref, in_sems.at[1])
+    load_v.start()
+    load_u.start()
     count, cells, width = slots_ref.shape[1], cache_ref.shape[0], cache_ref.shape[1]
     feats = u_ref.shape[0] // width
     looks = slots_ref.shape[0] // feats
@@ -114,6 +125,8 @@
         total = total + jnp.dot(counts, high[...], preferred_element_type=f32)
         pooled[:, f * width : (f + 1) * width] = total.astype(bf16)
 
+    load_v.wait()
+    load_u.wait()
     latent = jnp.dot(pooled[...], v_ref[...], preferred_element_type=f32).astype(bf16)
     across = (((1,), (1,)), ((), ()))
     logit_wide = jnp.zeros((count, width), f32)
@@ -155,40 +168,75 @@
     down = (((0,), (0,)), ((), ()))
     right_keep = jnp.where(mine, latent, dlatent)
     right_send = jnp.where(mine, dlatent, latent)
+    copies = []
+
+    def give(source, target):
+        copies.append(pltpu.make_async_copy(source, target, out_sems.at[len(copies)]))
+        copies[-1].start()
+
     for c in range(feats):
         cut = slice(c * width, (c + 1) * width)
-        lift, part = dlift[:, cut], pooled[:, cut]
         send_ref[c, :width, :] = lax.dot_general(
-            jnp.where(mine, part, lift), right_send, down, preferred_element_type=f32
+            jnp.where(mine, pooled[:, cut], dlift[:, cut]),
+            right_send,
+            down,
+            preferred_element_type=f32,
         )
+        give(send_ref.at[c], send_out.at[c])
+    for c in range(feats):
+        cut = slice(c * width, (c + 1) * width)
         keep_ref[c, :width, :] = lax.dot_general(
-            jnp.where(mine, lift, part), right_keep, down, preferred_element_type=f32
+            jnp.where(mine, dlift[:, cut], pooled[:, cut]),
+            right_keep,
+            down,
+            preferred_element_type=f32,
         )
+        give(keep_ref.at[c], keep_out.at[c])
     for c in range(feats):
         cut = slice(c * width, (c + 1) * width)
         through = lax.dot_general(dlatent, v_ref[cut, :], across, preferred_element_type=f32)
         through = through + dlogit * head_ref[:, cut] * (shifted[:, cut] + 1.0)
-        dpooled_ref[:, cut] = through.astype(bf16)
+        dpooled_ref[c] = through.astype(bf16)
+        give(dpooled_ref.at[c], dpooled_out.at[c])
+    for copy in copies:
+        copy.wait()
 
 
 def dense(core, slot_ids, labels, cache_rows, proj_u, proj_v, cross_bias, head):
     count, (cells, width) = slot_ids.shape[0], cache_rows.shape
     wide = proj_u.shape[0]
     blocks = wide // width
+    anywhere = pl.BlockSpec(memory_space=pl.ANY)
     vmem = pl.BlockSpec(memory_space=pltpu.VMEM)
     bundle = jax.ShapeDtypeStruct((blocks, width + 8, width), jnp.float32)
     return pl.pallas_call(
         dense_kernel,
-        out_shape=(bundle, bundle, jax.ShapeDtypeStruct((count, wide), jnp.bfloat16)),
-        in_specs=[pl.BlockSpec(memory_space=pltpu.SMEM)] + [vmem] * 7,
-        out_specs=(vmem, vmem, vmem),
-        scratch_shapes=[pltpu.VMEM((cells, width), jnp.bfloat16)] * 3
+        out_shape=(
+            bundle,
+            bundle,
+            jax.ShapeDtypeStruct((blocks, count, width), jnp.bfloat16),
+        ),
+        in_specs=[pl.BlockSpec(memory_space=pltpu.SMEM)]
+        + [vmem] * 3
+        + [anywhere] * 2
+        + [vmem] * 2,
+        out_specs=(anywhere, anywhere, anywhere),
+        scratch_shapes=[
+            pltpu.VMEM((wide, width), jnp.bfloat16),
+            pltpu.VMEM((wide, width), jnp.bfloat16),
+            pltpu.VMEM(bundle.shape, jnp.float32),
+            pltpu.VMEM(bundle.shape, jnp.float32),
+            pltpu.VMEM((blocks, count, width), jnp.bfloat16),
+        ]
+        + [pltpu.VMEM((cells, width), jnp.bfloat16)] * 3
         + [
             pltpu.VMEM((count, wide), jnp.bfloat16),
             pltpu.VMEM((count, wide), jnp.float32),
             pltpu.VMEM((count, wide), jnp.bfloat16),
+            pltpu.SemaphoreType.DMA((2,)),
+            pltpu.SemaphoreType.DMA((3 * blocks,)),
         ],
-        compiler_params=pltpu.CompilerParams(vmem_limit_bytes=32 * 1024 * 1024),
+        compiler_params=pltpu.CompilerParams(vmem_limit_bytes=60 * 1024 * 1024),
         cost_estimate=pl.CostEstimate(flops=5_000_000_000, bytes_accessed=9_000_000, transcendentals=1000),
         name="dense",
     )(
@@ -265,40 +313,115 @@
     )(evict_slot, evict_dest.T, miss_dest.T, cache_accum, cache_rows)
 
 
-def scaled(index, half_ref, proj_ref, stage, sems):
-    blocks, width = half_ref.shape[0], half_ref.shape[2]
+def refill_kernel(
+    slots_ref,
+    evict_ref,
+    place_ref,
+    cache_ref,
+    accum_ref,
+    dpooled_ref,
+    back_ref,
+    rows_ref,
+    accum_out,
+):
+    f32, bf16 = jnp.float32, jnp.bfloat16
+    (cells, width), (feats, count, _) = cache_ref.shape, dpooled_ref.shape
+    looks = slots_ref.shape[0] // feats
+    cell = lax.broadcasted_iota(jnp.int32, (cells, count), 0)
+    grad = jnp.zeros((cells, width), f32)
+    for f in range(feats):
+        counts = jnp.zeros((cells, count), f32)
+        for look in range(looks):
+            at = f * looks + look
+            counts = counts + jnp.where(cell == slots_ref[at : at + 1, :], 1.0, 0.0)
+        grad = grad + jnp.dot(counts.astype(bf16), dpooled_ref[f], preferred_element_type=f32)
+    mean = jnp.sum(grad * grad, axis=1, keepdims=True) / width
+    accum = jnp.transpose(accum_ref[...]) + mean
+    rows_ref[...] = cache_ref[...] - ETA * grad * lax.rsqrt(accum)
+    accum_out[...] = jnp.transpose(accum)
+
+    def refill(i, _):
+        rows_ref[pl.ds(evict_ref[i], 1), :] = back_ref[pl.ds(place_ref[i], 1), :]
+        return 0
+
+    lax.fori_loop(0, evict_ref.shape[0], refill, 0, unroll=8)
+
+
+def refilled(slot_ids, evict_slot, place, cache_rows, cache_accum, dpooled, back):
+    cells = cache_rows.shape[0]
+    smem = pl.BlockSpec(memory_space=pltpu.SMEM)
+    vmem = pl.BlockSpec(memory_space=pltpu.VMEM)
+    return pl.pallas_call(
+        refill_kernel,
+        out_shape=(
+            jax.ShapeDtypeStruct(cache_rows.shape, jnp.float32),
+            jax.ShapeDtypeStruct((1, cells), jnp.float32),
+        ),
+        in_specs=[vmem, smem, smem, vmem, vmem, vmem, vmem],
+        out_specs=(vmem, vmem),
+        compiler_params=pltpu.CompilerParams(vmem_limit_bytes=60 * 1024 * 1024),
+        cost_estimate=pl.CostEstimate(flops=1_100_000_000, bytes_accessed=4_000_000, transcendentals=1000),
+        name="refill",
+    )(
+        slot_ids.T,
+        evict_slot,
+        place,
+        cache_rows,
+        cache_accum[None, :],
+        dpooled,
+        back,
+    )
+
+
+def scaled(index, half_any, proj_ref, half, stage, in_sems, out_sems):
+    blocks, width = half.shape[0], half.shape[2]
+    loads = []
+    for c in range(blocks):
+        loads.append(pltpu.make_async_copy(half_any.at[c], half.at[c], in_sems.at[c]))
+        loads[-1].start()
     squares = jnp.zeros((width, width), jnp.float32)
     for c in range(blocks):
-        block = half_ref[c, :width, :]
+        loads[c].wait()
+        block = half[c, :width, :]
         squares = squares + block * block
     total = jnp.sum(jnp.sum(squares, axis=0, keepdims=True), axis=1, keepdims=True)
     scale = lax.rsqrt(total / (blocks * width * width) + EPS)
     copies = []
     for c in range(blocks):
-        stage[c] = half_ref[c, :width, :] * scale
+        stage[c] = half[c, :width, :] * scale
         copies.append(
             pltpu.make_async_copy(
-                stage.at[c], proj_ref.at[index, pl.ds(c * width, width), :], sems.at[c]
+                stage.at[c], proj_ref.at[index, pl.ds(c * width, width), :], out_sems.at[c]
             )
         )
         copies[-1].start()
     return copies
 
 
-def own_kernel(core_ref, half_ref, proj_ref, stage, sems):
-    for copy in scaled(core_ref[0], half_ref, proj_ref, stage, sems):
+def own_kernel(core_ref, half_any, proj_ref, half, stage, in_sems, out_sems):
+    for copy in scaled(core_ref[0], half_any, proj_ref, half, stage, in_sems, out_sems):
         copy.wait()
 
 
 def other_kernel(
-    core_ref, proj_in, own_ref, half_ref, proj_ref, vec_ref, loss_ref, stage, sems
+    core_ref,
+    proj_in,
+    own_ref,
+    half_any,
+    proj_ref,
+    vec_ref,
+    loss_ref,
+    half,
+    stage,
+    in_sems,
+    out_sems,
 ):
     core = core_ref[0]
-    copies = scaled(1 - core, half_ref, proj_ref, stage, sems)
-    blocks, width = half_ref.shape[0], half_ref.shape[2]
+    copies = scaled(1 - core, half_any, proj_ref, half, stage, in_sems, out_sems)
+    blocks, width = half.shape[0], half.shape[2]
     mine = core == 0
     own = [own_ref[c, 0:1, :] for c in range(blocks)]
-    far = [half_ref[c, width : width + 1, :] for c in range(blocks)]
+    far = [half[c, width : width + 1, :] for c in range(blocks)]
     for index in (0, 1):
         rows = [jnp.where(mine, *((a, b) if index == 0 else (b, a))) for a, b in zip(own, far)]
         squares = sum(row * row for row in rows)
@@ -307,7 +430,7 @@
         for c in range(blocks):
             vec_ref[index : index + 1, c * width : (c + 1) * width] = rows[c] * scale
     loss_ref[...] = jnp.where(
-        mine, half_ref[0, width + 1 : width + 2, :128], own_ref[0, 1:2, :128]
+        mine, half[0, width + 1 : width + 2, :128], own_ref[0, 1:2, :128]
     )
     for copy in copies:
         copy.wait()
@@ -320,7 +443,9 @@
     vmem = pl.BlockSpec(memory_space=pltpu.VMEM)
     anywhere = pl.BlockSpec(memory_space=pl.ANY)
     scratch = [
+        pltpu.VMEM((blocks, depth, width), jnp.float32),
         pltpu.VMEM((blocks, width, width), jnp.float32),
+        pltpu.SemaphoreType.DMA((blocks,)),
         pltpu.SemaphoreType.DMA((blocks,)),
     ]
     proj = jax.ShapeDtypeStruct((2, wide, width), jnp.float32)
@@ -328,7 +453,7 @@
     half = pl.pallas_call(
         own_kernel,
         out_shape=proj,
-        in_specs=[smem, vmem],
+        in_specs=[smem, anywhere],
         out_specs=anywhere,
         scratch_shapes=scratch,
         compiler_params=limit,
@@ -341,7 +466,7 @@
             jax.ShapeDtypeStruct((2, wide), jnp.float32),
             jax.ShapeDtypeStruct((1, 128), jnp.float32),
         ),
-        in_specs=[smem, anywhere, vmem, vmem],
+        in_specs=[smem, anywhere, vmem, anywhere],
         out_specs=(anywhere, vmem, vmem),
         scratch_shapes=scratch,
         input_output_aliases={1: 0},
@@ -383,7 +508,6 @@
 
     count = slot_ids.shape[0]
     feats = proj_u.shape[0] // width
-    looks = slot_ids.shape[1] // feats
     keep, send, dpooled = dense(
         core, slots_late, labels, cache_rows, proj_u, proj_v, cross_bias, head
     )
@@ -427,39 +551,27 @@
         axis=1,
     )
     held = exchange(pieces16, second_groups())
-    back = cross(back, 2)
+    back = cross(cross(back, 2), 4)
     held, back = lax.optimization_barrier((held, back))
     summed16 = jnp.sum(held, axis=0)
     extras = summed16[fine:]
     spread = jnp.broadcast_to(summed16[None, :fine], (16, fine, width))
     held = exchange(spread, second_groups())
-    back = cross(back, 4)
+    back = cross(back, 8)
     held, back = lax.optimization_barrier((held, back))
     whole = jnp.concatenate([held.reshape(depth, width), extras], axis=0)
     whole = exchange(jnp.broadcast_to(whole[None], (blocks, depth + 8, width)), first_groups())
-    back = cross(back, 8)
-    whole, back = lax.optimization_barrier((whole, back))
     in_place = (miss_dest[:, 0] ^ me) * per + ranks(miss_dest[:, 0])
-    fetched_rows = jnp.take(back.reshape(spots, width), in_place, axis=0, mode="clip")
+    rows_new, accum_new = refilled(
+        slot_ids, evict_slot, in_place, cache_rows, cache_accum, dpooled, back.reshape(spots, width)
+    )
     fetched_accum = picked(back[:, per - 1, :per].reshape(-1), in_place)
+    filled = evict_slot[:, None] == jnp.arange(cells, dtype=jnp.int32)[None, :]
+    filled_sum = jnp.sum(jnp.where(filled, fetched_accum[:, None], 0.0), axis=0)
+    accum_new = jnp.where(jnp.any(filled, axis=0), filled_sum, accum_new.reshape(cells))
+    whole, rows_new, accum_new = lax.optimization_barrier((whole, rows_new, accum_new))
     clipped_proj, clipped_vecs, loss_row = normalized(core, whole, swap_cores(whole))
     loss = loss_row[0, 0] / (count * 256)
-
-    slot_range = jnp.arange(cells, dtype=jnp.int32)
-    row_grad = jnp.zeros((cells, width), jnp.float32)
-    for feature in range(feats):
-        counts = jnp.zeros((count, cells), jnp.bfloat16)
-        for lookup in range(looks):
-            column = slot_ids[:, feature * looks + lookup]
-            counts = counts + (column[:, None] == slot_range[None, :]).astype(jnp.bfloat16)
-        block = dpooled[:, feature * width : (feature + 1) * width]
-        row_grad = row_grad + lax.dot_general(
-            counts, block, (((0,), (0,)), ((), ())), preferred_element_type=jnp.float32
-        )
-    accum_new = cache_accum + jnp.mean(row_grad * row_grad, axis=1)
-    rows_new = cache_rows - ETA * row_grad * lax.rsqrt(accum_new)[:, None]
-    rows_new = rows_new.at[evict_slot].set(fetched_rows)
-    accum_new = accum_new.at[evict_slot].set(fetched_accum)
     return (rows_new, accum_new, table_new, accum_table, clipped_proj, clipped_vecs, loss)
 
 

time: 155 us -> 148 us (0.955)
  local copies, waits for them, and re-layouts: 19.4 us -> 6.96 us
  matrix products: 10.7 us -> 0 us
  Pallas kernels: 17.8 us -> 28.5 us
  waiting for transfers between devices: 46 us -> 49.4 us
    dot_general x8 -> x0, matrix products: 10.7 us -> none  [shards(): lax.dot_general(counts, block, (((0,), (0,)), ((), ())), preferred_elemen...]
    pallas_call x1 -> x2, Pallas kernels: 1.69 us -> 10.1 us  [the longest x1 8.14 us: refilled(): pl.pallas_call(refill_kernel, out_shape=(jax.ShapeDtypeStruct(cache_rows....]
    unnamed x44 -> x20, local copies, waits for them, and re-layouts: 6.86 us -> 0.1 us
    scatter x2 -> x0, local copies, waits for them, and re-layouts: 3.95 us -> none  [the longest x1 3.16 us: shards(): rows_new = rows_new.at[evict_slot].set(fetched_rows)]
    pallas_call x1, Pallas kernels: 9.05 us -> 12.7 us  [dense(): pl.pallas_call(dense_kernel, out_shape=(bundle, bundle, jax.ShapeDtypeStr...]
    ppermute x2, starting transfers between devices: 5.64 us -> 2.82 us  [swap_cores(): return lax.ppermute(value, AXES, [(i, i ^ 1) for i in range(256)])]
    sub x1 -> x0, local copies, waits for them, and re-layouts: 2.53 us -> none  [shards(): rows_new = cache_rows - ETA * row_grad * lax.rsqrt(accum_new)[:, None]]
    all_to_all x4, waiting for transfers between devices: 2.32 us -> 4.81 us  [exchange(): lax.all_to_all(value, AXES, split_axis=0, concat_axis=0, tiled=True, axis...]
  transfers between devices with their start and end apart: 12 -> 12, of which waited for: 8 -> 9; matrix products, arithmetic and copies ran while one was open for 17% -> 6% of each run, Pallas kernels for 7% -> 16%
where the time goes in v4:
time: 148 us; the launch traced here: 145 us
  starting transfers between devices  50.4 us (34%)
  waiting for transfers between devices  49.4 us (33%)
  Pallas kernels  28.5 us (19%)
  other arithmetic  7.63 us (5%)
  local copies, waits for them, and re-layouts  6.96 us (5%)
  between operations  2.22 us (2%)
    ppermute x5, waiting for transfers between devices, cross(): came = lax.ppermute(split[:, 1], AXES, there)  38.7 us
    all_to_all x4, starting transfers between devices, exchange(): lax.all_to_all(value, AXES, split_axis=0, concat_axis=0, tiled=True, axis...  30.1 us
    pallas_call x1, Pallas kernels, dense(): pl.pallas_call(dense_kernel, out_shape=(bundle, bundle, jax.ShapeDtypeStr...  12.7 us
    all_to_all x1, starting transfers between devices, shards(): got = lax.all_to_all(sent, 'table', split_axis=0, concat_axis=0, tiled=True)  10.3 us
    pallas_call x1, Pallas kernels, refilled(): pl.pallas_call(refill_kernel, out_shape=(jax.ShapeDtypeStruct(cache_rows....  8.14 us
    ppermute x5, starting transfers between devices, cross(): came = lax.ppermute(split[:, 1], AXES, there)  7.16 us
    ppermute x2, waiting for transfers between devices, swap_cores(): return lax.ppermute(value, AXES, [(i, i ^ 1) for i in range(256)])  5.96 us
    all_to_all x4, waiting for transfers between devices, exchange(): lax.all_to_all(value, AXES, split_axis=0, concat_axis=0, tiled=True, axis...  4.81 us
  transfers between devices with their start and end apart: 12, of which 9 were waited for; matrix products, arithmetic and copies ran while one was open for 6% of the time, Pallas kernels for 16%

profile of v4, /device:TPU:3, one launch (start us, length us, event | category | flops | bytes accessed | tf_op | source)
XLA Modules:
  0.0 145.2 jit_solution(14643916304331285419)
XLA Ops:
  0.6 3.1 %payload.1 = f32[256,256]{1,0:T(8,128)} custom-call(s32[64]{0:T(128)} %evict_ref.1, s32[2,64]{1,0:T(2,128)} %bitcast.86, s32[2,64]{1,0:T(2,128)} %bitcast.84, f32[1024]{0:T(1024)} %accum_ref.1, f32[1024,256]{1,0:T(8,128)} %cache_ref.5), custom_call_target="tpu_custom_call" | custom-call | flops 100000 | bytes 1500000 | tf_op jit(solution)/shard_map/payload/pallas_call | solution.py:305
  3.7 10.3 %all-to-all-start = ((f32[32,8,256]{2,1,0:T(8,128)}), f32[32,8,256]{2,1,0:T(8,128)S(1)}, u32[]{:S(2)}, u32[]{:S(2)}) async-start(f32[32,8,256]{2,1,0:T(8,128)} %bitcast.66), calls=%async_computation | async-start | bytes 524288 | tf_op jit(solution)/shard_map/all_to_all | solution.py:507
  14.1 12.7 %dense.1 = (f32[8,264,256]{2,1,0:T(8,128)}, f32[8,264,256]{2,1,0:T(8,128)}, bf16[8,256,256]{2,1,0:T(8,128)(2,1)}) custom-call(s32[1]{0:T(128)} %bitcast.core_ref, s32[32,256]{1,0:T(8,128)} %bitcast.87, s32[1,256]{1,0:T(1,128)} %bitcast.91, f32[1024,256]{1,0:T(8,128)} %cache_ref.5, bf16[2048,256]{1,0:T(8,128)(2,1)} %u_any.1, bf16[2048,256]{1,0:T(8,128)(2,1)} %v_any.1, ...), custom_call_target="tpu_custom_call" | custom-call | flops 5000000000 | bytes 9000000 | tf_op jit(solution)/shard_map/dense/pallas_call | solution.py:212
  26.7 0.7 collective-permute-start
  27.5 4.1 %collective-permute-done = f32[8,264,256]{2,1,0:T(8,128)S(1)} collective-permute-done((f32[8,264,256]{2,1,0:T(8,128)}, f32[8,264,256]{2,1,0:T(8,128)S(1)}, u32[]{:S(2)}, u32[]{:S(2)}) %collective-permute-start) | collective-permute-done | bytes 2162720 | tf_op jit(solution)/shard_map/ppermute | solution.py:40
  31.6 3.2 %add.26 = f32[8,264,256]{2,1,0:T(8,128)} add(f32[8,264,256]{2,1,0:T(8,128)} %get-tuple-element.31, f32[8,264,256]{2,1,0:T(8,128)S(1)} %collective-permute-done) | non-fusion elementwise | flops 540672 | bytes 6488064 | tf_op jit(solution)/shard_map/add | solution.py:518
  34.8 6.4 %all-to-all-start.1 = ((f32[8,264,256]{2,1,0:T(8,128)}), f32[8,264,256]{2,1,0:T(8,128)S(1)}, u32[]{:S(2)}, u32[]{:S(2)}) async-start(f32[8,264,256]{2,1,0:T(8,128)} %add.26), calls=%async_computation.1 | async-start | bytes 4325376 | tf_op jit(solution)/shard_map/all_to_all | solution.py:44
  41.5 0.1 eq.102
  41.6 0.1 reshape.158
  41.8 0.1 broadcast_in_dim.156
  41.9 0.1 select_reduce_fusion.3
  42.0 0.1 convert_element_type.27
  42.1 0.2 fusion
  42.3 0.2 select_reduce_fusion.1
  42.5 0.2 select_reduce_fusion
  42.9 0.7 reshape.182
  43.6 2.0 %scatter_fusion = f32[1024,256]{1,0:T(8,128)S(1)} fusion(f32[1024,256]{1,0:T(8,128)S(1)} %copy-done.1, s32[192]{0:T(256)S(1)} %bitcast.83, f32[192,256]{1,0:T(8,128)} %reshape.182), kind=kCustom, calls=%fused_computation.1 | custom fusion | bytes 590592 | tf_op jit(solution)/shard_map/scatter | solution.py:524
  45.6 1.0 gather_fusion
  46.6 0.1 copy_select_fusion
  46.8 0.1 collective-permute-start.1
  46.9 1.3 collective-permute-done.1
  48.2 1.3 collective-permute-start.2
  49.5 8.4 %collective-permute-done.2 = f32[1,16,8,256]{3,2,1,0:T(8,128)S(1)} collective-permute-done((f32[1,16,8,256]{3,2,1,0:T(8,128)S(1)}, f32[1,16,8,256]{3,2,1,0:T(8,128)S(1)}, u32[]{:S(2)}, u32[]{:S(2)}) %collective-permute-start.2) | collective-permute-done | bytes 131104 | tf_op jit(solution)/shard_map/ppermute | solution.py:69
  58.1 0.2 reduce_sum.77
  58.3 0.8 pad_maximum_fusion
  59.0 9.0 %all-to-all-start.2 = ((f32[16,24,256]{2,1,0:T(8,128)}), f32[16,24,256]{2,1,0:T(8,128)S(1)}, u32[]{:S(2)}, u32[]{:S(2)}) async-start(f32[16,24,256]{2,1,0:T(8,128)} %pad_maximum_fusion), calls=%async_computation.2 | async-start | bytes 786432 | tf_op jit(solution)/shard_map/all_to_all | solution.py:44
  68.1 0.1 collective-permute-start.3
  68.2 10.9 %collective-permute-done.3 = f32[8,2,8,256]{3,2,1,0:T(8,128)S(1)} collective-permute-done((f32[8,2,8,256]{3,2,1,0:T(8,128)S(1)}, f32[8,2,8,256]{3,2,1,0:T(8,128)S(1)}, u32[]{:S(2)}, u32[]{:S(2)}) %collective-permute-start.3) | collective-permute-done | bytes 131104 | tf_op jit(solution)/shard_map/ppermute | solution.py:69
  79.2 0.5 collective-permute-start.4
  79.7 8.5 %collective-permute-done.4 = f32[4,4,8,256]{3,2,1,0:T(8,128)S(1)} collective-permute-done((f32[4,4,8,256]{3,2,1,0:T(8,128)S(1)}, f32[4,4,8,256]{3,2,1,0:T(8,128)S(1)}, u32[]{:S(2)}, u32[]{:S(2)}) %collective-permute-start.4) | collective-permute-done | bytes 131104 | tf_op jit(solution)/shard_map/ppermute | solution.py:69
  88.4 0.7 broadcast_in_dim.165
  89.1 8.0 %all-to-all-start.3 = ((f32[16,16,256]{2,1,0:T(8,128)}), f32[16,16,256]{2,1,0:T(8,128)S(1)}, u32[]{:S(2)}, u32[]{:S(2)}) async-start(f32[16,16,256]{2,1,0:T(8,128)} %broadcast_in_dim.165), calls=%async_computation.3 | async-start | bytes 524288 | tf_op jit(solution)/shard_map/all_to_all | solution.py:44
  97.1 5.2 %collective-permute-start.5 = (f32[2,8,8,256]{3,2,1,0:T(8,128)S(1)}, f32[2,8,8,256]{3,2,1,0:T(8,128)S(1)}, u32[]{:S(2)}, u32[]{:S(2)}) collective-permute-start(f32[2,8,8,256]{3,2,1,0:T(8,128)S(1)} %get-tuple-element.54), channel_id=1, source_target_pairs={{0,8},{1,9},{2,10},{3,11},{4,12},{5,13},{6,14},{7,15},{8,0},{9,1},... | collective-permute-start | bytes 393224 | tf_op jit(solution)/shard_map/ppermute | solution.py:69
  102.3 9.5 %collective-permute-done.5 = f32[2,8,8,256]{3,2,1,0:T(8,128)S(1)} collective-permute-done((f32[2,8,8,256]{3,2,1,0:T(8,128)S(1)}, f32[2,8,8,256]{3,2,1,0:T(8,128)S(1)}, u32[]{:S(2)}, u32[]{:S(2)}) %collective-permute-start.5) | collective-permute-done | bytes 131104 | tf_op jit(solution)/shard_map/ppermute | solution.py:69
  111.9 1.5 %broadcast_in_dim.166 = f32[8,264,256]{2,1,0:T(8,128)} broadcast(f32[264,256]{1,0:T(8,128)S(1)} %pad_maximum_fusion.1), dimensions={1,2} | broadcast | bytes 2433024 | tf_op jit(solution)/shard_map/broadcast_in_dim | solution.py:563
  113.3 6.6 %all-to-all-start.4 = ((f32[8,264,256]{2,1,0:T(8,128)}), f32[8,264,256]{2,1,0:T(8,128)S(1)}, u32[]{:S(2)}, u32[]{:S(2)}) async-start(f32[8,264,256]{2,1,0:T(8,128)} %broadcast_in_dim.166), calls=%async_computation.4 | async-start | bytes 4325376 | tf_op jit(solution)/shard_map/all_to_all | solution.py:44
  120.0 0.2 convert_reduce_fusion
  120.2 0.1 fusion.1
  120.3 0.5 multiply_add_fusion.place_ref
  121.0 8.1 %refill.1 = (f32[1024,256]{1,0:T(8,128)}, f32[1,1024]{1,0:T(1,128)}) custom-call(s32[32,256]{1,0:T(8,128)} %bitcast.88, s32[64]{0:T(128)} %evict_ref.1, s32[64]{0:T(128)} %multiply_add_fusion.place_ref, f32[1024,256]{1,0:T(8,128)} %cache_ref.5, f32[1,1024]{1,0:T(1,128)} %bitcast.82, bf16[8,256,256]{2,1,0:T(8,128)(2,1)} %get-tuple-element.43.dpooled_ref, ...), custom_call_target="tpu_custom_call" | custom-call | flops 1100000000 | bytes 4000000 | tf_op jit(solution)/shard_map/refill/pallas_call | solution.py:354
  129.1 0.2 select_reduce_fusion.4
  129.3 0.1 select_reduce_fusion.2
  129.4 1.3 select_n.76
  130.7 4.7 %all-to-all-done.4.half_any = f32[8,264,256]{2,1,0:T(8,128)S(1)} async-done(((f32[8,264,256]{2,1,0:T(8,128)}), f32[8,264,256]{2,1,0:T(8,128)S(1)}, u32[]{:S(2)}, u32[]{:S(2)}) %all-to-all-start.4) | async-done | bytes 2162720 | tf_op jit(solution)/shard_map/all_to_all | solution.py:44
  135.4 2.1 %collective-permute-start.6 = (f32[8,264,256]{2,1,0:T(8,128)S(1)}, f32[8,264,256]{2,1,0:T(8,128)S(1)}, u32[]{:S(2)}, u32[]{:S(2)}) collective-permute-start(f32[8,264,256]{2,1,0:T(8,128)S(1)} %all-to-all-done.4.half_any), channel_id=1, source_target_pairs={{0,1},{1,0},{2,3},{3,2},{4,5},{5,4},{6,7},{7,6},{8,9},{9,8},{10,11... | collective-permute-start | bytes 6488072 | tf_op jit(solution)/shard_map/ppermute | solution.py:40
  137.5 2.0 %scale_own.1.proj_in = f32[2,2048,256]{2,1,0:T(8,128)} custom-call(s32[1]{0:T(128)} %bitcast.core_ref, f32[8,264,256]{2,1,0:T(8,128)S(1)} %all-to-all-done.4.half_any), custom_call_target="tpu_custom_call" | custom-call | tf_op jit(solution)/shard_map/scale_own/pallas_call | solution.py:453
  139.5 1.9 %collective-permute-done.6.half_any = f32[8,264,256]{2,1,0:T(8,128)S(1)} collective-permute-done((f32[8,264,256]{2,1,0:T(8,128)S(1)}, f32[8,264,256]{2,1,0:T(8,128)S(1)}, u32[]{:S(2)}, u32[]{:S(2)}) %collective-permute-start.6) | collective-permute-done | bytes 2162720 | tf_op jit(solution)/shard_map/ppermute | solution.py:40
  141.4 2.6 %scale_other.1 = (f32[2,2048,256]{2,1,0:T(8,128)}, f32[2,2048]{1,0:T(2,128)}, f32[1,128]{1,0:T(1,128)S(1)}) custom-call(s32[1]{0:T(128)} %bitcast.core_ref, f32[2,2048,256]{2,1,0:T(8,128)} %scale_own.1.proj_in, f32[8,8,256]{2,1,0:T(8,128)S(1)} %slice.91.own_ref, f32[8,264,256]{2,1,0:T(8,128)S(1)} %collective-permute-done.6.half_any), custom_call_target="tpu_custom_call", output_to_operand_aliasing={{0}: (1, {})} | custom-call | tf_op jit(solution)/shard_map/scale_other/pallas_call | solution.py:462
  (61 shorter events, 1.1 us)
Async XLA Ops:
  3.7 23.0 %all-to-all-start = ((f32[32,8,256]{2,1,0:T(8,128)}), f32[32,8,256]{2,1,0:T(8,128)S(1)}, u32[]{:S(2)}, u32[]{:S(2)}) async-start(f32[32,8,256]{2,1,0:T(8,128)} %bitcast.66), calls=%async_computation | async-start | bytes 524288 | tf_op jit(solution)/shard_map/all_to_all | solution.py:507
  26.7 4.8 %collective-permute-start = (f32[8,264,256]{2,1,0:T(8,128)}, f32[8,264,256]{2,1,0:T(8,128)S(1)}, u32[]{:S(2)}, u32[]{:S(2)}) collective-permute-start(f32[8,264,256]{2,1,0:T(8,128)} %get-tuple-element.34), channel_id=1, source_target_pairs={{0,1},{1,0},{2,3},{3,2},{4,5},{5,4},{6,7},{7,6},{8,9},{9,8},{10,11... | collective-permute-start | bytes 6488072 | tf_op jit(solution)/shard_map/ppermute | solution.py:40
  34.8 7.7 %copy-start.5 = (f32[1024]{0:T(1024)S(1)}, f32[1024]{0:T(1024)}, u32[]{:S(2)}) copy-start(f32[1024]{0:T(1024)} %param.18) | copy-start | bytes 12292
  34.8 8.8 %copy-start.1 = (f32[1024,256]{1,0:T(8,128)S(1)}, f32[1024,256]{1,0:T(8,128)}, u32[]{:S(2)}) copy-start(f32[1024,256]{1,0:T(8,128)} %param.17) | copy-start | bytes 3145732
  34.8 23.3 %all-to-all-start.1 = ((f32[8,264,256]{2,1,0:T(8,128)}), f32[8,264,256]{2,1,0:T(8,128)S(1)}, u32[]{:S(2)}, u32[]{:S(2)}) async-start(f32[8,264,256]{2,1,0:T(8,128)} %add.26), calls=%async_computation.1 | async-start | bytes 4325376 | tf_op jit(solution)/shard_map/all_to_all | solution.py:44
  42.5 4.1 %copy-start.3 = (f32[1024]{0:T(1024)}, f32[1024]{0:T(1024)S(1)}, u32[]{:S(2)}) copy-start(f32[1024]{0:T(1024)S(1)} %select_n.69) | copy-start | bytes 12292
  45.6 2.6 %copy-start = (f32[1024,256]{1,0:T(8,128)}, f32[1024,256]{1,0:T(8,128)S(1)}, u32[]{:S(2)}) copy-start(f32[1024,256]{1,0:T(8,128)S(1)} %scatter_fusion) | copy-start | bytes 3145732
  46.8 1.4 collective-permute-start.1
  48.2 9.7 %collective-permute-start.2 = (f32[1,16,8,256]{3,2,1,0:T(8,128)S(1)}, f32[1,16,8,256]{3,2,1,0:T(8,128)S(1)}, u32[]{:S(2)}, u32[]{:S(2)}) collective-permute-start(f32[1,16,8,256]{3,2,1,0:T(8,128)S(1)} %get-tuple-element.60), channel_id=1, source_target_pairs={{0,16},{1,17},{2,18},{3,19},{4,20},{5,21},{6,22},{7,23},{8,24},{9,... | collective-permute-start | bytes 393224 | tf_op jit(solution)/shard_map/ppermute | solution.py:69
  59.0 29.3 %all-to-all-start.2 = ((f32[16,24,256]{2,1,0:T(8,128)}), f32[16,24,256]{2,1,0:T(8,128)S(1)}, u32[]{:S(2)}, u32[]{:S(2)}) async-start(f32[16,24,256]{2,1,0:T(8,128)} %pad_maximum_fusion), calls=%async_computation.2 | async-start | bytes 786432 | tf_op jit(solution)/shard_map/all_to_all | solution.py:44
  68.1 11.0 %collective-permute-start.3 = (f32[8,2,8,256]{3,2,1,0:T(8,128)S(1)}, f32[8,2,8,256]{3,2,1,0:T(8,128)S(1)}, u32[]{:S(2)}, u32[]{:S(2)}) collective-permute-start(f32[8,2,8,256]{3,2,1,0:T(8,128)S(1)} %get-tuple-element.58), channel_id=1, source_target_pairs={{0,2},{1,3},{2,0},{3,1},{4,6},{5,7},{6,4},{7,5},{8,10},{9,11},{10,... | collective-permute-start | bytes 393224 | tf_op jit(solution)/shard_map/ppermute | solution.py:69
  79.2 9.1 %collective-permute-start.4 = (f32[4,4,8,256]{3,2,1,0:T(8,128)S(1)}, f32[4,4,8,256]{3,2,1,0:T(8,128)S(1)}, u32[]{:S(2)}, u32[]{:S(2)}) collective-permute-start(f32[4,4,8,256]{3,2,1,0:T(8,128)S(1)} %get-tuple-element.56), channel_id=1, source_target_pairs={{0,4},{1,5},{2,6},{3,7},{4,0},{5,1},{6,2},{7,3},{8,12},{9,13},{10,... | collective-permute-start | bytes 393224 | tf_op jit(solution)/shard_map/ppermute | solution.py:69
  89.1 22.7 %all-to-all-start.3 = ((f32[16,16,256]{2,1,0:T(8,128)}), f32[16,16,256]{2,1,0:T(8,128)S(1)}, u32[]{:S(2)}, u32[]{:S(2)}) async-start(f32[16,16,256]{2,1,0:T(8,128)} %broadcast_in_dim.165), calls=%async_computation.3 | async-start | bytes 524288 | tf_op jit(solution)/shard_map/all_to_all | solution.py:44
  97.1 14.6 %collective-permute-start.5 = (f32[2,8,8,256]{3,2,1,0:T(8,128)S(1)}, f32[2,8,8,256]{3,2,1,0:T(8,128)S(1)}, u32[]{:S(2)}, u32[]{:S(2)}) collective-permute-start(f32[2,8,8,256]{3,2,1,0:T(8,128)S(1)} %get-tuple-element.54), channel_id=1, source_target_pairs={{0,8},{1,9},{2,10},{3,11},{4,12},{5,13},{6,14},{7,15},{8,0},{9,1},... | collective-permute-start | bytes 393224 | tf_op jit(solution)/shard_map/ppermute | solution.py:69
  111.8 9.0 %copy-start.2 = (f32[2,2,8,8,256]{4,3,2,1,0:T(8,128)}, f32[2,2,8,8,256]{4,3,2,1,0:T(8,128)S(1)}, u32[]{:S(2)}) copy-start(f32[2,2,8,8,256]{4,3,2,1,0:T(8,128)S(1)} %copy.51) | copy-start | bytes 786436
  113.3 6.7 %copy-start.4 = (s32[64,2]{0,1:T(2,128)S(1)}, s32[64,2]{0,1:T(2,128)}, u32[]{:S(2)}) copy-start(s32[64,2]{0,1:T(2,128)} %param.19) | copy-start | bytes 1540
  113.3 6.8 %copy-start.6 = (s32[64]{0:T(128)S(1)}, s32[64]{0:T(128)}, u32[]{:S(2)}) copy-start(s32[64]{0:T(128)} %evict_ref.1) | copy-start | bytes 772
  113.3 22.1 %all-to-all-start.4 = ((f32[8,264,256]{2,1,0:T(8,128)}), f32[8,264,256]{2,1,0:T(8,128)S(1)}, u32[]{:S(2)}, u32[]{:S(2)}) async-start(f32[8,264,256]{2,1,0:T(8,128)} %broadcast_in_dim.166), calls=%async_computation.4 | async-start | bytes 4325376 | tf_op jit(solution)/shard_map/all_to_all | solution.py:44
  120.0 9.3 %copy-start.7 = (s32[64]{0:T(128)S(1)}, s32[64]{0:T(128)}, u32[]{:S(2)}) copy-start(s32[64]{0:T(128)} %evict_ref.1) | copy-start | bytes 772
  135.4 6.0 %collective-permute-start.6 = (f32[8,264,256]{2,1,0:T(8,128)S(1)}, f32[8,264,256]{2,1,0:T(8,128)S(1)}, u32[]{:S(2)}, u32[]{:S(2)}) collective-permute-start(f32[8,264,256]{2,1,0:T(8,128)S(1)} %all-to-all-done.4.half_any), channel_id=1, source_target_pairs={{0,1},{1,0},{2,3},{3,2},{4,5},{5,4},{6,7},{7,6},{8,9},{9,8},{10,11... | collective-permute-start | bytes 6488072 | tf_op jit(solution)/shard_map/ppermute | solution.py:40

commit v5 on v4

--- a/solution.py
+++ b/solution.py
@@ -68,6 +68,15 @@
     there = [(i, i ^ bit) for i in range(256)]
     came = lax.ppermute(split[:, 1], AXES, there)
     return jnp.stack([split[:, 0], came], axis=1).reshape(value.shape)
+
+
+def cross_z(value):
+    split = value.reshape(2, 8, 2, *value.shape[1:])
+    came = [split[:, 0]]
+    for step in range(1, 8):
+        there = [(i, i ^ (2 * step)) for i in range(256)]
+        came.append(lax.ppermute(split[:, step], AXES, there))
+    return jnp.stack(came, axis=1).reshape(value.shape)
 
 
 def dense_kernel(
@@ -81,12 +90,13 @@
     head_ref,
     keep_out,
     send_out,
-    dpooled_out,
+    latent_ref,
+    dlatent_ref,
+    dlogit_ref,
     u_ref,
     v_ref,
     keep_ref,
     send_ref,
-    dpooled_ref,
     high,
     mid,
     low,
@@ -128,6 +138,7 @@
     load_v.wait()
     load_u.wait()
     latent = jnp.dot(pooled[...], v_ref[...], preferred_element_type=f32).astype(bf16)
+    latent_ref[...] = latent
     across = (((1,), (1,)), ((), ()))
     logit_wide = jnp.zeros((count, width), f32)
     for c in range(feats):
@@ -164,6 +175,8 @@
             ref[c, width + 1 : width + 2, :] = loss_row
             ref[c, width + 2 : width + 8, :] = jnp.zeros((6, width), f32)
     dlatent = back.astype(bf16)
+    dlatent_ref[...] = dlatent
+    dlogit_ref[...] = jnp.transpose(dlogit)
 
     down = (((0,), (0,)), ((), ()))
     right_keep = jnp.where(mine, latent, dlatent)
@@ -192,12 +205,6 @@
             preferred_element_type=f32,
         )
         give(keep_ref.at[c], keep_out.at[c])
-    for c in range(feats):
-        cut = slice(c * width, (c + 1) * width)
-        through = lax.dot_general(dlatent, v_ref[cut, :], across, preferred_element_type=f32)
-        through = through + dlogit * head_ref[:, cut] * (shifted[:, cut] + 1.0)
-        dpooled_ref[c] = through.astype(bf16)
-        give(dpooled_ref.at[c], dpooled_out.at[c])
     for copy in copies:
         copy.wait()
 
@@ -214,19 +221,20 @@
         out_shape=(
             bundle,
             bundle,
-            jax.ShapeDtypeStruct((blocks, count, width), jnp.bfloat16),
+            jax.ShapeDtypeStruct((count, width), jnp.bfloat16),
+            jax.ShapeDtypeStruct((count, width), jnp.bfloat16),
+            jax.ShapeDtypeStruct((1, count), jnp.float32),
         ),
         in_specs=[pl.BlockSpec(memory_space=pltpu.SMEM)]
         + [vmem] * 3
         + [anywhere] * 2
         + [vmem] * 2,
-        out_specs=(anywhere, anywhere, anywhere),
+        out_specs=(anywhere, anywhere, vmem, vmem, vmem),
         scratch_shapes=[
             pltpu.VMEM((wide, width), jnp.bfloat16),
             pltpu.VMEM((wide, width), jnp.bfloat16),
             pltpu.VMEM(bundle.shape, jnp.float32),
             pltpu.VMEM(bundle.shape, jnp.float32),
-            pltpu.VMEM((blocks, count, width), jnp.bfloat16),
         ]
         + [pltpu.VMEM((cells, width), jnp.bfloat16)] * 3
         + [
@@ -234,7 +242,7 @@
             pltpu.VMEM((count, wide), jnp.float32),
             pltpu.VMEM((count, wide), jnp.bfloat16),
             pltpu.SemaphoreType.DMA((2,)),
-            pltpu.SemaphoreType.DMA((3 * blocks,)),
+            pltpu.SemaphoreType.DMA((2 * blocks,)),
         ],
         compiler_params=pltpu.CompilerParams(vmem_limit_bytes=60 * 1024 * 1024),
         cost_estimate=pl.CostEstimate(flops=5_000_000_000, bytes_accessed=9_000_000, transcendentals=1000),
@@ -313,20 +321,66 @@
     )(evict_slot, evict_dest.T, miss_dest.T, cache_accum, cache_rows)
 
 
+def add_kernel(keep_any, came_any, out_any, keep, came, total, in_sems, out_sems):
+    blocks = keep.shape[0]
+    loads, stores = [], []
+    for c in range(blocks):
+        for k, (source, target) in enumerate(((keep_any, keep), (came_any, came))):
+            loads.append(
+                pltpu.make_async_copy(source.at[c], target.at[c], in_sems.at[2 * c + k])
+            )
+            loads[-1].start()
+    for c in range(blocks):
+        loads[2 * c].wait()
+        loads[2 * c + 1].wait()
+        total[c] = keep[c] + came[c]
+        stores.append(pltpu.make_async_copy(total.at[c], out_any.at[c], out_sems.at[c]))
+        stores[-1].start()
+    for store in stores:
+        store.wait()
+
+
+def added(keep, came):
+    anywhere = pl.BlockSpec(memory_space=pl.ANY)
+    return pl.pallas_call(
+        add_kernel,
+        out_shape=jax.ShapeDtypeStruct(keep.shape, jnp.float32),
+        in_specs=[anywhere, anywhere],
+        out_specs=anywhere,
+        scratch_shapes=[pltpu.VMEM(keep.shape, jnp.float32)] * 3
+        + [
+            pltpu.SemaphoreType.DMA((2 * keep.shape[0],)),
+            pltpu.SemaphoreType.DMA((keep.shape[0],)),
+        ],
+        compiler_params=pltpu.CompilerParams(vmem_limit_bytes=44 * 1024 * 1024),
+        name="add_halves",
+    )(keep, came)
+
+
 def refill_kernel(
     slots_ref,
     evict_ref,
     place_ref,
     cache_ref,
     accum_ref,
-    dpooled_ref,
+    latent_ref,
+    dlatent_ref,
+    dlogit_ref,
+    u_ref,
+    v_ref,
+    bias_ref,
+    head_ref,
     back_ref,
     rows_ref,
     accum_out,
 ):
     f32, bf16 = jnp.float32, jnp.bfloat16
-    (cells, width), (feats, count, _) = cache_ref.shape, dpooled_ref.shape
+    (cells, width), count = cache_ref.shape, latent_ref.shape[0]
+    feats = u_ref.shape[0] // width
     looks = slots_ref.shape[0] // feats
+    across = (((1,), (1,)), ((), ()))
+    latent, dlatent = latent_ref[...], dlatent_ref[...]
+    dlogit = jnp.transpose(dlogit_ref[...])
     cell = lax.broadcasted_iota(jnp.int32, (cells, count), 0)
     grad = jnp.zeros((cells, width), f32)
     for f in range(feats):
@@ -334,7 +388,12 @@
         for look in range(looks):
             at = f * looks + look
             counts = counts + jnp.where(cell == slots_ref[at : at + 1, :], 1.0, 0.0)
-        grad = grad + jnp.dot(counts.astype(bf16), dpooled_ref[f], preferred_element_type=f32)
+        cut = slice(f * width, (f + 1) * width)
+        moved = lax.dot_general(latent, u_ref[cut, :], across, preferred_element_type=f32)
+        moved = moved + bias_ref[:, cut]
+        through = lax.dot_general(dlatent, v_ref[cut, :], across, preferred_element_type=f32)
+        dpooled = (dlogit * head_ref[:, cut] * (moved + 1.0) + through).astype(bf16)
+        grad = grad + jnp.dot(counts.astype(bf16), dpooled, preferred_element_type=f32)
     mean = jnp.sum(grad * grad, axis=1, keepdims=True) / width
     accum = jnp.transpose(accum_ref[...]) + mean
     rows_ref[...] = cache_ref[...] - ETA * grad * lax.rsqrt(accum)
@@ -347,7 +406,7 @@
     lax.fori_loop(0, evict_ref.shape[0], refill, 0, unroll=8)
 
 
-def refilled(slot_ids, evict_slot, place, cache_rows, cache_accum, dpooled, back):
+def refilled(slot_ids, evict_slot, place, cache_rows, cache_accum, saved, params, back):
     cells = cache_rows.shape[0]
     smem = pl.BlockSpec(memory_space=pltpu.SMEM)
     vmem = pl.BlockSpec(memory_space=pltpu.VMEM)
@@ -357,7 +416,7 @@
             jax.ShapeDtypeStruct(cache_rows.shape, jnp.float32),
             jax.ShapeDtypeStruct((1, cells), jnp.float32),
         ),
-        in_specs=[vmem, smem, smem, vmem, vmem, vmem, vmem],
+        in_specs=[vmem, smem, smem] + [vmem] * 10,
         out_specs=(vmem, vmem),
         compiler_params=pltpu.CompilerParams(vmem_limit_bytes=60 * 1024 * 1024),
         cost_estimate=pl.CostEstimate(flops=1_100_000_000, bytes_accessed=4_000_000, transcendentals=1000),
@@ -368,7 +427,8 @@
         place,
         cache_rows,
         cache_accum[None, :],
-        dpooled,
+        *saved,
+        *params,
         back,
     )
 
@@ -508,14 +568,14 @@
 
     count = slot_ids.shape[0]
     feats = proj_u.shape[0] // width
-    keep, send, dpooled = dense(
+    keep, send, *saved = dense(
         core, slots_late, labels, cache_rows, proj_u, proj_v, cross_bias, head
     )
 
     blocks = feats
     depth = width
     send, got = lax.optimization_barrier((send, got))
-    held = keep + swap_cores(send)
+    held = added(keep, swap_cores(send))
     held, got = lax.optimization_barrier((held, got))
 
     got_meta = got[:, per - 1, :]
@@ -551,19 +611,24 @@
         axis=1,
     )
     held = exchange(pieces16, second_groups())
-    back = cross(cross(back, 2), 4)
+    back = cross_z(back)
     held, back = lax.optimization_barrier((held, back))
     summed16 = jnp.sum(held, axis=0)
     extras = summed16[fine:]
     spread = jnp.broadcast_to(summed16[None, :fine], (16, fine, width))
     held = exchange(spread, second_groups())
-    back = cross(back, 8)
-    held, back = lax.optimization_barrier((held, back))
     whole = jnp.concatenate([held.reshape(depth, width), extras], axis=0)
     whole = exchange(jnp.broadcast_to(whole[None], (blocks, depth + 8, width)), first_groups())
     in_place = (miss_dest[:, 0] ^ me) * per + ranks(miss_dest[:, 0])
     rows_new, accum_new = refilled(
-        slot_ids, evict_slot, in_place, cache_rows, cache_accum, dpooled, back.reshape(spots, width)
+        slot_ids,
+        evict_slot,
+        in_place,
+        cache_rows,
+        cache_accum,
+        saved,
+        (proj_u, proj_v, cross_bias[None, :], head[None, :]),
+        back.reshape(spots, width),
     )
     fetched_accum = picked(back[:, per - 1, :per].reshape(-1), in_place)
     filled = evict_slot[:, None] == jnp.arange(cells, dtype=jnp.int32)[None, :]

time: 148 us -> 146 us (0.986)
  waiting for transfers between devices: 49.4 us -> 36.1 us
  starting transfers between devices: 50.4 us -> 59.3 us
  Pallas kernels: 28.5 us -> 32.3 us
  other arithmetic: 7.63 us -> 4.35 us
  local copies, waits for them, and re-layouts: 6.96 us -> 8.54 us
    ppermute x5 -> x2, waiting for transfers between devices: 38.7 us -> 9.77 us  [cross(): came = lax.ppermute(split[:, 1], AXES, there)]
    ppermute x0 -> x7, starting transfers between devices: none -> 13.5 us  [cross_z(): came.append(lax.ppermute(split[:, step], AXES, there))]
    ppermute x0 -> x7, waiting for transfers between devices: none -> 8.57 us  [cross_z(): came.append(lax.ppermute(split[:, step], AXES, there))]
    all_to_all x4, waiting for transfers between devices: 4.81 us -> 11.8 us  [exchange(): lax.all_to_all(value, AXES, split_axis=0, concat_axis=0, tiled=True, axis...]
    ppermute x5 -> x2, starting transfers between devices: 7.16 us -> 1.36 us  [cross(): came = lax.ppermute(split[:, 1], AXES, there)]
    add x1 -> x0, other arithmetic: 3.23 us -> none  [shards(): held = keep + swap_cores(send)]
    pallas_call x0 -> x1, Pallas kernels: none -> 2.02 us  [added(): pl.pallas_call(add_kernel, out_shape=jax.ShapeDtypeStruct(keep.shape, jnp...]
    ppermute x2, starting transfers between devices: 2.82 us -> 4.77 us  [swap_cores(): return lax.ppermute(value, AXES, [(i, i ^ 1) for i in range(256)])]
  transfers between devices with their start and end apart: 12 -> 16, of which waited for: 9 -> 9; matrix products, arithmetic and copies ran while one was open for 6% -> 6% of each run, Pallas kernels for 16% -> 17%
where the time goes in v5:
time: 146 us; the launch traced here: 143 us
  starting transfers between devices  59.3 us (41%)
  waiting for transfers between devices  36.1 us (25%)
  Pallas kernels  32.3 us (22%)
  local copies, waits for them, and re-layouts  8.54 us (6%)
  other arithmetic  4.35 us (3%)
  between operations  2.26 us (2%)
    all_to_all x4, starting transfers between devices, exchange(): lax.all_to_all(value, AXES, split_axis=0, concat_axis=0, tiled=True, axis...  29.3 us
    ppermute x7, starting transfers between devices, cross_z(): came.append(lax.ppermute(split[:, step], AXES, there))  13.5 us
    pallas_call x1, Pallas kernels, dense(): pl.pallas_call(dense_kernel, out_shape=(bundle, bundle, jax.ShapeDtypeStr...  12.9 us
    all_to_all x4, waiting for transfers between devices, exchange(): lax.all_to_all(value, AXES, split_axis=0, concat_axis=0, tiled=True, axis...  11.8 us
    all_to_all x1, starting transfers between devices, shards(): got = lax.all_to_all(sent, 'table', split_axis=0, concat_axis=0, tiled=True)  10.3 us
    ppermute x2, waiting for transfers between devices, cross(): came = lax.ppermute(split[:, 1], AXES, there)  9.77 us
    pallas_call x1, Pallas kernels, refilled(): pl.pallas_call(refill_kernel, out_shape=(jax.ShapeDtypeStruct(cache_rows....  9.72 us
    ppermute x7, waiting for transfers between devices, cross_z(): came.append(lax.ppermute(split[:, step], AXES, there))  8.57 us
  transfers between devices with their start and end apart: 16, of which 9 were waited for; matrix products, arithmetic and copies ran while one was open for 6% of the time, Pallas kernels for 17%

profile of v5, /device:TPU:3, one launch (start us, length us, event | category | flops | bytes accessed | tf_op | source)
XLA Modules:
  0.0 142.9 jit_solution(3431558249280150267)
XLA Ops:
  0.6 3.1 %payload.1 = f32[256,256]{1,0:T(8,128)} custom-call(s32[64]{0:T(128)} %evict_ref.1, s32[2,64]{1,0:T(2,128)} %bitcast.108, s32[2,64]{1,0:T(2,128)} %bitcast.106, f32[1024]{0:T(1024)} %accum_ref.1, f32[1024,256]{1,0:T(8,128)} %cache_ref.5), custom_call_target="tpu_custom_call" | custom-call | flops 100000 | bytes 1500000 | tf_op jit(solution)/shard_map/payload/pallas_call | solution.py:313
  3.7 10.3 %all-to-all-start = ((f32[32,8,256]{2,1,0:T(8,128)}), f32[32,8,256]{2,1,0:T(8,128)S(1)}, u32[]{:S(2)}, u32[]{:S(2)}) async-start(f32[32,8,256]{2,1,0:T(8,128)} %bitcast.92), calls=%async_computation | async-start | bytes 524288 | tf_op jit(solution)/shard_map/all_to_all | solution.py:567
  14.1 12.9 %dense.1 = (f32[8,264,256]{2,1,0:T(8,128)}, f32[8,264,256]{2,1,0:T(8,128)}, bf16[256,256]{1,0:T(8,128)(2,1)}, bf16[256,256]{1,0:T(8,128)(2,1)}, f32[1,256]{1,0:T(1,128)}) custom-call(s32[1]{0:T(128)} %bitcast.core_ref, s32[32,256]{1,0:T(8,128)} %bitcast.109, s32[1,256]{1,0:T(1,128)} %bitcast.115, f32[1024,256]{1,0:T(8,128)} %cache_ref.5, ...), custom_call_target="tpu_custom_call" | custom-call | flops 5000000000 | bytes 9000000 | tf_op jit(solution)/shard_map/dense/pallas_call | solution.py:219
  26.9 0.5 collective-permute-start
  27.5 4.1 %collective-permute-done.came_any = f32[8,264,256]{2,1,0:T(8,128)S(1)} collective-permute-done((f32[8,264,256]{2,1,0:T(8,128)}, f32[8,264,256]{2,1,0:T(8,128)S(1)}, u32[]{:S(2)}, u32[]{:S(2)}) %collective-permute-start) | collective-permute-done | bytes 2162720 | tf_op jit(solution)/shard_map/ppermute | solution.py:40
  31.6 1.6 %copy-done = f32[8,264,256]{2,1,0:T(8,128)S(1)} copy-done((f32[8,264,256]{2,1,0:T(8,128)S(1)}, f32[8,264,256]{2,1,0:T(8,128)}, u32[]{:S(2)}) %copy-start) | copy-done | bytes 2162712
  33.2 2.0 %add_halves.1 = f32[8,264,256]{2,1,0:T(8,128)} custom-call(f32[8,264,256]{2,1,0:T(8,128)S(1)} %copy-done, f32[8,264,256]{2,1,0:T(8,128)S(1)} %collective-permute-done.came_any), custom_call_target="tpu_custom_call" | custom-call | tf_op jit(solution)/shard_map/add_halves/pallas_call | solution.py:345
  35.2 6.7 %all-to-all-start.1 = ((f32[8,264,256]{2,1,0:T(8,128)}), f32[8,264,256]{2,1,0:T(8,128)S(1)}, u32[]{:S(2)}, u32[]{:S(2)}) async-start(f32[8,264,256]{2,1,0:T(8,128)} %add_halves.1), calls=%async_computation.1 | async-start | bytes 4325376 | tf_op jit(solution)/shard_map/all_to_all | solution.py:44
  42.2 0.1 eq.102
  42.3 0.1 reshape.152
  42.4 0.1 broadcast_in_dim.158
  42.6 0.1 select_reduce_fusion.3
  42.8 0.2 fusion
  43.0 0.2 select_reduce_fusion.1
  43.2 0.2 select_reduce_fusion
  43.6 0.7 reshape.174
  44.3 2.0 %scatter_fusion = f32[1024,256]{1,0:T(8,128)S(1)} fusion(f32[1024,256]{1,0:T(8,128)S(1)} %copy-done.2, s32[192]{0:T(256)S(1)} %bitcast.105, f32[192,256]{1,0:T(8,128)} %reshape.174), kind=kCustom, calls=%fused_computation.1 | custom fusion | bytes 590592 | tf_op jit(solution)/shard_map/scatter | solution.py:584
  46.3 1.0 gather_fusion
  47.5 1.3 collective-permute-done.1
  48.9 1.3 collective-permute-start.2
  50.2 8.4 %collective-permute-done.2 = f32[1,16,8,256]{3,2,1,0:T(8,128)S(1)} collective-permute-done((f32[1,16,8,256]{3,2,1,0:T(8,128)S(1)}, f32[1,16,8,256]{3,2,1,0:T(8,128)S(1)}, u32[]{:S(2)}, u32[]{:S(2)}) %collective-permute-start.2) | collective-permute-done | bytes 131104 | tf_op jit(solution)/shard_map/ppermute | solution.py:69
  58.7 0.2 reduce_sum.77
  59.1 0.8 pad_maximum_fusion
  59.8 9.0 %all-to-all-start.2 = ((f32[16,24,256]{2,1,0:T(8,128)}), f32[16,24,256]{2,1,0:T(8,128)S(1)}, u32[]{:S(2)}, u32[]{:S(2)}) async-start(f32[16,24,256]{2,1,0:T(8,128)} %pad_maximum_fusion), calls=%async_computation.2 | async-start | bytes 786432 | tf_op jit(solution)/shard_map/all_to_all | solution.py:44
  68.9 3.6 %collective-permute-start.9 = (f32[2,2,8,256]{3,2,1,0:T(8,128)S(1)}, f32[2,2,8,256]{3,2,1,0:T(8,128)S(1)}, u32[]{:S(2)}, u32[]{:S(2)}) collective-permute-start(f32[2,2,8,256]{3,2,1,0:T(8,128)S(1)} %get-tuple-element.53), channel_id=1, source_target_pairs={{0,14},{1,15},{2,12},{3,13},{4,10},{5,11},{6,8},{7,9},{8,6},{9,7},... | collective-permute-start | bytes 98312 | tf_op jit(solution)/shard_map/ppermute | solution.py:78
  72.5 1.9 %collective-permute-start.7 = (f32[2,2,8,256]{3,2,1,0:T(8,128)S(1)}, f32[2,2,8,256]{3,2,1,0:T(8,128)S(1)}, u32[]{:S(2)}, u32[]{:S(2)}) collective-permute-start(f32[2,2,8,256]{3,2,1,0:T(8,128)S(1)} %get-tuple-element.54), channel_id=1, source_target_pairs={{0,10},{1,11},{2,8},{3,9},{4,14},{5,15},{6,12},{7,13},{8,2},{9,3},... | collective-permute-start | bytes 98312 | tf_op jit(solution)/shard_map/ppermute | solution.py:78
  74.3 3.2 %collective-permute-start.6 = (f32[2,2,8,256]{3,2,1,0:T(8,128)S(1)}, f32[2,2,8,256]{3,2,1,0:T(8,128)S(1)}, u32[]{:S(2)}, u32[]{:S(2)}) collective-permute-start(f32[2,2,8,256]{3,2,1,0:T(8,128)S(1)} %get-tuple-element.55), channel_id=1, source_target_pairs={{0,8},{1,9},{2,10},{3,11},{4,12},{5,13},{6,14},{7,15},{8,0},{9,1},... | collective-permute-start | bytes 98312 | tf_op jit(solution)/shard_map/ppermute | solution.py:78
  77.6 3.2 %collective-permute-start.5 = (f32[2,2,8,256]{3,2,1,0:T(8,128)S(1)}, f32[2,2,8,256]{3,2,1,0:T(8,128)S(1)}, u32[]{:S(2)}, u32[]{:S(2)}) collective-permute-start(f32[2,2,8,256]{3,2,1,0:T(8,128)S(1)} %get-tuple-element.56), channel_id=1, source_target_pairs={{0,6},{1,7},{2,4},{3,5},{4,2},{5,3},{6,0},{7,1},{8,14},{9,15},{10,... | collective-permute-start | bytes 98312 | tf_op jit(solution)/shard_map/ppermute | solution.py:78
  80.8 5.3 %collective-permute-done.4 = f32[2,2,8,256]{3,2,1,0:T(8,128)S(1)} collective-permute-done((f32[2,2,8,256]{3,2,1,0:T(8,128)S(1)}, f32[2,2,8,256]{3,2,1,0:T(8,128)S(1)}, u32[]{:S(2)}, u32[]{:S(2)}) %collective-permute-start.4) | collective-permute-done | bytes 32800 | tf_op jit(solution)/shard_map/ppermute | solution.py:78
  86.1 1.5 %collective-permute-start.8 = (f32[2,2,8,256]{3,2,1,0:T(8,128)S(1)}, f32[2,2,8,256]{3,2,1,0:T(8,128)S(1)}, u32[]{:S(2)}, u32[]{:S(2)}) collective-permute-start(f32[2,2,8,256]{3,2,1,0:T(8,128)S(1)} %get-tuple-element.59), channel_id=1, source_target_pairs={{0,12},{1,13},{2,14},{3,15},{4,8},{5,9},{6,10},{7,11},{8,4},{9,5},... | collective-permute-start | bytes 98312 | tf_op jit(solution)/shard_map/ppermute | solution.py:78
  87.7 3.3 %collective-permute-done.8 = f32[2,2,8,256]{3,2,1,0:T(8,128)S(1)} collective-permute-done((f32[2,2,8,256]{3,2,1,0:T(8,128)S(1)}, f32[2,2,8,256]{3,2,1,0:T(8,128)S(1)}, u32[]{:S(2)}, u32[]{:S(2)}) %collective-permute-start.8) | collective-permute-done | bytes 32800 | tf_op jit(solution)/shard_map/ppermute | solution.py:78
  91.1 0.7 broadcast_in_dim.167
  91.8 7.1 %all-to-all-start.3 = ((f32[16,16,256]{2,1,0:T(8,128)}), f32[16,16,256]{2,1,0:T(8,128)S(1)}, u32[]{:S(2)}, u32[]{:S(2)}) async-start(f32[16,16,256]{2,1,0:T(8,128)} %broadcast_in_dim.167), calls=%async_computation.3 | async-start | bytes 524288 | tf_op jit(solution)/shard_map/all_to_all | solution.py:44
  98.9 8.6 %all-to-all-done.3 = f32[16,16,256]{2,1,0:T(8,128)S(1)} async-done(((f32[16,16,256]{2,1,0:T(8,128)}), f32[16,16,256]{2,1,0:T(8,128)S(1)}, u32[]{:S(2)}, u32[]{:S(2)}) %all-to-all-start.3) | async-done | bytes 262176 | tf_op jit(solution)/shard_map/all_to_all | solution.py:44
  107.5 1.5 %broadcast_in_dim.168 = f32[8,264,256]{2,1,0:T(8,128)} broadcast(f32[264,256]{1,0:T(8,128)S(1)} %pad_maximum_fusion.1), dimensions={1,2} | broadcast | bytes 2433024 | tf_op jit(solution)/shard_map/broadcast_in_dim | solution.py:621
  109.0 6.5 %all-to-all-start.4 = ((f32[8,264,256]{2,1,0:T(8,128)}), f32[8,264,256]{2,1,0:T(8,128)S(1)}, u32[]{:S(2)}, u32[]{:S(2)}) async-start(f32[8,264,256]{2,1,0:T(8,128)} %broadcast_in_dim.168), calls=%async_computation.4 | async-start | bytes 4325376 | tf_op jit(solution)/shard_map/all_to_all | solution.py:44
  115.5 0.2 convert_reduce_fusion
  115.7 0.1 fusion.1
  115.8 0.5 multiply_add_fusion.place_ref
  116.5 9.7 %refill.1 = (f32[1024,256]{1,0:T(8,128)}, f32[1,1024]{1,0:T(1,128)}) custom-call(s32[32,256]{1,0:T(8,128)} %bitcast.110, s32[64]{0:T(128)} %evict_ref.1, s32[64]{0:T(128)} %multiply_add_fusion.place_ref, f32[1024,256]{1,0:T(8,128)} %cache_ref.5, f32[1,1024]{1,0:T(1,128)} %bitcast.104, bf16[256,256]{1,0:T(8,128)(2,1)} %get-tuple-element.41.latent_ref, ...), custom_call_target="tpu_custom_call" | custom-call | flops 1100000000 | bytes 4000000 | tf_op jit(solution)/shard_map/refill/pallas_call | solution.py:413
  126.2 0.2 select_reduce_fusion.4
  126.4 0.1 select_reduce_fusion.2
  126.5 1.3 select_n.76
  127.8 3.1 %all-to-all-done.4.half_any = f32[8,264,256]{2,1,0:T(8,128)S(1)} async-done(((f32[8,264,256]{2,1,0:T(8,128)}), f32[8,264,256]{2,1,0:T(8,128)S(1)}, u32[]{:S(2)}, u32[]{:S(2)}) %all-to-all-start.4) | async-done | bytes 2162720 | tf_op jit(solution)/shard_map/all_to_all | solution.py:44
  130.9 4.3 %collective-permute-start.10 = (f32[8,264,256]{2,1,0:T(8,128)S(1)}, f32[8,264,256]{2,1,0:T(8,128)S(1)}, u32[]{:S(2)}, u32[]{:S(2)}) collective-permute-start(f32[8,264,256]{2,1,0:T(8,128)S(1)} %all-to-all-done.4.half_any), channel_id=1, source_target_pairs={{0,1},{1,0},{2,3},{3,2},{4,5},{5,4},{6,7},{7,6},{8,9},{9,8},{10,11... | collective-permute-start | bytes 6488072 | tf_op jit(solution)/shard_map/ppermute | solution.py:40
  135.2 2.0 %scale_own.1.proj_in = f32[2,2048,256]{2,1,0:T(8,128)} custom-call(s32[1]{0:T(128)} %bitcast.core_ref, f32[8,264,256]{2,1,0:T(8,128)S(1)} %all-to-all-done.4.half_any), custom_call_target="tpu_custom_call" | custom-call | tf_op jit(solution)/shard_map/scale_own/pallas_call | solution.py:513
  137.2 1.9 %collective-permute-done.10.half_any = f32[8,264,256]{2,1,0:T(8,128)S(1)} collective-permute-done((f32[8,264,256]{2,1,0:T(8,128)S(1)}, f32[8,264,256]{2,1,0:T(8,128)S(1)}, u32[]{:S(2)}, u32[]{:S(2)}) %collective-permute-start.10) | collective-permute-done | bytes 2162720 | tf_op jit(solution)/shard_map/ppermute | solution.py:40
  139.1 2.6 %scale_other.1 = (f32[2,2048,256]{2,1,0:T(8,128)}, f32[2,2048]{1,0:T(2,128)}, f32[1,128]{1,0:T(1,128)S(1)}) custom-call(s32[1]{0:T(128)} %bitcast.core_ref, f32[2,2048,256]{2,1,0:T(8,128)} %scale_own.1.proj_in, f32[8,8,256]{2,1,0:T(8,128)S(1)} %slice.99.own_ref, f32[8,264,256]{2,1,0:T(8,128)S(1)} %collective-permute-done.10.half_any), custom_call_target="tpu_custom_call", output_to_operand_aliasing={{0}: (1, {})} | custom-call | tf_op jit(solution)/shard_map/scale_other/pallas_call | solution.py:522
  (72 shorter events, 1.4 us)
Async XLA Ops:
  3.7 23.2 %all-to-all-start = ((f32[32,8,256]{2,1,0:T(8,128)}), f32[32,8,256]{2,1,0:T(8,128)S(1)}, u32[]{:S(2)}, u32[]{:S(2)}) async-start(f32[32,8,256]{2,1,0:T(8,128)} %bitcast.92), calls=%async_computation | async-start | bytes 524288 | tf_op jit(solution)/shard_map/all_to_all | solution.py:567
  26.9 4.6 %collective-permute-start = (f32[8,264,256]{2,1,0:T(8,128)}, f32[8,264,256]{2,1,0:T(8,128)S(1)}, u32[]{:S(2)}, u32[]{:S(2)}) collective-permute-start(f32[8,264,256]{2,1,0:T(8,128)} %get-tuple-element.34), channel_id=1, source_target_pairs={{0,1},{1,0},{2,3},{3,2},{4,5},{5,4},{6,7},{7,6},{8,9},{9,8},{10,11... | collective-permute-start | bytes 6488072 | tf_op jit(solution)/shard_map/ppermute | solution.py:40
  31.6 1.6 %copy-start = (f32[8,264,256]{2,1,0:T(8,128)S(1)}, f32[8,264,256]{2,1,0:T(8,128)}, u32[]{:S(2)}) copy-start(f32[8,264,256]{2,1,0:T(8,128)} %get-tuple-element.31.keep_any) | copy-start | bytes 6488068
  35.2 7.9 %copy-start.6 = (f32[1024]{0:T(1024)S(1)}, f32[1024]{0:T(1024)}, u32[]{:S(2)}) copy-start(f32[1024]{0:T(1024)} %param.18) | copy-start | bytes 12292
  35.2 9.1 %copy-start.2 = (f32[1024,256]{1,0:T(8,128)S(1)}, f32[1024,256]{1,0:T(8,128)}, u32[]{:S(2)}) copy-start(f32[1024,256]{1,0:T(8,128)} %param.17) | copy-start | bytes 3145732
  35.2 23.5 %all-to-all-start.1 = ((f32[8,264,256]{2,1,0:T(8,128)}), f32[8,264,256]{2,1,0:T(8,128)S(1)}, u32[]{:S(2)}, u32[]{:S(2)}) async-start(f32[8,264,256]{2,1,0:T(8,128)} %add_halves.1), calls=%async_computation.1 | async-start | bytes 4325376 | tf_op jit(solution)/shard_map/all_to_all | solution.py:44
  43.1 4.1 %copy-start.4 = (f32[1024]{0:T(1024)}, f32[1024]{0:T(1024)S(1)}, u32[]{:S(2)}) copy-start(f32[1024]{0:T(1024)S(1)} %select_n.69) | copy-start | bytes 12292
  46.3 2.6 %copy-start.1 = (f32[1024,256]{1,0:T(8,128)}, f32[1024,256]{1,0:T(8,128)S(1)}, u32[]{:S(2)}) copy-start(f32[1024,256]{1,0:T(8,128)S(1)} %scatter_fusion) | copy-start | bytes 3145732
  47.4 1.4 %collective-permute-start.1 = (f32[16,1,8,256]{3,2,0,1:T(8,128)S(1)}, f32[16,1,8,256]{3,2,0,1:T(8,128)S(1)}, u32[]{:S(2)}, u32[]{:S(2)}) collective-permute-start(f32[16,1,8,256]{3,2,0,1:T(8,128)S(1)} %get-tuple-element.63), channel_id=1, source_target_pairs={{0,1},{1,0},{2,3},{3,2},{4,5},{5,4},{6,7},{7,6},{8,9},{9,8},{10,11... | collective-permute-start | bytes 393224 | tf_op jit(solution)/shard_map/ppermute | solution.py:69
  48.9 9.7 %collective-permute-start.2 = (f32[1,16,8,256]{3,2,1,0:T(8,128)S(1)}, f32[1,16,8,256]{3,2,1,0:T(8,128)S(1)}, u32[]{:S(2)}, u32[]{:S(2)}) collective-permute-start(f32[1,16,8,256]{3,2,1,0:T(8,128)S(1)} %get-tuple-element.61), channel_id=1, source_target_pairs={{0,16},{1,17},{2,18},{3,19},{4,20},{5,21},{6,22},{7,23},{8,24},{9,... | collective-permute-start | bytes 393224 | tf_op jit(solution)/shard_map/ppermute | solution.py:69
  58.9 21.9 %collective-permute-start.3 = (f32[2,2,8,256]{3,2,1,0:T(8,128)S(1)}, f32[2,2,8,256]{3,2,1,0:T(8,128)S(1)}, u32[]{:S(2)}, u32[]{:S(2)}) collective-permute-start(f32[2,2,8,256]{3,2,1,0:T(8,128)S(1)} %get-tuple-element.58), channel_id=1, source_target_pairs={{0,2},{1,3},{2,0},{3,1},{4,6},{5,7},{6,4},{7,5},{8,10},{9,11},{10,... | collective-permute-start | bytes 98312 | tf_op jit(solution)/shard_map/ppermute | solution.py:78
  59.8 31.2 %all-to-all-start.2 = ((f32[16,24,256]{2,1,0:T(8,128)}), f32[16,24,256]{2,1,0:T(8,128)S(1)}, u32[]{:S(2)}, u32[]{:S(2)}) async-start(f32[16,24,256]{2,1,0:T(8,128)} %pad_maximum_fusion), calls=%async_computation.2 | async-start | bytes 786432 | tf_op jit(solution)/shard_map/all_to_all | solution.py:44
  68.9 22.1 %collective-permute-start.9 = (f32[2,2,8,256]{3,2,1,0:T(8,128)S(1)}, f32[2,2,8,256]{3,2,1,0:T(8,128)S(1)}, u32[]{:S(2)}, u32[]{:S(2)}) collective-permute-start(f32[2,2,8,256]{3,2,1,0:T(8,128)S(1)} %get-tuple-element.53), channel_id=1, source_target_pairs={{0,14},{1,15},{2,12},{3,13},{4,10},{5,11},{6,8},{7,9},{8,6},{9,7},... | collective-permute-start | bytes 98312 | tf_op jit(solution)/shard_map/ppermute | solution.py:78
  72.5 15.2 %collective-permute-start.7 = (f32[2,2,8,256]{3,2,1,0:T(8,128)S(1)}, f32[2,2,8,256]{3,2,1,0:T(8,128)S(1)}, u32[]{:S(2)}, u32[]{:S(2)}) collective-permute-start(f32[2,2,8,256]{3,2,1,0:T(8,128)S(1)} %get-tuple-element.54), channel_id=1, source_target_pairs={{0,10},{1,11},{2,8},{3,9},{4,14},{5,15},{6,12},{7,13},{8,2},{9,3},... | collective-permute-start | bytes 98312 | tf_op jit(solution)/shard_map/ppermute | solution.py:78
  74.3 13.3 %collective-permute-start.6 = (f32[2,2,8,256]{3,2,1,0:T(8,128)S(1)}, f32[2,2,8,256]{3,2,1,0:T(8,128)S(1)}, u32[]{:S(2)}, u32[]{:S(2)}) collective-permute-start(f32[2,2,8,256]{3,2,1,0:T(8,128)S(1)} %get-tuple-element.55), channel_id=1, source_target_pairs={{0,8},{1,9},{2,10},{3,11},{4,12},{5,13},{6,14},{7,15},{8,0},{9,1},... | collective-permute-start | bytes 98312 | tf_op jit(solution)/shard_map/ppermute | solution.py:78
  77.6 10.1 %collective-permute-start.5 = (f32[2,2,8,256]{3,2,1,0:T(8,128)S(1)}, f32[2,2,8,256]{3,2,1,0:T(8,128)S(1)}, u32[]{:S(2)}, u32[]{:S(2)}) collective-permute-start(f32[2,2,8,256]{3,2,1,0:T(8,128)S(1)} %get-tuple-element.56), channel_id=1, source_target_pairs={{0,6},{1,7},{2,4},{3,5},{4,2},{5,3},{6,0},{7,1},{8,14},{9,15},{10,... | collective-permute-start | bytes 98312 | tf_op jit(solution)/shard_map/ppermute | solution.py:78
  80.8 5.3 %collective-permute-start.4 = (f32[2,2,8,256]{3,2,1,0:T(8,128)S(1)}, f32[2,2,8,256]{3,2,1,0:T(8,128)S(1)}, u32[]{:S(2)}, u32[]{:S(2)}) collective-permute-start(f32[2,2,8,256]{3,2,1,0:T(8,128)S(1)} %get-tuple-element.57), channel_id=1, source_target_pairs={{0,4},{1,5},{2,6},{3,7},{4,0},{5,1},{6,2},{7,3},{8,12},{9,13},{10,... | collective-permute-start | bytes 98312 | tf_op jit(solution)/shard_map/ppermute | solution.py:78
  86.1 4.9 %collective-permute-start.8 = (f32[2,2,8,256]{3,2,1,0:T(8,128)S(1)}, f32[2,2,8,256]{3,2,1,0:T(8,128)S(1)}, u32[]{:S(2)}, u32[]{:S(2)}) collective-permute-start(f32[2,2,8,256]{3,2,1,0:T(8,128)S(1)} %get-tuple-element.59), channel_id=1, source_target_pairs={{0,12},{1,13},{2,14},{3,15},{4,8},{5,9},{6,10},{7,11},{8,4},{9,5},... | collective-permute-start | bytes 98312 | tf_op jit(solution)/shard_map/ppermute | solution.py:78
  91.0 25.3 %copy-start.3 = (f32[2,8,2,8,256]{4,3,2,1,0:T(8,128)}, f32[2,8,2,8,256]{4,3,2,1,0:T(8,128)S(1)}, u32[]{:S(2)}) copy-start(f32[2,8,2,8,256]{4,3,2,1,0:T(8,128)S(1)} %copy.62) | copy-start | bytes 786436
  91.8 15.7 %all-to-all-start.3 = ((f32[16,16,256]{2,1,0:T(8,128)}), f32[16,16,256]{2,1,0:T(8,128)S(1)}, u32[]{:S(2)}, u32[]{:S(2)}) async-start(f32[16,16,256]{2,1,0:T(8,128)} %broadcast_in_dim.167), calls=%async_computation.3 | async-start | bytes 524288 | tf_op jit(solution)/shard_map/all_to_all | solution.py:44
  109.0 6.5 %copy-start.5 = (s32[64,2]{0,1:T(2,128)S(1)}, s32[64,2]{0,1:T(2,128)}, u32[]{:S(2)}) copy-start(s32[64,2]{0,1:T(2,128)} %param.19) | copy-start | bytes 1540
  109.0 6.7 %copy-start.7 = (s32[64]{0:T(128)S(1)}, s32[64]{0:T(128)}, u32[]{:S(2)}) copy-start(s32[64]{0:T(128)} %evict_ref.1) | copy-start | bytes 772
  109.0 21.9 %all-to-all-start.4 = ((f32[8,264,256]{2,1,0:T(8,128)}), f32[8,264,256]{2,1,0:T(8,128)S(1)}, u32[]{:S(2)}, u32[]{:S(2)}) async-start(f32[8,264,256]{2,1,0:T(8,128)} %broadcast_in_dim.168), calls=%async_computation.4 | async-start | bytes 4325376 | tf_op jit(solution)/shard_map/all_to_all | solution.py:44
  115.5 10.9 %copy-start.8 = (s32[64]{0:T(128)S(1)}, s32[64]{0:T(128)}, u32[]{:S(2)}) copy-start(s32[64]{0:T(128)} %evict_ref.1) | copy-start | bytes 772
  130.9 8.1 %collective-permute-start.10 = (f32[8,264,256]{2,1,0:T(8,128)S(1)}, f32[8,264,256]{2,1,0:T(8,128)S(1)}, u32[]{:S(2)}, u32[]{:S(2)}) collective-permute-start(f32[8,264,256]{2,1,0:T(8,128)S(1)} %all-to-all-done.4.half_any), channel_id=1, source_target_pairs={{0,1},{1,0},{2,3},{3,2},{4,5},{5,4},{6,7},{7,6},{8,9},{9,8},{10,11... | collective-permute-start | bytes 6488072 | tf_op jit(solution)/shard_map/ppermute | solution.py:40

commit v6 on v4

--- a/solution.py
+++ b/solution.py
@@ -74,19 +74,22 @@
     core_ref,
     slots_ref,
     labels_ref,
-    cache_ref,
+    cache_any,
     u_any,
     v_any,
     bias_ref,
     head_ref,
-    keep_out,
     send_out,
-    dpooled_out,
+    left_out,
+    latent_ref,
+    dlatent_ref,
+    dlogit_ref,
+    extra_ref,
+    cache,
     u_ref,
     v_ref,
-    keep_ref,
     send_ref,
-    dpooled_ref,
+    left,
     high,
     mid,
     low,
@@ -97,41 +100,55 @@
     out_sems,
 ):
     f32, bf16 = jnp.float32, jnp.bfloat16
-    load_v = pltpu.make_async_copy(v_any, v_ref, in_sems.at[0])
-    load_u = pltpu.make_async_copy(u_any, u_ref, in_sems.at[1])
-    load_v.start()
-    load_u.start()
-    count, cells, width = slots_ref.shape[1], cache_ref.shape[0], cache_ref.shape[1]
+    count, (cells, width) = slots_ref.shape[1], cache.shape
     feats = u_ref.shape[0] // width
     looks = slots_ref.shape[0] // feats
+    cuts = [slice(c * width, (c + 1) * width) for c in range(feats)]
+    loads = []
+    for source, target in ((cache_any, cache), (v_any, v_ref), (u_any, u_ref)):
+        step = target.shape[0] // 4
+        for part in range(4):
+            rows = pl.ds(part * step, step)
+            loads.append(
+                pltpu.make_async_copy(source.at[rows], target.at[rows], in_sems.at[len(loads)])
+            )
+            loads[-1].start()
     slots = jnp.transpose(slots_ref[...])
-    rows = cache_ref[...]
-    first = rows.astype(bf16)
-    rest = rows - first.astype(f32)
-    second = rest.astype(bf16)
-    high[...] = first
-    mid[...] = second
-    low[...] = (rest - second.astype(f32)).astype(bf16)
-
     lane = lax.broadcasted_iota(jnp.int32, (count, cells), 1)
-    for f in range(feats):
+
+    def counted(f):
         counts = jnp.zeros((count, cells), f32)
         for look in range(looks):
             at = f * looks + look
             counts = counts + jnp.where(lane == slots[:, at : at + 1], 1.0, 0.0)
-        counts = counts.astype(bf16)
+        return counts.astype(bf16)
+
+    counts = counted(0)
+    step = cells // 4
+    for part in range(4):
+        loads[part].wait()
+        rows = cache[part * step : (part + 1) * step, :]
+        first = rows.astype(bf16)
+        rest = rows - first.astype(f32)
+        second = rest.astype(bf16)
+        high[part * step : (part + 1) * step, :] = first
+        mid[part * step : (part + 1) * step, :] = second
+        low[part * step : (part + 1) * step, :] = (rest - second.astype(f32)).astype(bf16)
+    for f in range(feats):
+        if f > 0:
+            counts = counted(f)
         total = jnp.dot(counts, low[...], preferred_element_type=f32)
         total = total + jnp.dot(counts, mid[...], preferred_element_type=f32)
         total = total + jnp.dot(counts, high[...], preferred_element_type=f32)
-        pooled[:, f * width : (f + 1) * width] = total.astype(bf16)
-
-    load_v.wait()
-    load_u.wait()
+        pooled[:, cuts[f]] = total.astype(bf16)
+
+    for load in loads[4:]:
+        load.wait()
     latent = jnp.dot(pooled[...], v_ref[...], preferred_element_type=f32).astype(bf16)
+    latent_ref[...] = latent
     across = (((1,), (1,)), ((), ()))
     logit_wide = jnp.zeros((count, width), f32)
-    for c in range(feats):
-        cut = slice(c * width, (c + 1) * width)
+    for cut in cuts:
         moved = lax.dot_general(latent, u_ref[cut, :], across, preferred_element_type=f32)
         moved = moved + bias_ref[:, cut]
         shifted[:, cut] = moved
@@ -143,13 +160,13 @@
     losses = jnp.maximum(logit, 0.0) + jnp.log1p(small) - target * logit
     loss = jnp.sum(losses, axis=0, keepdims=True)
     dlogit = jnp.where(logit >= 0, 1.0, small) / (1.0 + small) - target
+    dlogit_ref[...] = jnp.transpose(dlogit)
 
     mine = core_ref[0] == 0
     lane1 = lax.broadcasted_iota(jnp.int32, (1, width), 1)
     loss_row = jnp.where(lane1 == 0, loss, 0.0)
     back = jnp.zeros((count, width), f32)
-    for c in range(feats):
-        cut = slice(c * width, (c + 1) * width)
+    for c, cut in enumerate(cuts):
         part = pooled[:, cut].astype(f32)
         lift = dlogit * head_ref[:, cut] * part
         crossed = part * shifted[:, cut] + part
@@ -158,46 +175,27 @@
         lift = lift.astype(bf16)
         dlift[:, cut] = lift
         back = back + jnp.dot(lift, u_ref[cut, :], preferred_element_type=f32)
-        keep_ref[c, width : width + 1, :] = jnp.where(mine, dbias, dhead)
+        extra_ref[c, 0:1, :] = jnp.where(mine, dbias, dhead)
+        extra_ref[c, 1:2, :] = loss_row
+        extra_ref[c, 2:8, :] = jnp.zeros((6, width), f32)
         send_ref[c, width : width + 1, :] = jnp.where(mine, dhead, dbias)
-        for ref in (keep_ref, send_ref):
-            ref[c, width + 1 : width + 2, :] = loss_row
-            ref[c, width + 2 : width + 8, :] = jnp.zeros((6, width), f32)
+        send_ref[c, width + 1 : width + 2, :] = loss_row
+        send_ref[c, width + 2 : width + 8, :] = jnp.zeros((6, width), f32)
+        left[:, cut] = jnp.where(mine, lift, pooled[:, cut])
     dlatent = back.astype(bf16)
-
-    down = (((0,), (0,)), ((), ()))
-    right_keep = jnp.where(mine, latent, dlatent)
-    right_send = jnp.where(mine, dlatent, latent)
-    copies = []
-
-    def give(source, target):
-        copies.append(pltpu.make_async_copy(source, target, out_sems.at[len(copies)]))
-        copies[-1].start()
-
-    for c in range(feats):
-        cut = slice(c * width, (c + 1) * width)
+    dlatent_ref[...] = dlatent
+    copies = [pltpu.make_async_copy(left, left_out, out_sems.at[feats])]
+    copies[0].start()
+    right = jnp.where(mine, dlatent, latent)
+    for c, cut in enumerate(cuts):
         send_ref[c, :width, :] = lax.dot_general(
             jnp.where(mine, pooled[:, cut], dlift[:, cut]),
-            right_send,
-            down,
+            right,
+            (((0,), (0,)), ((), ())),
             preferred_element_type=f32,
         )
-        give(send_ref.at[c], send_out.at[c])
-    for c in range(feats):
-        cut = slice(c * width, (c + 1) * width)
-        keep_ref[c, :width, :] = lax.dot_general(
-            jnp.where(mine, dlift[:, cut], pooled[:, cut]),
-            right_keep,
-            down,
-            preferred_element_type=f32,
-        )
-        give(keep_ref.at[c], keep_out.at[c])
-    for c in range(feats):
-        cut = slice(c * width, (c + 1) * width)
-        through = lax.dot_general(dlatent, v_ref[cut, :], across, preferred_element_type=f32)
-        through = through + dlogit * head_ref[:, cut] * (shifted[:, cut] + 1.0)
-        dpooled_ref[c] = through.astype(bf16)
-        give(dpooled_ref.at[c], dpooled_out.at[c])
+        copies.append(pltpu.make_async_copy(send_ref.at[c], send_out.at[c], out_sems.at[c]))
+        copies[-1].start()
     for copy in copies:
         copy.wait()
 
@@ -206,38 +204,44 @@
     count, (cells, width) = slot_ids.shape[0], cache_rows.shape
     wide = proj_u.shape[0]
     blocks = wide // width
+    f32, bf16 = jnp.float32, jnp.bfloat16
+    vmem = pl.BlockSpec(memory_space=pltpu.VMEM)
     anywhere = pl.BlockSpec(memory_space=pl.ANY)
-    vmem = pl.BlockSpec(memory_space=pltpu.VMEM)
-    bundle = jax.ShapeDtypeStruct((blocks, width + 8, width), jnp.float32)
+    bundle = (blocks, width + 8, width)
     return pl.pallas_call(
         dense_kernel,
         out_shape=(
-            bundle,
-            bundle,
-            jax.ShapeDtypeStruct((blocks, count, width), jnp.bfloat16),
+            jax.ShapeDtypeStruct(bundle, f32),
+            jax.ShapeDtypeStruct((count, wide), bf16),
+            jax.ShapeDtypeStruct((count, width), bf16),
+            jax.ShapeDtypeStruct((count, width), bf16),
+            jax.ShapeDtypeStruct((1, count), f32),
+            jax.ShapeDtypeStruct((blocks, 8, width), f32),
         ),
         in_specs=[pl.BlockSpec(memory_space=pltpu.SMEM)]
-        + [vmem] * 3
-        + [anywhere] * 2
+        + [vmem] * 2
+        + [anywhere] * 3
         + [vmem] * 2,
-        out_specs=(anywhere, anywhere, anywhere),
+        out_specs=[anywhere] * 2 + [vmem] * 4,
         scratch_shapes=[
-            pltpu.VMEM((wide, width), jnp.bfloat16),
-            pltpu.VMEM((wide, width), jnp.bfloat16),
-            pltpu.VMEM(bundle.shape, jnp.float32),
-            pltpu.VMEM(bundle.shape, jnp.float32),
-            pltpu.VMEM((blocks, count, width), jnp.bfloat16),
+            pltpu.VMEM((cells, width), f32),
+            pltpu.VMEM((wide, width), bf16),
+            pltpu.VMEM((wide, width), bf16),
+            pltpu.VMEM(bundle, f32),
+            pltpu.VMEM((count, wide), bf16),
         ]
-        + [pltpu.VMEM((cells, width), jnp.bfloat16)] * 3
+        + [pltpu.VMEM((cells, width), bf16)] * 3
         + [
-            pltpu.VMEM((count, wide), jnp.bfloat16),
-            pltpu.VMEM((count, wide), jnp.float32),
-            pltpu.VMEM((count, wide), jnp.bfloat16),
-            pltpu.SemaphoreType.DMA((2,)),
-            pltpu.SemaphoreType.DMA((3 * blocks,)),
+            pltpu.VMEM((count, wide), bf16),
+            pltpu.VMEM((count, wide), f32),
+            pltpu.VMEM((count, wide), bf16),
+            pltpu.SemaphoreType.DMA((12,)),
+            pltpu.SemaphoreType.DMA((blocks + 1,)),
         ],
         compiler_params=pltpu.CompilerParams(vmem_limit_bytes=60 * 1024 * 1024),
-        cost_estimate=pl.CostEstimate(flops=5_000_000_000, bytes_accessed=9_000_000, transcendentals=1000),
+        cost_estimate=pl.CostEstimate(
+            flops=5_000_000_000, bytes_accessed=9_000_000, transcendentals=1000
+        ),
         name="dense",
     )(
         core[None],
@@ -251,41 +255,68 @@
     )
 
 
+def keep_kernel(core_ref, left_ref, latent_ref, dlatent_ref, extra_ref, keep_ref):
+    width = latent_ref.shape[1]
+    right = jnp.where(core_ref[0] == 0, latent_ref[...], dlatent_ref[...])
+    for c in range(keep_ref.shape[0]):
+        keep_ref[c, :width, :] = lax.dot_general(
+            left_ref[:, c * width : (c + 1) * width],
+            right,
+            (((0,), (0,)), ((), ())),
+            preferred_element_type=jnp.float32,
+        )
+        keep_ref[c, width : width + 8, :] = extra_ref[c]
+
+
+def kept(core, left, latent, dlatent, extra):
+    blocks, _, width = extra.shape
+    vmem = pl.BlockSpec(memory_space=pltpu.VMEM)
+    return pl.pallas_call(
+        keep_kernel,
+        out_shape=jax.ShapeDtypeStruct((blocks, width + 8, width), jnp.float32),
+        in_specs=[pl.BlockSpec(memory_space=pltpu.SMEM)] + [vmem] * 4,
+        out_specs=vmem,
+        compiler_params=pltpu.CompilerParams(vmem_limit_bytes=16 * 1024 * 1024),
+        cost_estimate=pl.CostEstimate(
+            flops=300_000_000, bytes_accessed=4_000_000, transcendentals=0
+        ),
+        name="kept",
+    )(core[None], left, latent, dlatent, extra)
+
+
 def payload_kernel(
-    slot_ref, evict_ref, miss_ref, accum_ref, cache_ref, out_ref, taken
+    slot_ref, evict_ref, miss_ref, accum_ref, cache_any, out_ref, taken, place, cache, sems
 ):
     owners, per = taken.shape[0], out_ref.shape[0] // taken.shape[0]
     width = out_ref.shape[1]
+    listed = slot_ref.shape[0]
+    step = cache.shape[0] // 4
+    loads = []
+    for part in range(4):
+        rows = pl.ds(part * step, step)
+        loads.append(pltpu.make_async_copy(cache_any.at[rows], cache.at[rows], sems.at[part]))
+        loads[-1].start()
     lane = lax.broadcasted_iota(jnp.int32, (1, width), 1)
     base = jnp.where((lane >= per) & (lane < 2 * per), -1.0, 0.0)
-
-    def clear(o, _):
+    for o in range(owners):
         taken[o] = 0
-        out_ref[pl.ds(o * per, per - 1), :] = jnp.zeros((per - 1, width), jnp.float32)
-        out_ref[pl.ds(o * per + per - 1, 1), :] = base
-        return 0
-
-    lax.fori_loop(0, owners, clear, 0, unroll=True)
+        out_ref[o * per : o * per + per - 1, :] = jnp.zeros((per - 1, width), jnp.float32)
+        out_ref[o * per + per - 1 : (o + 1) * per, :] = base
 
     def leave(i, _):
         owner = evict_ref[0, i]
         rank = taken[owner]
         taken[owner] = rank + 1
-        slot = slot_ref[i]
-        out_ref[pl.ds(owner * per + rank, 1), :] = cache_ref[pl.ds(slot, 1), :]
+        place[i] = owner * per + rank
         spot = pl.ds(owner * per + per - 1, 1)
-        meta = jnp.where(lane == rank, accum_ref[slot], out_ref[spot, :])
+        meta = jnp.where(lane == rank, accum_ref[slot_ref[i]], out_ref[spot, :])
         row = evict_ref[1, i].astype(jnp.float32)
         out_ref[spot, :] = jnp.where(lane == per + rank, row, meta)
         return 0
 
-    lax.fori_loop(0, slot_ref.shape[0], leave, 0, unroll=8)
-
-    def reset(o, _):
+    lax.fori_loop(0, listed, leave, 0, unroll=8)
+    for o in range(owners):
         taken[o] = 0
-        return 0
-
-    lax.fori_loop(0, owners, reset, 0, unroll=True)
 
     def ask(i, _):
         owner = miss_ref[0, i]
@@ -296,37 +327,57 @@
         out_ref[spot, :] = jnp.where(lane == 2 * per + rank, row, out_ref[spot, :])
         return 0
 
-    lax.fori_loop(0, slot_ref.shape[0], ask, 0, unroll=8)
+    lax.fori_loop(0, listed, ask, 0, unroll=8)
+    for load in loads:
+        load.wait()
+
+    def move(i, _):
+        out_ref[pl.ds(place[i], 1), :] = cache[pl.ds(slot_ref[i], 1), :]
+        return 0
+
+    lax.fori_loop(0, listed, move, 0, unroll=8)
 
 
 def payload(evict_slot, evict_dest, miss_dest, cache_accum, cache_rows, owners, per):
     smem = pl.BlockSpec(memory_space=pltpu.SMEM)
-    vmem = pl.BlockSpec(memory_space=pltpu.VMEM)
     return pl.pallas_call(
         payload_kernel,
         out_shape=jax.ShapeDtypeStruct((owners * per, cache_rows.shape[1]), jnp.float32),
-        in_specs=[smem] * 4 + [vmem],
-        out_specs=vmem,
-        scratch_shapes=[pltpu.SMEM((owners,), jnp.int32)],
+        in_specs=[smem] * 4 + [pl.BlockSpec(memory_space=pl.ANY)],
+        out_specs=pl.BlockSpec(memory_space=pltpu.VMEM),
+        scratch_shapes=[
+            pltpu.SMEM((owners,), jnp.int32),
+            pltpu.SMEM(evict_slot.shape, jnp.int32),
+            pltpu.VMEM(cache_rows.shape, jnp.float32),
+            pltpu.SemaphoreType.DMA((4,)),
+        ],
+        compiler_params=pltpu.CompilerParams(vmem_limit_bytes=60 * 1024 * 1024),
         cost_estimate=pl.CostEstimate(flops=100_000, bytes_accessed=1_500_000, transcendentals=0),
         name="payload",
     )(evict_slot, evict_dest.T, miss_dest.T, cache_accum, cache_rows)
 
 
-def refill_kernel(
+def update_kernel(
     slots_ref,
-    evict_ref,
-    place_ref,
     cache_ref,
     accum_ref,
-    dpooled_ref,
-    back_ref,
+    latent_ref,
+    dlatent_ref,
+    dlogit_ref,
+    u_ref,
+    v_ref,
+    bias_ref,
+    head_ref,
     rows_ref,
     accum_out,
 ):
     f32, bf16 = jnp.float32, jnp.bfloat16
-    (cells, width), (feats, count, _) = cache_ref.shape, dpooled_ref.shape
+    (cells, width), count = cache_ref.shape, latent_ref.shape[0]
+    feats = u_ref.shape[0] // width
     looks = slots_ref.shape[0] // feats
+    across = (((1,), (1,)), ((), ()))
+    latent, dlatent = latent_ref[...], dlatent_ref[...]
+    dlogit = jnp.transpose(dlogit_ref[...])
     cell = lax.broadcasted_iota(jnp.int32, (cells, count), 0)
     grad = jnp.zeros((cells, width), f32)
     for f in range(feats):
@@ -334,12 +385,21 @@
         for look in range(looks):
             at = f * looks + look
             counts = counts + jnp.where(cell == slots_ref[at : at + 1, :], 1.0, 0.0)
-        grad = grad + jnp.dot(counts.astype(bf16), dpooled_ref[f], preferred_element_type=f32)
+        cut = slice(f * width, (f + 1) * width)
+        moved = lax.dot_general(latent, u_ref[cut, :], across, preferred_element_type=f32)
+        moved = moved + bias_ref[:, cut]
+        through = lax.dot_general(dlatent, v_ref[cut, :], across, preferred_element_type=f32)
+        dpooled = (dlogit * head_ref[:, cut] * (moved + 1.0) + through).astype(bf16)
+        grad = grad + jnp.dot(counts.astype(bf16), dpooled, preferred_element_type=f32)
     mean = jnp.sum(grad * grad, axis=1, keepdims=True) / width
     accum = jnp.transpose(accum_ref[...]) + mean
     rows_ref[...] = cache_ref[...] - ETA * grad * lax.rsqrt(accum)
     accum_out[...] = jnp.transpose(accum)
 
+
+def refill_kernel(evict_ref, place_ref, back_ref, old_ref, rows_ref):
+    rows_ref[...] = old_ref[...]
+
     def refill(i, _):
         rows_ref[pl.ds(evict_ref[i], 1), :] = back_ref[pl.ds(place_ref[i], 1), :]
         return 0
@@ -347,30 +407,37 @@
     lax.fori_loop(0, evict_ref.shape[0], refill, 0, unroll=8)
 
 
-def refilled(slot_ids, evict_slot, place, cache_rows, cache_accum, dpooled, back):
+def updated(slot_ids, cache_rows, cache_accum, saved, params):
     cells = cache_rows.shape[0]
+    vmem = pl.BlockSpec(memory_space=pltpu.VMEM)
+    return pl.pallas_call(
+        update_kernel,
+        out_shape=(
+            jax.ShapeDtypeStruct(cache_rows.shape, jnp.float32),
+            jax.ShapeDtypeStruct((1, cells), jnp.float32),
+        ),
+        in_specs=[vmem] * 10,
+        out_specs=(vmem, vmem),
+        compiler_params=pltpu.CompilerParams(vmem_limit_bytes=60 * 1024 * 1024),
+        cost_estimate=pl.CostEstimate(
+            flops=1_100_000_000, bytes_accessed=4_000_000, transcendentals=1000
+        ),
+        name="update",
+    )(slot_ids.T, cache_rows, cache_accum[None, :], *saved, *params)
+
+
+def refilled(evict_slot, place, back, rows):
     smem = pl.BlockSpec(memory_space=pltpu.SMEM)
     vmem = pl.BlockSpec(memory_space=pltpu.VMEM)
     return pl.pallas_call(
         refill_kernel,
-        out_shape=(
-            jax.ShapeDtypeStruct(cache_rows.shape, jnp.float32),
-            jax.ShapeDtypeStruct((1, cells), jnp.float32),
-        ),
-        in_specs=[vmem, smem, smem, vmem, vmem, vmem, vmem],
-        out_specs=(vmem, vmem),
+        out_shape=jax.ShapeDtypeStruct(rows.shape, jnp.float32),
+        in_specs=[smem, smem, vmem, vmem],
+        out_specs=vmem,
         compiler_params=pltpu.CompilerParams(vmem_limit_bytes=60 * 1024 * 1024),
-        cost_estimate=pl.CostEstimate(flops=1_100_000_000, bytes_accessed=4_000_000, transcendentals=1000),
+        cost_estimate=pl.CostEstimate(flops=100_000, bytes_accessed=2_000_000, transcendentals=0),
         name="refill",
-    )(
-        slot_ids.T,
-        evict_slot,
-        place,
-        cache_rows,
-        cache_accum[None, :],
-        dpooled,
-        back,
-    )
+    )(evict_slot, place, back, rows)
 
 
 def scaled(index, half_any, proj_ref, half, stage, in_sems, out_sems):
@@ -508,14 +575,14 @@
 
     count = slot_ids.shape[0]
     feats = proj_u.shape[0] // width
-    keep, send, dpooled = dense(
+    send, left, latent, dlatent, dlogit, extra = dense(
         core, slots_late, labels, cache_rows, proj_u, proj_v, cross_bias, head
     )
 
     blocks = feats
     depth = width
     send, got = lax.optimization_barrier((send, got))
-    held = keep + swap_cores(send)
+    held = kept(core, left, latent, dlatent, extra) + swap_cores(send)
     held, got = lax.optimization_barrier((held, got))
 
     got_meta = got[:, per - 1, :]
@@ -539,7 +606,7 @@
     back = jnp.where(is_meta, meta_row([reply_accum], width), reply_rows)
 
     held = exchange(held, first_groups())
-    back = cross(cross(back, 1), 16)
+    back = cross(cross(back, 1), 8)
     held, back = lax.optimization_barrier((held, back))
     held = jnp.sum(held, axis=0)
     fine = depth // 16
@@ -551,20 +618,28 @@
         axis=1,
     )
     held = exchange(pieces16, second_groups())
-    back = cross(cross(back, 2), 4)
-    held, back = lax.optimization_barrier((held, back))
+    back = cross(back, 2)
+    rows_new, accum_new = updated(
+        slot_ids,
+        cache_rows,
+        cache_accum,
+        (latent, dlatent, dlogit),
+        (proj_u, proj_v, cross_bias[None, :], head[None, :]),
+    )
+    held, back, rows_new, accum_new = lax.optimization_barrier(
+        (held, back, rows_new, accum_new)
+    )
     summed16 = jnp.sum(held, axis=0)
     extras = summed16[fine:]
     spread = jnp.broadcast_to(summed16[None, :fine], (16, fine, width))
     held = exchange(spread, second_groups())
-    back = cross(back, 8)
+    back = cross(back, 16)
     held, back = lax.optimization_barrier((held, back))
     whole = jnp.concatenate([held.reshape(depth, width), extras], axis=0)
     whole = exchange(jnp.broadcast_to(whole[None], (blocks, depth + 8, width)), first_groups())
     in_place = (miss_dest[:, 0] ^ me) * per + ranks(miss_dest[:, 0])
-    rows_new, accum_new = refilled(
-        slot_ids, evict_slot, in_place, cache_rows, cache_accum, dpooled, back.reshape(spots, width)
-    )
+    back = cross(back, 4)
+    rows_new = refilled(evict_slot, in_place, back.reshape(spots, width), rows_new)
     fetched_accum = picked(back[:, per - 1, :per].reshape(-1), in_place)
     filled = evict_slot[:, None] == jnp.arange(cells, dtype=jnp.int32)[None, :]
     filled_sum = jnp.sum(jnp.where(filled, fetched_accum[:, None], 0.0), axis=0)

time: 148 us -> 143 us (0.966)
  waiting for transfers between devices: 49.4 us -> 40 us
  local copies, waits for them, and re-layouts: 6.96 us -> 12.4 us
  Pallas kernels: 28.5 us -> 32.4 us
  other arithmetic: 7.63 us -> 5.34 us
    ppermute x5, waiting for transfers between devices: 38.7 us -> 32.8 us  [cross(): came = lax.ppermute(split[:, 1], AXES, there)]
    pallas_call x2 -> x4, Pallas kernels: 20.8 us -> 24.8 us  [the longest x1 12.3 us: dense(): pl.pallas_call(dense_kernel, out_shape=(jax.ShapeDtypeStruct(bundle, f32)...]
    unnamed x20 -> x27, local copies, waits for them, and re-layouts: 0.1 us -> 3.95 us
    ppermute x2, waiting for transfers between devices: 5.96 us -> 2.23 us  [swap_cores(): return lax.ppermute(value, AXES, [(i, i ^ 1) for i in range(256)])]
    ppermute x2, starting transfers between devices: 2.82 us -> 1.06 us  [swap_cores(): return lax.ppermute(value, AXES, [(i, i ^ 1) for i in range(256)])]
    ppermute x5, starting transfers between devices: 7.16 us -> 8.88 us  [cross(): came = lax.ppermute(split[:, 1], AXES, there)]
    add x1, other arithmetic: 3.23 us -> 1.62 us  [shards(): held = kept(core, left, latent, dlatent, extra) + swap_cores(send)]
  transfers between devices with their start and end apart: 12 -> 12, of which waited for: 9 -> 7; matrix products, arithmetic and copies ran while one was open for 6% -> 6% of each run, Pallas kernels for 16% -> 19%
where the time goes in v6:
time: 143 us; the launch traced here: 141 us
  starting transfers between devices  49.1 us (34%)
  waiting for transfers between devices  40 us (28%)
  Pallas kernels  32.4 us (23%)
  local copies, waits for them, and re-layouts  12.4 us (9%)
  other arithmetic  5.34 us (4%)
  between operations  2.24 us (2%)
    ppermute x5, waiting for transfers between devices, cross(): came = lax.ppermute(split[:, 1], AXES, there)  32.8 us
    all_to_all x4, starting transfers between devices, exchange(): lax.all_to_all(value, AXES, split_axis=0, concat_axis=0, tiled=True, axis...  28.9 us
    pallas_call x1, Pallas kernels, dense(): pl.pallas_call(dense_kernel, out_shape=(jax.ShapeDtypeStruct(bundle, f32)...  12.3 us
    all_to_all x1, starting transfers between devices, shards(): got = lax.all_to_all(sent, 'table', split_axis=0, concat_axis=0, tiled=True)  10.3 us
    pallas_call x1, Pallas kernels, updated(): pl.pallas_call(update_kernel, out_shape=(jax.ShapeDtypeStruct(cache_rows....  9.38 us
    ppermute x5, starting transfers between devices, cross(): came = lax.ppermute(split[:, 1], AXES, there)  8.88 us
    all_to_all x4, waiting for transfers between devices, exchange(): lax.all_to_all(value, AXES, split_axis=0, concat_axis=0, tiled=True, axis...  4.91 us
    unnamed x27, local copies, waits for them, and re-layouts  3.95 us
  transfers between devices with their start and end apart: 12, of which 7 were waited for; matrix products, arithmetic and copies ran while one was open for 6% of the time, Pallas kernels for 19%

profile of v6, /device:TPU:3, one launch (start us, length us, event | category | flops | bytes accessed | tf_op | source)
XLA Modules:
  0.0 141.5 jit_solution(4091857858418442612)
XLA Ops:
  0.6 2.9 %payload.1 = f32[256,256]{1,0:T(8,128)} custom-call(s32[64]{0:T(128)} %evict_ref.1, s32[2,64]{1,0:T(2,128)} %bitcast.87, s32[2,64]{1,0:T(2,128)} %bitcast.85, f32[1024]{0:T(1024)} %accum_ref.1, f32[1024,256]{1,0:T(8,128)} %cache_ref.1), custom_call_target="tpu_custom_call" | custom-call | flops 100000 | bytes 1500000 | tf_op jit(solution)/shard_map/payload/pallas_call | solution.py:343
  3.6 10.3 %all-to-all-start = ((f32[32,8,256]{2,1,0:T(8,128)}), f32[32,8,256]{2,1,0:T(8,128)S(1)}, u32[]{:S(2)}, u32[]{:S(2)}) async-start(f32[32,8,256]{2,1,0:T(8,128)} %bitcast.69), calls=%async_computation | async-start | bytes 524288 | tf_op jit(solution)/shard_map/all_to_all | solution.py:574
  13.9 12.3 %dense.1 = (f32[8,264,256]{2,1,0:T(8,128)}, bf16[256,2048]{1,0:T(8,128)(2,1)}, bf16[256,256]{1,0:T(8,128)(2,1)}, bf16[256,256]{1,0:T(8,128)(2,1)}, f32[1,256]{1,0:T(1,128)}, /*index=5*/f32[8,8,256]{2,1,0:T(8,128)}) custom-call(s32[1]{0:T(128)} %bitcast.core_ref, s32[32,256]{1,0:T(8,128)} %bitcast.88, s32[1,256]{1,0:T(1,128)} %bitcast.94, ...), custom_call_target="tpu_custom_call" | custom-call | flops 5000000000 | bytes 9000000 | tf_op jit(solution)/shard_map/dense/pallas_call | solution.py:211
  26.2 1.1 collective-permute-start
  27.3 1.2 copy-done
  28.5 0.9 copy-done.1
  29.4 0.9 copy-done.2
  30.3 0.8 copy-done.3
  31.2 0.5 kept.1
  31.7 1.6 %add.26 = f32[8,264,256]{2,1,0:T(8,128)} add(f32[8,264,256]{2,1,0:T(8,128)S(1)} %kept.1, f32[8,264,256]{2,1,0:T(8,128)S(1)} %collective-permute-done) | non-fusion elementwise | flops 540672 | bytes 6488064 | tf_op jit(solution)/shard_map/add | solution.py:585
  33.3 6.4 %all-to-all-start.1 = ((f32[8,264,256]{2,1,0:T(8,128)}), f32[8,264,256]{2,1,0:T(8,128)S(1)}, u32[]{:S(2)}, u32[]{:S(2)}) async-start(f32[8,264,256]{2,1,0:T(8,128)} %add.26), calls=%async_computation.1 | async-start | bytes 4325376 | tf_op jit(solution)/shard_map/all_to_all | solution.py:44
  40.0 0.1 eq.102
  40.3 0.1 broadcast_in_dim.159
  40.4 0.1 select_reduce_fusion.3
  40.6 0.2 fusion
  40.8 0.2 select_reduce_fusion.1
  41.0 0.2 select_reduce_fusion
  41.4 0.7 reshape.186
  42.1 2.0 %scatter_fusion = f32[1024,256]{1,0:T(8,128)S(1)} fusion(f32[1024,256]{1,0:T(8,128)S(1)} %copy-done.5, s32[192]{0:T(256)S(1)} %bitcast.84, f32[192,256]{1,0:T(8,128)} %reshape.186), kind=kCustom, calls=%fused_computation.1 | custom fusion | bytes 590592 | tf_op jit(solution)/shard_map/scatter | solution.py:591
  44.2 1.0 gather_fusion
  45.4 1.3 collective-permute-done.1
  46.8 4.8 %collective-permute-start.2 = (f32[2,8,8,256]{3,2,1,0:T(8,128)S(1)}, f32[2,8,8,256]{3,2,1,0:T(8,128)S(1)}, u32[]{:S(2)}, u32[]{:S(2)}) collective-permute-start(f32[2,8,8,256]{3,2,1,0:T(8,128)S(1)} %get-tuple-element.70), channel_id=1, source_target_pairs={{0,8},{1,9},{2,10},{3,11},{4,12},{5,13},{6,14},{7,15},{8,0},{9,1},... | collective-permute-start | bytes 393224 | tf_op jit(solution)/shard_map/ppermute | solution.py:69
  51.6 5.8 %collective-permute-done.2 = f32[2,8,8,256]{3,2,1,0:T(8,128)S(1)} collective-permute-done((f32[2,8,8,256]{3,2,1,0:T(8,128)S(1)}, f32[2,8,8,256]{3,2,1,0:T(8,128)S(1)}, u32[]{:S(2)}, u32[]{:S(2)}) %collective-permute-start.2) | collective-permute-done | bytes 131104 | tf_op jit(solution)/shard_map/ppermute | solution.py:69
  57.4 0.2 reduce_sum.77
  57.7 0.8 pad_maximum_fusion
  58.4 8.8 %all-to-all-start.2 = ((f32[16,24,256]{2,1,0:T(8,128)}), f32[16,24,256]{2,1,0:T(8,128)S(1)}, u32[]{:S(2)}, u32[]{:S(2)}) async-start(f32[16,24,256]{2,1,0:T(8,128)} %pad_maximum_fusion), calls=%async_computation.2 | async-start | bytes 786432 | tf_op jit(solution)/shard_map/all_to_all | solution.py:44
  67.3 3.1 %collective-permute-start.3 = (f32[8,2,8,256]{3,2,1,0:T(8,128)S(1)}, f32[8,2,8,256]{3,2,1,0:T(8,128)S(1)}, u32[]{:S(2)}, u32[]{:S(2)}) collective-permute-start(f32[8,2,8,256]{3,2,1,0:T(8,128)S(1)} %get-tuple-element.68), channel_id=1, source_target_pairs={{0,2},{1,3},{2,0},{3,1},{4,6},{5,7},{6,4},{7,5},{8,10},{9,11},{10,... | collective-permute-start | bytes 393224 | tf_op jit(solution)/shard_map/ppermute | solution.py:69
  70.4 9.4 %update.1 = (f32[1024,256]{1,0:T(8,128)}, f32[1,1024]{1,0:T(1,128)}) custom-call(s32[32,256]{1,0:T(8,128)} %bitcast.89, f32[1024,256]{1,0:T(8,128)} %cache_ref.1, f32[1,1024]{1,0:T(1,128)} %bitcast.83, bf16[256,256]{1,0:T(8,128)(2,1)} %get-tuple-element.37.latent_ref, bf16[256,256]{1,0:T(8,128)(2,1)} %get-tuple-element.38.dlatent_ref, ...), custom_call_target="tpu_custom_call" | custom-call | flops 1100000000 | bytes 4000000 | tf_op jit(solution)/shard_map/update/pallas_call | solution.py:413
  79.8 2.0 %collective-permute-done.3 = f32[8,2,8,256]{3,2,1,0:T(8,128)S(1)} collective-permute-done((f32[8,2,8,256]{3,2,1,0:T(8,128)S(1)}, f32[8,2,8,256]{3,2,1,0:T(8,128)S(1)}, u32[]{:S(2)}, u32[]{:S(2)}) %collective-permute-start.3) | collective-permute-done | bytes 131104 | tf_op jit(solution)/shard_map/ppermute | solution.py:69
  81.8 0.7 broadcast_in_dim.169
  82.6 8.6 %all-to-all-start.3 = ((f32[16,16,256]{2,1,0:T(8,128)}), f32[16,16,256]{2,1,0:T(8,128)S(1)}, u32[]{:S(2)}, u32[]{:S(2)}) async-start(f32[16,16,256]{2,1,0:T(8,128)} %broadcast_in_dim.169), calls=%async_computation.3 | async-start | bytes 524288 | tf_op jit(solution)/shard_map/all_to_all | solution.py:44
  91.3 5.1 %collective-permute-done.4 = f32[1,16,8,256]{3,2,1,0:T(8,128)S(1)} collective-permute-done((f32[1,16,8,256]{3,2,1,0:T(8,128)S(1)}, f32[1,16,8,256]{3,2,1,0:T(8,128)S(1)}, u32[]{:S(2)}, u32[]{:S(2)}) %collective-permute-start.4) | collective-permute-done | bytes 131104 | tf_op jit(solution)/shard_map/ppermute | solution.py:69
  96.5 4.9 %all-to-all-done.3 = f32[16,16,256]{2,1,0:T(8,128)S(1)} async-done(((f32[16,16,256]{2,1,0:T(8,128)}), f32[16,16,256]{2,1,0:T(8,128)S(1)}, u32[]{:S(2)}, u32[]{:S(2)}) %all-to-all-start.3) | async-done | bytes 262176 | tf_op jit(solution)/shard_map/all_to_all | solution.py:44
  101.4 1.5 %broadcast_in_dim.170 = f32[8,264,256]{2,1,0:T(8,128)} broadcast(f32[264,256]{1,0:T(8,128)S(1)} %pad_maximum_fusion.1), dimensions={1,2} | broadcast | bytes 2433024 | tf_op jit(solution)/shard_map/broadcast_in_dim | solution.py:639
  102.9 5.0 %all-to-all-start.4 = ((f32[8,264,256]{2,1,0:T(8,128)}), f32[8,264,256]{2,1,0:T(8,128)S(1)}, u32[]{:S(2)}, u32[]{:S(2)}) async-start(f32[8,264,256]{2,1,0:T(8,128)} %broadcast_in_dim.170), calls=%async_computation.4 | async-start | bytes 4325376 | tf_op jit(solution)/shard_map/all_to_all | solution.py:44
  107.9 0.2 convert_reduce_fusion
  108.1 0.8 collective-permute-start.5
  108.9 0.5 multiply_add_fusion.place_ref
  109.5 0.1 fusion.1
  109.6 18.5 %collective-permute-done.5 = f32[4,4,8,256]{3,2,1,0:T(8,128)S(1)} collective-permute-done((f32[4,4,8,256]{3,2,1,0:T(8,128)S(1)}, f32[4,4,8,256]{3,2,1,0:T(8,128)S(1)}, u32[]{:S(2)}, u32[]{:S(2)}) %collective-permute-start.5) | collective-permute-done | bytes 131104 | tf_op jit(solution)/shard_map/ppermute | solution.py:69
  128.1 0.7 copy.50
  128.9 2.6 %refill.1 = f32[1024,256]{1,0:T(8,128)} custom-call(s32[64]{0:T(128)} %evict_ref.1, s32[64]{0:T(128)} %multiply_add_fusion.place_ref, f32[256,256]{1,0:T(8,128)} %bitcast.66, f32[1024,256]{1,0:T(8,128)} %get-tuple-element.55.old_ref), custom_call_target="tpu_custom_call" | custom-call | flops 100000 | bytes 2000000 | tf_op jit(solution)/shard_map/refill/pallas_call | solution.py:432
  131.5 1.0 slice_reduce_fusion
  132.5 0.2 select_reduce_fusion.4
  132.8 0.6 select_n.76
  133.5 2.0 %scale_own.1.proj_in = f32[2,2048,256]{2,1,0:T(8,128)} custom-call(s32[1]{0:T(128)} %bitcast.core_ref, f32[8,264,256]{2,1,0:T(8,128)S(1)} %all-to-all-done.4.half_any), custom_call_target="tpu_custom_call" | custom-call | tf_op jit(solution)/shard_map/scale_own/pallas_call | solution.py:520
  135.5 2.2 %collective-permute-done.6.half_any = f32[8,264,256]{2,1,0:T(8,128)S(1)} collective-permute-done((f32[8,264,256]{2,1,0:T(8,128)S(1)}, f32[8,264,256]{2,1,0:T(8,128)S(1)}, u32[]{:S(2)}, u32[]{:S(2)}) %collective-permute-start.6) | collective-permute-done | bytes 2162720 | tf_op jit(solution)/shard_map/ppermute | solution.py:40
  137.7 2.6 %scale_other.1 = (f32[2,2048,256]{2,1,0:T(8,128)}, f32[2,2048]{1,0:T(2,128)}, f32[1,128]{1,0:T(1,128)S(1)}) custom-call(s32[1]{0:T(128)} %bitcast.core_ref, f32[2,2048,256]{2,1,0:T(8,128)} %scale_own.1.proj_in, f32[8,8,256]{2,1,0:T(8,128)S(1)} %slice.91.own_ref, f32[8,264,256]{2,1,0:T(8,128)S(1)} %collective-permute-done.6.half_any), custom_call_target="tpu_custom_call", output_to_operand_aliasing={{0}: (1, {})} | custom-call | tf_op jit(solution)/shard_map/scale_other/pallas_call | solution.py:529
  (70 shorter events, 1.5 us)
Async XLA Ops:
  3.6 22.7 %all-to-all-start = ((f32[32,8,256]{2,1,0:T(8,128)}), f32[32,8,256]{2,1,0:T(8,128)S(1)}, u32[]{:S(2)}, u32[]{:S(2)}) async-start(f32[32,8,256]{2,1,0:T(8,128)} %bitcast.69), calls=%async_computation | async-start | bytes 524288 | tf_op jit(solution)/shard_map/all_to_all | solution.py:574
  26.2 5.4 %collective-permute-start = (f32[8,264,256]{2,1,0:T(8,128)}, f32[8,264,256]{2,1,0:T(8,128)S(1)}, u32[]{:S(2)}, u32[]{:S(2)}) collective-permute-start(f32[8,264,256]{2,1,0:T(8,128)} %get-tuple-element.42), channel_id=1, source_target_pairs={{0,1},{1,0},{2,3},{3,2},{4,5},{5,4},{6,7},{7,6},{8,9},{9,8},{10,11... | collective-permute-start | bytes 6488072 | tf_op jit(solution)/shard_map/ppermute | solution.py:40
  27.3 1.2 copy-start
  28.5 0.9 copy-start.1
  29.4 0.9 copy-start.2
  30.3 0.8 copy-start.3
  33.3 7.7 %copy-start.10 = (f32[1024]{0:T(1024)S(1)}, f32[1024]{0:T(1024)}, u32[]{:S(2)}) copy-start(f32[1024]{0:T(1024)} %param.18) | copy-start | bytes 12292
  33.3 8.8 %copy-start.5 = (f32[1024,256]{1,0:T(8,128)S(1)}, f32[1024,256]{1,0:T(8,128)}, u32[]{:S(2)}) copy-start(f32[1024,256]{1,0:T(8,128)} %param.17) | copy-start | bytes 3145732
  33.3 24.1 %all-to-all-start.1 = ((f32[8,264,256]{2,1,0:T(8,128)}), f32[8,264,256]{2,1,0:T(8,128)S(1)}, u32[]{:S(2)}, u32[]{:S(2)}) async-start(f32[8,264,256]{2,1,0:T(8,128)} %add.26), calls=%async_computation.1 | async-start | bytes 4325376 | tf_op jit(solution)/shard_map/all_to_all | solution.py:44
  41.0 4.1 %copy-start.6 = (f32[1024]{0:T(1024)}, f32[1024]{0:T(1024)S(1)}, u32[]{:S(2)}) copy-start(f32[1024]{0:T(1024)S(1)} %select_n.69) | copy-start | bytes 12292
  44.1 2.6 %copy-start.4 = (f32[1024,256]{1,0:T(8,128)}, f32[1024,256]{1,0:T(8,128)S(1)}, u32[]{:S(2)}) copy-start(f32[1024,256]{1,0:T(8,128)S(1)} %scatter_fusion) | copy-start | bytes 3145732
  45.3 1.4 %collective-permute-start.1 = (f32[16,1,8,256]{3,2,0,1:T(8,128)S(1)}, f32[16,1,8,256]{3,2,0,1:T(8,128)S(1)}, u32[]{:S(2)}, u32[]{:S(2)}) collective-permute-start(f32[16,1,8,256]{3,2,0,1:T(8,128)S(1)} %get-tuple-element.72), channel_id=1, source_target_pairs={{0,1},{1,0},{2,3},{3,2},{4,5},{5,4},{6,7},{7,6},{8,9},{9,8},{10,11... | collective-permute-start | bytes 393224 | tf_op jit(solution)/shard_map/ppermute | solution.py:69
  46.8 10.6 %collective-permute-start.2 = (f32[2,8,8,256]{3,2,1,0:T(8,128)S(1)}, f32[2,8,8,256]{3,2,1,0:T(8,128)S(1)}, u32[]{:S(2)}, u32[]{:S(2)}) collective-permute-start(f32[2,8,8,256]{3,2,1,0:T(8,128)S(1)} %get-tuple-element.70), channel_id=1, source_target_pairs={{0,8},{1,9},{2,10},{3,11},{4,12},{5,13},{6,14},{7,15},{8,0},{9,1},... | collective-permute-start | bytes 393224 | tf_op jit(solution)/shard_map/ppermute | solution.py:69
  58.4 23.3 %all-to-all-start.2 = ((f32[16,24,256]{2,1,0:T(8,128)}), f32[16,24,256]{2,1,0:T(8,128)S(1)}, u32[]{:S(2)}, u32[]{:S(2)}) async-start(f32[16,24,256]{2,1,0:T(8,128)} %pad_maximum_fusion), calls=%async_computation.2 | async-start | bytes 786432 | tf_op jit(solution)/shard_map/all_to_all | solution.py:44
  67.3 14.5 %collective-permute-start.3 = (f32[8,2,8,256]{3,2,1,0:T(8,128)S(1)}, f32[8,2,8,256]{3,2,1,0:T(8,128)S(1)}, u32[]{:S(2)}, u32[]{:S(2)}) collective-permute-start(f32[8,2,8,256]{3,2,1,0:T(8,128)S(1)} %get-tuple-element.68), channel_id=1, source_target_pairs={{0,2},{1,3},{2,0},{3,1},{4,6},{5,7},{6,4},{7,5},{8,10},{9,11},{10,... | collective-permute-start | bytes 393224 | tf_op jit(solution)/shard_map/ppermute | solution.py:69
  82.6 18.8 %all-to-all-start.3 = ((f32[16,16,256]{2,1,0:T(8,128)}), f32[16,16,256]{2,1,0:T(8,128)S(1)}, u32[]{:S(2)}, u32[]{:S(2)}) async-start(f32[16,16,256]{2,1,0:T(8,128)} %broadcast_in_dim.169), calls=%async_computation.3 | async-start | bytes 524288 | tf_op jit(solution)/shard_map/all_to_all | solution.py:44
  91.2 5.2 %collective-permute-start.4 = (f32[1,16,8,256]{3,2,1,0:T(8,128)S(1)}, f32[1,16,8,256]{3,2,1,0:T(8,128)S(1)}, u32[]{:S(2)}, u32[]{:S(2)}) collective-permute-start(f32[1,16,8,256]{3,2,1,0:T(8,128)S(1)} %get-tuple-element.66), channel_id=1, source_target_pairs={{0,16},{1,17},{2,18},{3,19},{4,20},{5,21},{6,22},{7,23},{8,24},{9,... | collective-permute-start | bytes 393224 | tf_op jit(solution)/shard_map/ppermute | solution.py:69
  102.9 5.0 %copy-start.9 = (s32[64,2]{0,1:T(2,128)S(1)}, s32[64,2]{0,1:T(2,128)}, u32[]{:S(2)}) copy-start(s32[64,2]{0,1:T(2,128)} %param.19) | copy-start | bytes 1540
  102.9 6.5 %copy-start.7 = (s32[64]{0:T(128)S(1)}, s32[64]{0:T(128)}, u32[]{:S(2)}) copy-start(s32[64]{0:T(128)} %evict_ref.1) | copy-start | bytes 772
  102.9 30.5 %all-to-all-start.4 = ((f32[8,264,256]{2,1,0:T(8,128)}), f32[8,264,256]{2,1,0:T(8,128)S(1)}, u32[]{:S(2)}, u32[]{:S(2)}) async-start(f32[8,264,256]{2,1,0:T(8,128)} %broadcast_in_dim.170), calls=%async_computation.4 | async-start | bytes 4325376 | tf_op jit(solution)/shard_map/all_to_all | solution.py:44
  107.9 24.8 %copy-start.8 = (s32[64]{0:T(128)S(1)}, s32[64]{0:T(128)}, u32[]{:S(2)}) copy-start(s32[64]{0:T(128)} %evict_ref.1) | copy-start | bytes 772
  107.9 24.9 %copy-start.11 = (f32[1,1024]{1,0:T(1,128)S(1)}, f32[1,1024]{1,0:T(1,128)}, u32[]{:S(2)}) copy-start(f32[1,1024]{1,0:T(1,128)} %get-tuple-element.56) | copy-start | bytes 12292
  108.1 20.0 %collective-permute-start.5 = (f32[4,4,8,256]{3,2,1,0:T(8,128)S(1)}, f32[4,4,8,256]{3,2,1,0:T(8,128)S(1)}, u32[]{:S(2)}, u32[]{:S(2)}) collective-permute-start(f32[4,4,8,256]{3,2,1,0:T(8,128)S(1)} %get-tuple-element.64), channel_id=1, source_target_pairs={{0,4},{1,5},{2,6},{3,7},{4,0},{5,1},{6,2},{7,3},{8,12},{9,13},{10,... | collective-permute-start | bytes 393224 | tf_op jit(solution)/shard_map/ppermute | solution.py:69
  133.4 4.3 %collective-permute-start.6 = (f32[8,264,256]{2,1,0:T(8,128)S(1)}, f32[8,264,256]{2,1,0:T(8,128)S(1)}, u32[]{:S(2)}, u32[]{:S(2)}) collective-permute-start(f32[8,264,256]{2,1,0:T(8,128)S(1)} %all-to-all-done.4.half_any), channel_id=1, source_target_pairs={{0,1},{1,0},{2,3},{3,2},{4,5},{5,4},{6,7},{7,6},{8,9},{9,8},{10,11... | collective-permute-start | bytes 6488072 | tf_op jit(solution)/shard_map/ppermute | solution.py:40

commit v7 on v6

--- a/solution.py
+++ b/solution.py
@@ -53,28 +53,83 @@
     return jnp.sum(earlier.astype(jnp.int32), axis=1)
 
 
-def meta_row(columns, width):
-    block = jnp.concatenate(columns, axis=1)
-    return jnp.pad(block, ((0, 0), (0, width - block.shape[1])))[:, None, :]
-
-
 def picked(values, index):
     hit = index[:, None] == jnp.arange(values.shape[0], dtype=jnp.int32)[None, :]
     return jnp.sum(jnp.where(hit, values[None, :], 0.0), axis=1)
 
 
-def cross(value, bit):
-    split = value.reshape(value.shape[0] // (2 * bit), 2, bit, *value.shape[1:])
-    there = [(i, i ^ bit) for i in range(256)]
-    came = lax.ppermute(split[:, 1], AXES, there)
-    return jnp.stack([split[:, 0], came], axis=1).reshape(value.shape)
+def pool_kernel(slots_ref, cache_any, pooled_out, cache, high, mid, low, pooled, in_sems, out_sems):
+    f32, bf16 = jnp.float32, jnp.bfloat16
+    count, (cells, width) = slots_ref.shape[1], cache.shape
+    feats = pooled.shape[0]
+    looks = slots_ref.shape[0] // feats
+    loads = []
+    step = cells // 4
+    for part in range(4):
+        rows = pl.ds(part * step, step)
+        loads.append(pltpu.make_async_copy(cache_any.at[rows], cache.at[rows], in_sems.at[part]))
+        loads[-1].start()
+    slots = jnp.transpose(slots_ref[...])
+    lane = lax.broadcasted_iota(jnp.int32, (count, cells), 1)
+
+    def counted(f):
+        counts = jnp.zeros((count, cells), f32)
+        for look in range(looks):
+            at = f * looks + look
+            counts = counts + jnp.where(lane == slots[:, at : at + 1], 1.0, 0.0)
+        return counts.astype(bf16)
+
+    counts = counted(0)
+    for part in range(4):
+        loads[part].wait()
+        rows = cache[part * step : (part + 1) * step, :]
+        first = rows.astype(bf16)
+        rest = rows - first.astype(f32)
+        second = rest.astype(bf16)
+        high[part * step : (part + 1) * step, :] = first
+        mid[part * step : (part + 1) * step, :] = second
+        low[part * step : (part + 1) * step, :] = (rest - second.astype(f32)).astype(bf16)
+    copies = []
+    for f in range(feats):
+        if f > 0:
+            counts = counted(f)
+        total = jnp.dot(counts, low[...], preferred_element_type=f32)
+        total = total + jnp.dot(counts, mid[...], preferred_element_type=f32)
+        total = total + jnp.dot(counts, high[...], preferred_element_type=f32)
+        pooled[f] = total.astype(bf16)
+        copies.append(pltpu.make_async_copy(pooled.at[f], pooled_out.at[f], out_sems.at[f]))
+        copies[-1].start()
+    for copy in copies:
+        copy.wait()
+
+def pool(slot_ids, cache_rows, feats):
+    count, (cells, width) = slot_ids.shape[0], cache_rows.shape
+    f32, bf16 = jnp.float32, jnp.bfloat16
+    anywhere = pl.BlockSpec(memory_space=pl.ANY)
+    return pl.pallas_call(
+        pool_kernel,
+        out_shape=jax.ShapeDtypeStruct((feats, count, width), bf16),
+        in_specs=[pl.BlockSpec(memory_space=pltpu.VMEM), anywhere],
+        out_specs=anywhere,
+        scratch_shapes=[pltpu.VMEM((cells, width), f32)]
+        + [pltpu.VMEM((cells, width), bf16)] * 3
+        + [
+            pltpu.VMEM((feats, count, width), bf16),
+            pltpu.SemaphoreType.DMA((4,)),
+            pltpu.SemaphoreType.DMA((feats,)),
+        ],
+        compiler_params=pltpu.CompilerParams(vmem_limit_bytes=60 * 1024 * 1024),
+        cost_estimate=pl.CostEstimate(
+            flops=3_200_000_000, bytes_accessed=2_000_000, transcendentals=0
+        ),
+        name="pool",
+    )(slot_ids.T, cache_rows)
 
 
 def dense_kernel(
     core_ref,
-    slots_ref,
     labels_ref,
-    cache_any,
+    pooled_any,
     u_any,
     v_any,
     bias_ref,
@@ -85,14 +140,10 @@
     dlatent_ref,
     dlogit_ref,
     extra_ref,
-    cache,
     u_ref,
     v_ref,
     send_ref,
     left,
-    high,
-    mid,
-    low,
     pooled,
     shifted,
     dlift,
@@ -100,59 +151,36 @@
     out_sems,
 ):
     f32, bf16 = jnp.float32, jnp.bfloat16
-    count, (cells, width) = slots_ref.shape[1], cache.shape
-    feats = u_ref.shape[0] // width
-    looks = slots_ref.shape[0] // feats
+    feats, count, width = pooled.shape
     cuts = [slice(c * width, (c + 1) * width) for c in range(feats)]
     loads = []
-    for source, target in ((cache_any, cache), (v_any, v_ref), (u_any, u_ref)):
-        step = target.shape[0] // 4
-        for part in range(4):
-            rows = pl.ds(part * step, step)
-            loads.append(
-                pltpu.make_async_copy(source.at[rows], target.at[rows], in_sems.at[len(loads)])
+    for c, cut in enumerate(cuts):
+        rows = pl.ds(c * width, width)
+        for k, (source, target) in enumerate(
+            (
+                (pooled_any.at[c], pooled.at[c]),
+                (v_any.at[rows], v_ref.at[rows]),
+                (u_any.at[rows], u_ref.at[rows]),
             )
+        ):
+            loads.append(pltpu.make_async_copy(source, target, in_sems.at[3 * c + k]))
             loads[-1].start()
-    slots = jnp.transpose(slots_ref[...])
-    lane = lax.broadcasted_iota(jnp.int32, (count, cells), 1)
-
-    def counted(f):
-        counts = jnp.zeros((count, cells), f32)
-        for look in range(looks):
-            at = f * looks + look
-            counts = counts + jnp.where(lane == slots[:, at : at + 1], 1.0, 0.0)
-        return counts.astype(bf16)
-
-    counts = counted(0)
-    step = cells // 4
-    for part in range(4):
-        loads[part].wait()
-        rows = cache[part * step : (part + 1) * step, :]
-        first = rows.astype(bf16)
-        rest = rows - first.astype(f32)
-        second = rest.astype(bf16)
-        high[part * step : (part + 1) * step, :] = first
-        mid[part * step : (part + 1) * step, :] = second
-        low[part * step : (part + 1) * step, :] = (rest - second.astype(f32)).astype(bf16)
-    for f in range(feats):
-        if f > 0:
-            counts = counted(f)
-        total = jnp.dot(counts, low[...], preferred_element_type=f32)
-        total = total + jnp.dot(counts, mid[...], preferred_element_type=f32)
-        total = total + jnp.dot(counts, high[...], preferred_element_type=f32)
-        pooled[:, cuts[f]] = total.astype(bf16)
-
-    for load in loads[4:]:
-        load.wait()
-    latent = jnp.dot(pooled[...], v_ref[...], preferred_element_type=f32).astype(bf16)
+    forward = jnp.zeros((count, width), f32)
+    for c, cut in enumerate(cuts):
+        loads[3 * c].wait()
+        loads[3 * c + 1].wait()
+        forward = forward + jnp.dot(pooled[c], v_ref[cut, :], preferred_element_type=f32)
+    latent = forward.astype(bf16)
+    for c in range(feats):
+        loads[3 * c + 2].wait()
     latent_ref[...] = latent
     across = (((1,), (1,)), ((), ()))
     logit_wide = jnp.zeros((count, width), f32)
-    for cut in cuts:
+    for c, cut in enumerate(cuts):
         moved = lax.dot_general(latent, u_ref[cut, :], across, preferred_element_type=f32)
         moved = moved + bias_ref[:, cut]
         shifted[:, cut] = moved
-        part = pooled[:, cut].astype(f32)
+        part = pooled[c].astype(f32)
         logit_wide = logit_wide + (part * moved + part) * head_ref[:, cut]
     logit = jnp.sum(logit_wide, axis=1, keepdims=True)
     target = jnp.transpose(labels_ref[...]).astype(f32)
@@ -167,7 +195,7 @@
     loss_row = jnp.where(lane1 == 0, loss, 0.0)
     back = jnp.zeros((count, width), f32)
     for c, cut in enumerate(cuts):
-        part = pooled[:, cut].astype(f32)
+        part = pooled[c].astype(f32)
         lift = dlogit * head_ref[:, cut] * part
         crossed = part * shifted[:, cut] + part
         dbias = jnp.sum(lift, axis=0, keepdims=True)
@@ -181,7 +209,7 @@
         send_ref[c, width : width + 1, :] = jnp.where(mine, dhead, dbias)
         send_ref[c, width + 1 : width + 2, :] = loss_row
         send_ref[c, width + 2 : width + 8, :] = jnp.zeros((6, width), f32)
-        left[:, cut] = jnp.where(mine, lift, pooled[:, cut])
+        left[:, cut] = jnp.where(mine, lift, pooled[c])
     dlatent = back.astype(bf16)
     dlatent_ref[...] = dlatent
     copies = [pltpu.make_async_copy(left, left_out, out_sems.at[feats])]
@@ -189,7 +217,7 @@
     right = jnp.where(mine, dlatent, latent)
     for c, cut in enumerate(cuts):
         send_ref[c, :width, :] = lax.dot_general(
-            jnp.where(mine, pooled[:, cut], dlift[:, cut]),
+            jnp.where(mine, pooled[c], dlift[:, cut]),
             right,
             (((0,), (0,)), ((), ())),
             preferred_element_type=f32,
@@ -200,10 +228,9 @@
         copy.wait()
 
 
-def dense(core, slot_ids, labels, cache_rows, proj_u, proj_v, cross_bias, head):
-    count, (cells, width) = slot_ids.shape[0], cache_rows.shape
-    wide = proj_u.shape[0]
-    blocks = wide // width
+def dense(core, labels, pooled, proj_u, proj_v, cross_bias, head):
+    blocks, count, width = pooled.shape
+    wide = blocks * width
     f32, bf16 = jnp.float32, jnp.bfloat16
     vmem = pl.BlockSpec(memory_space=pltpu.VMEM)
     anywhere = pl.BlockSpec(memory_space=pl.ANY)
@@ -219,35 +246,30 @@
             jax.ShapeDtypeStruct((blocks, 8, width), f32),
         ),
         in_specs=[pl.BlockSpec(memory_space=pltpu.SMEM)]
-        + [vmem] * 2
+        + [vmem]
         + [anywhere] * 3
         + [vmem] * 2,
         out_specs=[anywhere] * 2 + [vmem] * 4,
         scratch_shapes=[
-            pltpu.VMEM((cells, width), f32),
             pltpu.VMEM((wide, width), bf16),
             pltpu.VMEM((wide, width), bf16),
             pltpu.VMEM(bundle, f32),
             pltpu.VMEM((count, wide), bf16),
-        ]
-        + [pltpu.VMEM((cells, width), bf16)] * 3
-        + [
-            pltpu.VMEM((count, wide), bf16),
+            pltpu.VMEM((blocks, count, width), bf16),
             pltpu.VMEM((count, wide), f32),
             pltpu.VMEM((count, wide), bf16),
-            pltpu.SemaphoreType.DMA((12,)),
+            pltpu.SemaphoreType.DMA((3 * blocks,)),
             pltpu.SemaphoreType.DMA((blocks + 1,)),
         ],
         compiler_params=pltpu.CompilerParams(vmem_limit_bytes=60 * 1024 * 1024),
         cost_estimate=pl.CostEstimate(
-            flops=5_000_000_000, bytes_accessed=9_000_000, transcendentals=1000
+            flops=1_600_000_000, bytes_accessed=9_000_000, transcendentals=1000
         ),
         name="dense",
     )(
         core[None],
-        slot_ids.T,
         labels[None, :],
-        cache_rows,
+        pooled,
         proj_u,
         proj_v,
         cross_bias[None, :],
@@ -359,6 +381,8 @@
 
 def update_kernel(
     slots_ref,
+    evict_ref,
+    place_ref,
     cache_ref,
     accum_ref,
     latent_ref,
@@ -368,6 +392,7 @@
     v_ref,
     bias_ref,
     head_ref,
+    back_ref,
     rows_ref,
     accum_out,
 ):
@@ -396,10 +421,6 @@
     rows_ref[...] = cache_ref[...] - ETA * grad * lax.rsqrt(accum)
     accum_out[...] = jnp.transpose(accum)
 
-
-def refill_kernel(evict_ref, place_ref, back_ref, old_ref, rows_ref):
-    rows_ref[...] = old_ref[...]
-
     def refill(i, _):
         rows_ref[pl.ds(evict_ref[i], 1), :] = back_ref[pl.ds(place_ref[i], 1), :]
         return 0
@@ -407,8 +428,9 @@
     lax.fori_loop(0, evict_ref.shape[0], refill, 0, unroll=8)
 
 
-def updated(slot_ids, cache_rows, cache_accum, saved, params):
+def updated(slot_ids, evict_slot, place, cache_rows, cache_accum, saved, params, back):
     cells = cache_rows.shape[0]
+    smem = pl.BlockSpec(memory_space=pltpu.SMEM)
     vmem = pl.BlockSpec(memory_space=pltpu.VMEM)
     return pl.pallas_call(
         update_kernel,
@@ -416,28 +438,108 @@
             jax.ShapeDtypeStruct(cache_rows.shape, jnp.float32),
             jax.ShapeDtypeStruct((1, cells), jnp.float32),
         ),
-        in_specs=[vmem] * 10,
+        in_specs=[vmem, smem, smem] + [vmem] * 10,
         out_specs=(vmem, vmem),
         compiler_params=pltpu.CompilerParams(vmem_limit_bytes=60 * 1024 * 1024),
         cost_estimate=pl.CostEstimate(
             flops=1_100_000_000, bytes_accessed=4_000_000, transcendentals=1000
         ),
         name="update",
-    )(slot_ids.T, cache_rows, cache_accum[None, :], *saved, *params)
-
-
-def refilled(evict_slot, place, back, rows):
+    )(
+        slot_ids.T,
+        evict_slot,
+        place,
+        cache_rows,
+        cache_accum[None, :],
+        *saved,
+        *params,
+        back,
+    )
+
+
+def reply_kernel(
+    ids_ref,
+    sums_ref,
+    got_ref,
+    table_any,
+    accum_any,
+    reply_ref,
+    table_out,
+    accum_out,
+    table,
+    accum,
+    sems,
+):
+    owners, per = sums_ref.shape
+    cap = per - 2
+    width = got_ref.shape[1]
+    step = table.shape[0] // 4
+    loads = [pltpu.make_async_copy(accum_any, accum, sems.at[4])]
+    stores = [pltpu.make_async_copy(accum, accum_out, sems.at[4])]
+    for part in range(4):
+        rows = pl.ds(part * step, step)
+        loads.append(pltpu.make_async_copy(table_any.at[rows], table.at[rows], sems.at[part]))
+        stores.append(pltpu.make_async_copy(table.at[rows], table_out.at[rows], sems.at[part]))
+    for load in loads:
+        load.start()
+    for load in loads:
+        load.wait()
+
+    def store(s, _):
+        for r in range(cap):
+            row = ids_ref[s, per + r]
+
+            @pl.when(row >= 0)
+            def _():
+                table[pl.ds(row, 1), :] = got_ref[pl.ds(s * per + r, 1), :]
+                accum[row] = sums_ref[s, r]
+
+        return 0
+
+    lax.fori_loop(0, owners, store, 0, unroll=2)
+    for copy in stores:
+        copy.start()
+    lane = lax.broadcasted_iota(jnp.int32, (1, width), 1)
+
+    def answer(s, _):
+        meta = jnp.zeros((1, width), jnp.float32)
+        for r in range(cap):
+            row = ids_ref[s, 2 * per + r]
+            reply_ref[pl.ds(s * per + r, 1), :] = table[pl.ds(row, 1), :]
+            meta = jnp.where(lane == r, accum[row], meta)
+        reply_ref[pl.ds(s * per + cap, 1), :] = jnp.zeros((1, width), jnp.float32)
+        reply_ref[pl.ds(s * per + per - 1, 1), :] = meta
+        return 0
+
+    lax.fori_loop(0, owners, answer, 0, unroll=4)
+    for copy in stores:
+        copy.wait()
+
+
+def replied(got, table_rows, table_accum):
+    owners, per, width = got.shape
     smem = pl.BlockSpec(memory_space=pltpu.SMEM)
     vmem = pl.BlockSpec(memory_space=pltpu.VMEM)
+    anywhere = pl.BlockSpec(memory_space=pl.ANY)
+    meta = got[:, per - 1, : 3 * per]
     return pl.pallas_call(
-        refill_kernel,
-        out_shape=jax.ShapeDtypeStruct(rows.shape, jnp.float32),
-        in_specs=[smem, smem, vmem, vmem],
-        out_specs=vmem,
+        reply_kernel,
+        out_shape=(
+            jax.ShapeDtypeStruct((owners * per, width), jnp.float32),
+            jax.ShapeDtypeStruct(table_rows.shape, jnp.float32),
+            jax.ShapeDtypeStruct(table_accum.shape, jnp.float32),
+        ),
+        in_specs=[smem, smem, vmem, anywhere, anywhere],
+        out_specs=(vmem, anywhere, anywhere),
+        scratch_shapes=[
+            pltpu.VMEM(table_rows.shape, jnp.float32),
+            pltpu.SMEM(table_accum.shape, jnp.float32),
+            pltpu.SemaphoreType.DMA((5,)),
+        ],
         compiler_params=pltpu.CompilerParams(vmem_limit_bytes=60 * 1024 * 1024),
-        cost_estimate=pl.CostEstimate(flops=100_000, bytes_accessed=2_000_000, transcendentals=0),
-        name="refill",
-    )(evict_slot, place, back, rows)
+        cost_estimate=pl.CostEstimate(flops=100_000, bytes_accessed=3_000_000, transcendentals=0),
+        name="reply",
+    )(meta.astype(jnp.int32), meta[:, :per], got.reshape(owners * per, width), table_rows, table_accum)
 
 
 def scaled(index, half_any, proj_ref, half, stage, in_sems, out_sems):
@@ -559,55 +661,36 @@
 ):
     owners = 32
     per = 8
-    cap = 6
     width = cache_rows.shape[1]
-    owned = table_rows.shape[0]
     cells = cache_rows.shape[0]
     spots = owners * per
     core = lax.axis_index("table") % 2
 
-    me = lax.axis_index("table")
     sent = payload(
         evict_slot, evict_dest, miss_dest, cache_accum, cache_rows, owners, per
     ).reshape(owners, per, width)
     sent, slots_late = lax.optimization_barrier((sent, slot_ids))
     got = lax.all_to_all(sent, "table", split_axis=0, concat_axis=0, tiled=True)
+    feats = proj_u.shape[0] // width
+    pooled = pool(slots_late, cache_rows, feats)
+
+    pooled, got = lax.optimization_barrier((pooled, got))
+    reply, table_new, accum_table = replied(got, table_rows, table_accum)
+    reply, pooled = lax.optimization_barrier((reply, pooled))
+    back = lax.all_to_all(
+        reply.reshape(owners, per, width), "table", split_axis=0, concat_axis=0, tiled=True
+    )
 
     count = slot_ids.shape[0]
-    feats = proj_u.shape[0] // width
     send, left, latent, dlatent, dlogit, extra = dense(
-        core, slots_late, labels, cache_rows, proj_u, proj_v, cross_bias, head
+        core, labels, pooled, proj_u, proj_v, cross_bias, head
     )
 
     blocks = feats
     depth = width
-    send, got = lax.optimization_barrier((send, got))
+    send, back = lax.optimization_barrier((send, back))
     held = kept(core, left, latent, dlatent, extra) + swap_cores(send)
-    held, got = lax.optimization_barrier((held, got))
-
-    got_meta = got[:, per - 1, :]
-    got_id = got_meta[:, per : per + cap].astype(jnp.int32)
-    flat = got_id.reshape(-1)
-    table_new = table_rows.at[jnp.where(flat < 0, owned, flat)].set(
-        got[:, :cap, :].reshape(-1, width), mode="drop"
-    )
-    stored = flat[:, None] == jnp.arange(owned, dtype=jnp.int32)[None, :]
-    stored_sum = jnp.sum(jnp.where(stored, got_meta[:, :cap].reshape(-1)[:, None], 0.0), axis=0)
-    accum_table = jnp.where(jnp.any(stored, axis=0), stored_sum, table_accum)
-    order = jnp.arange(owners, dtype=jnp.int32)
-    turned = (order ^ me)[:, None] == order[None, :]
-    asked = jnp.sum(
-        jnp.where(turned[:, :, None], got_meta[None, :, 2 * per : 3 * per], 0.0), axis=1
-    )
-    asked = asked.astype(jnp.int32).reshape(-1)
-    is_meta = (jnp.arange(per) == per - 1)[None, :, None]
-    reply_rows = jnp.take(table_new, asked, axis=0, mode="clip").reshape(owners, per, width)
-    reply_accum = picked(accum_table, asked).reshape(owners, per)
-    back = jnp.where(is_meta, meta_row([reply_accum], width), reply_rows)
-
     held = exchange(held, first_groups())
-    back = cross(cross(back, 1), 8)
-    held, back = lax.optimization_barrier((held, back))
     held = jnp.sum(held, axis=0)
     fine = depth // 16
     pieces16 = jnp.concatenate(
@@ -618,33 +701,28 @@
         axis=1,
     )
     held = exchange(pieces16, second_groups())
-    back = cross(back, 2)
+    place = miss_dest[:, 0] * per + ranks(miss_dest[:, 0])
     rows_new, accum_new = updated(
         slot_ids,
+        evict_slot,
+        place,
         cache_rows,
         cache_accum,
         (latent, dlatent, dlogit),
         (proj_u, proj_v, cross_bias[None, :], head[None, :]),
-    )
-    held, back, rows_new, accum_new = lax.optimization_barrier(
-        (held, back, rows_new, accum_new)
-    )
+        back.reshape(spots, width),
+    )
+    fetched_accum = picked(back[:, per - 1, :per].reshape(-1), place)
+    filled = evict_slot[:, None] == jnp.arange(cells, dtype=jnp.int32)[None, :]
+    filled_sum = jnp.sum(jnp.where(filled, fetched_accum[:, None], 0.0), axis=0)
+    accum_new = jnp.where(jnp.any(filled, axis=0), filled_sum, accum_new.reshape(cells))
+    held, rows_new, accum_new = lax.optimization_barrier((held, rows_new, accum_new))
     summed16 = jnp.sum(held, axis=0)
     extras = summed16[fine:]
     spread = jnp.broadcast_to(summed16[None, :fine], (16, fine, width))
     held = exchange(spread, second_groups())
-    back = cross(back, 16)
-    held, back = lax.optimization_barrier((held, back))
     whole = jnp.concatenate([held.reshape(depth, width), extras], axis=0)
     whole = exchange(jnp.broadcast_to(whole[None], (blocks, depth + 8, width)), first_groups())
-    in_place = (miss_dest[:, 0] ^ me) * per + ranks(miss_dest[:, 0])
-    back = cross(back, 4)
-    rows_new = refilled(evict_slot, in_place, back.reshape(spots, width), rows_new)
-    fetched_accum = picked(back[:, per - 1, :per].reshape(-1), in_place)
-    filled = evict_slot[:, None] == jnp.arange(cells, dtype=jnp.int32)[None, :]
-    filled_sum = jnp.sum(jnp.where(filled, fetched_accum[:, None], 0.0), axis=0)
-    accum_new = jnp.where(jnp.any(filled, axis=0), filled_sum, accum_new.reshape(cells))
-    whole, rows_new, accum_new = lax.optimization_barrier((whole, rows_new, accum_new))
     clipped_proj, clipped_vecs, loss_row = normalized(core, whole, swap_cores(whole))
     loss = loss_row[0, 0] / (count * 256)
     return (rows_new, accum_new, table_new, accum_table, clipped_proj, clipped_vecs, loss)

time: 143 us -> 151 us (1.056)
  blocking collectives: 0 us -> 21.8 us
  starting transfers between devices: 49.1 us -> 39.7 us
  local copies, waits for them, and re-layouts: 12.4 us -> 5.03 us
  Pallas kernels: 32.4 us -> 39.2 us
  waiting for transfers between devices: 40 us -> 35.1 us
    ppermute x5 -> x0, waiting for transfers between devices: 32.8 us -> none  [cross(): came = lax.ppermute(split[:, 1], AXES, there)]
    all_to_all x0 -> x1, blocking collectives: none -> 21.8 us  [exchange(): lax.all_to_all(value, AXES, split_axis=0, concat_axis=0, tiled=True, axis...]
    all_to_all x4 -> x3, waiting for transfers between devices: 4.91 us -> 24.8 us  [exchange(): lax.all_to_all(value, AXES, split_axis=0, concat_axis=0, tiled=True, axis...]
    pallas_call x1 -> x2, Pallas kernels: 2.63 us -> 14.1 us  [the longest x1 8.08 us: pool(): pl.pallas_call(pool_kernel, out_shape=jax.ShapeDtypeStruct((feats, count,...]
    all_to_all x4 -> x3, starting transfers between devices: 28.9 us -> 19.7 us  [exchange(): lax.all_to_all(value, AXES, split_axis=0, concat_axis=0, tiled=True, axis...]
    ppermute x5 -> x0, starting transfers between devices: 8.88 us -> none  [cross(): came = lax.ppermute(split[:, 1], AXES, there)]
    all_to_all x0 -> x1, starting transfers between devices: none -> 5 us  [shards(): lax.all_to_all(reply.reshape(owners, per, width), 'table', split_axis=0,...]
    pallas_call x1, Pallas kernels: 12.3 us -> 7.34 us  [dense(): pl.pallas_call(dense_kernel, out_shape=(jax.ShapeDtypeStruct(bundle, f32)...]
  transfers between devices with their start and end apart: 12 -> 7, of which waited for: 7 -> 5; matrix products, arithmetic and copies ran while one was open for 6% -> 2% of each run, Pallas kernels for 19% -> 19%
where the time goes in v7:
time: 151 us; the launch traced here: 148 us
  starting transfers between devices  39.7 us (26%)
  Pallas kernels  39.2 us (26%)
  waiting for transfers between devices  35.1 us (23%)
  blocking collectives  21.8 us (14%)
  other arithmetic  5.59 us (4%)
  local copies, waits for them, and re-layouts  5.03 us (3%)
  between operations  2 us (1%)
    all_to_all x3, waiting for transfers between devices, exchange(): lax.all_to_all(value, AXES, split_axis=0, concat_axis=0, tiled=True, axis...  24.8 us
    all_to_all x1, blocking collectives, exchange(): lax.all_to_all(value, AXES, split_axis=0, concat_axis=0, tiled=True, axis...  21.8 us
    all_to_all x3, starting transfers between devices, exchange(): lax.all_to_all(value, AXES, split_axis=0, concat_axis=0, tiled=True, axis...  19.7 us
    all_to_all x1, starting transfers between devices, shards(): got = lax.all_to_all(sent, 'table', split_axis=0, concat_axis=0, tiled=True)  10.3 us
    pallas_call x1, Pallas kernels, updated(): pl.pallas_call(update_kernel, out_shape=(jax.ShapeDtypeStruct(cache_rows....  9.73 us
    pallas_call x1, Pallas kernels, pool(): pl.pallas_call(pool_kernel, out_shape=jax.ShapeDtypeStruct((feats, count,...  8.08 us
    pallas_call x1, Pallas kernels, dense(): pl.pallas_call(dense_kernel, out_shape=(jax.ShapeDtypeStruct(bundle, f32)...  7.34 us
    pallas_call x1, Pallas kernels, replied(): pl.pallas_call(reply_kernel, out_shape=(jax.ShapeDtypeStruct((owners * pe...  6.01 us
  transfers between devices with their start and end apart: 7, of which 5 were waited for; matrix products, arithmetic and copies ran while one was open for 2% of the time, Pallas kernels for 19%

profile of v7, /device:TPU:3, one launch (start us, length us, event | category | flops | bytes accessed | tf_op | source)
XLA Modules:
  0.0 148.4 jit_solution(2054601535156943376)
XLA Ops:
  0.6 2.9 %payload.1 = f32[256,256]{1,0:T(8,128)} custom-call(s32[64]{0:T(128)} %evict_ref.1, s32[2,64]{1,0:T(2,128)} %bitcast.43, s32[2,64]{1,0:T(2,128)} %bitcast.44, f32[1024]{0:T(1024)} %accum_ref.1, f32[1024,256]{1,0:T(8,128)} %cache_ref.1), custom_call_target="tpu_custom_call" | custom-call | flops 100000 | bytes 1500000 | tf_op jit(solution)/shard_map/payload/pallas_call | solution.py:365
  3.6 10.3 %all-to-all-start = ((f32[32,8,256]{2,1,0:T(8,128)}), f32[32,8,256]{2,1,0:T(8,128)S(1)}, u32[]{:S(2)}, u32[]{:S(2)}) async-start(f32[32,8,256]{2,1,0:T(8,128)} %bitcast.35), calls=%async_computation | async-start | bytes 524288 | tf_op jit(solution)/shard_map/all_to_all | solution.py:673
  13.9 8.1 %pool.1.pooled_any = bf16[8,256,256]{2,1,0:T(8,128)(2,1)} custom-call(s32[32,256]{1,0:T(8,128)} %bitcast.45, f32[1024,256]{1,0:T(8,128)} %cache_ref.1), custom_call_target="tpu_custom_call" | custom-call | flops 3200000000 | bytes 2000000 | tf_op jit(solution)/shard_map/pool/pallas_call | solution.py:109
  22.0 3.8 %all-to-all-done = f32[32,8,256]{2,1,0:T(8,128)S(1)} async-done(((f32[32,8,256]{2,1,0:T(8,128)}), f32[32,8,256]{2,1,0:T(8,128)S(1)}, u32[]{:S(2)}, u32[]{:S(2)}) %all-to-all-start) | async-done | bytes 262176 | tf_op jit(solution)/shard_map/all_to_all | solution.py:673
  25.8 0.1 copy.27
  25.9 0.6 slice_bitcast_fusion
  26.5 0.0 copy-done.4
  26.5 6.0 %reply.1 = (f32[256,256]{1,0:T(8,128)}, f32[1024,256]{1,0:T(8,128)}, f32[1024]{0:T(1024)}) custom-call(s32[32,24]{1,0:T(8,128)} %get-tuple-element.58.ids_ref, f32[32,8]{1,0:T(8,128)} %bitcast.40, f32[256,256]{1,0:T(8,128)} %bitcast.34, f32[1024,256]{1,0:T(8,128)} %table_any.1, f32[1024]{0:T(1024)} %accum_any.1), custom_call_target="tpu_custom_call" | custom-call | flops 100000 | bytes 3000000 | tf_op jit(solution)/shard_map/reply/pallas_call | solution.py:525
  32.5 5.0 %all-to-all-start.1 = ((f32[32,8,256]{2,1,0:T(8,128)}), f32[32,8,256]{2,1,0:T(8,128)S(1)}, u32[]{:S(2)}, u32[]{:S(2)}) async-start(f32[32,8,256]{2,1,0:T(8,128)} %bitcast.39), calls=%async_computation.1 | async-start | bytes 524288 | tf_op jit(solution)/shard_map/all_to_all | solution.py:680
  37.6 7.3 %dense.1 = (f32[8,264,256]{2,1,0:T(8,128)}, bf16[256,2048]{1,0:T(8,128)(2,1)}, bf16[256,256]{1,0:T(8,128)(2,1)}, bf16[256,256]{1,0:T(8,128)(2,1)}, f32[1,256]{1,0:T(1,128)}, /*index=5*/f32[8,8,256]{2,1,0:T(8,128)}) custom-call(s32[1]{0:T(128)} %bitcast.core_ref, s32[1,256]{1,0:T(1,128)} %bitcast.51, bf16[8,256,256]{2,1,0:T(8,128)(2,1)} %pool.1.pooled_any, ...), custom_call_target="tpu_custom_call" | custom-call | flops 1600000000 | bytes 9000000 | tf_op jit(solution)/shard_map/dense/pallas_call | solution.py:238
  44.9 4.7 %all-to-all-done.1 = f32[32,8,256]{2,1,0:T(8,128)S(1)} async-done(((f32[32,8,256]{2,1,0:T(8,128)}), f32[32,8,256]{2,1,0:T(8,128)S(1)}, u32[]{:S(2)}, u32[]{:S(2)}) %all-to-all-start.1) | async-done | bytes 262176 | tf_op jit(solution)/shard_map/all_to_all | solution.py:680
  49.6 1.5 %collective-permute-start = (f32[8,264,256]{2,1,0:T(8,128)}, f32[8,264,256]{2,1,0:T(8,128)S(1)}, u32[]{:S(2)}, u32[]{:S(2)}) collective-permute-start(f32[8,264,256]{2,1,0:T(8,128)} %get-tuple-element.44), channel_id=1, source_target_pairs={{0,1},{1,0},{2,3},{3,2},{4,5},{5,4},{6,7},{7,6},{8,9},{9,8},{10,11... | collective-permute-start | bytes 6488072 | tf_op jit(solution)/shard_map/ppermute | solution.py:40
  51.1 1.2 copy-done
  52.3 0.9 copy-done.1
  53.2 0.9 copy-done.2
  54.1 0.8 copy-done.3
  55.0 0.5 kept.1
  55.4 0.0 collective-permute-done
  55.5 1.6 %add.13 = f32[8,264,256]{2,1,0:T(8,128)} add(f32[8,264,256]{2,1,0:T(8,128)S(1)} %kept.1, f32[8,264,256]{2,1,0:T(8,128)S(1)} %collective-permute-done) | non-fusion elementwise | flops 540672 | bytes 6488064 | tf_op jit(solution)/shard_map/add | solution.py:692
  57.1 6.5 %all-to-all-start.2 = ((f32[8,264,256]{2,1,0:T(8,128)}), f32[8,264,256]{2,1,0:T(8,128)S(1)}, u32[]{:S(2)}, u32[]{:S(2)}) async-start(f32[8,264,256]{2,1,0:T(8,128)} %add.13), calls=%async_computation.2 | async-start | bytes 4325376 | tf_op jit(solution)/shard_map/all_to_all | solution.py:44
  63.6 0.0 copy-done.8
  63.6 0.2 convert_reduce_fusion
  63.8 0.0 copy-start.6
  63.8 15.2 %all-to-all-done.2 = f32[8,264,256]{2,1,0:T(8,128)S(1)} async-done(((f32[8,264,256]{2,1,0:T(8,128)}), f32[8,264,256]{2,1,0:T(8,128)S(1)}, u32[]{:S(2)}, u32[]{:S(2)}) %all-to-all-start.2) | async-done | bytes 2162720 | tf_op jit(solution)/shard_map/all_to_all | solution.py:44
  79.0 0.2 reduce_sum.47
  79.2 0.8 pad_maximum_fusion
  80.0 4.1 %all-to-all-start.3 = ((f32[16,24,256]{2,1,0:T(8,128)}), f32[16,24,256]{2,1,0:T(8,128)S(1)}, u32[]{:S(2)}, u32[]{:S(2)}) async-start(f32[16,24,256]{2,1,0:T(8,128)} %pad_maximum_fusion), calls=%async_computation.3 | async-start | bytes 786432 | tf_op jit(solution)/shard_map/all_to_all | solution.py:44
  84.1 0.0 copy-done.6
  84.1 0.0 copy-start.7
  84.1 0.1 fusion
  84.3 0.5 multiply_add_fusion.place_ref
  84.8 0.0 copy-done.5
  84.8 0.1 slice_reduce_fusion
  84.8 0.1 broadcast_in_dim.77
  84.9 9.7 %update.1 = (f32[1024,256]{1,0:T(8,128)}, f32[1,1024]{1,0:T(1,128)}) custom-call(s32[32,256]{1,0:T(8,128)} %bitcast.46, s32[64]{0:T(128)} %evict_ref.1, s32[64]{0:T(128)} %multiply_add_fusion.place_ref, f32[1024,256]{1,0:T(8,128)} %cache_ref.1, f32[1,1024]{1,0:T(1,128)} %bitcast.41, bf16[256,256]{1,0:T(8,128)(2,1)} %get-tuple-element.39.latent_ref, ...), custom_call_target="tpu_custom_call" | custom-call | flops 1100000000 | bytes 4000000 | tf_op jit(solution)/shard_map/update/pallas_call | solution.py:435
  94.7 0.2 select_reduce_fusion.1
  94.8 0.1 select_reduce_fusion
  95.0 1.3 select_n.22
  96.2 0.0 all-to-all-done.3
  96.3 0.7 broadcast_in_dim.82
  97.0 9.1 %all-to-all-start.4 = ((f32[16,16,256]{2,1,0:T(8,128)}), f32[16,16,256]{2,1,0:T(8,128)S(1)}, u32[]{:S(2)}, u32[]{:S(2)}) async-start(f32[16,16,256]{2,1,0:T(8,128)} %broadcast_in_dim.82), calls=%async_computation.4 | async-start | bytes 524288 | tf_op jit(solution)/shard_map/all_to_all | solution.py:44
  106.1 9.5 %all-to-all-done.4 = f32[16,16,256]{2,1,0:T(8,128)S(1)} async-done(((f32[16,16,256]{2,1,0:T(8,128)}), f32[16,16,256]{2,1,0:T(8,128)S(1)}, u32[]{:S(2)}, u32[]{:S(2)}) %all-to-all-start.4) | async-done | bytes 262176 | tf_op jit(solution)/shard_map/all_to_all | solution.py:44
  115.7 0.1 broadcast_in_dim.83
  115.8 21.8 %all_to_all.30.half_any = f32[8,264,256]{2,1,0:T(8,128)S(1)} all-to-all(f32[8,264,256]{2,1,0:T(8,128)S(1)} %broadcast_in_dim.83), channel_id=1, replica_groups={{0,2,32,34,64,66,96,98},{4,6,36,38,68,70,100,102},{8,10,40,42,72,74,104..., dimensions={0} | all-to-all | bytes 4325376 | tf_op jit(solution)/shard_map/all_to_all | solution.py:44
  137.6 3.2 %collective-permute-start.1 = (f32[8,264,256]{2,1,0:T(8,128)S(1)}, f32[8,264,256]{2,1,0:T(8,128)S(1)}, u32[]{:S(2)}, u32[]{:S(2)}) collective-permute-start(f32[8,264,256]{2,1,0:T(8,128)S(1)} %all_to_all.30.half_any), channel_id=1, source_target_pairs={{0,1},{1,0},{2,3},{3,2},{4,5},{5,4},{6,7},{7,6},{8,9},{9,8},{10,11... | collective-permute-start | bytes 6488072 | tf_op jit(solution)/shard_map/ppermute | solution.py:40
  140.8 2.0 %scale_own.1.proj_in = f32[2,2048,256]{2,1,0:T(8,128)} custom-call(s32[1]{0:T(128)} %bitcast.core_ref, f32[8,264,256]{2,1,0:T(8,128)S(1)} %all_to_all.30.half_any), custom_call_target="tpu_custom_call" | custom-call | tf_op jit(solution)/shard_map/scale_own/pallas_call | solution.py:622
  142.8 1.9 %collective-permute-done.1.half_any = f32[8,264,256]{2,1,0:T(8,128)S(1)} collective-permute-done((f32[8,264,256]{2,1,0:T(8,128)S(1)}, f32[8,264,256]{2,1,0:T(8,128)S(1)}, u32[]{:S(2)}, u32[]{:S(2)}) %collective-permute-start.1) | collective-permute-done | bytes 2162720 | tf_op jit(solution)/shard_map/ppermute | solution.py:40
  144.7 2.6 %scale_other.1 = (f32[2,2048,256]{2,1,0:T(8,128)}, f32[2,2048]{1,0:T(2,128)}, f32[1,128]{1,0:T(1,128)S(1)}) custom-call(s32[1]{0:T(128)} %bitcast.core_ref, f32[2,2048,256]{2,1,0:T(8,128)} %scale_own.1.proj_in, f32[8,8,256]{2,1,0:T(8,128)S(1)} %slice.47.own_ref, f32[8,264,256]{2,1,0:T(8,128)S(1)} %collective-permute-done.1.half_any), custom_call_target="tpu_custom_call", output_to_operand_aliasing={{0}: (1, {})} | custom-call | tf_op jit(solution)/shard_map/scale_other/pallas_call | solution.py:631
  (18 shorter events, 0.1 us)
Async XLA Ops:
  3.6 22.2 %all-to-all-start = ((f32[32,8,256]{2,1,0:T(8,128)}), f32[32,8,256]{2,1,0:T(8,128)S(1)}, u32[]{:S(2)}, u32[]{:S(2)}) async-start(f32[32,8,256]{2,1,0:T(8,128)} %bitcast.35), calls=%async_computation | async-start | bytes 524288 | tf_op jit(solution)/shard_map/all_to_all | solution.py:673
  25.8 0.7 copy-start.4
  32.5 17.0 %all-to-all-start.1 = ((f32[32,8,256]{2,1,0:T(8,128)}), f32[32,8,256]{2,1,0:T(8,128)S(1)}, u32[]{:S(2)}, u32[]{:S(2)}) async-start(f32[32,8,256]{2,1,0:T(8,128)} %bitcast.39), calls=%async_computation.1 | async-start | bytes 524288 | tf_op jit(solution)/shard_map/all_to_all | solution.py:680
  49.6 35.2 %copy-start.5 = (f32[32,8,256]{2,1,0:T(8,128)}, f32[32,8,256]{2,1,0:T(8,128)S(1)}, u32[]{:S(2)}) copy-start(f32[32,8,256]{2,1,0:T(8,128)S(1)} %all-to-all-done.1) | copy-start | bytes 786436
  49.6 5.9 %collective-permute-start = (f32[8,264,256]{2,1,0:T(8,128)}, f32[8,264,256]{2,1,0:T(8,128)S(1)}, u32[]{:S(2)}, u32[]{:S(2)}) collective-permute-start(f32[8,264,256]{2,1,0:T(8,128)} %get-tuple-element.44), channel_id=1, source_target_pairs={{0,1},{1,0},{2,3},{3,2},{4,5},{5,4},{6,7},{7,6},{8,9},{9,8},{10,11... | collective-permute-start | bytes 6488072 | tf_op jit(solution)/shard_map/ppermute | solution.py:40
  51.1 1.2 copy-start
  52.3 0.9 copy-start.1
  53.2 0.9 copy-start.2
  54.1 0.8 copy-start.3
  57.1 6.5 %copy-start.8 = (s32[64,2]{0,1:T(2,128)S(1)}, s32[64,2]{0,1:T(2,128)}, u32[]{:S(2)}) copy-start(s32[64,2]{0,1:T(2,128)} %param.19) | copy-start | bytes 1540
  57.1 21.9 %all-to-all-start.2 = ((f32[8,264,256]{2,1,0:T(8,128)}), f32[8,264,256]{2,1,0:T(8,128)S(1)}, u32[]{:S(2)}, u32[]{:S(2)}) async-start(f32[8,264,256]{2,1,0:T(8,128)} %add.13), calls=%async_computation.2 | async-start | bytes 4325376 | tf_op jit(solution)/shard_map/all_to_all | solution.py:44
  63.8 20.4 %copy-start.6 = (s32[64]{0:T(128)S(1)}, s32[64]{0:T(128)}, u32[]{:S(2)}) copy-start(s32[64]{0:T(128)} %evict_ref.1) | copy-start | bytes 772
  80.0 16.2 %all-to-all-start.3 = ((f32[16,24,256]{2,1,0:T(8,128)}), f32[16,24,256]{2,1,0:T(8,128)S(1)}, u32[]{:S(2)}, u32[]{:S(2)}) async-start(f32[16,24,256]{2,1,0:T(8,128)} %pad_maximum_fusion), calls=%async_computation.3 | async-start | bytes 786432 | tf_op jit(solution)/shard_map/all_to_all | solution.py:44
  84.1 10.7 %copy-start.7 = (s32[64]{0:T(128)S(1)}, s32[64]{0:T(128)}, u32[]{:S(2)}) copy-start(s32[64]{0:T(128)} %evict_ref.1) | copy-start | bytes 772
  97.0 18.6 %all-to-all-start.4 = ((f32[16,16,256]{2,1,0:T(8,128)}), f32[16,16,256]{2,1,0:T(8,128)S(1)}, u32[]{:S(2)}, u32[]{:S(2)}) async-start(f32[16,16,256]{2,1,0:T(8,128)} %broadcast_in_dim.82), calls=%async_computation.4 | async-start | bytes 524288 | tf_op jit(solution)/shard_map/all_to_all | solution.py:44
  137.6 7.1 %collective-permute-start.1 = (f32[8,264,256]{2,1,0:T(8,128)S(1)}, f32[8,264,256]{2,1,0:T(8,128)S(1)}, u32[]{:S(2)}, u32[]{:S(2)}) collective-permute-start(f32[8,264,256]{2,1,0:T(8,128)S(1)} %all_to_all.30.half_any), channel_id=1, source_target_pairs={{0,1},{1,0},{2,3},{3,2},{4,5},{5,4},{6,7},{7,6},{8,9},{9,8},{10,11... | collective-permute-start | bytes 6488072 | tf_op jit(solution)/shard_map/ppermute | solution.py:40

commit v8 on v6

--- a/solution.py
+++ b/solution.py
@@ -14,26 +14,23 @@
     return (((y // 2 * 4 + x) * 2 + y % 2) * 8 + z % 8) * 2 + core
 
 
-def first_groups():
-    groups = []
-    for y in range(4):
-        for pair in range(4):
-            groups.append([device_at(y, x, 2 * pair + b, 0) for x in range(4) for b in range(2)])
-    for x in range(4):
-        for pair in range(4):
-            groups.append([device_at(y, x, 2 * pair + 1 + b, 1) for y in range(4) for b in range(2)])
-    return groups
-
-
-def second_groups():
-    groups = []
-    for x in range(4):
-        for b in range(2):
-            groups.append([device_at(y, x, 2 * k + b, 0) for y in range(4) for k in range(4)])
-    for y in range(4):
-        for b in range(2):
-            groups.append([device_at(y, x, 2 * k + b, 1) for x in range(4) for k in range(4)])
-    return groups
+def plane_groups():
+    return [
+        [device_at(y, x, 2 * pair + core + b, core) for y in range(4) for x in range(4) for b in (0, 1)]
+        for core in range(2)
+        for pair in range(4)
+    ]
+
+
+def shift_z(value, step):
+    there = [
+        (device_at(y, x, z, core), device_at(y, x, z + step, core))
+        for y in range(4)
+        for x in range(4)
+        for z in range(8)
+        for core in range(2)
+    ]
+    return lax.ppermute(value, AXES, there)
 
 
 def swap_cores(value):
@@ -68,6 +65,15 @@
     there = [(i, i ^ bit) for i in range(256)]
     came = lax.ppermute(split[:, 1], AXES, there)
     return jnp.stack([split[:, 0], came], axis=1).reshape(value.shape)
+
+
+def put_blocks(ref, c, grad):
+    half = grad.shape[1] // 2
+    rows = grad.shape[0] // 4
+    for q in range(4):
+        part = grad[q * rows : (q + 1) * rows, :]
+        ref[4 * c + q, :rows, :] = part[:, :half]
+        ref[4 * c + q, rows : 2 * rows, :] = part[:, half:]
 
 
 def dense_kernel(
@@ -163,7 +169,8 @@
     dlogit_ref[...] = jnp.transpose(dlogit)
 
     mine = core_ref[0] == 0
-    lane1 = lax.broadcasted_iota(jnp.int32, (1, width), 1)
+    half = width // 2
+    lane1 = lax.broadcasted_iota(jnp.int32, (1, half), 1)
     loss_row = jnp.where(lane1 == 0, loss, 0.0)
     back = jnp.zeros((count, width), f32)
     for c, cut in enumerate(cuts):
@@ -175,12 +182,17 @@
         lift = lift.astype(bf16)
         dlift[:, cut] = lift
         back = back + jnp.dot(lift, u_ref[cut, :], preferred_element_type=f32)
-        extra_ref[c, 0:1, :] = jnp.where(mine, dbias, dhead)
-        extra_ref[c, 1:2, :] = loss_row
-        extra_ref[c, 2:8, :] = jnp.zeros((6, width), f32)
-        send_ref[c, width : width + 1, :] = jnp.where(mine, dhead, dbias)
-        send_ref[c, width + 1 : width + 2, :] = loss_row
-        send_ref[c, width + 2 : width + 8, :] = jnp.zeros((6, width), f32)
+        for ref, row in (
+            (extra_ref, jnp.where(mine, dbias, dhead)),
+            (send_ref, jnp.where(mine, dhead, dbias)),
+        ):
+            top = ref.shape[1] - 8
+            for q in range(4):
+                at = 4 * c + q
+                ref[at, top : top + 8, :] = jnp.zeros((8, half), f32)
+                ref[at, top + 1 : top + 2, :] = loss_row
+                if q % 2 == 0:
+                    ref[at, top : top + 1, :] = row[:, q // 2 * half : (q // 2 + 1) * half]
         left[:, cut] = jnp.where(mine, lift, pooled[:, cut])
     dlatent = back.astype(bf16)
     dlatent_ref[...] = dlatent
@@ -188,13 +200,17 @@
     copies[0].start()
     right = jnp.where(mine, dlatent, latent)
     for c, cut in enumerate(cuts):
-        send_ref[c, :width, :] = lax.dot_general(
+        grad = lax.dot_general(
             jnp.where(mine, pooled[:, cut], dlift[:, cut]),
             right,
             (((0,), (0,)), ((), ())),
             preferred_element_type=f32,
         )
-        copies.append(pltpu.make_async_copy(send_ref.at[c], send_out.at[c], out_sems.at[c]))
+        put_blocks(send_ref, c, grad)
+        four = pl.ds(4 * c, 4)
+        copies.append(
+            pltpu.make_async_copy(send_ref.at[four], send_out.at[four], out_sems.at[c])
+        )
         copies[-1].start()
     for copy in copies:
         copy.wait()
@@ -207,7 +223,7 @@
     f32, bf16 = jnp.float32, jnp.bfloat16
     vmem = pl.BlockSpec(memory_space=pltpu.VMEM)
     anywhere = pl.BlockSpec(memory_space=pl.ANY)
-    bundle = (blocks, width + 8, width)
+    bundle = (4 * blocks, width // 2 + 8, width // 2)
     return pl.pallas_call(
         dense_kernel,
         out_shape=(
@@ -216,7 +232,7 @@
             jax.ShapeDtypeStruct((count, width), bf16),
             jax.ShapeDtypeStruct((count, width), bf16),
             jax.ShapeDtypeStruct((1, count), f32),
-            jax.ShapeDtypeStruct((blocks, 8, width), f32),
+            jax.ShapeDtypeStruct((4 * blocks, 8, width // 2), f32),
         ),
         in_specs=[pl.BlockSpec(memory_space=pltpu.SMEM)]
         + [vmem] * 2
@@ -258,22 +274,23 @@
 def keep_kernel(core_ref, left_ref, latent_ref, dlatent_ref, extra_ref, keep_ref):
     width = latent_ref.shape[1]
     right = jnp.where(core_ref[0] == 0, latent_ref[...], dlatent_ref[...])
-    for c in range(keep_ref.shape[0]):
-        keep_ref[c, :width, :] = lax.dot_general(
+    for c in range(keep_ref.shape[0] // 4):
+        grad = lax.dot_general(
             left_ref[:, c * width : (c + 1) * width],
             right,
             (((0,), (0,)), ((), ())),
             preferred_element_type=jnp.float32,
         )
-        keep_ref[c, width : width + 8, :] = extra_ref[c]
+        put_blocks(keep_ref, c, grad)
+    keep_ref[:, width // 2 :, :] = extra_ref[...]
 
 
 def kept(core, left, latent, dlatent, extra):
-    blocks, _, width = extra.shape
+    blocks, _, half = extra.shape
     vmem = pl.BlockSpec(memory_space=pltpu.VMEM)
     return pl.pallas_call(
         keep_kernel,
-        out_shape=jax.ShapeDtypeStruct((blocks, width + 8, width), jnp.float32),
+        out_shape=jax.ShapeDtypeStruct((blocks, half + 8, half), jnp.float32),
         in_specs=[pl.BlockSpec(memory_space=pltpu.SMEM)] + [vmem] * 4,
         out_specs=vmem,
         compiler_params=pltpu.CompilerParams(vmem_limit_bytes=16 * 1024 * 1024),
@@ -441,21 +458,27 @@
 
 
 def scaled(index, half_any, proj_ref, half, stage, in_sems, out_sems):
-    blocks, width = half.shape[0], half.shape[2]
+    chunks, width = stage.shape[0], stage.shape[2]
+    edge, rows = width // 2, width // 4
     loads = []
-    for c in range(blocks):
-        loads.append(pltpu.make_async_copy(half_any.at[c], half.at[c], in_sems.at[c]))
+    for c in range(chunks):
+        four = pl.ds(4 * c, 4)
+        loads.append(pltpu.make_async_copy(half_any.at[four], half.at[four], in_sems.at[c]))
         loads[-1].start()
-    squares = jnp.zeros((width, width), jnp.float32)
-    for c in range(blocks):
+    squares = jnp.zeros((edge, edge), jnp.float32)
+    for c in range(chunks):
         loads[c].wait()
-        block = half[c, :width, :]
-        squares = squares + block * block
+        for q in range(4):
+            block = half[4 * c + q, :edge, :]
+            squares = squares + block * block
     total = jnp.sum(jnp.sum(squares, axis=0, keepdims=True), axis=1, keepdims=True)
-    scale = lax.rsqrt(total / (blocks * width * width) + EPS)
+    scale = lax.rsqrt(total / (chunks * width * width) + EPS)
     copies = []
-    for c in range(blocks):
-        stage[c] = half[c, :width, :] * scale
+    for c in range(chunks):
+        for q in range(4):
+            at = slice(q * rows, (q + 1) * rows)
+            stage[c, at, :edge] = half[4 * c + q, :rows, :] * scale
+            stage[c, at, edge:] = half[4 * c + q, rows:edge, :] * scale
         copies.append(
             pltpu.make_async_copy(
                 stage.at[c], proj_ref.at[index, pl.ds(c * width, width), :], out_sems.at[c]
@@ -485,35 +508,35 @@
 ):
     core = core_ref[0]
     copies = scaled(1 - core, half_any, proj_ref, half, stage, in_sems, out_sems)
-    blocks, width = half.shape[0], half.shape[2]
+    edge = half.shape[2]
+    tiles = vec_ref.shape[1] // edge
     mine = core == 0
-    own = [own_ref[c, 0:1, :] for c in range(blocks)]
-    far = [half[c, width : width + 1, :] for c in range(blocks)]
+    own = [own_ref[2 * t, 0:1, :] for t in range(tiles)]
+    far = [half[2 * t, edge : edge + 1, :] for t in range(tiles)]
     for index in (0, 1):
         rows = [jnp.where(mine, *((a, b) if index == 0 else (b, a))) for a, b in zip(own, far)]
         squares = sum(row * row for row in rows)
         total = jnp.sum(squares, axis=1, keepdims=True)
-        scale = lax.rsqrt(total / (blocks * width) + EPS)
-        for c in range(blocks):
-            vec_ref[index : index + 1, c * width : (c + 1) * width] = rows[c] * scale
-    loss_ref[...] = jnp.where(
-        mine, half[0, width + 1 : width + 2, :128], own_ref[0, 1:2, :128]
-    )
+        scale = lax.rsqrt(total / (tiles * edge) + EPS)
+        for t in range(tiles):
+            vec_ref[index : index + 1, t * edge : (t + 1) * edge] = rows[t] * scale
+    loss_ref[...] = jnp.where(mine, half[0, edge + 1 : edge + 2, :], own_ref[0, 1:2, :])
     for copy in copies:
         copy.wait()
 
 
 def normalized(core, own, other):
-    blocks, depth, width = own.shape
-    wide = blocks * width
+    blocks, depth, edge = own.shape
+    chunks, width = blocks // 4, 2 * edge
+    wide = chunks * width
     smem = pl.BlockSpec(memory_space=pltpu.SMEM)
     vmem = pl.BlockSpec(memory_space=pltpu.VMEM)
     anywhere = pl.BlockSpec(memory_space=pl.ANY)
     scratch = [
-        pltpu.VMEM((blocks, depth, width), jnp.float32),
-        pltpu.VMEM((blocks, width, width), jnp.float32),
-        pltpu.SemaphoreType.DMA((blocks,)),
-        pltpu.SemaphoreType.DMA((blocks,)),
+        pltpu.VMEM(own.shape, jnp.float32),
+        pltpu.VMEM((chunks, width, width), jnp.float32),
+        pltpu.SemaphoreType.DMA((chunks,)),
+        pltpu.SemaphoreType.DMA((chunks,)),
     ]
     proj = jax.ShapeDtypeStruct((2, wide, width), jnp.float32)
     limit = pltpu.CompilerParams(vmem_limit_bytes=16 * 1024 * 1024)
@@ -539,7 +562,7 @@
         input_output_aliases={1: 0},
         compiler_params=limit,
         name="scale_other",
-    )(core[None], half, own[:, width:, :], other)
+    )(core[None], half, own[:, edge:, :], other)
 
 
 def shards(
@@ -579,8 +602,6 @@
         core, slots_late, labels, cache_rows, proj_u, proj_v, cross_bias, head
     )
 
-    blocks = feats
-    depth = width
     send, got = lax.optimization_barrier((send, got))
     held = kept(core, left, latent, dlatent, extra) + swap_cores(send)
     held, got = lax.optimization_barrier((held, got))
@@ -605,20 +626,8 @@
     reply_accum = picked(accum_table, asked).reshape(owners, per)
     back = jnp.where(is_meta, meta_row([reply_accum], width), reply_rows)
 
-    held = exchange(held, first_groups())
-    back = cross(cross(back, 1), 8)
-    held, back = lax.optimization_barrier((held, back))
-    held = jnp.sum(held, axis=0)
-    fine = depth // 16
-    pieces16 = jnp.concatenate(
-        [
-            held[:depth].reshape(16, fine, width),
-            jnp.broadcast_to(held[None, depth:], (16, 8, width)),
-        ],
-        axis=1,
-    )
-    held = exchange(pieces16, second_groups())
-    back = cross(back, 2)
+    held = exchange(held, plane_groups())
+    back = cross(cross(cross(back, 1), 16), 2)
     rows_new, accum_new = updated(
         slot_ids,
         cache_rows,
@@ -629,16 +638,13 @@
     held, back, rows_new, accum_new = lax.optimization_barrier(
         (held, back, rows_new, accum_new)
     )
-    summed16 = jnp.sum(held, axis=0)
-    extras = summed16[fine:]
-    spread = jnp.broadcast_to(summed16[None, :fine], (16, fine, width))
-    held = exchange(spread, second_groups())
-    back = cross(back, 16)
-    held, back = lax.optimization_barrier((held, back))
-    whole = jnp.concatenate([held.reshape(depth, width), extras], axis=0)
-    whole = exchange(jnp.broadcast_to(whole[None], (blocks, depth + 8, width)), first_groups())
+    held = jnp.sum(held, axis=0)
+    held = (held + shift_z(held, 4)) + (shift_z(held, 2) + shift_z(held, -2))
+    whole = jnp.broadcast_to(held[None], (4 * feats, *held.shape))
+    whole, back = lax.optimization_barrier((whole, back))
+    whole = exchange(whole, plane_groups())
+    back = cross(cross(back, 4), 8)
     in_place = (miss_dest[:, 0] ^ me) * per + ranks(miss_dest[:, 0])
-    back = cross(back, 4)
     rows_new = refilled(evict_slot, in_place, back.reshape(spots, width), rows_new)
     fetched_accum = picked(back[:, per - 1, :per].reshape(-1), in_place)
     filled = evict_slot[:, None] == jnp.arange(cells, dtype=jnp.int32)[None, :]

time: 143 us -> 157 us (1.098)
  the two profiles are of different devices: /device:TPU:3 before, /device:TPU:13 now
where the time goes in v8:
time: 157 us; the launch traced here: 156 us
  starting transfers between devices  46.7 us (30%)
  waiting for transfers between devices  42.5 us (27%)
  Pallas kernels  32.5 us (21%)
  local copies, waits for them, and re-layouts  20.7 us (13%)
  other arithmetic  11.5 us (7%)
  between operations  2.16 us (1%)
    ppermute x5, waiting for transfers between devices, cross(): came = lax.ppermute(split[:, 1], AXES, there)  35.8 us
    all_to_all x2, starting transfers between devices, exchange(): lax.all_to_all(value, AXES, split_axis=0, concat_axis=0, tiled=True, axis...  24.7 us
    pallas_call x1, Pallas kernels, dense(): pl.pallas_call(dense_kernel, out_shape=(jax.ShapeDtypeStruct(bundle, f32)...  12.4 us
    all_to_all x1, starting transfers between devices, shards(): got = lax.all_to_all(sent, 'table', split_axis=0, concat_axis=0, tiled=True)  10.4 us
    pallas_call x1, Pallas kernels, updated(): pl.pallas_call(update_kernel, out_shape=(jax.ShapeDtypeStruct(cache_rows....  9.38 us
    ppermute x3, starting transfers between devices, shift_z(): return lax.ppermute(value, AXES, there)  7.08 us
    unnamed x28, local copies, waits for them, and re-layouts  4.58 us
    ppermute x3, waiting for transfers between devices, shift_z(): return lax.ppermute(value, AXES, there)  4.41 us
  transfers between devices with their start and end apart: 13, of which 7 were waited for; matrix products, arithmetic and copies ran while one was open for 16% of the time, Pallas kernels for 17%

profile of v8, /device:TPU:13, one launch (start us, length us, event | category | flops | bytes accessed | tf_op | source)
XLA Modules:
  0.0 156.0 jit_solution(14377177473332319336)
XLA Ops:
  0.6 2.9 %payload.1 = f32[256,256]{1,0:T(8,128)} custom-call(s32[64]{0:T(128)} %evict_ref.1, s32[2,64]{1,0:T(2,128)} %bitcast.81, s32[2,64]{1,0:T(2,128)} %bitcast.79, f32[1024]{0:T(1024)} %accum_ref.1, f32[1024,256]{1,0:T(8,128)} %cache_ref.1), custom_call_target="tpu_custom_call" | custom-call | flops 100000 | bytes 1500000 | tf_op jit(solution)/shard_map/payload/pallas_call | solution.py:360
  3.6 10.4 %all-to-all-start = ((f32[32,8,256]{2,1,0:T(8,128)}), f32[32,8,256]{2,1,0:T(8,128)S(1)}, u32[]{:S(2)}, u32[]{:S(2)}) async-start(f32[32,8,256]{2,1,0:T(8,128)} %bitcast.65), calls=%async_computation | async-start | bytes 524288 | tf_op jit(solution)/shard_map/all_to_all | solution.py:597
  14.0 12.4 %dense.1 = (f32[32,136,128]{2,1,0:T(8,128)}, bf16[256,2048]{1,0:T(8,128)(2,1)}, bf16[256,256]{1,0:T(8,128)(2,1)}, bf16[256,256]{1,0:T(8,128)(2,1)}, f32[1,256]{1,0:T(1,128)}, /*index=5*/f32[32,8,128]{2,1,0:T(8,128)}) custom-call(s32[1]{0:T(128)} %bitcast.core_ref, s32[32,256]{1,0:T(8,128)} %bitcast.82, s32[1,256]{1,0:T(1,128)} %bitcast.88, ...), custom_call_target="tpu_custom_call" | custom-call | flops 5000000000 | bytes 9000000 | tf_op jit(solution)/shard_map/dense/pallas_call | solution.py:227
  26.9 1.2 copy-done
  28.1 0.9 copy-done.1
  29.0 0.9 copy-done.2
  29.9 0.9 copy-done.3
  31.3 1.6 %add.35 = f32[32,136,128]{2,1,0:T(8,128)} add(f32[32,136,128]{2,1,0:T(8,128)S(1)} %kept.1, f32[32,136,128]{2,1,0:T(8,128)S(1)} %collective-permute-done) | non-fusion elementwise | flops 557056 | bytes 6684672 | tf_op jit(solution)/shard_map/add | solution.py:606
  32.9 9.3 %all-to-all-start.1 = ((f32[32,136,128]{2,1,0:T(8,128)}), f32[32,136,128]{2,1,0:T(8,128)S(1)}, u32[]{:S(2)}, u32[]{:S(2)}) async-start(f32[32,136,128]{2,1,0:T(8,128)} %add.35), calls=%async_computation.1 | async-start | bytes 4456448 | tf_op jit(solution)/shard_map/all_to_all | solution.py:41
  42.8 0.7 iota_compare_fusion.5
  43.5 0.7 slice.79
  44.8 0.7 eq.102
  45.4 0.7 reshape.141
  46.1 0.8 copy.40
  46.9 1.4 broadcast_in_dim.147
  48.3 0.8 select_reduce_fusion.3
  49.1 0.7 convert_element_type.27
  49.7 0.9 fusion
  50.6 0.8 select_reduce_fusion.1
  51.4 0.7 select_n.69
  52.7 1.5 select_reduce_fusion
  54.2 0.8 reshape.140
  55.0 0.6 pad.4
  55.6 1.4 broadcast_in_dim.152
  57.0 1.4 copy.41
  58.4 0.7 reshape.160
  59.1 0.7 compare_select_fusion
  59.8 2.0 %scatter_fusion = f32[1024,256]{1,0:T(8,128)S(1)} fusion(f32[1024,256]{1,0:T(8,128)S(1)} %copy-done.5, s32[192]{0:T(256)S(1)} %bitcast.78, f32[192,256]{1,0:T(8,128)} %reshape.160), kind=kCustom, calls=%fused_computation.1 | custom fusion | bytes 590592 | tf_op jit(solution)/shard_map/scatter | solution.py:612
  61.8 1.0 gather_fusion
  62.8 0.8 copy_select_fusion
  63.8 1.3 collective-permute-done.1
  65.6 4.7 %collective-permute-done.2 = f32[1,16,8,256]{3,2,1,0:T(8,128)S(1)} collective-permute-done((f32[1,16,8,256]{3,2,1,0:T(8,128)S(1)}, f32[1,16,8,256]{3,2,1,0:T(8,128)S(1)}, u32[]{:S(2)}, u32[]{:S(2)}) %collective-permute-start.2) | collective-permute-done | bytes 131104 | tf_op jit(solution)/shard_map/ppermute | solution.py:66
  70.5 9.4 %update.1 = (f32[1024,256]{1,0:T(8,128)}, f32[1,1024]{1,0:T(1,128)}) custom-call(s32[32,256]{1,0:T(8,128)} %bitcast.83, f32[1024,256]{1,0:T(8,128)} %cache_ref.1, f32[1,1024]{1,0:T(1,128)} %bitcast.77, bf16[256,256]{1,0:T(8,128)(2,1)} %get-tuple-element.35.latent_ref, bf16[256,256]{1,0:T(8,128)(2,1)} %get-tuple-element.36.dlatent_ref, ...), custom_call_target="tpu_custom_call" | custom-call | flops 1100000000 | bytes 4000000 | tf_op jit(solution)/shard_map/update/pallas_call | solution.py:430
  80.1 2.1 %collective-permute-start.6 = (f32[136,128]{1,0:T(8,128)S(1)}, f32[136,128]{1,0:T(8,128)S(1)}, u32[]{:S(2)}, u32[]{:S(2)}) collective-permute-start(f32[136,128]{1,0:T(8,128)S(1)} %reduce_sum.68), channel_id=1, source_target_pairs={{0,12},{1,13},{2,14},{3,15},{4,0},{5,1},{6,2},{7,3},{8,4},{9,5},{1... | collective-permute-start | bytes 208904 | tf_op jit(solution)/shard_map/ppermute | solution.py:33
  82.2 0.8 collective-permute-start.5
  83.0 4.1 %collective-permute-start.4 = (f32[136,128]{1,0:T(8,128)S(1)}, f32[136,128]{1,0:T(8,128)S(1)}, u32[]{:S(2)}, u32[]{:S(2)}) collective-permute-start(f32[136,128]{1,0:T(8,128)S(1)} %reduce_sum.68), channel_id=1, source_target_pairs={{0,8},{1,9},{2,10},{3,11},{4,12},{5,13},{6,14},{7,15},{8,0},{9,1},... | collective-permute-start | bytes 208904 | tf_op jit(solution)/shard_map/ppermute | solution.py:33
  87.6 4.0 %collective-permute-done.4 = f32[136,128]{1,0:T(8,128)S(1)} collective-permute-done((f32[136,128]{1,0:T(8,128)S(1)}, f32[136,128]{1,0:T(8,128)S(1)}, u32[]{:S(2)}, u32[]{:S(2)}) %collective-permute-start.4) | collective-permute-done | bytes 69664 | tf_op jit(solution)/shard_map/ppermute | solution.py:33
  91.6 1.5 broadcast_in_dim.156
  93.1 15.3 %all-to-all-start.2 = ((f32[32,136,128]{2,1,0:T(8,128)}), f32[32,136,128]{2,1,0:T(8,128)S(1)}, u32[]{:S(2)}, u32[]{:S(2)}) async-start(f32[32,136,128]{2,1,0:T(8,128)} %broadcast_in_dim.156), calls=%async_computation.2 | async-start | bytes 4456448 | tf_op jit(solution)/shard_map/all_to_all | solution.py:41
  108.8 23.0 %collective-permute-done.7 = f32[4,4,8,256]{3,2,1,0:T(8,128)S(1)} collective-permute-done((f32[4,4,8,256]{3,2,1,0:T(8,128)S(1)}, f32[4,4,8,256]{3,2,1,0:T(8,128)S(1)}, u32[]{:S(2)}, u32[]{:S(2)}) %collective-permute-start.7) | collective-permute-done | bytes 131104 | tf_op jit(solution)/shard_map/ppermute | solution.py:66
  131.9 3.2 %collective-permute-start.8 = (f32[2,8,8,256]{3,2,1,0:T(8,128)S(1)}, f32[2,8,8,256]{3,2,1,0:T(8,128)S(1)}, u32[]{:S(2)}, u32[]{:S(2)}) collective-permute-start(f32[2,8,8,256]{3,2,1,0:T(8,128)S(1)} %get-tuple-element.60), channel_id=1, source_target_pairs={{0,8},{1,9},{2,10},{3,11},{4,12},{5,13},{6,14},{7,15},{8,0},{9,1},... | collective-permute-start | bytes 393224 | tf_op jit(solution)/shard_map/ppermute | solution.py:66
  135.7 6.7 %collective-permute-done.8 = f32[2,8,8,256]{3,2,1,0:T(8,128)S(1)} collective-permute-done((f32[2,8,8,256]{3,2,1,0:T(8,128)S(1)}, f32[2,8,8,256]{3,2,1,0:T(8,128)S(1)}, u32[]{:S(2)}, u32[]{:S(2)}) %collective-permute-start.8) | collective-permute-done | bytes 131104 | tf_op jit(solution)/shard_map/ppermute | solution.py:66
  142.5 0.7 copy.47
  143.2 2.6 %refill.1 = f32[1024,256]{1,0:T(8,128)} custom-call(s32[64]{0:T(128)} %evict_ref.1, s32[64]{0:T(128)} %multiply_add_fusion.place_ref, f32[256,256]{1,0:T(8,128)} %bitcast.62, f32[1024,256]{1,0:T(8,128)} %get-tuple-element.51.old_ref), custom_call_target="tpu_custom_call" | custom-call | flops 100000 | bytes 2000000 | tf_op jit(solution)/shard_map/refill/pallas_call | solution.py:449
  145.9 1.0 slice_reduce_fusion
  147.8 2.0 %scale_own.1.proj_in = f32[2,2048,256]{2,1,0:T(8,128)} custom-call(s32[1]{0:T(128)} %bitcast.core_ref, f32[32,136,128]{2,1,0:T(8,128)S(1)} %all-to-all-done.2.half_any), custom_call_target="tpu_custom_call" | custom-call | tf_op jit(solution)/shard_map/scale_own/pallas_call | solution.py:543
  149.9 2.3 %collective-permute-done.9.half_any = f32[32,136,128]{2,1,0:T(8,128)S(1)} collective-permute-done((f32[32,136,128]{2,1,0:T(8,128)S(1)}, f32[32,136,128]{2,1,0:T(8,128)S(1)}, u32[]{:S(2)}, u32[]{:S(2)}) %collective-permute-start.9) | collective-permute-done | bytes 2228256 | tf_op jit(solution)/shard_map/ppermute | solution.py:37
  152.2 2.6 %scale_other.1 = (f32[2,2048,256]{2,1,0:T(8,128)}, f32[2,2048]{1,0:T(2,128)}, f32[1,128]{1,0:T(1,128)S(1)}) custom-call(s32[1]{0:T(128)} %bitcast.core_ref, f32[2,2048,256]{2,1,0:T(8,128)} %scale_own.1.proj_in, f32[32,8,128]{2,1,0:T(8,128)S(1)} %slice.75.own_ref, f32[32,136,128]{2,1,0:T(8,128)S(1)} %collective-permute-done.9.half_any), custom_call_target="tpu_custom_call", output_to_operand_aliasing={{0}: (1, {})} | custom-call | tf_op jit(solution)/shard_map/scale_other/pallas_call | solution.py:552
  (65 shorter events, 6.1 us)
Async XLA Ops:
  3.6 22.8 %all-to-all-start = ((f32[32,8,256]{2,1,0:T(8,128)}), f32[32,8,256]{2,1,0:T(8,128)S(1)}, u32[]{:S(2)}, u32[]{:S(2)}) async-start(f32[32,8,256]{2,1,0:T(8,128)} %bitcast.65), calls=%async_computation | async-start | bytes 524288 | tf_op jit(solution)/shard_map/all_to_all | solution.py:597
  26.4 4.9 %collective-permute-start = (f32[32,136,128]{2,1,0:T(8,128)}, f32[32,136,128]{2,1,0:T(8,128)S(1)}, u32[]{:S(2)}, u32[]{:S(2)}) collective-permute-start(f32[32,136,128]{2,1,0:T(8,128)} %get-tuple-element.40), channel_id=1, source_target_pairs={{0,1},{1,0},{2,3},{3,2},{4,5},{5,4},{6,7},{7,6},{8,9},{9,8},{10,11... | collective-permute-start | bytes 6684680 | tf_op jit(solution)/shard_map/ppermute | solution.py:37
  26.9 1.2 copy-start
  28.1 0.9 copy-start.1
  29.0 0.9 copy-start.2
  29.9 0.9 copy-start.3
  32.9 26.9 %copy-start.5 = (f32[1024,256]{1,0:T(8,128)S(1)}, f32[1024,256]{1,0:T(8,128)}, u32[]{:S(2)}) copy-start(f32[1024,256]{1,0:T(8,128)} %param.17) | copy-start | bytes 3145732
  32.9 47.0 %all-to-all-start.1 = ((f32[32,136,128]{2,1,0:T(8,128)}), f32[32,136,128]{2,1,0:T(8,128)S(1)}, u32[]{:S(2)}, u32[]{:S(2)}) async-start(f32[32,136,128]{2,1,0:T(8,128)} %add.35), calls=%async_computation.1 | async-start | bytes 4456448 | tf_op jit(solution)/shard_map/all_to_all | solution.py:41
  52.1 0.6 copy-start.6
  55.6 6.2 %copy-start.7 = (s32[256]{0:T(256)S(1)}, s32[256]{0:T(256)}, u32[]{:S(2)}) copy-start(s32[256]{0:T(256)} %convert_element_type.27) | copy-start | bytes 3076
  59.8 3.0 %copy-start.12 = (pred[8]{0:T(512)(128)(4,1)S(1)}, pred[8]{0:T(512)(128)(4,1)}, u32[]{:S(2)}) copy-start(pred[8]{0:T(512)(128)(4,1)} %iota_compare_fusion.6) | copy-start | bytes 28
  61.8 3.4 %copy-start.4 = (f32[1024,256]{1,0:T(8,128)}, f32[1024,256]{1,0:T(8,128)S(1)}, u32[]{:S(2)}) copy-start(f32[1024,256]{1,0:T(8,128)S(1)} %scatter_fusion) | copy-start | bytes 3145732
  63.7 1.4 collective-permute-start.1
  65.2 5.0 %collective-permute-start.2 = (f32[1,16,8,256]{3,2,1,0:T(8,128)S(1)}, f32[1,16,8,256]{3,2,1,0:T(8,128)S(1)}, u32[]{:S(2)}, u32[]{:S(2)}) collective-permute-start(f32[1,16,8,256]{3,2,1,0:T(8,128)S(1)} %get-tuple-element.66), channel_id=1, source_target_pairs={{0,16},{1,17},{2,18},{3,19},{4,20},{5,21},{6,22},{7,23},{8,24},{9,... | collective-permute-start | bytes 393224 | tf_op jit(solution)/shard_map/ppermute | solution.py:66
  70.3 9.6 %collective-permute-start.3 = (f32[8,2,8,256]{3,2,1,0:T(8,128)S(1)}, f32[8,2,8,256]{3,2,1,0:T(8,128)S(1)}, u32[]{:S(2)}, u32[]{:S(2)}) collective-permute-start(f32[8,2,8,256]{3,2,1,0:T(8,128)S(1)} %get-tuple-element.64), channel_id=1, source_target_pairs={{0,2},{1,3},{2,0},{3,1},{4,6},{5,7},{6,4},{7,5},{8,10},{9,11},{10,... | collective-permute-start | bytes 393224 | tf_op jit(solution)/shard_map/ppermute | solution.py:66
  80.1 7.1 %collective-permute-start.6 = (f32[136,128]{1,0:T(8,128)S(1)}, f32[136,128]{1,0:T(8,128)S(1)}, u32[]{:S(2)}, u32[]{:S(2)}) collective-permute-start(f32[136,128]{1,0:T(8,128)S(1)} %reduce_sum.68), channel_id=1, source_target_pairs={{0,12},{1,13},{2,14},{3,15},{4,0},{5,1},{6,2},{7,3},{8,4},{9,5},{1... | collective-permute-start | bytes 208904 | tf_op jit(solution)/shard_map/ppermute | solution.py:33
  82.2 5.4 %collective-permute-start.5 = (f32[136,128]{1,0:T(8,128)S(1)}, f32[136,128]{1,0:T(8,128)S(1)}, u32[]{:S(2)}, u32[]{:S(2)}) collective-permute-start(f32[136,128]{1,0:T(8,128)S(1)} %reduce_sum.68), channel_id=1, source_target_pairs={{0,4},{1,5},{2,6},{3,7},{4,8},{5,9},{6,10},{7,11},{8,12},{9,13},{1... | collective-permute-start | bytes 208904 | tf_op jit(solution)/shard_map/ppermute | solution.py:33
  83.0 8.5 %collective-permute-start.4 = (f32[136,128]{1,0:T(8,128)S(1)}, f32[136,128]{1,0:T(8,128)S(1)}, u32[]{:S(2)}, u32[]{:S(2)}) collective-permute-start(f32[136,128]{1,0:T(8,128)S(1)} %reduce_sum.68), channel_id=1, source_target_pairs={{0,8},{1,9},{2,10},{3,11},{4,12},{5,13},{6,14},{7,15},{8,0},{9,1},... | collective-permute-start | bytes 208904 | tf_op jit(solution)/shard_map/ppermute | solution.py:33
  93.1 15.3 %copy-start.10 = (s32[64,2]{0,1:T(2,128)S(1)}, s32[64,2]{0,1:T(2,128)}, u32[]{:S(2)}) copy-start(s32[64,2]{0,1:T(2,128)} %param.19) | copy-start | bytes 1540
  93.1 42.5 %copy-start.8 = (s32[64]{0:T(128)S(1)}, s32[64]{0:T(128)}, u32[]{:S(2)}) copy-start(s32[64]{0:T(128)} %evict_ref.1) | copy-start | bytes 772
  93.1 54.7 %all-to-all-start.2 = ((f32[32,136,128]{2,1,0:T(8,128)}), f32[32,136,128]{2,1,0:T(8,128)S(1)}, u32[]{:S(2)}, u32[]{:S(2)}) async-start(f32[32,136,128]{2,1,0:T(8,128)} %broadcast_in_dim.156), calls=%async_computation.2 | async-start | bytes 4456448 | tf_op jit(solution)/shard_map/all_to_all | solution.py:41
  108.7 23.2 %collective-permute-start.7 = (f32[4,4,8,256]{3,2,1,0:T(8,128)S(1)}, f32[4,4,8,256]{3,2,1,0:T(8,128)S(1)}, u32[]{:S(2)}, u32[]{:S(2)}) collective-permute-start(f32[4,4,8,256]{3,2,1,0:T(8,128)S(1)} %get-tuple-element.62), channel_id=1, source_target_pairs={{0,4},{1,5},{2,6},{3,7},{4,0},{5,1},{6,2},{7,3},{8,12},{9,13},{10,... | collective-permute-start | bytes 393224 | tf_op jit(solution)/shard_map/ppermute | solution.py:66
  131.8 15.3 %copy-start.9 = (s32[64]{0:T(128)S(1)}, s32[64]{0:T(128)}, u32[]{:S(2)}) copy-start(s32[64]{0:T(128)} %evict_ref.1) | copy-start | bytes 772
  131.8 15.4 %copy-start.11 = (f32[1,1024]{1,0:T(1,128)S(1)}, f32[1,1024]{1,0:T(1,128)}, u32[]{:S(2)}) copy-start(f32[1,1024]{1,0:T(1,128)} %get-tuple-element.52) | copy-start | bytes 12292
  131.9 10.6 %collective-permute-start.8 = (f32[2,8,8,256]{3,2,1,0:T(8,128)S(1)}, f32[2,8,8,256]{3,2,1,0:T(8,128)S(1)}, u32[]{:S(2)}, u32[]{:S(2)}) collective-permute-start(f32[2,8,8,256]{3,2,1,0:T(8,128)S(1)} %get-tuple-element.60), channel_id=1, source_target_pairs={{0,8},{1,9},{2,10},{3,11},{4,12},{5,13},{6,14},{7,15},{8,0},{9,1},... | collective-permute-start | bytes 393224 | tf_op jit(solution)/shard_map/ppermute | solution.py:66
  147.8 4.3 %collective-permute-start.9 = (f32[32,136,128]{2,1,0:T(8,128)S(1)}, f32[32,136,128]{2,1,0:T(8,128)S(1)}, u32[]{:S(2)}, u32[]{:S(2)}) collective-permute-start(f32[32,136,128]{2,1,0:T(8,128)S(1)} %all-to-all-done.2.half_any), channel_id=1, source_target_pairs={{0,1},{1,0},{2,3},{3,2},{4,5},{5,4},{6,7},{7,6},{8,9},{9,8},{10,11... | collective-permute-start | bytes 6684680 | tf_op jit(solution)/shard_map/ppermute | solution.py:37

commit v9 on v8

--- a/solution.py
+++ b/solution.py
@@ -48,11 +48,6 @@
     order = jnp.arange(listed, dtype=jnp.int32)
     earlier = (owner[:, None] == owner[None, :]) & (order[None, :] < order[:, None])
     return jnp.sum(earlier.astype(jnp.int32), axis=1)
-
-
-def meta_row(columns, width):
-    block = jnp.concatenate(columns, axis=1)
-    return jnp.pad(block, ((0, 0), (0, width - block.shape[1])))[:, None, :]
 
 
 def picked(values, index):
@@ -457,6 +452,100 @@
     )(evict_slot, place, back, rows)
 
 
+def reply_kernel(
+    me_ref,
+    ids_ref,
+    sums_ref,
+    got_ref,
+    table_any,
+    accum_any,
+    reply_ref,
+    table_out,
+    accum_out,
+    table,
+    accum,
+    sems,
+):
+    owners, per = sums_ref.shape
+    cap = per - 2
+    width = got_ref.shape[1]
+    step = table.shape[0] // 4
+    loads = [pltpu.make_async_copy(accum_any, accum, sems.at[4])]
+    stores = [pltpu.make_async_copy(accum, accum_out, sems.at[4])]
+    for part in range(4):
+        rows = pl.ds(part * step, step)
+        loads.append(pltpu.make_async_copy(table_any.at[rows], table.at[rows], sems.at[part]))
+        stores.append(pltpu.make_async_copy(table.at[rows], table_out.at[rows], sems.at[part]))
+    for load in loads:
+        load.start()
+    for load in loads:
+        load.wait()
+
+    def store(s, _):
+        for r in range(cap):
+            row = ids_ref[s, per + r]
+
+            @pl.when(row >= 0)
+            def _():
+                table[pl.ds(row, 1), :] = got_ref[pl.ds(s * per + r, 1), :]
+                accum[row] = sums_ref[s, r]
+
+        return 0
+
+    lax.fori_loop(0, owners, store, 0, unroll=2)
+    for copy in stores:
+        copy.start()
+    lane = lax.broadcasted_iota(jnp.int32, (1, width), 1)
+
+    def answer(s, _):
+        block = (s ^ me_ref[0]) * per
+        meta = jnp.zeros((1, width), jnp.float32)
+        for r in range(cap):
+            row = ids_ref[s, 2 * per + r]
+            reply_ref[pl.ds(block + r, 1), :] = table[pl.ds(row, 1), :]
+            meta = jnp.where(lane == r, accum[row], meta)
+        reply_ref[pl.ds(block + cap, 1), :] = jnp.zeros((1, width), jnp.float32)
+        reply_ref[pl.ds(block + per - 1, 1), :] = meta
+        return 0
+
+    lax.fori_loop(0, owners, answer, 0, unroll=4)
+    for copy in stores:
+        copy.wait()
+
+
+def replied(me, got, table_rows, table_accum):
+    owners, per, width = got.shape
+    smem = pl.BlockSpec(memory_space=pltpu.SMEM)
+    vmem = pl.BlockSpec(memory_space=pltpu.VMEM)
+    anywhere = pl.BlockSpec(memory_space=pl.ANY)
+    meta = got[:, per - 1, : 3 * per]
+    return pl.pallas_call(
+        reply_kernel,
+        out_shape=(
+            jax.ShapeDtypeStruct((owners * per, width), jnp.float32),
+            jax.ShapeDtypeStruct(table_rows.shape, jnp.float32),
+            jax.ShapeDtypeStruct(table_accum.shape, jnp.float32),
+        ),
+        in_specs=[smem, smem, smem, vmem, anywhere, anywhere],
+        out_specs=(vmem, anywhere, anywhere),
+        scratch_shapes=[
+            pltpu.VMEM(table_rows.shape, jnp.float32),
+            pltpu.SMEM(table_accum.shape, jnp.float32),
+            pltpu.SemaphoreType.DMA((5,)),
+        ],
+        compiler_params=pltpu.CompilerParams(vmem_limit_bytes=60 * 1024 * 1024),
+        cost_estimate=pl.CostEstimate(flops=100_000, bytes_accessed=3_000_000, transcendentals=0),
+        name="reply",
+    )(
+        me[None],
+        meta.astype(jnp.int32),
+        meta[:, :per],
+        got.reshape(owners * per, width),
+        table_rows,
+        table_accum,
+    )
+
+
 def scaled(index, half_any, proj_ref, half, stage, in_sems, out_sems):
     chunks, width = stage.shape[0], stage.shape[2]
     edge, rows = width // 2, width // 4
@@ -582,9 +671,7 @@
 ):
     owners = 32
     per = 8
-    cap = 6
     width = cache_rows.shape[1]
-    owned = table_rows.shape[0]
     cells = cache_rows.shape[0]
     spots = owners * per
     core = lax.axis_index("table") % 2
@@ -606,25 +693,8 @@
     held = kept(core, left, latent, dlatent, extra) + swap_cores(send)
     held, got = lax.optimization_barrier((held, got))
 
-    got_meta = got[:, per - 1, :]
-    got_id = got_meta[:, per : per + cap].astype(jnp.int32)
-    flat = got_id.reshape(-1)
-    table_new = table_rows.at[jnp.where(flat < 0, owned, flat)].set(
-        got[:, :cap, :].reshape(-1, width), mode="drop"
-    )
-    stored = flat[:, None] == jnp.arange(owned, dtype=jnp.int32)[None, :]
-    stored_sum = jnp.sum(jnp.where(stored, got_meta[:, :cap].reshape(-1)[:, None], 0.0), axis=0)
-    accum_table = jnp.where(jnp.any(stored, axis=0), stored_sum, table_accum)
-    order = jnp.arange(owners, dtype=jnp.int32)
-    turned = (order ^ me)[:, None] == order[None, :]
-    asked = jnp.sum(
-        jnp.where(turned[:, :, None], got_meta[None, :, 2 * per : 3 * per], 0.0), axis=1
-    )
-    asked = asked.astype(jnp.int32).reshape(-1)
-    is_meta = (jnp.arange(per) == per - 1)[None, :, None]
-    reply_rows = jnp.take(table_new, asked, axis=0, mode="clip").reshape(owners, per, width)
-    reply_accum = picked(accum_table, asked).reshape(owners, per)
-    back = jnp.where(is_meta, meta_row([reply_accum], width), reply_rows)
+    reply, table_new, accum_table = replied(me, got, table_rows, table_accum)
+    back = reply.reshape(owners, per, width)
 
     held = exchange(held, plane_groups())
     back = cross(cross(cross(back, 1), 16), 2)
@@ -640,10 +710,11 @@
     )
     held = jnp.sum(held, axis=0)
     held = (held + shift_z(held, 4)) + (shift_z(held, 2) + shift_z(held, -2))
+    back = cross(back, 4)
+    held, back = lax.optimization_barrier((held, back))
     whole = jnp.broadcast_to(held[None], (4 * feats, *held.shape))
-    whole, back = lax.optimization_barrier((whole, back))
     whole = exchange(whole, plane_groups())
-    back = cross(cross(back, 4), 8)
+    back = cross(back, 8)
     in_place = (miss_dest[:, 0] ^ me) * per + ranks(miss_dest[:, 0])
     rows_new = refilled(evict_slot, in_place, back.reshape(spots, width), rows_new)
     fetched_accum = picked(back[:, per - 1, :per].reshape(-1), in_place)

time: 157 us -> 153 us (0.975)
  the two profiles are of different devices: /device:TPU:13 before, /device:TPU:3 now
where the time goes in v9:
time: 153 us; the launch traced here: 151 us
  waiting for transfers between devices  50.3 us (33%)
  starting transfers between devices  47.2 us (31%)
  Pallas kernels  38.6 us (25%)
  local copies, waits for them, and re-layouts  8.41 us (5%)
  other arithmetic  4.12 us (3%)
  between operations  2.08 us (1%)
    ppermute x5, waiting for transfers between devices, cross(): came = lax.ppermute(split[:, 1], AXES, there)  28.6 us
    all_to_all x2, starting transfers between devices, exchange(): lax.all_to_all(value, AXES, split_axis=0, concat_axis=0, tiled=True, axis...  19.9 us
    all_to_all x2, waiting for transfers between devices, exchange(): lax.all_to_all(value, AXES, split_axis=0, concat_axis=0, tiled=True, axis...  14.6 us
    pallas_call x1, Pallas kernels, dense(): pl.pallas_call(dense_kernel, out_shape=(jax.ShapeDtypeStruct(bundle, f32)...  12.4 us
    all_to_all x1, starting transfers between devices, shards(): got = lax.all_to_all(sent, 'table', split_axis=0, concat_axis=0, tiled=True)  10.3 us
    pallas_call x1, Pallas kernels, updated(): pl.pallas_call(update_kernel, out_shape=(jax.ShapeDtypeStruct(cache_rows....  9.39 us
    ppermute x5, starting transfers between devices, cross(): came = lax.ppermute(split[:, 1], AXES, there)  7.92 us
    pallas_call x1, Pallas kernels, replied(): pl.pallas_call(reply_kernel, out_shape=(jax.ShapeDtypeStruct((owners * pe...  6.09 us
  transfers between devices with their start and end apart: 13, of which 7 were waited for; matrix products, arithmetic and copies ran while one was open for 4% of the time, Pallas kernels for 22%

profile of v9, /device:TPU:3, one launch (start us, length us, event | category | flops | bytes accessed | tf_op | source)
XLA Modules:
  0.0 150.7 jit_solution(12663309545023370893)
XLA Ops:
  0.6 2.9 %payload.1 = f32[256,256]{1,0:T(8,128)} custom-call(s32[64]{0:T(128)} %evict_ref.1, s32[2,64]{1,0:T(2,128)} %bitcast.81, s32[2,64]{1,0:T(2,128)} %bitcast.79, f32[1024]{0:T(1024)} %accum_ref.1, f32[1024,256]{1,0:T(8,128)} %cache_ref.1), custom_call_target="tpu_custom_call" | custom-call | flops 100000 | bytes 1500000 | tf_op jit(solution)/shard_map/payload/pallas_call | solution.py:355
  3.6 10.3 %all-to-all-start = ((f32[32,8,256]{2,1,0:T(8,128)}), f32[32,8,256]{2,1,0:T(8,128)S(1)}, u32[]{:S(2)}, u32[]{:S(2)}) async-start(f32[32,8,256]{2,1,0:T(8,128)} %bitcast.66), calls=%async_computation | async-start | bytes 524288 | tf_op jit(solution)/shard_map/all_to_all | solution.py:684
  13.9 12.4 %dense.1 = (f32[32,136,128]{2,1,0:T(8,128)}, bf16[256,2048]{1,0:T(8,128)(2,1)}, bf16[256,256]{1,0:T(8,128)(2,1)}, bf16[256,256]{1,0:T(8,128)(2,1)}, f32[1,256]{1,0:T(1,128)}, /*index=5*/f32[32,8,128]{2,1,0:T(8,128)}) custom-call(s32[1]{0:T(128)} %bitcast.core_ref, s32[32,256]{1,0:T(8,128)} %bitcast.82, s32[1,256]{1,0:T(1,128)} %bitcast.88, ...), custom_call_target="tpu_custom_call" | custom-call | flops 5000000000 | bytes 9000000 | tf_op jit(solution)/shard_map/dense/pallas_call | solution.py:222
  26.3 1.0 collective-permute-start
  27.3 1.2 copy-done
  28.5 0.9 copy-done.1
  29.4 0.9 copy-done.2
  30.3 0.9 copy-done.3
  31.2 0.5 kept.1
  31.8 1.6 %add.22 = f32[32,136,128]{2,1,0:T(8,128)} add(f32[32,136,128]{2,1,0:T(8,128)S(1)} %kept.1, f32[32,136,128]{2,1,0:T(8,128)S(1)} %collective-permute-done) | non-fusion elementwise | flops 557056 | bytes 6684672 | tf_op jit(solution)/shard_map/add | solution.py:693
  33.3 8.9 %all-to-all-start.1 = ((f32[32,136,128]{2,1,0:T(8,128)}), f32[32,136,128]{2,1,0:T(8,128)S(1)}, u32[]{:S(2)}, u32[]{:S(2)}) async-start(f32[32,136,128]{2,1,0:T(8,128)} %add.22), calls=%async_computation.1 | async-start | bytes 4456448 | tf_op jit(solution)/shard_map/all_to_all | solution.py:41
  42.2 0.1 copy.48
  42.3 0.6 slice_bitcast_fusion.6
  43.0 6.1 %reply.1 = (f32[256,256]{1,0:T(8,128)}, f32[1024,256]{1,0:T(8,128)}, f32[1024]{0:T(1024)}) custom-call(s32[1]{0:T(128)} %bitcast.8.me_ref, s32[32,24]{1,0:T(8,128)} %get-tuple-element.76.ids_ref, f32[32,8]{1,0:T(8,128)} %bitcast.77, f32[256,256]{1,0:T(8,128)} %bitcast.63, f32[1024,256]{1,0:T(8,128)} %table_any.1, f32[1024]{0:T(1024)} %accum_any.1), custom_call_target="tpu_custom_call" | custom-call | flops 100000 | bytes 3000000 | tf_op jit(solution)/shard_map/reply/pallas_call | solution.py:522
  49.0 1.0 fusion.7
  50.0 0.3 collective-permute-start.1
  50.3 1.3 collective-permute-done.1
  51.7 1.3 collective-permute-start.2
  53.0 16.0 %collective-permute-done.2 = f32[1,16,8,256]{3,2,1,0:T(8,128)S(1)} collective-permute-done((f32[1,16,8,256]{3,2,1,0:T(8,128)S(1)}, f32[1,16,8,256]{3,2,1,0:T(8,128)S(1)}, u32[]{:S(2)}, u32[]{:S(2)}) %collective-permute-start.2) | collective-permute-done | bytes 131104 | tf_op jit(solution)/shard_map/ppermute | solution.py:61
  69.0 2.0 %collective-permute-start.3 = (f32[8,2,8,256]{3,2,1,0:T(8,128)S(1)}, f32[8,2,8,256]{3,2,1,0:T(8,128)S(1)}, u32[]{:S(2)}, u32[]{:S(2)}) collective-permute-start(f32[8,2,8,256]{3,2,1,0:T(8,128)S(1)} %get-tuple-element.70), channel_id=1, source_target_pairs={{0,2},{1,3},{2,0},{3,1},{4,6},{5,7},{6,4},{7,5},{8,10},{9,11},{10,... | collective-permute-start | bytes 393224 | tf_op jit(solution)/shard_map/ppermute | solution.py:61
  71.0 9.4 %update.1 = (f32[1024,256]{1,0:T(8,128)}, f32[1,1024]{1,0:T(1,128)}) custom-call(s32[32,256]{1,0:T(8,128)} %bitcast.83, f32[1024,256]{1,0:T(8,128)} %cache_ref.1, f32[1,1024]{1,0:T(1,128)} %bitcast.78, bf16[256,256]{1,0:T(8,128)(2,1)} %get-tuple-element.38.latent_ref, bf16[256,256]{1,0:T(8,128)(2,1)} %get-tuple-element.39.dlatent_ref, ...), custom_call_target="tpu_custom_call" | custom-call | flops 1100000000 | bytes 4000000 | tf_op jit(solution)/shard_map/update/pallas_call | solution.py:425
  80.4 0.1 reduce_sum.38
  80.5 0.1 collective-permute-start.6
  80.6 2.4 %collective-permute-start.5 = (f32[136,128]{1,0:T(8,128)S(1)}, f32[136,128]{1,0:T(8,128)S(1)}, u32[]{:S(2)}, u32[]{:S(2)}) collective-permute-start(f32[136,128]{1,0:T(8,128)S(1)} %reduce_sum.38), channel_id=1, source_target_pairs={{0,4},{1,5},{2,6},{3,7},{4,8},{5,9},{6,10},{7,11},{8,12},{9,13},{1... | collective-permute-start | bytes 208904 | tf_op jit(solution)/shard_map/ppermute | solution.py:33
  83.0 2.5 %collective-permute-start.4 = (f32[136,128]{1,0:T(8,128)S(1)}, f32[136,128]{1,0:T(8,128)S(1)}, u32[]{:S(2)}, u32[]{:S(2)}) collective-permute-start(f32[136,128]{1,0:T(8,128)S(1)} %reduce_sum.38), channel_id=1, source_target_pairs={{0,8},{1,9},{2,10},{3,11},{4,12},{5,13},{6,14},{7,15},{8,0},{9,1},... | collective-permute-start | bytes 208904 | tf_op jit(solution)/shard_map/ppermute | solution.py:33
  85.5 1.0 collective-permute-start.7
  86.5 5.1 %collective-permute-done.4 = f32[136,128]{1,0:T(8,128)S(1)} collective-permute-done((f32[136,128]{1,0:T(8,128)S(1)}, f32[136,128]{1,0:T(8,128)S(1)}, u32[]{:S(2)}, u32[]{:S(2)}) %collective-permute-start.4) | collective-permute-done | bytes 69664 | tf_op jit(solution)/shard_map/ppermute | solution.py:33
  91.6 5.1 %collective-permute-done.7 = f32[4,4,8,256]{3,2,1,0:T(8,128)S(1)} collective-permute-done((f32[4,4,8,256]{3,2,1,0:T(8,128)S(1)}, f32[4,4,8,256]{3,2,1,0:T(8,128)S(1)}, u32[]{:S(2)}, u32[]{:S(2)}) %collective-permute-start.7) | collective-permute-done | bytes 131104 | tf_op jit(solution)/shard_map/ppermute | solution.py:61
  96.8 1.5 broadcast_in_dim.68
  98.3 11.0 %all-to-all-start.2 = ((f32[32,136,128]{2,1,0:T(8,128)}), f32[32,136,128]{2,1,0:T(8,128)S(1)}, u32[]{:S(2)}, u32[]{:S(2)}) async-start(f32[32,136,128]{2,1,0:T(8,128)} %broadcast_in_dim.68), calls=%async_computation.2 | async-start | bytes 4456448 | tf_op jit(solution)/shard_map/all_to_all | solution.py:41
  109.3 0.0 copy-start.8
  109.4 0.2 convert_reduce_fusion
  109.6 3.5 %collective-permute-start.8 = (f32[2,8,8,256]{3,2,1,0:T(8,128)S(1)}, f32[2,8,8,256]{3,2,1,0:T(8,128)S(1)}, u32[]{:S(2)}, u32[]{:S(2)}) collective-permute-start(f32[2,8,8,256]{3,2,1,0:T(8,128)S(1)} %get-tuple-element.66), channel_id=1, source_target_pairs={{0,8},{1,9},{2,10},{3,11},{4,12},{5,13},{6,14},{7,15},{8,0},{9,1},... | collective-permute-start | bytes 393224 | tf_op jit(solution)/shard_map/ppermute | solution.py:61
  113.0 0.5 multiply_add_fusion.place_ref
  113.6 0.1 fusion
  113.7 6.1 %collective-permute-done.8 = f32[2,8,8,256]{3,2,1,0:T(8,128)S(1)} collective-permute-done((f32[2,8,8,256]{3,2,1,0:T(8,128)S(1)}, f32[2,8,8,256]{3,2,1,0:T(8,128)S(1)}, u32[]{:S(2)}, u32[]{:S(2)}) %collective-permute-start.8) | collective-permute-done | bytes 131104 | tf_op jit(solution)/shard_map/ppermute | solution.py:61
  119.8 0.7 copy.53
  120.6 2.6 %refill.1 = f32[1024,256]{1,0:T(8,128)} custom-call(s32[64]{0:T(128)} %evict_ref.1, s32[64]{0:T(128)} %multiply_add_fusion.place_ref, f32[256,256]{1,0:T(8,128)} %bitcast.64, f32[1024,256]{1,0:T(8,128)} %get-tuple-element.55.old_ref), custom_call_target="tpu_custom_call" | custom-call | flops 100000 | bytes 2000000 | tf_op jit(solution)/shard_map/refill/pallas_call | solution.py:444
  123.2 1.0 slice_reduce_fusion
  124.1 0.1 broadcast_in_dim.69
  124.2 0.2 select_reduce_fusion.1
  124.4 0.1 select_reduce_fusion
  124.5 0.6 select_n.22
  125.1 14.6 %all-to-all-done.2.half_any = f32[32,136,128]{2,1,0:T(8,128)S(1)} async-done(((f32[32,136,128]{2,1,0:T(8,128)}), f32[32,136,128]{2,1,0:T(8,128)S(1)}, u32[]{:S(2)}, u32[]{:S(2)}) %all-to-all-start.2) | async-done | bytes 2228256 | tf_op jit(solution)/shard_map/all_to_all | solution.py:41
  139.8 3.1 %collective-permute-start.9 = (f32[32,136,128]{2,1,0:T(8,128)S(1)}, f32[32,136,128]{2,1,0:T(8,128)S(1)}, u32[]{:S(2)}, u32[]{:S(2)}) collective-permute-start(f32[32,136,128]{2,1,0:T(8,128)S(1)} %all-to-all-done.2.half_any), channel_id=1, source_target_pairs={{0,1},{1,0},{2,3},{3,2},{4,5},{5,4},{6,7},{7,6},{8,9},{9,8},{10,11... | collective-permute-start | bytes 6684680 | tf_op jit(solution)/shard_map/ppermute | solution.py:37
  142.9 2.0 %scale_own.1.proj_in = f32[2,2048,256]{2,1,0:T(8,128)} custom-call(s32[1]{0:T(128)} %bitcast.core_ref, f32[32,136,128]{2,1,0:T(8,128)S(1)} %all-to-all-done.2.half_any), custom_call_target="tpu_custom_call" | custom-call | tf_op jit(solution)/shard_map/scale_own/pallas_call | solution.py:632
  144.9 1.9 %collective-permute-done.9.half_any = f32[32,136,128]{2,1,0:T(8,128)S(1)} collective-permute-done((f32[32,136,128]{2,1,0:T(8,128)S(1)}, f32[32,136,128]{2,1,0:T(8,128)S(1)}, u32[]{:S(2)}, u32[]{:S(2)}) %collective-permute-start.9) | collective-permute-done | bytes 2228256 | tf_op jit(solution)/shard_map/ppermute | solution.py:37
  146.9 2.6 %scale_other.1 = (f32[2,2048,256]{2,1,0:T(8,128)}, f32[2,2048]{1,0:T(2,128)}, f32[1,128]{1,0:T(1,128)S(1)}) custom-call(s32[1]{0:T(128)} %bitcast.core_ref, f32[2,2048,256]{2,1,0:T(8,128)} %scale_own.1.proj_in, f32[32,8,128]{2,1,0:T(8,128)S(1)} %slice.63.own_ref, f32[32,136,128]{2,1,0:T(8,128)S(1)} %collective-permute-done.9.half_any), custom_call_target="tpu_custom_call", output_to_operand_aliasing={{0}: (1, {})} | custom-call | tf_op jit(solution)/shard_map/scale_other/pallas_call | solution.py:641
  (32 shorter events, 0.2 us)
Async XLA Ops:
  3.6 22.8 %all-to-all-start = ((f32[32,8,256]{2,1,0:T(8,128)}), f32[32,8,256]{2,1,0:T(8,128)S(1)}, u32[]{:S(2)}, u32[]{:S(2)}) async-start(f32[32,8,256]{2,1,0:T(8,128)} %bitcast.66), calls=%async_computation | async-start | bytes 524288 | tf_op jit(solution)/shard_map/all_to_all | solution.py:684
  26.3 15.9 %copy-start.4 = (f32[32,8,256]{2,1,0:T(8,128)}, f32[32,8,256]{2,1,0:T(8,128)S(1)}, u32[]{:S(2)}) copy-start(f32[32,8,256]{2,1,0:T(8,128)S(1)} %all-to-all-done) | copy-start | bytes 786436
  26.3 5.4 %collective-permute-start = (f32[32,136,128]{2,1,0:T(8,128)}, f32[32,136,128]{2,1,0:T(8,128)S(1)}, u32[]{:S(2)}, u32[]{:S(2)}) collective-permute-start(f32[32,136,128]{2,1,0:T(8,128)} %get-tuple-element.43), channel_id=1, source_target_pairs={{0,1},{1,0},{2,3},{3,2},{4,5},{5,4},{6,7},{7,6},{8,9},{9,8},{10,11... | collective-permute-start | bytes 6684680 | tf_op jit(solution)/shard_map/ppermute | solution.py:37
  27.3 1.2 copy-start
  28.5 0.9 copy-start.1
  29.4 0.9 copy-start.2
  30.3 0.9 copy-start.3
  33.3 47.1 %all-to-all-start.1 = ((f32[32,136,128]{2,1,0:T(8,128)}), f32[32,136,128]{2,1,0:T(8,128)S(1)}, u32[]{:S(2)}, u32[]{:S(2)}) async-start(f32[32,136,128]{2,1,0:T(8,128)} %add.22), calls=%async_computation.1 | async-start | bytes 4456448 | tf_op jit(solution)/shard_map/all_to_all | solution.py:41
  50.0 1.6 %collective-permute-start.1 = (f32[16,1,8,256]{3,2,0,1:T(8,128)S(1)}, f32[16,1,8,256]{3,2,0,1:T(8,128)S(1)}, u32[]{:S(2)}, u32[]{:S(2)}) collective-permute-start(f32[16,1,8,256]{3,2,0,1:T(8,128)S(1)} %get-tuple-element.74), channel_id=1, source_target_pairs={{0,1},{1,0},{2,3},{3,2},{4,5},{5,4},{6,7},{7,6},{8,9},{9,8},{10,11... | collective-permute-start | bytes 393224 | tf_op jit(solution)/shard_map/ppermute | solution.py:61
  51.7 17.3 %collective-permute-start.2 = (f32[1,16,8,256]{3,2,1,0:T(8,128)S(1)}, f32[1,16,8,256]{3,2,1,0:T(8,128)S(1)}, u32[]{:S(2)}, u32[]{:S(2)}) collective-permute-start(f32[1,16,8,256]{3,2,1,0:T(8,128)S(1)} %get-tuple-element.72), channel_id=1, source_target_pairs={{0,16},{1,17},{2,18},{3,19},{4,20},{5,21},{6,22},{7,23},{8,24},{9,... | collective-permute-start | bytes 393224 | tf_op jit(solution)/shard_map/ppermute | solution.py:61
  69.0 11.4 %collective-permute-start.3 = (f32[8,2,8,256]{3,2,1,0:T(8,128)S(1)}, f32[8,2,8,256]{3,2,1,0:T(8,128)S(1)}, u32[]{:S(2)}, u32[]{:S(2)}) collective-permute-start(f32[8,2,8,256]{3,2,1,0:T(8,128)S(1)} %get-tuple-element.70), channel_id=1, source_target_pairs={{0,2},{1,3},{2,0},{3,1},{4,6},{5,7},{6,4},{7,5},{8,10},{9,11},{10,... | collective-permute-start | bytes 393224 | tf_op jit(solution)/shard_map/ppermute | solution.py:61
  80.5 5.9 %collective-permute-start.6 = (f32[136,128]{1,0:T(8,128)S(1)}, f32[136,128]{1,0:T(8,128)S(1)}, u32[]{:S(2)}, u32[]{:S(2)}) collective-permute-start(f32[136,128]{1,0:T(8,128)S(1)} %reduce_sum.38), channel_id=1, source_target_pairs={{0,12},{1,13},{2,14},{3,15},{4,0},{5,1},{6,2},{7,3},{8,4},{9,5},{1... | collective-permute-start | bytes 208904 | tf_op jit(solution)/shard_map/ppermute | solution.py:33
  80.6 5.8 %collective-permute-start.5 = (f32[136,128]{1,0:T(8,128)S(1)}, f32[136,128]{1,0:T(8,128)S(1)}, u32[]{:S(2)}, u32[]{:S(2)}) collective-permute-start(f32[136,128]{1,0:T(8,128)S(1)} %reduce_sum.38), channel_id=1, source_target_pairs={{0,4},{1,5},{2,6},{3,7},{4,8},{5,9},{6,10},{7,11},{8,12},{9,13},{1... | collective-permute-start | bytes 208904 | tf_op jit(solution)/shard_map/ppermute | solution.py:33
  83.0 8.6 %collective-permute-start.4 = (f32[136,128]{1,0:T(8,128)S(1)}, f32[136,128]{1,0:T(8,128)S(1)}, u32[]{:S(2)}, u32[]{:S(2)}) collective-permute-start(f32[136,128]{1,0:T(8,128)S(1)} %reduce_sum.38), channel_id=1, source_target_pairs={{0,8},{1,9},{2,10},{3,11},{4,12},{5,13},{6,14},{7,15},{8,0},{9,1},... | collective-permute-start | bytes 208904 | tf_op jit(solution)/shard_map/ppermute | solution.py:33
  85.5 11.2 %collective-permute-start.7 = (f32[4,4,8,256]{3,2,1,0:T(8,128)S(1)}, f32[4,4,8,256]{3,2,1,0:T(8,128)S(1)}, u32[]{:S(2)}, u32[]{:S(2)}) collective-permute-start(f32[4,4,8,256]{3,2,1,0:T(8,128)S(1)} %get-tuple-element.68), channel_id=1, source_target_pairs={{0,4},{1,5},{2,6},{3,7},{4,0},{5,1},{6,2},{7,3},{8,12},{9,13},{10,... | collective-permute-start | bytes 393224 | tf_op jit(solution)/shard_map/ppermute | solution.py:61
  98.3 11.1 %copy-start.7 = (s32[64,2]{0,1:T(2,128)S(1)}, s32[64,2]{0,1:T(2,128)}, u32[]{:S(2)}) copy-start(s32[64,2]{0,1:T(2,128)} %param.19) | copy-start | bytes 1540
  98.3 15.3 %copy-start.5 = (s32[64]{0:T(128)S(1)}, s32[64]{0:T(128)}, u32[]{:S(2)}) copy-start(s32[64]{0:T(128)} %evict_ref.1) | copy-start | bytes 772
  98.3 41.5 %all-to-all-start.2 = ((f32[32,136,128]{2,1,0:T(8,128)}), f32[32,136,128]{2,1,0:T(8,128)S(1)}, u32[]{:S(2)}, u32[]{:S(2)}) async-start(f32[32,136,128]{2,1,0:T(8,128)} %broadcast_in_dim.68), calls=%async_computation.2 | async-start | bytes 4456448 | tf_op jit(solution)/shard_map/all_to_all | solution.py:41
  109.3 15.1 %copy-start.6 = (s32[64]{0:T(128)S(1)}, s32[64]{0:T(128)}, u32[]{:S(2)}) copy-start(s32[64]{0:T(128)} %evict_ref.1) | copy-start | bytes 772
  109.3 15.2 %copy-start.8 = (f32[1,1024]{1,0:T(1,128)S(1)}, f32[1,1024]{1,0:T(1,128)}, u32[]{:S(2)}) copy-start(f32[1,1024]{1,0:T(1,128)} %get-tuple-element.56) | copy-start | bytes 12292
  109.6 10.2 %collective-permute-start.8 = (f32[2,8,8,256]{3,2,1,0:T(8,128)S(1)}, f32[2,8,8,256]{3,2,1,0:T(8,128)S(1)}, u32[]{:S(2)}, u32[]{:S(2)}) collective-permute-start(f32[2,8,8,256]{3,2,1,0:T(8,128)S(1)} %get-tuple-element.66), channel_id=1, source_target_pairs={{0,8},{1,9},{2,10},{3,11},{4,12},{5,13},{6,14},{7,15},{8,0},{9,1},... | collective-permute-start | bytes 393224 | tf_op jit(solution)/shard_map/ppermute | solution.py:61
  139.8 7.1 %collective-permute-start.9 = (f32[32,136,128]{2,1,0:T(8,128)S(1)}, f32[32,136,128]{2,1,0:T(8,128)S(1)}, u32[]{:S(2)}, u32[]{:S(2)}) collective-permute-start(f32[32,136,128]{2,1,0:T(8,128)S(1)} %all-to-all-done.2.half_any), channel_id=1, source_target_pairs={{0,1},{1,0},{2,3},{3,2},{4,5},{5,4},{6,7},{7,6},{8,9},{9,8},{10,11... | collective-permute-start | bytes 6684680 | tf_op jit(solution)/shard_map/ppermute | solution.py:37

commit v10 on v9

--- a/solution.py
+++ b/solution.py
@@ -697,7 +697,7 @@
     back = reply.reshape(owners, per, width)
 
     held = exchange(held, plane_groups())
-    back = cross(cross(cross(back, 1), 16), 2)
+    back = cross(cross(back, 1), 8)
     rows_new, accum_new = updated(
         slot_ids,
         cache_rows,
@@ -710,11 +710,11 @@
     )
     held = jnp.sum(held, axis=0)
     held = (held + shift_z(held, 4)) + (shift_z(held, 2) + shift_z(held, -2))
-    back = cross(back, 4)
+    back = cross(cross(back, 16), 2)
     held, back = lax.optimization_barrier((held, back))
     whole = jnp.broadcast_to(held[None], (4 * feats, *held.shape))
     whole = exchange(whole, plane_groups())
-    back = cross(back, 8)
+    back = cross(back, 4)
     in_place = (miss_dest[:, 0] ^ me) * per + ranks(miss_dest[:, 0])
     rows_new = refilled(evict_slot, in_place, back.reshape(spots, width), rows_new)
     fetched_accum = picked(back[:, per - 1, :per].reshape(-1), in_place)

time: 153 us -> 140 us (0.915)
  waiting for transfers between devices: 50.3 us -> 40.3 us
  starting transfers between devices: 47.2 us -> 44.8 us
    all_to_all x2, waiting for transfers between devices: 14.6 us -> 9.47 us  [exchange(): lax.all_to_all(value, AXES, split_axis=0, concat_axis=0, tiled=True, axis...]
    ppermute x3, waiting for transfers between devices: 5.11 us -> 2.4 us  [shift_z(): return lax.ppermute(value, AXES, there)]
    ppermute x2, starting transfers between devices: 4.1 us -> 1.46 us  [swap_cores(): return lax.ppermute(value, AXES, [(i, i ^ 1) for i in range(256)])]
    all_to_all x2, starting transfers between devices: 19.9 us -> 17.8 us  [exchange(): lax.all_to_all(value, AXES, split_axis=0, concat_axis=0, tiled=True, axis...]
    ppermute x5, waiting for transfers between devices: 28.6 us -> 26.5 us  [cross(): came = lax.ppermute(split[:, 1], AXES, there)]
    unnamed x19 -> x21, local copies, waits for them, and re-layouts: 3.98 us -> 4.02 us
  transfers between devices with their start and end apart: 13 -> 13, of which waited for: 7 -> 8; matrix products, arithmetic and copies ran while one was open for 4% -> 4% of each run, Pallas kernels for 22% -> 24%
where the time goes in v10:
time: 140 us; the launch traced here: 138 us
  starting transfers between devices  44.8 us (32%)
  waiting for transfers between devices  40.3 us (29%)
  Pallas kernels  38.6 us (28%)
  local copies, waits for them, and re-layouts  8.45 us (6%)
  other arithmetic  4.12 us (3%)
  between operations  2.09 us (1%)
    ppermute x5, waiting for transfers between devices, cross(): came = lax.ppermute(split[:, 1], AXES, there)  26.5 us
    all_to_all x2, starting transfers between devices, exchange(): lax.all_to_all(value, AXES, split_axis=0, concat_axis=0, tiled=True, axis...  17.8 us
    pallas_call x1, Pallas kernels, dense(): pl.pallas_call(dense_kernel, out_shape=(jax.ShapeDtypeStruct(bundle, f32)...  12.4 us
    all_to_all x1, starting transfers between devices, shards(): got = lax.all_to_all(sent, 'table', split_axis=0, concat_axis=0, tiled=True)  10.3 us
    all_to_all x2, waiting for transfers between devices, exchange(): lax.all_to_all(value, AXES, split_axis=0, concat_axis=0, tiled=True, axis...  9.47 us
    pallas_call x1, Pallas kernels, updated(): pl.pallas_call(update_kernel, out_shape=(jax.ShapeDtypeStruct(cache_rows....  9.39 us
    ppermute x5, starting transfers between devices, cross(): came = lax.ppermute(split[:, 1], AXES, there)  9 us
    ppermute x3, starting transfers between devices, shift_z(): return lax.ppermute(value, AXES, there)  6.19 us
  transfers between devices with their start and end apart: 13, of which 8 were waited for; matrix products, arithmetic and copies ran while one was open for 4% of the time, Pallas kernels for 24%

profile of v10, /device:TPU:3, one launch (start us, length us, event | category | flops | bytes accessed | tf_op | source)
XLA Modules:
  0.0 138.4 jit_solution(7989085791319954431)
XLA Ops:
  0.6 2.9 %payload.1 = f32[256,256]{1,0:T(8,128)} custom-call(s32[64]{0:T(128)} %evict_ref.1, s32[2,64]{1,0:T(2,128)} %bitcast.81, s32[2,64]{1,0:T(2,128)} %bitcast.79, f32[1024]{0:T(1024)} %accum_ref.1, f32[1024,256]{1,0:T(8,128)} %cache_ref.1), custom_call_target="tpu_custom_call" | custom-call | flops 100000 | bytes 1500000 | tf_op jit(solution)/shard_map/payload/pallas_call | solution.py:355
  3.6 10.3 %all-to-all-start = ((f32[32,8,256]{2,1,0:T(8,128)}), f32[32,8,256]{2,1,0:T(8,128)S(1)}, u32[]{:S(2)}, u32[]{:S(2)}) async-start(f32[32,8,256]{2,1,0:T(8,128)} %bitcast.66), calls=%async_computation | async-start | bytes 524288 | tf_op jit(solution)/shard_map/all_to_all | solution.py:684
  13.9 12.4 %dense.1 = (f32[32,136,128]{2,1,0:T(8,128)}, bf16[256,2048]{1,0:T(8,128)(2,1)}, bf16[256,256]{1,0:T(8,128)(2,1)}, bf16[256,256]{1,0:T(8,128)(2,1)}, f32[1,256]{1,0:T(1,128)}, /*index=5*/f32[32,8,128]{2,1,0:T(8,128)}) custom-call(s32[1]{0:T(128)} %bitcast.core_ref, s32[32,256]{1,0:T(8,128)} %bitcast.82, s32[1,256]{1,0:T(1,128)} %bitcast.88, ...), custom_call_target="tpu_custom_call" | custom-call | flops 5000000000 | bytes 9000000 | tf_op jit(solution)/shard_map/dense/pallas_call | solution.py:222
  26.3 1.0 collective-permute-start
  27.3 1.2 copy-done
  28.5 0.9 copy-done.1
  29.4 0.9 copy-done.2
  30.3 0.9 copy-done.3
  31.2 0.5 kept.1
  31.8 1.6 %add.22 = f32[32,136,128]{2,1,0:T(8,128)} add(f32[32,136,128]{2,1,0:T(8,128)S(1)} %kept.1, f32[32,136,128]{2,1,0:T(8,128)S(1)} %collective-permute-done) | non-fusion elementwise | flops 557056 | bytes 6684672 | tf_op jit(solution)/shard_map/add | solution.py:693
  33.4 8.9 %all-to-all-start.1 = ((f32[32,136,128]{2,1,0:T(8,128)}), f32[32,136,128]{2,1,0:T(8,128)S(1)}, u32[]{:S(2)}, u32[]{:S(2)}) async-start(f32[32,136,128]{2,1,0:T(8,128)} %add.22), calls=%async_computation.1 | async-start | bytes 4456448 | tf_op jit(solution)/shard_map/all_to_all | solution.py:41
  42.2 0.1 copy.53
  42.3 0.6 slice_bitcast_fusion.8
  43.0 6.1 %reply.1 = (f32[256,256]{1,0:T(8,128)}, f32[1024,256]{1,0:T(8,128)}, f32[1024]{0:T(1024)}) custom-call(s32[1]{0:T(128)} %bitcast.8.me_ref, s32[32,24]{1,0:T(8,128)} %get-tuple-element.76.ids_ref, f32[32,8]{1,0:T(8,128)} %bitcast.77, f32[256,256]{1,0:T(8,128)} %bitcast.63, f32[1024,256]{1,0:T(8,128)} %table_any.1, f32[1024]{0:T(1024)} %accum_any.1), custom_call_target="tpu_custom_call" | custom-call | flops 100000 | bytes 3000000 | tf_op jit(solution)/shard_map/reply/pallas_call | solution.py:522
  49.1 1.0 fusion.5
  50.1 0.3 collective-permute-start.1
  50.4 1.3 collective-permute-done.1
  51.8 4.9 %collective-permute-start.2 = (f32[2,8,8,256]{3,2,1,0:T(8,128)S(1)}, f32[2,8,8,256]{3,2,1,0:T(8,128)S(1)}, u32[]{:S(2)}, u32[]{:S(2)}) collective-permute-start(f32[2,8,8,256]{3,2,1,0:T(8,128)S(1)} %get-tuple-element.72), channel_id=1, source_target_pairs={{0,8},{1,9},{2,10},{3,11},{4,12},{5,13},{6,14},{7,15},{8,0},{9,1},... | collective-permute-start | bytes 393224 | tf_op jit(solution)/shard_map/ppermute | solution.py:61
  56.7 9.4 %update.1 = (f32[1024,256]{1,0:T(8,128)}, f32[1,1024]{1,0:T(1,128)}) custom-call(s32[32,256]{1,0:T(8,128)} %bitcast.83, f32[1024,256]{1,0:T(8,128)} %cache_ref.1, f32[1,1024]{1,0:T(1,128)} %bitcast.78, bf16[256,256]{1,0:T(8,128)(2,1)} %get-tuple-element.38.latent_ref, bf16[256,256]{1,0:T(8,128)(2,1)} %get-tuple-element.39.dlatent_ref, ...), custom_call_target="tpu_custom_call" | custom-call | flops 1100000000 | bytes 4000000 | tf_op jit(solution)/shard_map/update/pallas_call | solution.py:425
  66.1 5.6 %all-to-all-done.1 = f32[32,136,128]{2,1,0:T(8,128)S(1)} async-done(((f32[32,136,128]{2,1,0:T(8,128)}), f32[32,136,128]{2,1,0:T(8,128)S(1)}, u32[]{:S(2)}, u32[]{:S(2)}) %all-to-all-start.1) | async-done | bytes 2228256 | tf_op jit(solution)/shard_map/all_to_all | solution.py:41
  71.8 1.8 %collective-permute-start.6 = (f32[1,16,8,256]{3,2,1,0:T(8,128)S(1)}, f32[1,16,8,256]{3,2,1,0:T(8,128)S(1)}, u32[]{:S(2)}, u32[]{:S(2)}) collective-permute-start(f32[1,16,8,256]{3,2,1,0:T(8,128)S(1)} %get-tuple-element.70), channel_id=1, source_target_pairs={{0,16},{1,17},{2,18},{3,19},{4,20},{5,21},{6,22},{7,23},{8,24},{9,... | collective-permute-start | bytes 393224 | tf_op jit(solution)/shard_map/ppermute | solution.py:61
  73.5 0.1 reduce_sum.38
  73.6 3.3 %collective-permute-start.5 = (f32[136,128]{1,0:T(8,128)S(1)}, f32[136,128]{1,0:T(8,128)S(1)}, u32[]{:S(2)}, u32[]{:S(2)}) collective-permute-start(f32[136,128]{1,0:T(8,128)S(1)} %reduce_sum.38), channel_id=1, source_target_pairs={{0,12},{1,13},{2,14},{3,15},{4,0},{5,1},{6,2},{7,3},{8,4},{9,5},{1... | collective-permute-start | bytes 208904 | tf_op jit(solution)/shard_map/ppermute | solution.py:33
  77.0 2.9 %collective-permute-start.3 = (f32[136,128]{1,0:T(8,128)S(1)}, f32[136,128]{1,0:T(8,128)S(1)}, u32[]{:S(2)}, u32[]{:S(2)}) collective-permute-start(f32[136,128]{1,0:T(8,128)S(1)} %reduce_sum.38), channel_id=1, source_target_pairs={{0,8},{1,9},{2,10},{3,11},{4,12},{5,13},{6,14},{7,15},{8,0},{9,1},... | collective-permute-start | bytes 208904 | tf_op jit(solution)/shard_map/ppermute | solution.py:33
  79.9 1.9 %collective-permute-start.7 = (f32[8,2,8,256]{3,2,1,0:T(8,128)S(1)}, f32[8,2,8,256]{3,2,1,0:T(8,128)S(1)}, u32[]{:S(2)}, u32[]{:S(2)}) collective-permute-start(f32[8,2,8,256]{3,2,1,0:T(8,128)S(1)} %get-tuple-element.68), channel_id=1, source_target_pairs={{0,2},{1,3},{2,0},{3,1},{4,6},{5,7},{6,4},{7,5},{8,10},{9,11},{10,... | collective-permute-start | bytes 393224 | tf_op jit(solution)/shard_map/ppermute | solution.py:61
  81.8 0.9 collective-permute-done.4
  82.7 1.5 %collective-permute-done.3 = f32[136,128]{1,0:T(8,128)S(1)} collective-permute-done((f32[136,128]{1,0:T(8,128)S(1)}, f32[136,128]{1,0:T(8,128)S(1)}, u32[]{:S(2)}, u32[]{:S(2)}) %collective-permute-start.3) | collective-permute-done | bytes 69664 | tf_op jit(solution)/shard_map/ppermute | solution.py:33
  84.3 3.5 %collective-permute-done.7 = f32[8,2,8,256]{3,2,1,0:T(8,128)S(1)} collective-permute-done((f32[8,2,8,256]{3,2,1,0:T(8,128)S(1)}, f32[8,2,8,256]{3,2,1,0:T(8,128)S(1)}, u32[]{:S(2)}, u32[]{:S(2)}) %collective-permute-start.7) | collective-permute-done | bytes 131104 | tf_op jit(solution)/shard_map/ppermute | solution.py:61
  87.8 1.5 %broadcast_in_dim.68 = f32[32,136,128]{2,1,0:T(8,128)} broadcast(f32[136,128]{1,0:T(8,128)S(1)} %add_add_fusion), dimensions={1,2} | broadcast | bytes 2297856 | tf_op jit(solution)/shard_map/broadcast_in_dim | solution.py:715
  89.3 8.9 %all-to-all-start.2 = ((f32[32,136,128]{2,1,0:T(8,128)}), f32[32,136,128]{2,1,0:T(8,128)S(1)}, u32[]{:S(2)}, u32[]{:S(2)}) async-start(f32[32,136,128]{2,1,0:T(8,128)} %broadcast_in_dim.68), calls=%async_computation.2 | async-start | bytes 4456448 | tf_op jit(solution)/shard_map/all_to_all | solution.py:41
  98.3 0.0 copy-start.6
  98.3 0.2 convert_reduce_fusion
  98.5 0.1 collective-permute-start.8
  98.6 0.5 multiply_add_fusion.place_ref
  99.1 0.1 fusion
  99.2 21.7 %collective-permute-done.8 = f32[4,4,8,256]{3,2,1,0:T(8,128)S(1)} collective-permute-done((f32[4,4,8,256]{3,2,1,0:T(8,128)S(1)}, f32[4,4,8,256]{3,2,1,0:T(8,128)S(1)}, u32[]{:S(2)}, u32[]{:S(2)}) %collective-permute-start.8) | collective-permute-done | bytes 131104 | tf_op jit(solution)/shard_map/ppermute | solution.py:61
  121.0 0.7 copy.60
  121.7 2.6 %refill.1 = f32[1024,256]{1,0:T(8,128)} custom-call(s32[64]{0:T(128)} %evict_ref.1, s32[64]{0:T(128)} %multiply_add_fusion.place_ref, f32[256,256]{1,0:T(8,128)} %bitcast.64, f32[1024,256]{1,0:T(8,128)} %get-tuple-element.55.old_ref), custom_call_target="tpu_custom_call" | custom-call | flops 100000 | bytes 2000000 | tf_op jit(solution)/shard_map/refill/pallas_call | solution.py:444
  124.3 1.0 slice_reduce_fusion
  125.3 0.1 broadcast_in_dim.69
  125.4 0.2 select_reduce_fusion.1
  125.6 0.1 select_reduce_fusion
  125.7 0.6 select_n.22
  126.3 3.9 %all-to-all-done.2.half_any = f32[32,136,128]{2,1,0:T(8,128)S(1)} async-done(((f32[32,136,128]{2,1,0:T(8,128)}), f32[32,136,128]{2,1,0:T(8,128)S(1)}, u32[]{:S(2)}, u32[]{:S(2)}) %all-to-all-start.2) | async-done | bytes 2228256 | tf_op jit(solution)/shard_map/all_to_all | solution.py:41
  130.2 0.5 collective-permute-start.9
  130.7 2.0 %scale_own.1.proj_in = f32[2,2048,256]{2,1,0:T(8,128)} custom-call(s32[1]{0:T(128)} %bitcast.core_ref, f32[32,136,128]{2,1,0:T(8,128)S(1)} %all-to-all-done.2.half_any), custom_call_target="tpu_custom_call" | custom-call | tf_op jit(solution)/shard_map/scale_own/pallas_call | solution.py:632
  132.7 1.9 %collective-permute-done.9.half_any = f32[32,136,128]{2,1,0:T(8,128)S(1)} collective-permute-done((f32[32,136,128]{2,1,0:T(8,128)S(1)}, f32[32,136,128]{2,1,0:T(8,128)S(1)}, u32[]{:S(2)}, u32[]{:S(2)}) %collective-permute-start.9) | collective-permute-done | bytes 2228256 | tf_op jit(solution)/shard_map/ppermute | solution.py:37
  134.6 2.6 %scale_other.1 = (f32[2,2048,256]{2,1,0:T(8,128)}, f32[2,2048]{1,0:T(2,128)}, f32[1,128]{1,0:T(1,128)S(1)}) custom-call(s32[1]{0:T(128)} %bitcast.core_ref, f32[2,2048,256]{2,1,0:T(8,128)} %scale_own.1.proj_in, f32[32,8,128]{2,1,0:T(8,128)S(1)} %slice.63.own_ref, f32[32,136,128]{2,1,0:T(8,128)S(1)} %collective-permute-done.9.half_any), custom_call_target="tpu_custom_call", output_to_operand_aliasing={{0}: (1, {})} | custom-call | tf_op jit(solution)/shard_map/scale_other/pallas_call | solution.py:641
  (34 shorter events, 0.3 us)
Async XLA Ops:
  3.6 22.8 %all-to-all-start = ((f32[32,8,256]{2,1,0:T(8,128)}), f32[32,8,256]{2,1,0:T(8,128)S(1)}, u32[]{:S(2)}, u32[]{:S(2)}) async-start(f32[32,8,256]{2,1,0:T(8,128)} %bitcast.66), calls=%async_computation | async-start | bytes 524288 | tf_op jit(solution)/shard_map/all_to_all | solution.py:684
  26.3 15.9 %copy-start.4 = (f32[32,8,256]{2,1,0:T(8,128)}, f32[32,8,256]{2,1,0:T(8,128)S(1)}, u32[]{:S(2)}) copy-start(f32[32,8,256]{2,1,0:T(8,128)S(1)} %all-to-all-done) | copy-start | bytes 786436
  26.3 5.4 %collective-permute-start = (f32[32,136,128]{2,1,0:T(8,128)}, f32[32,136,128]{2,1,0:T(8,128)S(1)}, u32[]{:S(2)}, u32[]{:S(2)}) collective-permute-start(f32[32,136,128]{2,1,0:T(8,128)} %get-tuple-element.43), channel_id=1, source_target_pairs={{0,1},{1,0},{2,3},{3,2},{4,5},{5,4},{6,7},{7,6},{8,9},{9,8},{10,11... | collective-permute-start | bytes 6684680 | tf_op jit(solution)/shard_map/ppermute | solution.py:37
  27.3 1.2 copy-start
  28.5 0.9 copy-start.1
  29.4 0.9 copy-start.2
  30.3 0.9 copy-start.3
  33.4 38.4 %all-to-all-start.1 = ((f32[32,136,128]{2,1,0:T(8,128)}), f32[32,136,128]{2,1,0:T(8,128)S(1)}, u32[]{:S(2)}, u32[]{:S(2)}) async-start(f32[32,136,128]{2,1,0:T(8,128)} %add.22), calls=%async_computation.1 | async-start | bytes 4456448 | tf_op jit(solution)/shard_map/all_to_all | solution.py:41
  50.1 1.6 %collective-permute-start.1 = (f32[16,1,8,256]{3,2,0,1:T(8,128)S(1)}, f32[16,1,8,256]{3,2,0,1:T(8,128)S(1)}, u32[]{:S(2)}, u32[]{:S(2)}) collective-permute-start(f32[16,1,8,256]{3,2,0,1:T(8,128)S(1)} %get-tuple-element.74), channel_id=1, source_target_pairs={{0,1},{1,0},{2,3},{3,2},{4,5},{5,4},{6,7},{7,6},{8,9},{9,8},{10,11... | collective-permute-start | bytes 393224 | tf_op jit(solution)/shard_map/ppermute | solution.py:61
  51.8 14.3 %collective-permute-start.2 = (f32[2,8,8,256]{3,2,1,0:T(8,128)S(1)}, f32[2,8,8,256]{3,2,1,0:T(8,128)S(1)}, u32[]{:S(2)}, u32[]{:S(2)}) collective-permute-start(f32[2,8,8,256]{3,2,1,0:T(8,128)S(1)} %get-tuple-element.72), channel_id=1, source_target_pairs={{0,8},{1,9},{2,10},{3,11},{4,12},{5,13},{6,14},{7,15},{8,0},{9,1},... | collective-permute-start | bytes 393224 | tf_op jit(solution)/shard_map/ppermute | solution.py:61
  71.8 8.1 %collective-permute-start.6 = (f32[1,16,8,256]{3,2,1,0:T(8,128)S(1)}, f32[1,16,8,256]{3,2,1,0:T(8,128)S(1)}, u32[]{:S(2)}, u32[]{:S(2)}) collective-permute-start(f32[1,16,8,256]{3,2,1,0:T(8,128)S(1)} %get-tuple-element.70), channel_id=1, source_target_pairs={{0,16},{1,17},{2,18},{3,19},{4,20},{5,21},{6,22},{7,23},{8,24},{9,... | collective-permute-start | bytes 393224 | tf_op jit(solution)/shard_map/ppermute | solution.py:61
  73.6 8.2 %collective-permute-start.5 = (f32[136,128]{1,0:T(8,128)S(1)}, f32[136,128]{1,0:T(8,128)S(1)}, u32[]{:S(2)}, u32[]{:S(2)}) collective-permute-start(f32[136,128]{1,0:T(8,128)S(1)} %reduce_sum.38), channel_id=1, source_target_pairs={{0,12},{1,13},{2,14},{3,15},{4,0},{5,1},{6,2},{7,3},{8,4},{9,5},{1... | collective-permute-start | bytes 208904 | tf_op jit(solution)/shard_map/ppermute | solution.py:33
  77.0 5.8 %collective-permute-start.4 = (f32[136,128]{1,0:T(8,128)S(1)}, f32[136,128]{1,0:T(8,128)S(1)}, u32[]{:S(2)}, u32[]{:S(2)}) collective-permute-start(f32[136,128]{1,0:T(8,128)S(1)} %reduce_sum.38), channel_id=1, source_target_pairs={{0,4},{1,5},{2,6},{3,7},{4,8},{5,9},{6,10},{7,11},{8,12},{9,13},{1... | collective-permute-start | bytes 208904 | tf_op jit(solution)/shard_map/ppermute | solution.py:33
  77.0 7.3 %collective-permute-start.3 = (f32[136,128]{1,0:T(8,128)S(1)}, f32[136,128]{1,0:T(8,128)S(1)}, u32[]{:S(2)}, u32[]{:S(2)}) collective-permute-start(f32[136,128]{1,0:T(8,128)S(1)} %reduce_sum.38), channel_id=1, source_target_pairs={{0,8},{1,9},{2,10},{3,11},{4,12},{5,13},{6,14},{7,15},{8,0},{9,1},... | collective-permute-start | bytes 208904 | tf_op jit(solution)/shard_map/ppermute | solution.py:33
  79.9 7.8 %collective-permute-start.7 = (f32[8,2,8,256]{3,2,1,0:T(8,128)S(1)}, f32[8,2,8,256]{3,2,1,0:T(8,128)S(1)}, u32[]{:S(2)}, u32[]{:S(2)}) collective-permute-start(f32[8,2,8,256]{3,2,1,0:T(8,128)S(1)} %get-tuple-element.68), channel_id=1, source_target_pairs={{0,2},{1,3},{2,0},{3,1},{4,6},{5,7},{6,4},{7,5},{8,10},{9,11},{10,... | collective-permute-start | bytes 393224 | tf_op jit(solution)/shard_map/ppermute | solution.py:61
  89.3 9.0 %copy-start.7 = (s32[64,2]{0,1:T(2,128)S(1)}, s32[64,2]{0,1:T(2,128)}, u32[]{:S(2)}) copy-start(s32[64,2]{0,1:T(2,128)} %param.19) | copy-start | bytes 1540
  89.3 9.8 %copy-start.5 = (s32[64]{0:T(128)S(1)}, s32[64]{0:T(128)}, u32[]{:S(2)}) copy-start(s32[64]{0:T(128)} %evict_ref.1) | copy-start | bytes 772
  89.3 40.9 %all-to-all-start.2 = ((f32[32,136,128]{2,1,0:T(8,128)}), f32[32,136,128]{2,1,0:T(8,128)S(1)}, u32[]{:S(2)}, u32[]{:S(2)}) async-start(f32[32,136,128]{2,1,0:T(8,128)} %broadcast_in_dim.68), calls=%async_computation.2 | async-start | bytes 4456448 | tf_op jit(solution)/shard_map/all_to_all | solution.py:41
  98.3 27.3 %copy-start.6 = (s32[64]{0:T(128)S(1)}, s32[64]{0:T(128)}, u32[]{:S(2)}) copy-start(s32[64]{0:T(128)} %evict_ref.1) | copy-start | bytes 772
  98.3 27.4 %copy-start.8 = (f32[1,1024]{1,0:T(1,128)S(1)}, f32[1,1024]{1,0:T(1,128)}, u32[]{:S(2)}) copy-start(f32[1,1024]{1,0:T(1,128)} %get-tuple-element.56) | copy-start | bytes 12292
  98.5 22.5 %collective-permute-start.8 = (f32[4,4,8,256]{3,2,1,0:T(8,128)S(1)}, f32[4,4,8,256]{3,2,1,0:T(8,128)S(1)}, u32[]{:S(2)}, u32[]{:S(2)}) collective-permute-start(f32[4,4,8,256]{3,2,1,0:T(8,128)S(1)} %get-tuple-element.66), channel_id=1, source_target_pairs={{0,4},{1,5},{2,6},{3,7},{4,0},{5,1},{6,2},{7,3},{8,12},{9,13},{10,... | collective-permute-start | bytes 393224 | tf_op jit(solution)/shard_map/ppermute | solution.py:61
  130.2 4.5 %collective-permute-start.9 = (f32[32,136,128]{2,1,0:T(8,128)S(1)}, f32[32,136,128]{2,1,0:T(8,128)S(1)}, u32[]{:S(2)}, u32[]{:S(2)}) collective-permute-start(f32[32,136,128]{2,1,0:T(8,128)S(1)} %all-to-all-done.2.half_any), channel_id=1, source_target_pairs={{0,1},{1,0},{2,3},{3,2},{4,5},{5,4},{6,7},{7,6},{8,9},{9,8},{10,11... | collective-permute-start | bytes 6684680 | tf_op jit(solution)/shard_map/ppermute | solution.py:37

commit v11 on v10

--- a/solution.py
+++ b/solution.py
@@ -53,6 +53,21 @@
 def picked(values, index):
     hit = index[:, None] == jnp.arange(values.shape[0], dtype=jnp.int32)[None, :]
     return jnp.sum(jnp.where(hit, values[None, :], 0.0), axis=1)
+
+
+def cross_two(value, high, low):
+    split = value.reshape(value.shape[0] // (2 * high), 2, high // (2 * low), 2, low, *value.shape[1:])
+    rows = []
+    for first in (0, 1):
+        row = []
+        for second in (0, 1):
+            bits = first * high + second * low
+            part = split[:, first, :, second]
+            if bits:
+                part = lax.ppermute(part, AXES, [(i, i ^ bits) for i in range(256)])
+            row.append(part)
+        rows.append(jnp.stack(row, axis=2))
+    return jnp.stack(rows, axis=1).reshape(value.shape)
 
 
 def cross(value, bit):
@@ -115,14 +130,21 @@
             )
             loads[-1].start()
     slots = jnp.transpose(slots_ref[...])
-    lane = lax.broadcasted_iota(jnp.int32, (count, cells), 1)
+    lanes = 128
+    lane = lax.broadcasted_iota(jnp.int32, (count, lanes), 1)
+    one = jnp.ones((count, lanes), bf16)
 
     def counted(f):
-        counts = jnp.zeros((count, cells), f32)
-        for look in range(looks):
-            at = f * looks + look
-            counts = counts + jnp.where(lane == slots[:, at : at + 1], 1.0, 0.0)
-        return counts.astype(bf16)
+        keys = []
+        for at in range(f * looks, (f + 1) * looks):
+            slot = slots[:, at : at + 1]
+            key = jnp.where(lane == slot % lanes, slot // lanes, -1)
+            keys.append(key.astype(f32).astype(bf16))
+        tiles = []
+        for tile in range(cells // lanes):
+            this = jnp.full((count, lanes), tile, bf16)
+            tiles.append(sum(jnp.where(key == this, one, 0 * one) for key in keys))
+        return jnp.concatenate(tiles, axis=1)
 
     counts = counted(0)
     step = cells // 4
@@ -546,17 +568,11 @@
     )
 
 
-def scaled(index, half_any, proj_ref, half, stage, in_sems, out_sems):
+def scaled(index, half, proj_ref, stage, out_sems):
     chunks, width = stage.shape[0], stage.shape[2]
     edge, rows = width // 2, width // 4
-    loads = []
-    for c in range(chunks):
-        four = pl.ds(4 * c, 4)
-        loads.append(pltpu.make_async_copy(half_any.at[four], half.at[four], in_sems.at[c]))
-        loads[-1].start()
     squares = jnp.zeros((edge, edge), jnp.float32)
     for c in range(chunks):
-        loads[c].wait()
         for q in range(4):
             block = half[4 * c + q, :edge, :]
             squares = squares + block * block
@@ -577,8 +593,8 @@
     return copies
 
 
-def own_kernel(core_ref, half_any, proj_ref, half, stage, in_sems, out_sems):
-    for copy in scaled(core_ref[0], half_any, proj_ref, half, stage, in_sems, out_sems):
+def own_kernel(core_ref, half, proj_ref, stage, out_sems):
+    for copy in scaled(core_ref[0], half, proj_ref, stage, out_sems):
         copy.wait()
 
 
@@ -586,17 +602,15 @@
     core_ref,
     proj_in,
     own_ref,
-    half_any,
+    half,
     proj_ref,
     vec_ref,
     loss_ref,
-    half,
     stage,
-    in_sems,
     out_sems,
 ):
     core = core_ref[0]
-    copies = scaled(1 - core, half_any, proj_ref, half, stage, in_sems, out_sems)
+    copies = scaled(1 - core, half, proj_ref, stage, out_sems)
     edge = half.shape[2]
     tiles = vec_ref.shape[1] // edge
     mine = core == 0
@@ -622,9 +636,7 @@
     vmem = pl.BlockSpec(memory_space=pltpu.VMEM)
     anywhere = pl.BlockSpec(memory_space=pl.ANY)
     scratch = [
-        pltpu.VMEM(own.shape, jnp.float32),
         pltpu.VMEM((chunks, width, width), jnp.float32),
-        pltpu.SemaphoreType.DMA((chunks,)),
         pltpu.SemaphoreType.DMA((chunks,)),
     ]
     proj = jax.ShapeDtypeStruct((2, wide, width), jnp.float32)
@@ -632,7 +644,7 @@
     half = pl.pallas_call(
         own_kernel,
         out_shape=proj,
-        in_specs=[smem, anywhere],
+        in_specs=[smem, vmem],
         out_specs=anywhere,
         scratch_shapes=scratch,
         compiler_params=limit,
@@ -645,7 +657,7 @@
             jax.ShapeDtypeStruct((2, wide), jnp.float32),
             jax.ShapeDtypeStruct((1, 128), jnp.float32),
         ),
-        in_specs=[smem, anywhere, vmem, anywhere],
+        in_specs=[smem, anywhere, vmem, vmem],
         out_specs=(anywhere, vmem, vmem),
         scratch_shapes=scratch,
         input_output_aliases={1: 0},
@@ -697,7 +709,7 @@
     back = reply.reshape(owners, per, width)
 
     held = exchange(held, plane_groups())
-    back = cross(cross(back, 1), 8)
+    back = cross_two(cross(back, 1), 16, 8)
     rows_new, accum_new = updated(
         slot_ids,
         cache_rows,
@@ -710,11 +722,10 @@
     )
     held = jnp.sum(held, axis=0)
     held = (held + shift_z(held, 4)) + (shift_z(held, 2) + shift_z(held, -2))
-    back = cross(cross(back, 16), 2)
+    back = cross(cross(back, 2), 4)
     held, back = lax.optimization_barrier((held, back))
     whole = jnp.broadcast_to(held[None], (4 * feats, *held.shape))
     whole = exchange(whole, plane_groups())
-    back = cross(back, 4)
     in_place = (miss_dest[:, 0] ^ me) * per + ranks(miss_dest[:, 0])
     rows_new = refilled(evict_slot, in_place, back.reshape(spots, width), rows_new)
     fetched_accum = picked(back[:, per - 1, :per].reshape(-1), in_place)

time: 140 us -> 143 us (1.021)
  waiting for transfers between devices: 40.3 us -> 43.8 us
  Pallas kernels: 38.6 us -> 36.3 us
    ppermute x5 -> x3, waiting for transfers between devices: 26.5 us -> 7.52 us  [cross(): came = lax.ppermute(split[:, 1], AXES, there)]
    all_to_all x2, waiting for transfers between devices: 9.47 us -> 25 us  [exchange(): lax.all_to_all(value, AXES, split_axis=0, concat_axis=0, tiled=True, axis...]
    ppermute x0 -> x3, starting transfers between devices: none -> 6.91 us  [cross_two(): part = lax.ppermute(part, AXES, [(i, i ^ bits) for i in range(256)])]
    ppermute x5 -> x3, starting transfers between devices: 9 us -> 2.6 us  [cross(): came = lax.ppermute(split[:, 1], AXES, there)]
    ppermute x0 -> x3, waiting for transfers between devices: none -> 4.96 us  [cross_two(): part = lax.ppermute(part, AXES, [(i, i ^ bits) for i in range(256)])]
    pallas_call x1, Pallas kernels: 12.4 us -> 10.9 us  [dense(): pl.pallas_call(dense_kernel, out_shape=(jax.ShapeDtypeStruct(bundle, f32)...]
    unnamed x21 -> x20, local copies, waits for them, and re-layouts: 4.02 us -> 4 us
  transfers between devices with their start and end apart: 13 -> 14, of which waited for: 8 -> 8; matrix products, arithmetic and copies ran while one was open for 4% -> 3% of each run, Pallas kernels for 24% -> 22%
where the time goes in v11:
time: 143 us; the launch traced here: 141 us
  starting transfers between devices  46 us (32%)
  waiting for transfers between devices  43.8 us (31%)
  Pallas kernels  36.3 us (25%)
  local copies, waits for them, and re-layouts  8.41 us (6%)
  other arithmetic  4.12 us (3%)
  between operations  2.08 us (1%)
    all_to_all x2, waiting for transfers between devices, exchange(): lax.all_to_all(value, AXES, split_axis=0, concat_axis=0, tiled=True, axis...  25 us
    all_to_all x2, starting transfers between devices, exchange(): lax.all_to_all(value, AXES, split_axis=0, concat_axis=0, tiled=True, axis...  18.1 us
    pallas_call x1, Pallas kernels, dense(): pl.pallas_call(dense_kernel, out_shape=(jax.ShapeDtypeStruct(bundle, f32)...  10.9 us
    all_to_all x1, starting transfers between devices, shards(): got = lax.all_to_all(sent, 'table', split_axis=0, concat_axis=0, tiled=True)  10.3 us
    pallas_call x1, Pallas kernels, updated(): pl.pallas_call(update_kernel, out_shape=(jax.ShapeDtypeStruct(cache_rows....  9.39 us
    ppermute x3, waiting for transfers between devices, cross(): came = lax.ppermute(split[:, 1], AXES, there)  7.52 us
    ppermute x3, starting transfers between devices, cross_two(): part = lax.ppermute(part, AXES, [(i, i ^ bits) for i in range(256)])  6.91 us
    ppermute x3, starting transfers between devices, shift_z(): return lax.ppermute(value, AXES, there)  6.23 us
  transfers between devices with their start and end apart: 14, of which 8 were waited for; matrix products, arithmetic and copies ran while one was open for 3% of the time, Pallas kernels for 22%

profile of v11, /device:TPU:3, one launch (start us, length us, event | category | flops | bytes accessed | tf_op | source)
XLA Modules:
  0.0 140.6 jit_solution(15375528815910588069)
XLA Ops:
  0.6 2.9 %payload.1 = f32[256,256]{1,0:T(8,128)} custom-call(s32[64]{0:T(128)} %evict_ref.1, s32[2,64]{1,0:T(2,128)} %bitcast.89, s32[2,64]{1,0:T(2,128)} %bitcast.87, f32[1024]{0:T(1024)} %accum_ref.1, f32[1024,256]{1,0:T(8,128)} %cache_ref.1), custom_call_target="tpu_custom_call" | custom-call | flops 100000 | bytes 1500000 | tf_op jit(solution)/shard_map/payload/pallas_call | solution.py:377
  3.6 10.3 %all-to-all-start = ((f32[32,8,256]{2,1,0:T(8,128)}), f32[32,8,256]{2,1,0:T(8,128)S(1)}, u32[]{:S(2)}, u32[]{:S(2)}) async-start(f32[32,8,256]{2,1,0:T(8,128)} %bitcast.73), calls=%async_computation | async-start | bytes 524288 | tf_op jit(solution)/shard_map/all_to_all | solution.py:696
  13.9 10.9 %dense.1 = (f32[32,136,128]{2,1,0:T(8,128)}, bf16[256,2048]{1,0:T(8,128)(2,1)}, bf16[256,256]{1,0:T(8,128)(2,1)}, bf16[256,256]{1,0:T(8,128)(2,1)}, f32[1,256]{1,0:T(1,128)}, /*index=5*/f32[32,8,128]{2,1,0:T(8,128)}) custom-call(s32[1]{0:T(128)} %bitcast.core_ref, s32[32,256]{1,0:T(8,128)} %bitcast.90, s32[1,256]{1,0:T(1,128)} %bitcast.96, ...), custom_call_target="tpu_custom_call" | custom-call | flops 5000000000 | bytes 9000000 | tf_op jit(solution)/shard_map/dense/pallas_call | solution.py:244
  24.8 1.0 all-to-all-done
  25.8 1.5 %collective-permute-start = (f32[32,136,128]{2,1,0:T(8,128)}, f32[32,136,128]{2,1,0:T(8,128)S(1)}, u32[]{:S(2)}, u32[]{:S(2)}) collective-permute-start(f32[32,136,128]{2,1,0:T(8,128)} %get-tuple-element.43), channel_id=1, source_target_pairs={{0,1},{1,0},{2,3},{3,2},{4,5},{5,4},{6,7},{7,6},{8,9},{9,8},{10,11... | collective-permute-start | bytes 6684680 | tf_op jit(solution)/shard_map/ppermute | solution.py:37
  27.3 1.2 copy-done
  28.5 0.9 copy-done.1
  29.4 0.9 copy-done.2
  30.3 0.9 copy-done.3
  31.2 0.5 kept.1
  31.8 1.6 %add.22 = f32[32,136,128]{2,1,0:T(8,128)} add(f32[32,136,128]{2,1,0:T(8,128)S(1)} %kept.1, f32[32,136,128]{2,1,0:T(8,128)S(1)} %collective-permute-done) | non-fusion elementwise | flops 557056 | bytes 6684672 | tf_op jit(solution)/shard_map/add | solution.py:705
  33.4 8.9 %all-to-all-start.1 = ((f32[32,136,128]{2,1,0:T(8,128)}), f32[32,136,128]{2,1,0:T(8,128)S(1)}, u32[]{:S(2)}, u32[]{:S(2)}) async-start(f32[32,136,128]{2,1,0:T(8,128)} %add.22), calls=%async_computation.1 | async-start | bytes 4456448 | tf_op jit(solution)/shard_map/all_to_all | solution.py:41
  42.2 0.1 copy.53
  42.3 0.6 slice_bitcast_fusion.9
  43.0 6.0 %reply.1 = (f32[256,256]{1,0:T(8,128)}, f32[1024,256]{1,0:T(8,128)}, f32[1024]{0:T(1024)}) custom-call(s32[1]{0:T(128)} %bitcast.8.me_ref, s32[32,24]{1,0:T(8,128)} %get-tuple-element.75.ids_ref, f32[32,8]{1,0:T(8,128)} %bitcast.82, f32[256,256]{1,0:T(8,128)} %bitcast.70, f32[1024,256]{1,0:T(8,128)} %table_any.1, f32[1024]{0:T(1024)} %accum_any.1), custom_call_target="tpu_custom_call" | custom-call | flops 100000 | bytes 3000000 | tf_op jit(solution)/shard_map/reply/pallas_call | solution.py:544
  49.0 1.0 fusion.4
  50.0 0.1 collective-permute-start.1
  50.1 1.3 collective-permute-done.1
  51.5 4.3 %collective-permute-start.4 = (f32[1,1,8,8,256]{4,3,2,1,0:T(8,128)S(1)}, f32[1,1,8,8,256]{4,3,2,1,0:T(8,128)S(1)}, u32[]{:S(2)}, u32[]{:S(2)}) collective-permute-start(f32[1,1,8,8,256]{4,3,2,1,0:T(8,128)S(1)} %slice_bitcast_fusion.5), channel_id=1, source_target_pairs={{0,24},{1,25},{2,26},{3,27},{4,28},{5,29},{6,30},{7,31},{8,16},{9,... | collective-permute-start | bytes 196616 | tf_op jit(solution)/shard_map/ppermute | solution.py:67
  55.8 0.6 collective-permute-start.3
  56.3 9.4 %update.1 = (f32[1024,256]{1,0:T(8,128)}, f32[1,1024]{1,0:T(1,128)}) custom-call(s32[32,256]{1,0:T(8,128)} %bitcast.91, f32[1024,256]{1,0:T(8,128)} %cache_ref.1, f32[1,1024]{1,0:T(1,128)} %bitcast.86, bf16[256,256]{1,0:T(8,128)(2,1)} %get-tuple-element.38.latent_ref, bf16[256,256]{1,0:T(8,128)(2,1)} %get-tuple-element.39.dlatent_ref, ...), custom_call_target="tpu_custom_call" | custom-call | flops 1100000000 | bytes 4000000 | tf_op jit(solution)/shard_map/update/pallas_call | solution.py:447
  65.7 2.1 %collective-permute-start.2 = (f32[1,1,8,8,256]{4,3,2,1,0:T(8,128)S(1)}, f32[1,1,8,8,256]{4,3,2,1,0:T(8,128)S(1)}, u32[]{:S(2)}, u32[]{:S(2)}) collective-permute-start(f32[1,1,8,8,256]{4,3,2,1,0:T(8,128)S(1)} %get-tuple-element.71), channel_id=1, source_target_pairs={{0,8},{1,9},{2,10},{3,11},{4,12},{5,13},{6,14},{7,15},{8,0},{9,1},... | collective-permute-start | bytes 196616 | tf_op jit(solution)/shard_map/ppermute | solution.py:67
  67.8 0.9 collective-permute-done.3
  68.7 4.0 %collective-permute-done.2 = f32[1,1,8,8,256]{4,3,2,1,0:T(8,128)S(1)} collective-permute-done((f32[1,1,8,8,256]{4,3,2,1,0:T(8,128)S(1)}, f32[1,1,8,8,256]{4,3,2,1,0:T(8,128)S(1)}, u32[]{:S(2)}, u32[]{:S(2)}) %collective-permute-start.2) | collective-permute-done | bytes 65568 | tf_op jit(solution)/shard_map/ppermute | solution.py:67
  72.8 0.3 collective-permute-start.8
  73.1 0.1 reduce_sum.38
  73.2 2.7 %collective-permute-start.7 = (f32[136,128]{1,0:T(8,128)S(1)}, f32[136,128]{1,0:T(8,128)S(1)}, u32[]{:S(2)}, u32[]{:S(2)}) collective-permute-start(f32[136,128]{1,0:T(8,128)S(1)} %reduce_sum.38), channel_id=1, source_target_pairs={{0,12},{1,13},{2,14},{3,15},{4,0},{5,1},{6,2},{7,3},{8,4},{9,5},{1... | collective-permute-start | bytes 208904 | tf_op jit(solution)/shard_map/ppermute | solution.py:33
  75.9 3.5 %collective-permute-start.5 = (f32[136,128]{1,0:T(8,128)S(1)}, f32[136,128]{1,0:T(8,128)S(1)}, u32[]{:S(2)}, u32[]{:S(2)}) collective-permute-start(f32[136,128]{1,0:T(8,128)S(1)} %reduce_sum.38), channel_id=1, source_target_pairs={{0,8},{1,9},{2,10},{3,11},{4,12},{5,13},{6,14},{7,15},{8,0},{9,1},... | collective-permute-start | bytes 208904 | tf_op jit(solution)/shard_map/ppermute | solution.py:33
  79.5 2.2 %collective-permute-start.9 = (f32[4,4,8,256]{3,2,1,0:T(8,128)S(1)}, f32[4,4,8,256]{3,2,1,0:T(8,128)S(1)}, u32[]{:S(2)}, u32[]{:S(2)}) collective-permute-start(f32[4,4,8,256]{3,2,1,0:T(8,128)S(1)} %get-tuple-element.66), channel_id=1, source_target_pairs={{0,4},{1,5},{2,6},{3,7},{4,0},{5,1},{6,2},{7,3},{8,12},{9,13},{10,... | collective-permute-start | bytes 393224 | tf_op jit(solution)/shard_map/ppermute | solution.py:76
  81.8 3.0 %collective-permute-done.5 = f32[136,128]{1,0:T(8,128)S(1)} collective-permute-done((f32[136,128]{1,0:T(8,128)S(1)}, f32[136,128]{1,0:T(8,128)S(1)}, u32[]{:S(2)}, u32[]{:S(2)}) %collective-permute-start.5) | collective-permute-done | bytes 69664 | tf_op jit(solution)/shard_map/ppermute | solution.py:33
  84.8 6.2 %collective-permute-done.9 = f32[4,4,8,256]{3,2,1,0:T(8,128)S(1)} collective-permute-done((f32[4,4,8,256]{3,2,1,0:T(8,128)S(1)}, f32[4,4,8,256]{3,2,1,0:T(8,128)S(1)}, u32[]{:S(2)}, u32[]{:S(2)}) %collective-permute-start.9) | collective-permute-done | bytes 131104 | tf_op jit(solution)/shard_map/ppermute | solution.py:76
  91.0 0.7 copy.61
  91.7 1.5 %broadcast_in_dim.68 = f32[32,136,128]{2,1,0:T(8,128)} broadcast(f32[136,128]{1,0:T(8,128)S(1)} %add_add_fusion), dimensions={1,2} | broadcast | bytes 2297856 | tf_op jit(solution)/shard_map/broadcast_in_dim | solution.py:727
  93.2 9.2 %all-to-all-start.2 = ((f32[32,136,128]{2,1,0:T(8,128)}), f32[32,136,128]{2,1,0:T(8,128)S(1)}, u32[]{:S(2)}, u32[]{:S(2)}) async-start(f32[32,136,128]{2,1,0:T(8,128)} %broadcast_in_dim.68), calls=%async_computation.2 | async-start | bytes 4456448 | tf_op jit(solution)/shard_map/all_to_all | solution.py:41
  102.5 0.2 convert_reduce_fusion
  102.7 0.1 fusion
  102.8 0.5 multiply_add_fusion.place_ref
  103.3 2.6 %refill.1 = f32[1024,256]{1,0:T(8,128)} custom-call(s32[64]{0:T(128)} %evict_ref.1, s32[64]{0:T(128)} %multiply_add_fusion.place_ref, f32[256,256]{1,0:T(8,128)} %bitcast.71, f32[1024,256]{1,0:T(8,128)} %get-tuple-element.55.old_ref), custom_call_target="tpu_custom_call" | custom-call | flops 100000 | bytes 2000000 | tf_op jit(solution)/shard_map/refill/pallas_call | solution.py:466
  106.0 1.0 slice_reduce_fusion
  106.9 0.1 broadcast_in_dim.69
  107.0 0.2 select_reduce_fusion.1
  107.2 0.1 select_reduce_fusion
  107.3 0.6 select_n.22
  107.9 25.0 %all-to-all-done.2.half = f32[32,136,128]{2,1,0:T(8,128)S(1)} async-done(((f32[32,136,128]{2,1,0:T(8,128)}), f32[32,136,128]{2,1,0:T(8,128)S(1)}, u32[]{:S(2)}, u32[]{:S(2)}) %all-to-all-start.2) | async-done | bytes 2228256 | tf_op jit(solution)/shard_map/all_to_all | solution.py:41
  132.9 0.3 collective-permute-start.10
  133.2 1.6 %scale_own.1.proj_in = f32[2,2048,256]{2,1,0:T(8,128)} custom-call(s32[1]{0:T(128)} %bitcast.core_ref, f32[32,136,128]{2,1,0:T(8,128)S(1)} %all-to-all-done.2.half), custom_call_target="tpu_custom_call" | custom-call | tf_op jit(solution)/shard_map/scale_own/pallas_call | solution.py:644
  134.9 2.4 %collective-permute-done.10.half = f32[32,136,128]{2,1,0:T(8,128)S(1)} collective-permute-done((f32[32,136,128]{2,1,0:T(8,128)S(1)}, f32[32,136,128]{2,1,0:T(8,128)S(1)}, u32[]{:S(2)}, u32[]{:S(2)}) %collective-permute-start.10) | collective-permute-done | bytes 2228256 | tf_op jit(solution)/shard_map/ppermute | solution.py:37
  137.2 2.2 %scale_other.1 = (f32[2,2048,256]{2,1,0:T(8,128)}, f32[2,2048]{1,0:T(2,128)}, f32[1,128]{1,0:T(1,128)S(1)}) custom-call(s32[1]{0:T(128)} %bitcast.core_ref, f32[2,2048,256]{2,1,0:T(8,128)} %scale_own.1.proj_in, f32[32,8,128]{2,1,0:T(8,128)S(1)} %slice.63.own_ref, f32[32,136,128]{2,1,0:T(8,128)S(1)} %collective-permute-done.10.half), custom_call_target="tpu_custom_call", output_to_operand_aliasing={{0}: (1, {})} | custom-call | tf_op jit(solution)/shard_map/scale_other/pallas_call | solution.py:653
  (36 shorter events, 0.3 us)
Async XLA Ops:
  3.6 22.2 %all-to-all-start = ((f32[32,8,256]{2,1,0:T(8,128)}), f32[32,8,256]{2,1,0:T(8,128)S(1)}, u32[]{:S(2)}, u32[]{:S(2)}) async-start(f32[32,8,256]{2,1,0:T(8,128)} %bitcast.73), calls=%async_computation | async-start | bytes 524288 | tf_op jit(solution)/shard_map/all_to_all | solution.py:696
  25.8 16.4 %copy-start.4 = (f32[32,8,256]{2,1,0:T(8,128)}, f32[32,8,256]{2,1,0:T(8,128)S(1)}, u32[]{:S(2)}) copy-start(f32[32,8,256]{2,1,0:T(8,128)S(1)} %all-to-all-done) | copy-start | bytes 786436
  25.8 5.9 %collective-permute-start = (f32[32,136,128]{2,1,0:T(8,128)}, f32[32,136,128]{2,1,0:T(8,128)S(1)}, u32[]{:S(2)}, u32[]{:S(2)}) collective-permute-start(f32[32,136,128]{2,1,0:T(8,128)} %get-tuple-element.43), channel_id=1, source_target_pairs={{0,1},{1,0},{2,3},{3,2},{4,5},{5,4},{6,7},{7,6},{8,9},{9,8},{10,11... | collective-permute-start | bytes 6684680 | tf_op jit(solution)/shard_map/ppermute | solution.py:37
  27.3 1.2 copy-start
  28.5 0.9 copy-start.1
  29.4 0.9 copy-start.2
  30.3 0.9 copy-start.3
  33.4 39.4 %all-to-all-start.1 = ((f32[32,136,128]{2,1,0:T(8,128)}), f32[32,136,128]{2,1,0:T(8,128)S(1)}, u32[]{:S(2)}, u32[]{:S(2)}) async-start(f32[32,136,128]{2,1,0:T(8,128)} %add.22), calls=%async_computation.1 | async-start | bytes 4456448 | tf_op jit(solution)/shard_map/all_to_all | solution.py:41
  50.0 1.4 %collective-permute-start.1 = (f32[16,1,8,256]{3,2,0,1:T(8,128)S(1)}, f32[16,1,8,256]{3,2,0,1:T(8,128)S(1)}, u32[]{:S(2)}, u32[]{:S(2)}) collective-permute-start(f32[16,1,8,256]{3,2,0,1:T(8,128)S(1)} %get-tuple-element.73), channel_id=1, source_target_pairs={{0,1},{1,0},{2,3},{3,2},{4,5},{5,4},{6,7},{7,6},{8,9},{9,8},{10,11... | collective-permute-start | bytes 393224 | tf_op jit(solution)/shard_map/ppermute | solution.py:76
  51.5 16.3 %collective-permute-start.4 = (f32[1,1,8,8,256]{4,3,2,1,0:T(8,128)S(1)}, f32[1,1,8,8,256]{4,3,2,1,0:T(8,128)S(1)}, u32[]{:S(2)}, u32[]{:S(2)}) collective-permute-start(f32[1,1,8,8,256]{4,3,2,1,0:T(8,128)S(1)} %slice_bitcast_fusion.5), channel_id=1, source_target_pairs={{0,24},{1,25},{2,26},{3,27},{4,28},{5,29},{6,30},{7,31},{8,16},{9,... | collective-permute-start | bytes 196616 | tf_op jit(solution)/shard_map/ppermute | solution.py:67
  55.8 12.9 %collective-permute-start.3 = (f32[1,1,8,8,256]{4,3,2,1,0:T(8,128)S(1)}, f32[1,1,8,8,256]{4,3,2,1,0:T(8,128)S(1)}, u32[]{:S(2)}, u32[]{:S(2)}) collective-permute-start(f32[1,1,8,8,256]{4,3,2,1,0:T(8,128)S(1)} %get-tuple-element.70), channel_id=1, source_target_pairs={{0,16},{1,17},{2,18},{3,19},{4,20},{5,21},{6,22},{7,23},{8,24},{9,... | collective-permute-start | bytes 196616 | tf_op jit(solution)/shard_map/ppermute | solution.py:67
  65.7 7.0 %collective-permute-start.2 = (f32[1,1,8,8,256]{4,3,2,1,0:T(8,128)S(1)}, f32[1,1,8,8,256]{4,3,2,1,0:T(8,128)S(1)}, u32[]{:S(2)}, u32[]{:S(2)}) collective-permute-start(f32[1,1,8,8,256]{4,3,2,1,0:T(8,128)S(1)} %get-tuple-element.71), channel_id=1, source_target_pairs={{0,8},{1,9},{2,10},{3,11},{4,12},{5,13},{6,14},{7,15},{8,0},{9,1},... | collective-permute-start | bytes 196616 | tf_op jit(solution)/shard_map/ppermute | solution.py:67
  72.8 6.6 %collective-permute-start.8 = (f32[8,2,8,256]{3,2,1,0:T(8,128)S(1)}, f32[8,2,8,256]{3,2,1,0:T(8,128)S(1)}, u32[]{:S(2)}, u32[]{:S(2)}) collective-permute-start(f32[8,2,8,256]{3,2,1,0:T(8,128)S(1)} %get-tuple-element.68), channel_id=1, source_target_pairs={{0,2},{1,3},{2,0},{3,1},{4,6},{5,7},{6,4},{7,5},{8,10},{9,11},{10,... | collective-permute-start | bytes 393224 | tf_op jit(solution)/shard_map/ppermute | solution.py:76
  73.2 8.6 %collective-permute-start.7 = (f32[136,128]{1,0:T(8,128)S(1)}, f32[136,128]{1,0:T(8,128)S(1)}, u32[]{:S(2)}, u32[]{:S(2)}) collective-permute-start(f32[136,128]{1,0:T(8,128)S(1)} %reduce_sum.38), channel_id=1, source_target_pairs={{0,12},{1,13},{2,14},{3,15},{4,0},{5,1},{6,2},{7,3},{8,4},{9,5},{1... | collective-permute-start | bytes 208904 | tf_op jit(solution)/shard_map/ppermute | solution.py:33
  75.9 5.8 %collective-permute-start.6 = (f32[136,128]{1,0:T(8,128)S(1)}, f32[136,128]{1,0:T(8,128)S(1)}, u32[]{:S(2)}, u32[]{:S(2)}) collective-permute-start(f32[136,128]{1,0:T(8,128)S(1)} %reduce_sum.38), channel_id=1, source_target_pairs={{0,4},{1,5},{2,6},{3,7},{4,8},{5,9},{6,10},{7,11},{8,12},{9,13},{1... | collective-permute-start | bytes 208904 | tf_op jit(solution)/shard_map/ppermute | solution.py:33
  75.9 8.8 %collective-permute-start.5 = (f32[136,128]{1,0:T(8,128)S(1)}, f32[136,128]{1,0:T(8,128)S(1)}, u32[]{:S(2)}, u32[]{:S(2)}) collective-permute-start(f32[136,128]{1,0:T(8,128)S(1)} %reduce_sum.38), channel_id=1, source_target_pairs={{0,8},{1,9},{2,10},{3,11},{4,12},{5,13},{6,14},{7,15},{8,0},{9,1},... | collective-permute-start | bytes 208904 | tf_op jit(solution)/shard_map/ppermute | solution.py:33
  79.5 11.4 %collective-permute-start.9 = (f32[4,4,8,256]{3,2,1,0:T(8,128)S(1)}, f32[4,4,8,256]{3,2,1,0:T(8,128)S(1)}, u32[]{:S(2)}, u32[]{:S(2)}) collective-permute-start(f32[4,4,8,256]{3,2,1,0:T(8,128)S(1)} %get-tuple-element.66), channel_id=1, source_target_pairs={{0,4},{1,5},{2,6},{3,7},{4,0},{5,1},{6,2},{7,3},{8,12},{9,13},{10,... | collective-permute-start | bytes 393224 | tf_op jit(solution)/shard_map/ppermute | solution.py:76
  93.2 9.2 %copy-start.7 = (s32[64,2]{0,1:T(2,128)S(1)}, s32[64,2]{0,1:T(2,128)}, u32[]{:S(2)}) copy-start(s32[64,2]{0,1:T(2,128)} %param.19) | copy-start | bytes 1540
  93.2 9.4 %copy-start.5 = (s32[64]{0:T(128)S(1)}, s32[64]{0:T(128)}, u32[]{:S(2)}) copy-start(s32[64]{0:T(128)} %evict_ref.1) | copy-start | bytes 772
  93.2 39.6 %all-to-all-start.2 = ((f32[32,136,128]{2,1,0:T(8,128)}), f32[32,136,128]{2,1,0:T(8,128)S(1)}, u32[]{:S(2)}, u32[]{:S(2)}) async-start(f32[32,136,128]{2,1,0:T(8,128)} %broadcast_in_dim.68), calls=%async_computation.2 | async-start | bytes 4456448 | tf_op jit(solution)/shard_map/all_to_all | solution.py:41
  102.5 4.7 %copy-start.6 = (s32[64]{0:T(128)S(1)}, s32[64]{0:T(128)}, u32[]{:S(2)}) copy-start(s32[64]{0:T(128)} %evict_ref.1) | copy-start | bytes 772
  102.5 4.8 %copy-start.8 = (f32[1,1024]{1,0:T(1,128)S(1)}, f32[1,1024]{1,0:T(1,128)}, u32[]{:S(2)}) copy-start(f32[1,1024]{1,0:T(1,128)} %get-tuple-element.56) | copy-start | bytes 12292
  132.9 4.3 %collective-permute-start.10 = (f32[32,136,128]{2,1,0:T(8,128)S(1)}, f32[32,136,128]{2,1,0:T(8,128)S(1)}, u32[]{:S(2)}, u32[]{:S(2)}) collective-permute-start(f32[32,136,128]{2,1,0:T(8,128)S(1)} %all-to-all-done.2.half), channel_id=1, source_target_pairs={{0,1},{1,0},{2,3},{3,2},{4,5},{5,4},{6,7},{7,6},{8,9},{9,8},{10,11... | collective-permute-start | bytes 6684680 | tf_op jit(solution)/shard_map/ppermute | solution.py:37

commit v12 on v11

--- a/solution.py
+++ b/solution.py
@@ -53,21 +53,6 @@
 def picked(values, index):
     hit = index[:, None] == jnp.arange(values.shape[0], dtype=jnp.int32)[None, :]
     return jnp.sum(jnp.where(hit, values[None, :], 0.0), axis=1)
-
-
-def cross_two(value, high, low):
-    split = value.reshape(value.shape[0] // (2 * high), 2, high // (2 * low), 2, low, *value.shape[1:])
-    rows = []
-    for first in (0, 1):
-        row = []
-        for second in (0, 1):
-            bits = first * high + second * low
-            part = split[:, first, :, second]
-            if bits:
-                part = lax.ppermute(part, AXES, [(i, i ^ bits) for i in range(256)])
-            row.append(part)
-        rows.append(jnp.stack(row, axis=2))
-    return jnp.stack(rows, axis=1).reshape(value.shape)
 
 
 def cross(value, bit):
@@ -709,7 +694,7 @@
     back = reply.reshape(owners, per, width)
 
     held = exchange(held, plane_groups())
-    back = cross_two(cross(back, 1), 16, 8)
+    back = cross(cross(back, 1), 8)
     rows_new, accum_new = updated(
         slot_ids,
         cache_rows,
@@ -722,10 +707,11 @@
     )
     held = jnp.sum(held, axis=0)
     held = (held + shift_z(held, 4)) + (shift_z(held, 2) + shift_z(held, -2))
-    back = cross(cross(back, 2), 4)
+    back = cross(cross(back, 16), 2)
     held, back = lax.optimization_barrier((held, back))
     whole = jnp.broadcast_to(held[None], (4 * feats, *held.shape))
     whole = exchange(whole, plane_groups())
+    back = cross(back, 4)
     in_place = (miss_dest[:, 0] ^ me) * per + ranks(miss_dest[:, 0])
     rows_new = refilled(evict_slot, in_place, back.reshape(spots, width), rows_new)
     fetched_accum = picked(back[:, per - 1, :per].reshape(-1), in_place)

time: 143 us -> 138 us (0.965); the launches traced: 141 us -> 137 us
  waiting for transfers between devices: 43.8 us -> 40.2 us
    ppermute x3 -> x5, waiting for transfers between devices: 7.52 us -> 24.3 us  [cross(): came = lax.ppermute(split[:, 1], AXES, there)]
    all_to_all x2, waiting for transfers between devices: 25 us -> 10.3 us  [exchange(): lax.all_to_all(value, AXES, split_axis=0, concat_axis=0, tiled=True, axis...]
    ppermute x3 -> x0, starting transfers between devices: 6.91 us -> none  [cross_two(): part = lax.ppermute(part, AXES, [(i, i ^ bits) for i in range(256)])]
    ppermute x3 -> x0, waiting for transfers between devices: 4.96 us -> none  [cross_two(): part = lax.ppermute(part, AXES, [(i, i ^ bits) for i in range(256)])]
    ppermute x3 -> x5, starting transfers between devices: 2.6 us -> 7.27 us  [cross(): came = lax.ppermute(split[:, 1], AXES, there)]
    all_to_all x2, starting transfers between devices: 18.1 us -> 20.5 us  [exchange(): lax.all_to_all(value, AXES, split_axis=0, concat_axis=0, tiled=True, axis...]
    unnamed x20 -> x21, local copies, waits for them, and re-layouts: 4 us -> 4.02 us
  transfers between devices with their start and end apart: 14 -> 13, of which waited for: 8 -> 9; matrix products, arithmetic and copies ran while one was open for 3% -> 4% of each run, Pallas kernels for 22% -> 23%
where the time goes in v12:
time: 138 us; the launch traced here: 137 us
  starting transfers between devices  46 us (33%)
  waiting for transfers between devices  40.2 us (29%)
  Pallas kernels  36.4 us (26%)
  local copies, waits for them, and re-layouts  8.45 us (6%)
  other arithmetic  4.12 us (3%)
  between operations  2.07 us (1%)
    ppermute x5, waiting for transfers between devices, cross(): came = lax.ppermute(split[:, 1], AXES, there)  24.3 us
    all_to_all x2, starting transfers between devices, exchange(): lax.all_to_all(value, AXES, split_axis=0, concat_axis=0, tiled=True, axis...  20.5 us
    pallas_call x1, Pallas kernels, dense(): pl.pallas_call(dense_kernel, out_shape=(jax.ShapeDtypeStruct(bundle, f32)...  10.9 us
    all_to_all x1, starting transfers between devices, shards(): got = lax.all_to_all(sent, 'table', split_axis=0, concat_axis=0, tiled=True)  10.3 us
    all_to_all x2, waiting for transfers between devices, exchange(): lax.all_to_all(value, AXES, split_axis=0, concat_axis=0, tiled=True, axis...  10.3 us
    pallas_call x1, Pallas kernels, updated(): pl.pallas_call(update_kernel, out_shape=(jax.ShapeDtypeStruct(cache_rows....  9.39 us
    ppermute x5, starting transfers between devices, cross(): came = lax.ppermute(split[:, 1], AXES, there)  7.27 us
    pallas_call x1, Pallas kernels, replied(): pl.pallas_call(reply_kernel, out_shape=(jax.ShapeDtypeStruct((owners * pe...  6.15 us
  transfers between devices with their start and end apart: 13, of which 9 were waited for; matrix products, arithmetic and copies ran while one was open for 4% of the time, Pallas kernels for 23%

profile of v12, /device:TPU:3, one launch (start us, length us, event | category | flops | bytes accessed | tf_op | source)
XLA Modules:
  0.0 137.1 jit_solution(2329861494783783453)
XLA Ops:
  0.6 2.9 %payload.1 = f32[256,256]{1,0:T(8,128)} custom-call(s32[64]{0:T(128)} %evict_ref.1, s32[2,64]{1,0:T(2,128)} %bitcast.81, s32[2,64]{1,0:T(2,128)} %bitcast.79, f32[1024]{0:T(1024)} %accum_ref.1, f32[1024,256]{1,0:T(8,128)} %cache_ref.1), custom_call_target="tpu_custom_call" | custom-call | flops 100000 | bytes 1500000 | tf_op jit(solution)/shard_map/payload/pallas_call | solution.py:362
  3.6 10.3 %all-to-all-start = ((f32[32,8,256]{2,1,0:T(8,128)}), f32[32,8,256]{2,1,0:T(8,128)S(1)}, u32[]{:S(2)}, u32[]{:S(2)}) async-start(f32[32,8,256]{2,1,0:T(8,128)} %bitcast.66), calls=%async_computation | async-start | bytes 524288 | tf_op jit(solution)/shard_map/all_to_all | solution.py:681
  13.9 10.9 %dense.1 = (f32[32,136,128]{2,1,0:T(8,128)}, bf16[256,2048]{1,0:T(8,128)(2,1)}, bf16[256,256]{1,0:T(8,128)(2,1)}, bf16[256,256]{1,0:T(8,128)(2,1)}, f32[1,256]{1,0:T(1,128)}, /*index=5*/f32[32,8,128]{2,1,0:T(8,128)}) custom-call(s32[1]{0:T(128)} %bitcast.core_ref, s32[32,256]{1,0:T(8,128)} %bitcast.82, s32[1,256]{1,0:T(1,128)} %bitcast.88, ...), custom_call_target="tpu_custom_call" | custom-call | flops 5000000000 | bytes 9000000 | tf_op jit(solution)/shard_map/dense/pallas_call | solution.py:229
  24.8 1.0 all-to-all-done
  25.8 1.5 %collective-permute-start = (f32[32,136,128]{2,1,0:T(8,128)}, f32[32,136,128]{2,1,0:T(8,128)S(1)}, u32[]{:S(2)}, u32[]{:S(2)}) collective-permute-start(f32[32,136,128]{2,1,0:T(8,128)} %get-tuple-element.43), channel_id=1, source_target_pairs={{0,1},{1,0},{2,3},{3,2},{4,5},{5,4},{6,7},{7,6},{8,9},{9,8},{10,11... | collective-permute-start | bytes 6684680 | tf_op jit(solution)/shard_map/ppermute | solution.py:37
  27.3 1.2 copy-done
  28.5 0.9 copy-done.1
  29.4 0.9 copy-done.2
  30.3 0.9 copy-done.3
  31.2 0.5 kept.1
  31.8 1.6 %add.22 = f32[32,136,128]{2,1,0:T(8,128)} add(f32[32,136,128]{2,1,0:T(8,128)S(1)} %kept.1, f32[32,136,128]{2,1,0:T(8,128)S(1)} %collective-permute-done) | non-fusion elementwise | flops 557056 | bytes 6684672 | tf_op jit(solution)/shard_map/add | solution.py:690
  33.4 8.9 %all-to-all-start.1 = ((f32[32,136,128]{2,1,0:T(8,128)}), f32[32,136,128]{2,1,0:T(8,128)S(1)}, u32[]{:S(2)}, u32[]{:S(2)}) async-start(f32[32,136,128]{2,1,0:T(8,128)} %add.22), calls=%async_computation.1 | async-start | bytes 4456448 | tf_op jit(solution)/shard_map/all_to_all | solution.py:41
  42.2 0.1 copy.53
  42.3 0.6 slice_bitcast_fusion.8
  43.0 6.2 %reply.1 = (f32[256,256]{1,0:T(8,128)}, f32[1024,256]{1,0:T(8,128)}, f32[1024]{0:T(1024)}) custom-call(s32[1]{0:T(128)} %bitcast.8.me_ref, s32[32,24]{1,0:T(8,128)} %get-tuple-element.76.ids_ref, f32[32,8]{1,0:T(8,128)} %bitcast.77, f32[256,256]{1,0:T(8,128)} %bitcast.63, f32[1024,256]{1,0:T(8,128)} %table_any.1, f32[1024]{0:T(1024)} %accum_any.1), custom_call_target="tpu_custom_call" | custom-call | flops 100000 | bytes 3000000 | tf_op jit(solution)/shard_map/reply/pallas_call | solution.py:529
  49.1 1.0 fusion.5
  50.1 0.1 collective-permute-start.1
  50.2 1.3 collective-permute-done.1
  51.6 3.6 %collective-permute-start.2 = (f32[2,8,8,256]{3,2,1,0:T(8,128)S(1)}, f32[2,8,8,256]{3,2,1,0:T(8,128)S(1)}, u32[]{:S(2)}, u32[]{:S(2)}) collective-permute-start(f32[2,8,8,256]{3,2,1,0:T(8,128)S(1)} %get-tuple-element.72), channel_id=1, source_target_pairs={{0,8},{1,9},{2,10},{3,11},{4,12},{5,13},{6,14},{7,15},{8,0},{9,1},... | collective-permute-start | bytes 393224 | tf_op jit(solution)/shard_map/ppermute | solution.py:61
  55.2 9.4 %update.1 = (f32[1024,256]{1,0:T(8,128)}, f32[1,1024]{1,0:T(1,128)}) custom-call(s32[32,256]{1,0:T(8,128)} %bitcast.83, f32[1024,256]{1,0:T(8,128)} %cache_ref.1, f32[1,1024]{1,0:T(1,128)} %bitcast.78, bf16[256,256]{1,0:T(8,128)(2,1)} %get-tuple-element.38.latent_ref, bf16[256,256]{1,0:T(8,128)(2,1)} %get-tuple-element.39.dlatent_ref, ...), custom_call_target="tpu_custom_call" | custom-call | flops 1100000000 | bytes 4000000 | tf_op jit(solution)/shard_map/update/pallas_call | solution.py:432
  64.6 6.2 %all-to-all-done.1 = f32[32,136,128]{2,1,0:T(8,128)S(1)} async-done(((f32[32,136,128]{2,1,0:T(8,128)}), f32[32,136,128]{2,1,0:T(8,128)S(1)}, u32[]{:S(2)}, u32[]{:S(2)}) %all-to-all-start.1) | async-done | bytes 2228256 | tf_op jit(solution)/shard_map/all_to_all | solution.py:41
  70.8 1.5 %collective-permute-start.6 = (f32[1,16,8,256]{3,2,1,0:T(8,128)S(1)}, f32[1,16,8,256]{3,2,1,0:T(8,128)S(1)}, u32[]{:S(2)}, u32[]{:S(2)}) collective-permute-start(f32[1,16,8,256]{3,2,1,0:T(8,128)S(1)} %get-tuple-element.70), channel_id=1, source_target_pairs={{0,16},{1,17},{2,18},{3,19},{4,20},{5,21},{6,22},{7,23},{8,24},{9,... | collective-permute-start | bytes 393224 | tf_op jit(solution)/shard_map/ppermute | solution.py:61
  72.3 0.1 reduce_sum.38
  72.4 3.0 %collective-permute-start.5 = (f32[136,128]{1,0:T(8,128)S(1)}, f32[136,128]{1,0:T(8,128)S(1)}, u32[]{:S(2)}, u32[]{:S(2)}) collective-permute-start(f32[136,128]{1,0:T(8,128)S(1)} %reduce_sum.38), channel_id=1, source_target_pairs={{0,12},{1,13},{2,14},{3,15},{4,0},{5,1},{6,2},{7,3},{8,4},{9,5},{1... | collective-permute-start | bytes 208904 | tf_op jit(solution)/shard_map/ppermute | solution.py:33
  75.4 2.9 %collective-permute-start.3 = (f32[136,128]{1,0:T(8,128)S(1)}, f32[136,128]{1,0:T(8,128)S(1)}, u32[]{:S(2)}, u32[]{:S(2)}) collective-permute-start(f32[136,128]{1,0:T(8,128)S(1)} %reduce_sum.38), channel_id=1, source_target_pairs={{0,8},{1,9},{2,10},{3,11},{4,12},{5,13},{6,14},{7,15},{8,0},{9,1},... | collective-permute-start | bytes 208904 | tf_op jit(solution)/shard_map/ppermute | solution.py:33
  78.4 2.0 %collective-permute-start.7 = (f32[8,2,8,256]{3,2,1,0:T(8,128)S(1)}, f32[8,2,8,256]{3,2,1,0:T(8,128)S(1)}, u32[]{:S(2)}, u32[]{:S(2)}) collective-permute-start(f32[8,2,8,256]{3,2,1,0:T(8,128)S(1)} %get-tuple-element.68), channel_id=1, source_target_pairs={{0,2},{1,3},{2,0},{3,1},{4,6},{5,7},{6,4},{7,5},{8,10},{9,11},{10,... | collective-permute-start | bytes 393224 | tf_op jit(solution)/shard_map/ppermute | solution.py:61
  80.4 0.9 collective-permute-done.4
  81.3 1.5 %collective-permute-done.3 = f32[136,128]{1,0:T(8,128)S(1)} collective-permute-done((f32[136,128]{1,0:T(8,128)S(1)}, f32[136,128]{1,0:T(8,128)S(1)}, u32[]{:S(2)}, u32[]{:S(2)}) %collective-permute-start.3) | collective-permute-done | bytes 69664 | tf_op jit(solution)/shard_map/ppermute | solution.py:33
  82.7 1.3 collective-permute-done.7
  84.1 1.5 %broadcast_in_dim.68 = f32[32,136,128]{2,1,0:T(8,128)} broadcast(f32[136,128]{1,0:T(8,128)S(1)} %add_add_fusion), dimensions={1,2} | broadcast | bytes 2297856 | tf_op jit(solution)/shard_map/broadcast_in_dim | solution.py:712
  85.6 11.6 %all-to-all-start.2 = ((f32[32,136,128]{2,1,0:T(8,128)}), f32[32,136,128]{2,1,0:T(8,128)S(1)}, u32[]{:S(2)}, u32[]{:S(2)}) async-start(f32[32,136,128]{2,1,0:T(8,128)} %broadcast_in_dim.68), calls=%async_computation.2 | async-start | bytes 4456448 | tf_op jit(solution)/shard_map/all_to_all | solution.py:41
  97.3 0.2 convert_reduce_fusion
  97.5 0.1 collective-permute-start.8
  97.6 0.5 multiply_add_fusion.place_ref
  98.1 0.1 fusion
  98.2 21.6 %collective-permute-done.8 = f32[4,4,8,256]{3,2,1,0:T(8,128)S(1)} collective-permute-done((f32[4,4,8,256]{3,2,1,0:T(8,128)S(1)}, f32[4,4,8,256]{3,2,1,0:T(8,128)S(1)}, u32[]{:S(2)}, u32[]{:S(2)}) %collective-permute-start.8) | collective-permute-done | bytes 131104 | tf_op jit(solution)/shard_map/ppermute | solution.py:61
  119.9 0.7 copy.60
  120.6 2.6 %refill.1 = f32[1024,256]{1,0:T(8,128)} custom-call(s32[64]{0:T(128)} %evict_ref.1, s32[64]{0:T(128)} %multiply_add_fusion.place_ref, f32[256,256]{1,0:T(8,128)} %bitcast.64, f32[1024,256]{1,0:T(8,128)} %get-tuple-element.55.old_ref), custom_call_target="tpu_custom_call" | custom-call | flops 100000 | bytes 2000000 | tf_op jit(solution)/shard_map/refill/pallas_call | solution.py:451
  123.2 1.0 slice_reduce_fusion
  124.2 0.1 broadcast_in_dim.69
  124.3 0.2 select_reduce_fusion.1
  124.5 0.1 select_reduce_fusion
  124.6 0.6 select_n.22
  125.2 4.1 %all-to-all-done.2.half = f32[32,136,128]{2,1,0:T(8,128)S(1)} async-done(((f32[32,136,128]{2,1,0:T(8,128)}), f32[32,136,128]{2,1,0:T(8,128)S(1)}, u32[]{:S(2)}, u32[]{:S(2)}) %all-to-all-start.2) | async-done | bytes 2228256 | tf_op jit(solution)/shard_map/all_to_all | solution.py:41
  129.2 0.5 collective-permute-start.9
  129.8 1.6 %scale_own.1.proj_in = f32[2,2048,256]{2,1,0:T(8,128)} custom-call(s32[1]{0:T(128)} %bitcast.core_ref, f32[32,136,128]{2,1,0:T(8,128)S(1)} %all-to-all-done.2.half), custom_call_target="tpu_custom_call" | custom-call | tf_op jit(solution)/shard_map/scale_own/pallas_call | solution.py:629
  131.4 2.3 %collective-permute-done.9.half = f32[32,136,128]{2,1,0:T(8,128)S(1)} collective-permute-done((f32[32,136,128]{2,1,0:T(8,128)S(1)}, f32[32,136,128]{2,1,0:T(8,128)S(1)}, u32[]{:S(2)}, u32[]{:S(2)}) %collective-permute-start.9) | collective-permute-done | bytes 2228256 | tf_op jit(solution)/shard_map/ppermute | solution.py:37
  133.7 2.2 %scale_other.1 = (f32[2,2048,256]{2,1,0:T(8,128)}, f32[2,2048]{1,0:T(2,128)}, f32[1,128]{1,0:T(1,128)S(1)}) custom-call(s32[1]{0:T(128)} %bitcast.core_ref, f32[2,2048,256]{2,1,0:T(8,128)} %scale_own.1.proj_in, f32[32,8,128]{2,1,0:T(8,128)S(1)} %slice.63.own_ref, f32[32,136,128]{2,1,0:T(8,128)S(1)} %collective-permute-done.9.half), custom_call_target="tpu_custom_call", output_to_operand_aliasing={{0}: (1, {})} | custom-call | tf_op jit(solution)/shard_map/scale_other/pallas_call | solution.py:638
  (34 shorter events, 0.3 us)
Async XLA Ops:
  3.6 22.2 %all-to-all-start = ((f32[32,8,256]{2,1,0:T(8,128)}), f32[32,8,256]{2,1,0:T(8,128)S(1)}, u32[]{:S(2)}, u32[]{:S(2)}) async-start(f32[32,8,256]{2,1,0:T(8,128)} %bitcast.66), calls=%async_computation | async-start | bytes 524288 | tf_op jit(solution)/shard_map/all_to_all | solution.py:681
  25.8 16.4 %copy-start.4 = (f32[32,8,256]{2,1,0:T(8,128)}, f32[32,8,256]{2,1,0:T(8,128)S(1)}, u32[]{:S(2)}) copy-start(f32[32,8,256]{2,1,0:T(8,128)S(1)} %all-to-all-done) | copy-start | bytes 786436
  25.8 5.9 %collective-permute-start = (f32[32,136,128]{2,1,0:T(8,128)}, f32[32,136,128]{2,1,0:T(8,128)S(1)}, u32[]{:S(2)}, u32[]{:S(2)}) collective-permute-start(f32[32,136,128]{2,1,0:T(8,128)} %get-tuple-element.43), channel_id=1, source_target_pairs={{0,1},{1,0},{2,3},{3,2},{4,5},{5,4},{6,7},{7,6},{8,9},{9,8},{10,11... | collective-permute-start | bytes 6684680 | tf_op jit(solution)/shard_map/ppermute | solution.py:37
  27.3 1.2 copy-start
  28.5 0.9 copy-start.1
  29.4 0.9 copy-start.2
  30.3 0.9 copy-start.3
  33.4 37.5 %all-to-all-start.1 = ((f32[32,136,128]{2,1,0:T(8,128)}), f32[32,136,128]{2,1,0:T(8,128)S(1)}, u32[]{:S(2)}, u32[]{:S(2)}) async-start(f32[32,136,128]{2,1,0:T(8,128)} %add.22), calls=%async_computation.1 | async-start | bytes 4456448 | tf_op jit(solution)/shard_map/all_to_all | solution.py:41
  50.1 1.4 %collective-permute-start.1 = (f32[16,1,8,256]{3,2,0,1:T(8,128)S(1)}, f32[16,1,8,256]{3,2,0,1:T(8,128)S(1)}, u32[]{:S(2)}, u32[]{:S(2)}) collective-permute-start(f32[16,1,8,256]{3,2,0,1:T(8,128)S(1)} %get-tuple-element.74), channel_id=1, source_target_pairs={{0,1},{1,0},{2,3},{3,2},{4,5},{5,4},{6,7},{7,6},{8,9},{9,8},{10,11... | collective-permute-start | bytes 393224 | tf_op jit(solution)/shard_map/ppermute | solution.py:61
  51.6 13.0 %collective-permute-start.2 = (f32[2,8,8,256]{3,2,1,0:T(8,128)S(1)}, f32[2,8,8,256]{3,2,1,0:T(8,128)S(1)}, u32[]{:S(2)}, u32[]{:S(2)}) collective-permute-start(f32[2,8,8,256]{3,2,1,0:T(8,128)S(1)} %get-tuple-element.72), channel_id=1, source_target_pairs={{0,8},{1,9},{2,10},{3,11},{4,12},{5,13},{6,14},{7,15},{8,0},{9,1},... | collective-permute-start | bytes 393224 | tf_op jit(solution)/shard_map/ppermute | solution.py:61
  70.8 7.5 %collective-permute-start.6 = (f32[1,16,8,256]{3,2,1,0:T(8,128)S(1)}, f32[1,16,8,256]{3,2,1,0:T(8,128)S(1)}, u32[]{:S(2)}, u32[]{:S(2)}) collective-permute-start(f32[1,16,8,256]{3,2,1,0:T(8,128)S(1)} %get-tuple-element.70), channel_id=1, source_target_pairs={{0,16},{1,17},{2,18},{3,19},{4,20},{5,21},{6,22},{7,23},{8,24},{9,... | collective-permute-start | bytes 393224 | tf_op jit(solution)/shard_map/ppermute | solution.py:61
  72.4 7.9 %collective-permute-start.5 = (f32[136,128]{1,0:T(8,128)S(1)}, f32[136,128]{1,0:T(8,128)S(1)}, u32[]{:S(2)}, u32[]{:S(2)}) collective-permute-start(f32[136,128]{1,0:T(8,128)S(1)} %reduce_sum.38), channel_id=1, source_target_pairs={{0,12},{1,13},{2,14},{3,15},{4,0},{5,1},{6,2},{7,3},{8,4},{9,5},{1... | collective-permute-start | bytes 208904 | tf_op jit(solution)/shard_map/ppermute | solution.py:33
  75.4 5.8 %collective-permute-start.4 = (f32[136,128]{1,0:T(8,128)S(1)}, f32[136,128]{1,0:T(8,128)S(1)}, u32[]{:S(2)}, u32[]{:S(2)}) collective-permute-start(f32[136,128]{1,0:T(8,128)S(1)} %reduce_sum.38), channel_id=1, source_target_pairs={{0,4},{1,5},{2,6},{3,7},{4,8},{5,9},{6,10},{7,11},{8,12},{9,13},{1... | collective-permute-start | bytes 208904 | tf_op jit(solution)/shard_map/ppermute | solution.py:33
  75.4 7.3 %collective-permute-start.3 = (f32[136,128]{1,0:T(8,128)S(1)}, f32[136,128]{1,0:T(8,128)S(1)}, u32[]{:S(2)}, u32[]{:S(2)}) collective-permute-start(f32[136,128]{1,0:T(8,128)S(1)} %reduce_sum.38), channel_id=1, source_target_pairs={{0,8},{1,9},{2,10},{3,11},{4,12},{5,13},{6,14},{7,15},{8,0},{9,1},... | collective-permute-start | bytes 208904 | tf_op jit(solution)/shard_map/ppermute | solution.py:33
  78.4 5.7 %collective-permute-start.7 = (f32[8,2,8,256]{3,2,1,0:T(8,128)S(1)}, f32[8,2,8,256]{3,2,1,0:T(8,128)S(1)}, u32[]{:S(2)}, u32[]{:S(2)}) collective-permute-start(f32[8,2,8,256]{3,2,1,0:T(8,128)S(1)} %get-tuple-element.68), channel_id=1, source_target_pairs={{0,2},{1,3},{2,0},{3,1},{4,6},{5,7},{6,4},{7,5},{8,10},{9,11},{10,... | collective-permute-start | bytes 393224 | tf_op jit(solution)/shard_map/ppermute | solution.py:61
  85.6 11.6 %copy-start.7 = (s32[64,2]{0,1:T(2,128)S(1)}, s32[64,2]{0,1:T(2,128)}, u32[]{:S(2)}) copy-start(s32[64,2]{0,1:T(2,128)} %param.19) | copy-start | bytes 1540
  85.6 12.5 %copy-start.5 = (s32[64]{0:T(128)S(1)}, s32[64]{0:T(128)}, u32[]{:S(2)}) copy-start(s32[64]{0:T(128)} %evict_ref.1) | copy-start | bytes 772
  85.6 43.6 %all-to-all-start.2 = ((f32[32,136,128]{2,1,0:T(8,128)}), f32[32,136,128]{2,1,0:T(8,128)S(1)}, u32[]{:S(2)}, u32[]{:S(2)}) async-start(f32[32,136,128]{2,1,0:T(8,128)} %broadcast_in_dim.68), calls=%async_computation.2 | async-start | bytes 4456448 | tf_op jit(solution)/shard_map/all_to_all | solution.py:41
  97.3 27.2 %copy-start.6 = (s32[64]{0:T(128)S(1)}, s32[64]{0:T(128)}, u32[]{:S(2)}) copy-start(s32[64]{0:T(128)} %evict_ref.1) | copy-start | bytes 772
  97.3 27.3 %copy-start.8 = (f32[1,1024]{1,0:T(1,128)S(1)}, f32[1,1024]{1,0:T(1,128)}, u32[]{:S(2)}) copy-start(f32[1,1024]{1,0:T(1,128)} %get-tuple-element.56) | copy-start | bytes 12292
  97.5 22.3 %collective-permute-start.8 = (f32[4,4,8,256]{3,2,1,0:T(8,128)S(1)}, f32[4,4,8,256]{3,2,1,0:T(8,128)S(1)}, u32[]{:S(2)}, u32[]{:S(2)}) collective-permute-start(f32[4,4,8,256]{3,2,1,0:T(8,128)S(1)} %get-tuple-element.66), channel_id=1, source_target_pairs={{0,4},{1,5},{2,6},{3,7},{4,0},{5,1},{6,2},{7,3},{8,12},{9,13},{10,... | collective-permute-start | bytes 393224 | tf_op jit(solution)/shard_map/ppermute | solution.py:61
  129.2 4.5 %collective-permute-start.9 = (f32[32,136,128]{2,1,0:T(8,128)S(1)}, f32[32,136,128]{2,1,0:T(8,128)S(1)}, u32[]{:S(2)}, u32[]{:S(2)}) collective-permute-start(f32[32,136,128]{2,1,0:T(8,128)S(1)} %all-to-all-done.2.half), channel_id=1, source_target_pairs={{0,1},{1,0},{2,3},{3,2},{4,5},{5,4},{6,7},{7,6},{8,9},{9,8},{10,11... | collective-permute-start | bytes 6684680 | tf_op jit(solution)/shard_map/ppermute | solution.py:37

commit v13 on v12

--- a/solution.py
+++ b/solution.py
@@ -376,6 +376,32 @@
     )(evict_slot, evict_dest.T, miss_dest.T, cache_accum, cache_rows)
 
 
+def add_kernel(keep_ref, came_ref, out_any, total, sems):
+    chunks = sems.shape[0]
+    size = keep_ref.shape[0] // chunks
+    copies = []
+    for c in range(chunks):
+        part = pl.ds(c * size, size)
+        total[part] = keep_ref[part] + came_ref[part]
+        copies.append(pltpu.make_async_copy(total.at[part], out_any.at[part], sems.at[c]))
+        copies[-1].start()
+    for copy in copies:
+        copy.wait()
+
+
+def added(keep, came):
+    vmem = pl.BlockSpec(memory_space=pltpu.VMEM)
+    return pl.pallas_call(
+        add_kernel,
+        out_shape=jax.ShapeDtypeStruct(keep.shape, jnp.float32),
+        in_specs=[vmem, vmem],
+        out_specs=pl.BlockSpec(memory_space=pl.ANY),
+        scratch_shapes=[pltpu.VMEM(keep.shape, jnp.float32), pltpu.SemaphoreType.DMA((8,))],
+        compiler_params=pltpu.CompilerParams(vmem_limit_bytes=16 * 1024 * 1024),
+        name="add_halves",
+    )(keep, came)
+
+
 def update_kernel(
     slots_ref,
     cache_ref,
@@ -687,7 +713,7 @@
     )
 
     send, got = lax.optimization_barrier((send, got))
-    held = kept(core, left, latent, dlatent, extra) + swap_cores(send)
+    held = added(kept(core, left, latent, dlatent, extra), swap_cores(send))
     held, got = lax.optimization_barrier((held, got))
 
     reply, table_new, accum_table = replied(me, got, table_rows, table_accum)
@@ -707,11 +733,11 @@
     )
     held = jnp.sum(held, axis=0)
     held = (held + shift_z(held, 4)) + (shift_z(held, 2) + shift_z(held, -2))
-    back = cross(cross(back, 16), 2)
+    back = cross(cross(back, 16), 4)
     held, back = lax.optimization_barrier((held, back))
     whole = jnp.broadcast_to(held[None], (4 * feats, *held.shape))
     whole = exchange(whole, plane_groups())
-    back = cross(back, 4)
+    back = cross(back, 2)
     in_place = (miss_dest[:, 0] ^ me) * per + ranks(miss_dest[:, 0])
     rows_new = refilled(evict_slot, in_place, back.reshape(spots, width), rows_new)
     fetched_accum = picked(back[:, per - 1, :per].reshape(-1), in_place)

time: 138 us -> 141 us (1.022)
  waiting for transfers between devices: 40.2 us -> 43.1 us
  other arithmetic: 4.12 us -> 2.53 us
    all_to_all x2, waiting for transfers between devices: 10.3 us -> 24.3 us  [exchange(): lax.all_to_all(value, AXES, split_axis=0, concat_axis=0, tiled=True, axis...]
    ppermute x5, waiting for transfers between devices: 24.3 us -> 13.6 us  [cross(): came = lax.ppermute(split[:, 1], AXES, there)]
    add x1 -> x0, other arithmetic: 1.59 us -> none  [shards(): held = kept(core, left, latent, dlatent, extra) + swap_cores(send)]
    pallas_call x0 -> x1, Pallas kernels: none -> 1.45 us  [added(): pl.pallas_call(add_kernel, out_shape=jax.ShapeDtypeStruct(keep.shape, jnp...]
  transfers between devices with their start and end apart: 13 -> 13, of which waited for: 9 -> 8; matrix products, arithmetic and copies ran while one was open for 4% -> 4% of each run, Pallas kernels for 23% -> 22%
where the time goes in v13:
time: 141 us; the launch traced here: 139 us
  starting transfers between devices  45.3 us (32%)
  waiting for transfers between devices  43.1 us (31%)
  Pallas kernels  37.7 us (27%)
  local copies, waits for them, and re-layouts  8.44 us (6%)
  other arithmetic  2.53 us (2%)
  between operations  2.08 us (1%)
    all_to_all x2, waiting for transfers between devices, exchange(): lax.all_to_all(value, AXES, split_axis=0, concat_axis=0, tiled=True, axis...  24.3 us
    all_to_all x2, starting transfers between devices, exchange(): lax.all_to_all(value, AXES, split_axis=0, concat_axis=0, tiled=True, axis...  19.3 us
    ppermute x5, waiting for transfers between devices, cross(): came = lax.ppermute(split[:, 1], AXES, there)  13.6 us
    pallas_call x1, Pallas kernels, dense(): pl.pallas_call(dense_kernel, out_shape=(jax.ShapeDtypeStruct(bundle, f32)...  10.9 us
    all_to_all x1, starting transfers between devices, shards(): got = lax.all_to_all(sent, 'table', split_axis=0, concat_axis=0, tiled=True)  10.3 us
    pallas_call x1, Pallas kernels, updated(): pl.pallas_call(update_kernel, out_shape=(jax.ShapeDtypeStruct(cache_rows....  9.39 us
    ppermute x5, starting transfers between devices, cross(): came = lax.ppermute(split[:, 1], AXES, there)  8.24 us
    pallas_call x1, Pallas kernels, replied(): pl.pallas_call(reply_kernel, out_shape=(jax.ShapeDtypeStruct((owners * pe...  6.01 us
  transfers between devices with their start and end apart: 13, of which 8 were waited for; matrix products, arithmetic and copies ran while one was open for 4% of the time, Pallas kernels for 22%

profile of v13, /device:TPU:3, one launch (start us, length us, event | category | flops | bytes accessed | tf_op | source)
XLA Modules:
  0.0 139.1 jit_solution(5338308739625893663)
XLA Ops:
  0.6 2.9 %payload.1 = f32[256,256]{1,0:T(8,128)} custom-call(s32[64]{0:T(128)} %evict_ref.1, s32[2,64]{1,0:T(2,128)} %bitcast.81, s32[2,64]{1,0:T(2,128)} %bitcast.79, f32[1024]{0:T(1024)} %accum_ref.1, f32[1024,256]{1,0:T(8,128)} %cache_ref.1), custom_call_target="tpu_custom_call" | custom-call | flops 100000 | bytes 1500000 | tf_op jit(solution)/shard_map/payload/pallas_call | solution.py:362
  3.6 10.3 %all-to-all-start = ((f32[32,8,256]{2,1,0:T(8,128)}), f32[32,8,256]{2,1,0:T(8,128)S(1)}, u32[]{:S(2)}, u32[]{:S(2)}) async-start(f32[32,8,256]{2,1,0:T(8,128)} %bitcast.66), calls=%async_computation | async-start | bytes 524288 | tf_op jit(solution)/shard_map/all_to_all | solution.py:707
  13.9 10.9 %dense.1 = (f32[32,136,128]{2,1,0:T(8,128)}, bf16[256,2048]{1,0:T(8,128)(2,1)}, bf16[256,256]{1,0:T(8,128)(2,1)}, bf16[256,256]{1,0:T(8,128)(2,1)}, f32[1,256]{1,0:T(1,128)}, /*index=5*/f32[32,8,128]{2,1,0:T(8,128)}) custom-call(s32[1]{0:T(128)} %bitcast.core_ref, s32[32,256]{1,0:T(8,128)} %bitcast.82, s32[1,256]{1,0:T(1,128)} %bitcast.88, ...), custom_call_target="tpu_custom_call" | custom-call | flops 5000000000 | bytes 9000000 | tf_op jit(solution)/shard_map/dense/pallas_call | solution.py:229
  24.8 1.0 all-to-all-done
  25.8 1.5 %collective-permute-start = (f32[32,136,128]{2,1,0:T(8,128)}, f32[32,136,128]{2,1,0:T(8,128)S(1)}, u32[]{:S(2)}, u32[]{:S(2)}) collective-permute-start(f32[32,136,128]{2,1,0:T(8,128)} %get-tuple-element.43), channel_id=1, source_target_pairs={{0,1},{1,0},{2,3},{3,2},{4,5},{5,4},{6,7},{7,6},{8,9},{9,8},{10,11... | collective-permute-start | bytes 6684680 | tf_op jit(solution)/shard_map/ppermute | solution.py:37
  27.3 1.2 copy-done
  28.5 0.9 copy-done.1
  29.4 0.9 copy-done.2
  30.3 0.9 copy-done.3
  31.2 0.5 kept.1.keep_ref
  31.8 1.5 %add_halves.1 = f32[32,136,128]{2,1,0:T(8,128)} custom-call(f32[32,136,128]{2,1,0:T(8,128)S(1)} %kept.1.keep_ref, f32[32,136,128]{2,1,0:T(8,128)S(1)} %collective-permute-done.came_ref), custom_call_target="tpu_custom_call" | custom-call | tf_op jit(solution)/shard_map/add_halves/pallas_call | solution.py:394
  33.2 8.9 %all-to-all-start.1 = ((f32[32,136,128]{2,1,0:T(8,128)}), f32[32,136,128]{2,1,0:T(8,128)S(1)}, u32[]{:S(2)}, u32[]{:S(2)}) async-start(f32[32,136,128]{2,1,0:T(8,128)} %add_halves.1), calls=%async_computation.1 | async-start | bytes 4456448 | tf_op jit(solution)/shard_map/all_to_all | solution.py:41
  42.1 0.1 copy.53
  42.2 0.6 slice_bitcast_fusion.8
  42.8 6.0 %reply.1 = (f32[256,256]{1,0:T(8,128)}, f32[1024,256]{1,0:T(8,128)}, f32[1024]{0:T(1024)}) custom-call(s32[1]{0:T(128)} %bitcast.8.me_ref, s32[32,24]{1,0:T(8,128)} %get-tuple-element.76.ids_ref, f32[32,8]{1,0:T(8,128)} %bitcast.77, f32[256,256]{1,0:T(8,128)} %bitcast.63, f32[1024,256]{1,0:T(8,128)} %table_any.1, f32[1024]{0:T(1024)} %accum_any.1), custom_call_target="tpu_custom_call" | custom-call | flops 100000 | bytes 3000000 | tf_op jit(solution)/shard_map/reply/pallas_call | solution.py:555
  48.9 1.0 fusion.5
  49.8 0.1 collective-permute-start.1
  49.9 1.3 collective-permute-done.1
  51.3 3.7 %collective-permute-start.2 = (f32[2,8,8,256]{3,2,1,0:T(8,128)S(1)}, f32[2,8,8,256]{3,2,1,0:T(8,128)S(1)}, u32[]{:S(2)}, u32[]{:S(2)}) collective-permute-start(f32[2,8,8,256]{3,2,1,0:T(8,128)S(1)} %get-tuple-element.72), channel_id=1, source_target_pairs={{0,8},{1,9},{2,10},{3,11},{4,12},{5,13},{6,14},{7,15},{8,0},{9,1},... | collective-permute-start | bytes 393224 | tf_op jit(solution)/shard_map/ppermute | solution.py:61
  55.0 9.4 %update.1 = (f32[1024,256]{1,0:T(8,128)}, f32[1,1024]{1,0:T(1,128)}) custom-call(s32[32,256]{1,0:T(8,128)} %bitcast.83, f32[1024,256]{1,0:T(8,128)} %cache_ref.1, f32[1,1024]{1,0:T(1,128)} %bitcast.78, bf16[256,256]{1,0:T(8,128)(2,1)} %get-tuple-element.38.latent_ref, bf16[256,256]{1,0:T(8,128)(2,1)} %get-tuple-element.39.dlatent_ref, ...), custom_call_target="tpu_custom_call" | custom-call | flops 1100000000 | bytes 4000000 | tf_op jit(solution)/shard_map/update/pallas_call | solution.py:458
  64.5 6.2 %all-to-all-done.1 = f32[32,136,128]{2,1,0:T(8,128)S(1)} async-done(((f32[32,136,128]{2,1,0:T(8,128)}), f32[32,136,128]{2,1,0:T(8,128)S(1)}, u32[]{:S(2)}, u32[]{:S(2)}) %all-to-all-start.1) | async-done | bytes 2228256 | tf_op jit(solution)/shard_map/all_to_all | solution.py:41
  70.7 1.5 %collective-permute-start.6 = (f32[1,16,8,256]{3,2,1,0:T(8,128)S(1)}, f32[1,16,8,256]{3,2,1,0:T(8,128)S(1)}, u32[]{:S(2)}, u32[]{:S(2)}) collective-permute-start(f32[1,16,8,256]{3,2,1,0:T(8,128)S(1)} %get-tuple-element.70), channel_id=1, source_target_pairs={{0,16},{1,17},{2,18},{3,19},{4,20},{5,21},{6,22},{7,23},{8,24},{9,... | collective-permute-start | bytes 393224 | tf_op jit(solution)/shard_map/ppermute | solution.py:61
  72.2 0.1 reduce_sum.38
  72.3 3.0 %collective-permute-start.5 = (f32[136,128]{1,0:T(8,128)S(1)}, f32[136,128]{1,0:T(8,128)S(1)}, u32[]{:S(2)}, u32[]{:S(2)}) collective-permute-start(f32[136,128]{1,0:T(8,128)S(1)} %reduce_sum.38), channel_id=1, source_target_pairs={{0,12},{1,13},{2,14},{3,15},{4,0},{5,1},{6,2},{7,3},{8,4},{9,5},{1... | collective-permute-start | bytes 208904 | tf_op jit(solution)/shard_map/ppermute | solution.py:33
  75.3 2.9 %collective-permute-start.3 = (f32[136,128]{1,0:T(8,128)S(1)}, f32[136,128]{1,0:T(8,128)S(1)}, u32[]{:S(2)}, u32[]{:S(2)}) collective-permute-start(f32[136,128]{1,0:T(8,128)S(1)} %reduce_sum.38), channel_id=1, source_target_pairs={{0,8},{1,9},{2,10},{3,11},{4,12},{5,13},{6,14},{7,15},{8,0},{9,1},... | collective-permute-start | bytes 208904 | tf_op jit(solution)/shard_map/ppermute | solution.py:33
  78.3 2.9 %collective-permute-start.7 = (f32[4,4,8,256]{3,2,1,0:T(8,128)S(1)}, f32[4,4,8,256]{3,2,1,0:T(8,128)S(1)}, u32[]{:S(2)}, u32[]{:S(2)}) collective-permute-start(f32[4,4,8,256]{3,2,1,0:T(8,128)S(1)} %get-tuple-element.68), channel_id=1, source_target_pairs={{0,4},{1,5},{2,6},{3,7},{4,0},{5,1},{6,2},{7,3},{8,12},{9,13},{10,... | collective-permute-start | bytes 393224 | tf_op jit(solution)/shard_map/ppermute | solution.py:61
  81.1 0.0 collective-permute-done.4
  81.1 1.5 %collective-permute-done.3 = f32[136,128]{1,0:T(8,128)S(1)} collective-permute-done((f32[136,128]{1,0:T(8,128)S(1)}, f32[136,128]{1,0:T(8,128)S(1)}, u32[]{:S(2)}, u32[]{:S(2)}) %collective-permute-start.3) | collective-permute-done | bytes 69664 | tf_op jit(solution)/shard_map/ppermute | solution.py:33
  82.6 7.3 %collective-permute-done.7 = f32[4,4,8,256]{3,2,1,0:T(8,128)S(1)} collective-permute-done((f32[4,4,8,256]{3,2,1,0:T(8,128)S(1)}, f32[4,4,8,256]{3,2,1,0:T(8,128)S(1)}, u32[]{:S(2)}, u32[]{:S(2)}) %collective-permute-start.7) | collective-permute-done | bytes 131104 | tf_op jit(solution)/shard_map/ppermute | solution.py:61
  90.0 1.5 %broadcast_in_dim.68 = f32[32,136,128]{2,1,0:T(8,128)} broadcast(f32[136,128]{1,0:T(8,128)S(1)} %add_add_fusion), dimensions={1,2} | broadcast | bytes 2297856 | tf_op jit(solution)/shard_map/broadcast_in_dim | solution.py:738
  91.5 10.4 %all-to-all-start.2 = ((f32[32,136,128]{2,1,0:T(8,128)}), f32[32,136,128]{2,1,0:T(8,128)S(1)}, u32[]{:S(2)}, u32[]{:S(2)}) async-start(f32[32,136,128]{2,1,0:T(8,128)} %broadcast_in_dim.68), calls=%async_computation.2 | async-start | bytes 4456448 | tf_op jit(solution)/shard_map/all_to_all | solution.py:41
  102.0 0.0 copy-start.6
  102.0 0.2 convert_reduce_fusion
  102.2 0.1 collective-permute-start.8
  102.3 0.5 multiply_add_fusion.place_ref
  102.8 0.1 fusion
  103.0 5.0 %collective-permute-done.8 = f32[8,2,8,256]{3,2,1,0:T(8,128)S(1)} collective-permute-done((f32[8,2,8,256]{3,2,1,0:T(8,128)S(1)}, f32[8,2,8,256]{3,2,1,0:T(8,128)S(1)}, u32[]{:S(2)}, u32[]{:S(2)}) %collective-permute-start.8) | collective-permute-done | bytes 131104 | tf_op jit(solution)/shard_map/ppermute | solution.py:61
  107.9 0.7 copy.60
  108.7 2.6 %refill.1 = f32[1024,256]{1,0:T(8,128)} custom-call(s32[64]{0:T(128)} %evict_ref.1, s32[64]{0:T(128)} %multiply_add_fusion.place_ref, f32[256,256]{1,0:T(8,128)} %bitcast.64, f32[1024,256]{1,0:T(8,128)} %get-tuple-element.55.old_ref), custom_call_target="tpu_custom_call" | custom-call | flops 100000 | bytes 2000000 | tf_op jit(solution)/shard_map/refill/pallas_call | solution.py:477
  111.3 1.0 slice_reduce_fusion
  112.3 0.1 broadcast_in_dim.69
  112.4 0.2 select_reduce_fusion.1
  112.6 0.1 select_reduce_fusion
  112.7 0.6 select_n.22
  113.3 18.1 %all-to-all-done.2.half = f32[32,136,128]{2,1,0:T(8,128)S(1)} async-done(((f32[32,136,128]{2,1,0:T(8,128)}), f32[32,136,128]{2,1,0:T(8,128)S(1)}, u32[]{:S(2)}, u32[]{:S(2)}) %all-to-all-start.2) | async-done | bytes 2228256 | tf_op jit(solution)/shard_map/all_to_all | solution.py:41
  131.4 1.6 %scale_own.1.proj_in = f32[2,2048,256]{2,1,0:T(8,128)} custom-call(s32[1]{0:T(128)} %bitcast.core_ref, f32[32,136,128]{2,1,0:T(8,128)S(1)} %all-to-all-done.2.half), custom_call_target="tpu_custom_call" | custom-call | tf_op jit(solution)/shard_map/scale_own/pallas_call | solution.py:655
  133.0 2.7 %collective-permute-done.9.half = f32[32,136,128]{2,1,0:T(8,128)S(1)} collective-permute-done((f32[32,136,128]{2,1,0:T(8,128)S(1)}, f32[32,136,128]{2,1,0:T(8,128)S(1)}, u32[]{:S(2)}, u32[]{:S(2)}) %collective-permute-start.9) | collective-permute-done | bytes 2228256 | tf_op jit(solution)/shard_map/ppermute | solution.py:37
  135.7 2.2 %scale_other.1 = (f32[2,2048,256]{2,1,0:T(8,128)}, f32[2,2048]{1,0:T(2,128)}, f32[1,128]{1,0:T(1,128)S(1)}) custom-call(s32[1]{0:T(128)} %bitcast.core_ref, f32[2,2048,256]{2,1,0:T(8,128)} %scale_own.1.proj_in, f32[32,8,128]{2,1,0:T(8,128)S(1)} %slice.63.own_ref, f32[32,136,128]{2,1,0:T(8,128)S(1)} %collective-permute-done.9.half), custom_call_target="tpu_custom_call", output_to_operand_aliasing={{0}: (1, {})} | custom-call | tf_op jit(solution)/shard_map/scale_other/pallas_call | solution.py:664
  (34 shorter events, 0.3 us)
Async XLA Ops:
  3.6 22.2 %all-to-all-start = ((f32[32,8,256]{2,1,0:T(8,128)}), f32[32,8,256]{2,1,0:T(8,128)S(1)}, u32[]{:S(2)}, u32[]{:S(2)}) async-start(f32[32,8,256]{2,1,0:T(8,128)} %bitcast.66), calls=%async_computation | async-start | bytes 524288 | tf_op jit(solution)/shard_map/all_to_all | solution.py:707
  25.8 16.3 %copy-start.4 = (f32[32,8,256]{2,1,0:T(8,128)}, f32[32,8,256]{2,1,0:T(8,128)S(1)}, u32[]{:S(2)}) copy-start(f32[32,8,256]{2,1,0:T(8,128)S(1)} %all-to-all-done) | copy-start | bytes 786436
  25.8 5.9 %collective-permute-start = (f32[32,136,128]{2,1,0:T(8,128)}, f32[32,136,128]{2,1,0:T(8,128)S(1)}, u32[]{:S(2)}, u32[]{:S(2)}) collective-permute-start(f32[32,136,128]{2,1,0:T(8,128)} %get-tuple-element.43), channel_id=1, source_target_pairs={{0,1},{1,0},{2,3},{3,2},{4,5},{5,4},{6,7},{7,6},{8,9},{9,8},{10,11... | collective-permute-start | bytes 6684680 | tf_op jit(solution)/shard_map/ppermute | solution.py:37
  27.3 1.2 copy-start
  28.5 0.9 copy-start.1
  29.4 0.9 copy-start.2
  30.3 0.9 copy-start.3
  33.2 37.5 %all-to-all-start.1 = ((f32[32,136,128]{2,1,0:T(8,128)}), f32[32,136,128]{2,1,0:T(8,128)S(1)}, u32[]{:S(2)}, u32[]{:S(2)}) async-start(f32[32,136,128]{2,1,0:T(8,128)} %add_halves.1), calls=%async_computation.1 | async-start | bytes 4456448 | tf_op jit(solution)/shard_map/all_to_all | solution.py:41
  49.8 1.4 %collective-permute-start.1 = (f32[16,1,8,256]{3,2,0,1:T(8,128)S(1)}, f32[16,1,8,256]{3,2,0,1:T(8,128)S(1)}, u32[]{:S(2)}, u32[]{:S(2)}) collective-permute-start(f32[16,1,8,256]{3,2,0,1:T(8,128)S(1)} %get-tuple-element.74), channel_id=1, source_target_pairs={{0,1},{1,0},{2,3},{3,2},{4,5},{5,4},{6,7},{7,6},{8,9},{9,8},{10,11... | collective-permute-start | bytes 393224 | tf_op jit(solution)/shard_map/ppermute | solution.py:61
  51.3 13.1 %collective-permute-start.2 = (f32[2,8,8,256]{3,2,1,0:T(8,128)S(1)}, f32[2,8,8,256]{3,2,1,0:T(8,128)S(1)}, u32[]{:S(2)}, u32[]{:S(2)}) collective-permute-start(f32[2,8,8,256]{3,2,1,0:T(8,128)S(1)} %get-tuple-element.72), channel_id=1, source_target_pairs={{0,8},{1,9},{2,10},{3,11},{4,12},{5,13},{6,14},{7,15},{8,0},{9,1},... | collective-permute-start | bytes 393224 | tf_op jit(solution)/shard_map/ppermute | solution.py:61
  70.7 7.5 %collective-permute-start.6 = (f32[1,16,8,256]{3,2,1,0:T(8,128)S(1)}, f32[1,16,8,256]{3,2,1,0:T(8,128)S(1)}, u32[]{:S(2)}, u32[]{:S(2)}) collective-permute-start(f32[1,16,8,256]{3,2,1,0:T(8,128)S(1)} %get-tuple-element.70), channel_id=1, source_target_pairs={{0,16},{1,17},{2,18},{3,19},{4,20},{5,21},{6,22},{7,23},{8,24},{9,... | collective-permute-start | bytes 393224 | tf_op jit(solution)/shard_map/ppermute | solution.py:61
  72.3 8.8 %collective-permute-start.5 = (f32[136,128]{1,0:T(8,128)S(1)}, f32[136,128]{1,0:T(8,128)S(1)}, u32[]{:S(2)}, u32[]{:S(2)}) collective-permute-start(f32[136,128]{1,0:T(8,128)S(1)} %reduce_sum.38), channel_id=1, source_target_pairs={{0,12},{1,13},{2,14},{3,15},{4,0},{5,1},{6,2},{7,3},{8,4},{9,5},{1... | collective-permute-start | bytes 208904 | tf_op jit(solution)/shard_map/ppermute | solution.py:33
  75.3 5.8 %collective-permute-start.4 = (f32[136,128]{1,0:T(8,128)S(1)}, f32[136,128]{1,0:T(8,128)S(1)}, u32[]{:S(2)}, u32[]{:S(2)}) collective-permute-start(f32[136,128]{1,0:T(8,128)S(1)} %reduce_sum.38), channel_id=1, source_target_pairs={{0,4},{1,5},{2,6},{3,7},{4,8},{5,9},{6,10},{7,11},{8,12},{9,13},{1... | collective-permute-start | bytes 208904 | tf_op jit(solution)/shard_map/ppermute | solution.py:33
  75.3 7.3 %collective-permute-start.3 = (f32[136,128]{1,0:T(8,128)S(1)}, f32[136,128]{1,0:T(8,128)S(1)}, u32[]{:S(2)}, u32[]{:S(2)}) collective-permute-start(f32[136,128]{1,0:T(8,128)S(1)} %reduce_sum.38), channel_id=1, source_target_pairs={{0,8},{1,9},{2,10},{3,11},{4,12},{5,13},{6,14},{7,15},{8,0},{9,1},... | collective-permute-start | bytes 208904 | tf_op jit(solution)/shard_map/ppermute | solution.py:33
  78.3 11.7 %collective-permute-start.7 = (f32[4,4,8,256]{3,2,1,0:T(8,128)S(1)}, f32[4,4,8,256]{3,2,1,0:T(8,128)S(1)}, u32[]{:S(2)}, u32[]{:S(2)}) collective-permute-start(f32[4,4,8,256]{3,2,1,0:T(8,128)S(1)} %get-tuple-element.68), channel_id=1, source_target_pairs={{0,4},{1,5},{2,6},{3,7},{4,0},{5,1},{6,2},{7,3},{8,12},{9,13},{10,... | collective-permute-start | bytes 393224 | tf_op jit(solution)/shard_map/ppermute | solution.py:61
  91.5 10.5 %copy-start.7 = (s32[64,2]{0,1:T(2,128)S(1)}, s32[64,2]{0,1:T(2,128)}, u32[]{:S(2)}) copy-start(s32[64,2]{0,1:T(2,128)} %param.19) | copy-start | bytes 1540
  91.5 11.3 %copy-start.5 = (s32[64]{0:T(128)S(1)}, s32[64]{0:T(128)}, u32[]{:S(2)}) copy-start(s32[64]{0:T(128)} %evict_ref.1) | copy-start | bytes 772
  91.5 39.9 %all-to-all-start.2 = ((f32[32,136,128]{2,1,0:T(8,128)}), f32[32,136,128]{2,1,0:T(8,128)S(1)}, u32[]{:S(2)}, u32[]{:S(2)}) async-start(f32[32,136,128]{2,1,0:T(8,128)} %broadcast_in_dim.68), calls=%async_computation.2 | async-start | bytes 4456448 | tf_op jit(solution)/shard_map/all_to_all | solution.py:41
  102.0 10.6 %copy-start.6 = (s32[64]{0:T(128)S(1)}, s32[64]{0:T(128)}, u32[]{:S(2)}) copy-start(s32[64]{0:T(128)} %evict_ref.1) | copy-start | bytes 772
  102.0 10.7 %copy-start.8 = (f32[1,1024]{1,0:T(1,128)S(1)}, f32[1,1024]{1,0:T(1,128)}, u32[]{:S(2)}) copy-start(f32[1,1024]{1,0:T(1,128)} %get-tuple-element.56) | copy-start | bytes 12292
  102.2 5.7 %collective-permute-start.8 = (f32[8,2,8,256]{3,2,1,0:T(8,128)S(1)}, f32[8,2,8,256]{3,2,1,0:T(8,128)S(1)}, u32[]{:S(2)}, u32[]{:S(2)}) collective-permute-start(f32[8,2,8,256]{3,2,1,0:T(8,128)S(1)} %get-tuple-element.66), channel_id=1, source_target_pairs={{0,2},{1,3},{2,0},{3,1},{4,6},{5,7},{6,4},{7,5},{8,10},{9,11},{10,... | collective-permute-start | bytes 393224 | tf_op jit(solution)/shard_map/ppermute | solution.py:61
  131.4 4.3 %collective-permute-start.9 = (f32[32,136,128]{2,1,0:T(8,128)S(1)}, f32[32,136,128]{2,1,0:T(8,128)S(1)}, u32[]{:S(2)}, u32[]{:S(2)}) collective-permute-start(f32[32,136,128]{2,1,0:T(8,128)S(1)} %all-to-all-done.2.half), channel_id=1, source_target_pairs={{0,1},{1,0},{2,3},{3,2},{4,5},{5,4},{6,7},{7,6},{8,9},{9,8},{10,11... | collective-permute-start | bytes 6684680 | tf_op jit(solution)/shard_map/ppermute | solution.py:37
